TPU v7x, 32 devices: a whole 2x2x4 slice. The times are simulated.
32 devices in a mesh: rep: 4 (over y, core), grp: 8 (over z, x).
Axes of the slice: x: 2, y: 2, z: 4, core: 2. Of those that a mesh axis runs over, the one named last changes fastest.
Arguments:
- master_weight: float32 [16, 384, 2048], P('grp', 'rep'), may hold values from -0.3125 to 0.3125
- m_code: bfloat16 [16, 384, 2048], P('grp', 'rep'), may hold values from -1 to 1
- m_scale: float32 [16, 384, 16], P('grp', 'rep'), may hold values from 0.1 to 3
- v_code: bfloat16 [16, 384, 2048], P('grp', 'rep'), may hold values from 0.0099487305 to 1
- v_scale: float32 [16, 384, 16], P('grp', 'rep'), may hold values from 0.1 to 3
- placement: int32 [16], replicated, may hold values from 0 to 15, each once
- route: int32 [8192], P(('rep', 'grp')), may hold values from 0 to 15, as said below
- x_rows: bfloat16 [8192, 384], P(('rep', 'grp')), may hold values from -6 to 6
- y_cot: bfloat16 [8192, 2048], P(('rep', 'grp')), may hold values from -6 to 6
Outputs:
- y_rows: bfloat16 [8192, 2048], P(('rep', 'grp'))
- x_grad: bfloat16 [8192, 384], P(('rep', 'grp'))
- master_next: float32 [16, 384, 2048], P('grp', 'rep')
- m_code_next: bfloat16 [16, 384, 2048], P('grp', 'rep')
- m_scale_next: float32 [16, 384, 16], P('grp', 'rep')
- v_code_next: bfloat16 [16, 384, 2048], P('grp', 'rep')
- v_scale_next: float32 [16, 384, 16], P('grp', 'rep')
Inputs may be any that keep to these rules, and one draw needn't show every extreme that they name: Each expert once; slot s of the weight and moment arrays holds the expert placement[s]. `route`: in the 256 rows of one device no expert appears more than 24 times, and one expert appears exactly 24 times in the rows of every device.
All inputs are finite; a program needn't handle non-finite values. Where the computation divides by a largest or mean magnitude, that divisor is 1e-20 or more.
Results may differ from a plain program's by a relative error of at most 0.015.
Values may be sent and summed in bfloat16 or wider, within the bound.
No kernel may reach another device: no remote copies, remote signals or barrier semaphores. Data moves between devices by JAX's collectives and lax.ppermute only.
A program may use at most 64 MiB of HBM per device.

v0:
```python
import jax
import jax.numpy as jnp
from jax import lax
from jax.sharding import PartitionSpec as P

BLOCK = 128
ADAM_STEP = 100


beta_one = 0.9
beta_two = 0.95
learn_rate = 0.01


def adam_update(master_weight, grad, m_code, m_scale, v_code, v_scale):
    full_shape = master_weight.shape
    blocked = full_shape[:-1] + (full_shape[-1] // BLOCK, BLOCK)
    m_old = (m_code.astype(jnp.float32).reshape(blocked) * m_scale[..., None]).reshape(full_shape)
    v_old = (v_code.astype(jnp.float32).reshape(blocked) * v_scale[..., None]).reshape(full_shape)
    m_next = beta_one * m_old + (1.0 - beta_one) * grad
    v_next = beta_two * v_old + (1.0 - beta_two) * grad * grad
    corr_one = 1.0 - beta_one**ADAM_STEP
    corr_two = 1.0 - beta_two**ADAM_STEP
    step_size = m_next / corr_one / (jnp.sqrt(v_next / corr_two) + 1e-08)
    master_next = master_weight - learn_rate * step_size
    m_blocks = m_next.reshape(blocked)
    v_blocks = v_next.reshape(blocked)
    m_scale_next = jnp.max(jnp.abs(m_blocks), axis=-1) + 1e-06
    v_scale_next = jnp.max(v_blocks, axis=-1) + 1e-06
    m_code_next = (m_blocks / m_scale_next[..., None]).reshape(full_shape).astype(jnp.bfloat16)
    v_code_next = (v_blocks / v_scale_next[..., None]).reshape(full_shape).astype(jnp.bfloat16)
    return (master_next, m_code_next, m_scale_next, v_code_next, v_scale_next)


def per_device(master_weight, m_code, m_scale, v_code, v_scale, placement, route, x_rows, y_cot):
    local_count, slice_rows, model_width = master_weight.shape
    row_count, hidden_width = x_rows.shape
    expert_count = placement.shape[0]
    groups = lax.axis_size("grp")
    replicas = lax.axis_size("rep")
    grad_factor = float(row_count * groups * replicas // expert_count) ** (-0.5)
    capacity = max(2, (3 * row_count + 2 * expert_count - 1) // (2 * expert_count))
    slot_rows = groups * capacity
    expert_ids = lax.iota(jnp.int32, expert_count)
    route_hot = (route[:, None] == expert_ids[None, :]).astype(jnp.int32)
    position = jnp.sum(route_hot * (jnp.cumsum(route_hot, axis=0) - 1), axis=1)
    slot = jnp.sum(jnp.where(placement[None, :] == route[:, None], expert_ids[None, :], 0), axis=1)
    target = slot % local_count * slot_rows + slot // local_count * capacity + position
    places = (target[:, None] == lax.iota(jnp.int32, local_count * slot_rows)[None, :]).astype(
        jnp.bfloat16
    )
    column_dims = (((0,), (0,)), ((), ()))
    send_x = lax.dot_general(
        places, x_rows, column_dims, preferred_element_type=jnp.float32
    ).astype(jnp.bfloat16)
    send_g = lax.dot_general(places, y_cot, column_dims, preferred_element_type=jnp.float32).astype(
        jnp.bfloat16
    )
    send_x = send_x.reshape(local_count, groups, capacity, hidden_width)
    send_g = send_g.reshape(local_count, groups, capacity, model_width)
    recv_x, recv_g = (
        lax.all_to_all(send_x, "grp", split_axis=1, concat_axis=1, tiled=True),
        lax.all_to_all(send_g, "grp", split_axis=1, concat_axis=1, tiled=True),
    )
    local_x = recv_x.reshape(local_count, slot_rows, hidden_width)
    local_g = recv_g.reshape(local_count, slot_rows, model_width)
    weight_slice = master_weight.astype(jnp.bfloat16)
    weight_rows = lax.all_gather(weight_slice, "rep", axis=1, tiled=True)
    y_total = jnp.einsum("esn,end->esd", local_x, weight_rows, preferred_element_type=jnp.float32)
    dx_part = jnp.einsum("esd,end->esn", local_g, weight_rows, preferred_element_type=jnp.float32)
    dx_total = dx_part
    y_total, dx_total = (y_total, dx_total)
    back_y = y_total.astype(jnp.bfloat16).reshape(local_count, groups, capacity, model_width)
    back_dx = dx_total.astype(jnp.bfloat16).reshape(local_count, groups, capacity, hidden_width)
    home_y, home_dx = (
        lax.all_to_all(back_y, "grp", split_axis=1, concat_axis=1, tiled=True),
        lax.all_to_all(back_dx, "grp", split_axis=1, concat_axis=1, tiled=True),
    )
    y_rows = jnp.dot(
        places, home_y.reshape(-1, model_width), preferred_element_type=jnp.float32
    ).astype(jnp.bfloat16)
    x_grad = jnp.dot(
        places, home_dx.reshape(-1, hidden_width), preferred_element_type=jnp.float32
    ).astype(jnp.bfloat16)
    grad_parts = []
    for member in range(local_count):
        outer = jnp.einsum(
            "sf,sd->fd", local_x[member], local_g[member], preferred_element_type=jnp.float32
        )
        grad_parts.append((outer * grad_factor).astype(jnp.bfloat16))
    part_grad = jnp.stack(grad_parts)
    grad = lax.psum_scatter(part_grad, "rep", scatter_dimension=1, tiled=True).astype(jnp.float32)
    master_next, m_code_next, m_scale_next, v_code_next, v_scale_next = adam_update(
        master_weight, grad, m_code, m_scale, v_code, v_scale
    )
    return (y_rows, x_grad, master_next, m_code_next, m_scale_next, v_code_next, v_scale_next)


def solution(mesh):
    return jax.shard_map(
        per_device,
        mesh=mesh,
        in_specs=(
            P("grp", "rep", None),
            P("grp", "rep", None),
            P("grp", "rep", None),
            P("grp", "rep", None),
            P("grp", "rep", None),
            P(),
            P(("rep", "grp")),
            P(("rep", "grp"), None),
            P(("rep", "grp"), None),
        ),
        out_specs=(
            P(("rep", "grp"), None),
            P(("rep", "grp"), None),
            P("grp", "rep", None),
            P("grp", "rep", None),
            P("grp", "rep", None),
            P("grp", "rep", None),
            P("grp", "rep", None),
        ),
        check_vma=False,
    )
```

profile of v0, /device:TPU:0, one launch (start us, length us, event | category | flops | bytes accessed | tf_op | source)
XLA Modules:
  0.0 219.7 jit_solution(9549217842946027149)
XLA Ops:
  7.2 0.0 copy-start
  7.2 0.8 fusion.12
  8.0 0.6 reduce-window.6
  8.5 0.2 slice_reduce_fusion
  8.8 0.8 select_reduce_fusion
  9.5 1.3 convolution_convert_fusion.3
  10.9 0.7 copy.41
  11.6 7.3 %all-to-all-start = ((bf16[2,8,24,384]{3,2,0,1:T(8,128)(2,1)}), bf16[2,8,24,384]{3,2,0,1:T(8,128)(2,1)S(1)}, u32[]{:S(2)}, u32[]{:S(2)}) async-start(bf16[2,8,24,384]{3,2,0,1:T(8,128)(2,1)} %copy.41), calls=%async_computation | async-start | bytes 589824 | tf_op jit(solution)/shard_map/all_to_all | solution.py:62
  18.9 0.0 reduce-scatter.2.cloned.1.call-start
  18.9 0.0 copy-done
  18.9 0.7 convolution_convert_fusion.1
  19.6 0.2 copy.45
  19.8 8.7 %all-to-all-done = bf16[2,8,24,384]{3,2,0,1:T(8,128)(2,1)S(1)} async-done(((bf16[2,8,24,384]{3,2,0,1:T(8,128)(2,1)}), bf16[2,8,24,384]{3,2,0,1:T(8,128)(2,1)S(1)}, u32[]{:S(2)}, u32[]{:S(2)}) %all-to-all-start) | async-done | bytes 294944 | tf_op jit(solution)/shard_map/all_to_all | solution.py:62
  28.5 0.0 copy-start.4
  28.5 40.0 %all_to_all.20 = bf16[2,8,24,2048]{3,2,0,1:T(8,128)(2,1)S(1)} all-to-all(bf16[2,8,24,2048]{3,2,0,1:T(8,128)(2,1)S(1)} %copy.45), channel_id=1, replica_groups=mesh['rep'=4,'grp'=8] {'grp'}, dimensions={1} | all-to-all | bytes 3145728 | tf_op jit(solution)/shard_map/all_to_all | solution.py:63
  68.5 0.0 copy-start.2
  68.5 0.6 fusion.2
  69.1 0.0 copy-done.4
  69.1 0.5 copy-done.2
  69.7 0.6 fusion.3
  70.3 1.9 pad_maximum_fusion
  72.2 0.0 copy-start.6
  72.2 0.0 reduce-scatter.2.cloned.1.call-update
  72.2 0.0 all-gather.2.cloned.1.call-start
  72.3 0.6 copy-done.6
  72.9 0.1 copy.49
  73.0 1.6 mul.89
  74.6 1.5 mul.90
  76.2 0.0 copy-done.7
  76.2 0.0 copy-start.1
  76.2 0.1 copy.54
  76.3 1.6 mul.98
  77.9 2.8 %mul.99 = f32[2,96,2048]{2,1,0:T(8,128)} reshape(f32[2,96,16,128]{3,2,1,0:T(8,128)} %mul.98) | data formatting | bytes 3145728 | tf_op jit(solution)/shard_map/mul | solution.py:19
  80.7 28.6 %reduce-scatter.2.cloned.1.call-done = bf16[2,96,2048]{2,1,0:T(8,128)(2,1)} async-done(((bf16[2,384,2048]{2,1,0:T(8,128)(2,1)}), bf16[2,96,2048]{2,1,0:T(8,128)(2,1)}) %reduce-scatter.2.cloned.1.call-update) | async-done | bytes 786448 | tf_op jit(solution)/shard_map/reduce_scatter | solution.py:92
  109.3 0.0 copy-done.1
  109.3 0.0 copy-done.3
  109.3 1.5 fusion.16
  110.8 0.3 copy.58
  111.1 0.5 bitcast_reduce_fusion.1
  111.6 0.5 div.55
  112.1 1.4 div.56
  113.5 6.7 %multiply_subtract_fusion = (f32[2,96,2048]{2,1,0:T(8,128)}, f32[2,96,2048]{2,1,0:T(8,128)S(1)}, bf16[2,96,2048]{2,1,0:T(8,128)(2,1)}, bf16[2,96,2048]{2,1,0:T(8,128)(2,1)}) fusion(f32[2,96,2048]{2,1,0:T(8,128)} %param.9, bf16[2,96,2048]{2,1,0:T(8,128)(2,1)} %reduce-scatter.2.cloned.1.call-done, f32[2,96,2048]{2,1,0:T(8,128)} %copy-done.1, ...), kind=kLoop, calls=%fused_computation.18 | loop fusion | flops 8257536 | bytes 13369344 | tf_op jit(solution)/shard_map/sub | solution.py:25
  120.2 0.0 all-gather.2.cloned.1.call-update
  120.2 2.8 %copy.46 = bf16[2,8,24,2048]{3,2,1,0:T(8,128)(2,1)} copy(bf16[2,8,24,2048]{3,2,0,1:T(8,128)(2,1)} %copy-done.2) | data formatting | bytes 3145728 | tf_op jit(solution)/shard_map/all_to_all | solution.py:63
  123.0 26.0 %all-gather.2.cloned.1.call-done = bf16[2,384,2048]{2,1,0:T(8,128)(2,1)} async-done(((bf16[2,96,2048]{2,1,0:T(8,128)(2,1)}), bf16[2,384,2048]{2,1,0:T(8,128)(2,1)}) %all-gather.2.cloned.1.call-update) | async-done | bytes 3145744 | tf_op jit(solution)/shard_map/all_gather | solution.py:68
  148.9 3.6 %convolution_convert_fusion.4 = bf16[2,192,384]{2,1,0:T(8,128)(2,1)S(1)} fusion(bf16[2,192,2048]{2,1,0:T(8,128)(2,1)} %bitcast.81, bf16[2,384,2048]{2,1,0:T(8,128)(2,1)} %all-gather.2.cloned.1.call-done), kind=kOutput, calls=%fused_computation.20 | convolution fusion | flops 604127232 | bytes 5013504 | tf_op jit(solution)/shard_map/esd,end->esn/dot_general | solution.py:70
  152.5 0.7 copy.47
  153.2 5.5 %all-to-all-start.3 = ((bf16[2,8,24,384]{3,2,0,1:T(8,128)(2,1)}), bf16[2,8,24,384]{3,2,0,1:T(8,128)(2,1)S(1)}, u32[]{:S(2)}, u32[]{:S(2)}) async-start(bf16[2,8,24,384]{3,2,0,1:T(8,128)(2,1)} %copy.47), calls=%async_computation.3 | async-start | bytes 589824 | tf_op jit(solution)/shard_map/all_to_all | solution.py:77
  158.7 0.0 copy-done.5
  158.8 2.9 %convolution_convert_fusion = bf16[2,192,2048]{2,1,0:T(8,128)(2,1)S(1)} fusion(bf16[2,192,384]{2,1,0:T(8,128)(2,1)S(1)} %bitcast.88, bf16[2,384,2048]{2,1,0:T(8,128)(2,1)} %all-gather.2.cloned.1.call-done), kind=kOutput, calls=%fused_computation.5 | convolution fusion | flops 604766208 | bytes 5013504 | tf_op jit(solution)/shard_map/esn,end->esd/dot_general | solution.py:69
  161.7 1.2 copy.43
  162.9 5.8 %all-to-all-done.3 = bf16[2,8,24,384]{3,2,0,1:T(8,128)(2,1)S(1)} async-done(((bf16[2,8,24,384]{3,2,0,1:T(8,128)(2,1)}), bf16[2,8,24,384]{3,2,0,1:T(8,128)(2,1)S(1)}, u32[]{:S(2)}, u32[]{:S(2)}) %all-to-all-start.3) | async-done | bytes 294944 | tf_op jit(solution)/shard_map/all_to_all | solution.py:77
  168.7 4.5 %all-to-all-start.1 = ((bf16[2,8,24,2048]{3,2,0,1:T(8,128)(2,1)}), bf16[2,8,24,2048]{3,2,0,1:T(8,128)(2,1)}, u32[]{:S(2)}, u32[]{:S(2)}) async-start(bf16[2,8,24,2048]{3,2,0,1:T(8,128)(2,1)} %copy.43), calls=%async_computation.1 | async-start | bytes 3145728 | tf_op jit(solution)/shard_map/all_to_all | solution.py:76
  173.2 0.7 copy.55
  173.9 0.3 copy.59
  174.1 0.5 bitcast_reduce_fusion
  174.6 0.7 copy.56
  175.3 1.6 div.58
  176.9 2.6 %div.59 = f32[2,96,2048]{2,1,0:T(8,128)} reshape(f32[2,96,16,128]{3,2,1,0:T(8,128)} %div.58) | data formatting | bytes 3145728 | tf_op jit(solution)/shard_map/div | solution.py:31
  179.5 2.5 %divide_convert_fusion = bf16[2,96,2048]{2,1,0:T(8,128)(2,1)} fusion(f32[2,96,2048]{2,1,0:T(8,128)S(1)} %get-tuple-element.24, f32[2,96,2048]{2,1,0:T(8,128)} %div.59), kind=kLoop, calls=%fused_computation.16 | loop fusion | flops 786432 | bytes 3932160 | tf_op jit(solution)/shard_map/convert_element_type | solution.py:31
  182.0 1.0 convolution_convert_fusion.5
  183.1 26.5 %all-to-all-done.1 = bf16[2,8,24,2048]{3,2,0,1:T(8,128)(2,1)} async-done(((bf16[2,8,24,2048]{3,2,0,1:T(8,128)(2,1)}), bf16[2,8,24,2048]{3,2,0,1:T(8,128)(2,1)}, u32[]{:S(2)}, u32[]{:S(2)}) %all-to-all-start.1) | async-done | bytes 1572896 | tf_op jit(solution)/shard_map/all_to_all | solution.py:76
  209.6 1.5 copy.44
  211.1 1.7 convolution_convert_fusion.2
  (10 shorter events, 0.1 us)
Async XLA Ops:
  7.2 11.8 %copy-start = (bf16[256,2048]{1,0:T(8,128)(2,1)S(1)}, bf16[256,2048]{1,0:T(8,128)(2,1)}, u32[]{:S(2)}) copy-start(bf16[256,2048]{1,0:T(8,128)(2,1)} %param.17) | copy-start | bytes 3145732
  11.6 16.9 %all-to-all-start = ((bf16[2,8,24,384]{3,2,0,1:T(8,128)(2,1)}), bf16[2,8,24,384]{3,2,0,1:T(8,128)(2,1)S(1)}, u32[]{:S(2)}, u32[]{:S(2)}) async-start(bf16[2,8,24,384]{3,2,0,1:T(8,128)(2,1)} %copy.41), calls=%async_computation | async-start | bytes 589824 | tf_op jit(solution)/shard_map/all_to_all | solution.py:62
  18.9 90.4 %reduce-scatter.2.cloned.1.call-start = ((), (), s32[]{:S(2)}) async-start(), calls=%async_computation.6 | async-start | bytes 3932160 | tf_op jit(solution)/shard_map/reduce_scatter | solution.py:92
  28.5 40.6 %copy-start.4 = (bf16[2,8,24,384]{3,2,0,1:T(8,128)(2,1)}, bf16[2,8,24,384]{3,2,0,1:T(8,128)(2,1)S(1)}, u32[]{:S(2)}) copy-start(bf16[2,8,24,384]{3,2,0,1:T(8,128)(2,1)S(1)} %all-to-all-done) | copy-start | bytes 884740
  68.5 1.1 copy-start.2
  72.2 0.7 copy-start.6
  72.2 76.7 %all-gather.2.cloned.1.call-start = ((), (), s32[]{:S(2)}) async-start(), calls=%async_computation.5 | async-start | bytes 3932160 | tf_op jit(solution)/shard_map/all_gather | solution.py:68
  74.6 1.5 copy-start.7
  76.2 33.1 %copy-start.1 = (f32[2,96,2048]{2,1,0:T(8,128)}, f32[2,96,2048]{2,1,0:T(8,128)S(1)}, u32[]{:S(2)}) copy-start(f32[2,96,2048]{2,1,0:T(8,128)S(1)} %mul.90) | copy-start | bytes 4718596
  77.9 31.4 %copy-start.3 = (bf16[2,96,2048]{2,1,0:T(8,128)(2,1)S(1)}, bf16[2,96,2048]{2,1,0:T(8,128)(2,1)}, u32[]{:S(2)}) copy-start(bf16[2,96,2048]{2,1,0:T(8,128)(2,1)} %param.10) | copy-start | bytes 2359300
  148.9 9.8 %copy-start.5 = (bf16[2,8,24,384]{3,2,0,1:T(8,128)(2,1)S(1)}, bf16[2,8,24,384]{3,2,0,1:T(8,128)(2,1)}, u32[]{:S(2)}) copy-start(bf16[2,8,24,384]{3,2,0,1:T(8,128)(2,1)} %copy-done.4) | copy-start | bytes 884740
  153.2 15.5 %all-to-all-start.3 = ((bf16[2,8,24,384]{3,2,0,1:T(8,128)(2,1)}), bf16[2,8,24,384]{3,2,0,1:T(8,128)(2,1)S(1)}, u32[]{:S(2)}, u32[]{:S(2)}) async-start(bf16[2,8,24,384]{3,2,0,1:T(8,128)(2,1)} %copy.47), calls=%async_computation.3 | async-start | bytes 589824 | tf_op jit(solution)/shard_map/all_to_all | solution.py:77
  168.7 40.9 %all-to-all-start.1 = ((bf16[2,8,24,2048]{3,2,0,1:T(8,128)(2,1)}), bf16[2,8,24,2048]{3,2,0,1:T(8,128)(2,1)}, u32[]{:S(2)}, u32[]{:S(2)}) async-start(bf16[2,8,24,2048]{3,2,0,1:T(8,128)(2,1)} %copy.43), calls=%async_computation.1 | async-start | bytes 3145728 | tf_op jit(solution)/shard_map/all_to_all | solution.py:76
Sparse Core Ops, SparseCore 0:
  72.4 36.9 reduce-scatter.1
  120.3 28.5 all-gather.1
where the time goes:
time: 220 us
  waiting for transfers between devices  95.6 us (43%)
  blocking collectives  40 us (18%)
  local copies, waits for them, and re-layouts  24.3 us (11%)
  starting transfers between devices  17.3 us (8%)
  other arithmetic  15.8 us (7%)
  between operations  14.2 us (6%)
  matrix products  12.4 us (6%)
    all_to_all x1, blocking collectives, per_device(): lax.all_to_all(send_g, 'grp', split_axis=1, concat_axis=1, tiled=True)  40 us
    reduce_scatter x1, waiting for transfers between devices, per_device(): lax.psum_scatter(part_grad, 'rep', scatter_dimension=1, tiled=True)  28.6 us
    all_to_all x1, waiting for transfers between devices, per_device(): lax.all_to_all(back_y, 'grp', split_axis=1, concat_axis=1, tiled=True)  26.5 us
    all_gather x1, waiting for transfers between devices, per_device(): weight_rows = lax.all_gather(weight_slice, 'rep', axis=1, tiled=True)  26 us
    all_to_all x1, waiting for transfers between devices, per_device(): lax.all_to_all(send_x, 'grp', split_axis=1, concat_axis=1, tiled=True)  8.7 us
    all_to_all x1, starting transfers between devices, per_device(): lax.all_to_all(send_x, 'grp', split_axis=1, concat_axis=1, tiled=True)  7.25 us
    sub x1, other arithmetic, adam_update(): master_next = master_weight - learn_rate * step_size  6.69 us
    all_to_all x1, waiting for transfers between devices, per_device(): lax.all_to_all(back_dx, 'grp', split_axis=1, concat_axis=1, tiled=True)  5.79 us
  transfers between devices with their start and end apart: 5, of which 5 were waited for; matrix products, arithmetic and copies ran while one was open for 12% of the time, Pallas kernels for 0%

commit v1 on v0

v1 whole, which is shorter than its diff:
```python
import functools

import jax
import jax.numpy as jnp
from jax import lax
from jax.experimental import pallas as pl
from jax.experimental.pallas import tpu as pltpu
from jax.sharding import PartitionSpec as P

BLOCK = 128
ADAM_STEP = 100

beta_one = 0.9
beta_two = 0.95
learn_rate = 0.01

VMEM_LIMIT = 40 * 1024 * 1024
F32 = jnp.float32
BF16 = jnp.bfloat16


def cost(flops, nbytes):
    return pl.CostEstimate(flops=int(flops), bytes_accessed=int(nbytes), transcendentals=0)


def params(*semantics):
    if semantics:
        return pltpu.CompilerParams(vmem_limit_bytes=VMEM_LIMIT, dimension_semantics=semantics)
    return pltpu.CompilerParams(vmem_limit_bytes=VMEM_LIMIT)


def row_targets(route_row, placement_col, capacity):
    expert_count = placement_col.shape[0]
    row_count = route_row.shape[1]
    hot = (placement_col == route_row).astype(F32)
    earlier = lax.broadcasted_iota(jnp.int32, (row_count, row_count), 0)
    later = lax.broadcasted_iota(jnp.int32, (row_count, row_count), 1)
    before = (earlier < later).astype(F32).astype(BF16)
    position = jnp.dot(hot.astype(BF16), before, preferred_element_type=F32)
    start = lax.broadcasted_iota(jnp.int32, (expert_count, row_count), 0) * capacity
    return jnp.sum(hot * (start.astype(F32) + position), axis=0, keepdims=True).astype(jnp.int32)


def place_matrix(target, places):
    slots = lax.broadcasted_iota(jnp.int32, (places, target.shape[1]), 0)
    return (slots == target).astype(F32).astype(BF16)


def dispatch_x_kernel(capacity, route_ref, placement_ref, x_ref, sent_ref, target_ref):
    target = row_targets(route_ref[...], placement_ref[...], capacity)
    target_ref[...] = target
    places = place_matrix(target, sent_ref.shape[0])
    sent_ref[...] = jnp.dot(places, x_ref[...], preferred_element_type=F32).astype(BF16)


def dispatch_x(route, placement, x_rows, capacity):
    row_count, hidden = x_rows.shape
    places = placement.shape[0] * capacity
    return pl.pallas_call(
        functools.partial(dispatch_x_kernel, capacity),
        out_shape=(
            jax.ShapeDtypeStruct((places, hidden), BF16),
            jax.ShapeDtypeStruct((1, row_count), jnp.int32),
        ),
        compiler_params=params(),
        cost_estimate=cost(2 * places * row_count * hidden, 2 * (places + row_count) * hidden),
    )(route.reshape(1, row_count), placement.reshape(-1, 1), x_rows)


def dispatch_g_kernel(target_ref, g_ref, sent_ref):
    places = place_matrix(target_ref[...], sent_ref.shape[0])
    sent_ref[...] = jnp.dot(places, g_ref[...], preferred_element_type=F32).astype(BF16)


def dispatch_g(target, y_cot, places):
    row_count, width = y_cot.shape
    tile = min(width, 512)
    return pl.pallas_call(
        dispatch_g_kernel,
        grid=(width // tile,),
        in_specs=[
            pl.BlockSpec((1, row_count), lambda j: (0, 0)),
            pl.BlockSpec((row_count, tile), lambda j: (0, j)),
        ],
        out_specs=pl.BlockSpec((places, tile), lambda j: (0, j)),
        out_shape=jax.ShapeDtypeStruct((places, width), BF16),
        compiler_params=params("arbitrary"),
        cost_estimate=cost(2 * places * row_count * width, 2 * (places + row_count) * width),
    )(target, y_cot)


def collect_kernel(target_ref, home_ref, out_ref):
    places = place_matrix(target_ref[...], home_ref.shape[0])
    out_ref[...] = lax.dot_general(
        places, home_ref[...], (((0,), (0,)), ((), ())), preferred_element_type=F32
    ).astype(BF16)


def collect(target, home):
    places, width = home.shape
    row_count = target.shape[1]
    tile = min(width, 512)
    return pl.pallas_call(
        collect_kernel,
        grid=(width // tile,),
        in_specs=[
            pl.BlockSpec((1, row_count), lambda j: (0, 0)),
            pl.BlockSpec((places, tile), lambda j: (0, j)),
        ],
        out_specs=pl.BlockSpec((row_count, tile), lambda j: (0, j)),
        out_shape=jax.ShapeDtypeStruct((row_count, width), BF16),
        compiler_params=params("arbitrary"),
        cost_estimate=cost(2 * places * row_count * width, 2 * (places + row_count) * width),
    )(target, home)


def member_rows(rows, capacity, local_count):
    index = lax.broadcasted_iota(jnp.int32, (rows, 1), 0)
    return lax.rem(index, capacity * local_count) // capacity


def spread(x, capacity, local_count):
    member = member_rows(x.shape[0], capacity, local_count)
    zero = jnp.zeros_like(x)
    return jnp.concatenate([jnp.where(member == e, x, zero) for e in range(local_count)], axis=1)


def forward_kernel(capacity, local_count, x_ref, w_ref, y_ref):
    wide = spread(x_ref[...], capacity, local_count)
    weight = w_ref[...].reshape(wide.shape[1], w_ref.shape[-1])
    y_ref[...] = jnp.dot(wide, weight, preferred_element_type=F32).astype(BF16)


def forward(x, weight, capacity):
    rows, hidden = x.shape
    local_count, _, width = weight.shape
    tile = min(width, 512)
    return pl.pallas_call(
        functools.partial(forward_kernel, capacity, local_count),
        grid=(width // tile,),
        in_specs=[
            pl.BlockSpec((rows, hidden), lambda j: (0, 0)),
            pl.BlockSpec((local_count, hidden, tile), lambda j: (0, 0, j)),
        ],
        out_specs=pl.BlockSpec((rows, tile), lambda j: (0, j)),
        out_shape=jax.ShapeDtypeStruct((rows, width), BF16),
        compiler_params=params("arbitrary"),
        cost_estimate=cost(
            2 * rows * local_count * hidden * width,
            2 * (local_count * hidden + rows) * width,
        ),
    )(x, weight)


def gradient_kernel(capacity, local_count, factor, x_ref, g_ref, out_ref):
    wide = spread(x_ref[...], capacity, local_count)
    outer = lax.dot_general(
        wide, g_ref[...], (((0,), (0,)), ((), ())), preferred_element_type=F32
    )
    out_ref[...] = (outer * factor).astype(BF16).reshape(out_ref.shape)


def gradient(x, g, capacity, local_count, factor):
    rows, hidden = x.shape
    width = g.shape[1]
    tile = min(width, 512)
    return pl.pallas_call(
        functools.partial(gradient_kernel, capacity, local_count, factor),
        grid=(width // tile,),
        in_specs=[
            pl.BlockSpec((rows, hidden), lambda j: (0, 0)),
            pl.BlockSpec((rows, tile), lambda j: (0, j)),
        ],
        out_specs=pl.BlockSpec((local_count, hidden, tile), lambda j: (0, 0, j)),
        out_shape=jax.ShapeDtypeStruct((local_count, hidden, width), BF16),
        compiler_params=params("arbitrary"),
        cost_estimate=cost(
            2 * rows * local_count * hidden * width,
            2 * (local_count * hidden + rows) * width,
        ),
    )(x, g)


def backward_kernel(capacity, local_count, g_ref, w_ref, dx_ref, total_ref):
    step = pl.program_id(0)
    hidden = dx_ref.shape[1]
    weight = w_ref[...].reshape(local_count * hidden, w_ref.shape[-1])
    part = lax.dot_general(
        g_ref[...], weight, (((1,), (1,)), ((), ())), preferred_element_type=F32
    )

    @pl.when(step == 0)
    def _():
        total_ref[...] = part

    @pl.when(step > 0)
    def _():
        total_ref[...] += part

    @pl.when(step == pl.num_programs(0) - 1)
    def _():
        member = member_rows(dx_ref.shape[0], capacity, local_count)
        picked = total_ref[:, :hidden]
        for e in range(1, local_count):
            picked = jnp.where(member == e, total_ref[:, e * hidden : (e + 1) * hidden], picked)
        dx_ref[...] = picked.astype(BF16)


def backward(g, weight, capacity):
    rows, width = g.shape
    local_count, hidden, _ = weight.shape
    tile = min(width, 512)
    return pl.pallas_call(
        functools.partial(backward_kernel, capacity, local_count),
        grid=(width // tile,),
        in_specs=[
            pl.BlockSpec((rows, tile), lambda j: (0, j)),
            pl.BlockSpec((local_count, hidden, tile), lambda j: (0, 0, j)),
        ],
        out_specs=pl.BlockSpec((rows, hidden), lambda j: (0, 0)),
        out_shape=jax.ShapeDtypeStruct((rows, hidden), BF16),
        scratch_shapes=[pltpu.VMEM((rows, local_count * hidden), F32)],
        compiler_params=params("arbitrary"),
        cost_estimate=cost(
            2 * rows * local_count * hidden * width,
            2 * (local_count * hidden + rows) * width,
        ),
    )(g, weight)


def adam_kernel(
    master_ref, grad_ref, mc_ref, ms_ref, vc_ref, vs_ref,
    master_out, mc_out, ms_out, vc_out, vs_out,
):
    blocks = ms_ref.shape[-1]
    rows = ms_ref.shape[1]
    corr_one = 1.0 - beta_one**ADAM_STEP
    corr_two = 1.0 - beta_two**ADAM_STEP
    m_scales = ms_ref[0]
    v_scales = vs_ref[0]
    lane = lax.broadcasted_iota(jnp.int32, (rows, blocks), 1)
    m_tops = jnp.zeros((rows, blocks), F32)
    v_tops = jnp.zeros((rows, blocks), F32)
    for b in range(blocks):
        cols = slice(b * BLOCK, (b + 1) * BLOCK)
        grad = grad_ref[0, :, cols].astype(F32)
        m_old = mc_ref[0, :, cols].astype(F32) * m_scales[:, b : b + 1]
        v_old = vc_ref[0, :, cols].astype(F32) * v_scales[:, b : b + 1]
        m_next = beta_one * m_old + (1.0 - beta_one) * grad
        v_next = beta_two * v_old + (1.0 - beta_two) * grad * grad
        step_size = m_next / corr_one / (jnp.sqrt(v_next / corr_two) + 1e-08)
        master_out[0, :, cols] = master_ref[0, :, cols] - learn_rate * step_size
        m_top = jnp.max(jnp.abs(m_next), axis=-1, keepdims=True) + 1e-06
        v_top = jnp.max(v_next, axis=-1, keepdims=True) + 1e-06
        mc_out[0, :, cols] = (m_next * (1.0 / m_top)).astype(BF16)
        vc_out[0, :, cols] = (v_next * (1.0 / v_top)).astype(BF16)
        m_tops = jnp.where(lane == b, m_top, m_tops)
        v_tops = jnp.where(lane == b, v_top, v_tops)
    ms_out[0] = m_tops
    vs_out[0] = v_tops


def adam(master_weight, grad, m_code, m_scale, v_code, v_scale):
    members, rows, width = master_weight.shape
    blocks = m_scale.shape[-1]
    tile = rows // 3 if rows % 48 == 0 else rows
    big = pl.BlockSpec((1, tile, width), lambda e, i: (e, i, 0))
    small = pl.BlockSpec((1, tile, blocks), lambda e, i: (e, i, 0))
    return pl.pallas_call(
        adam_kernel,
        grid=(members, rows // tile),
        in_specs=[big, big, big, small, big, small],
        out_specs=(big, big, small, big, small),
        out_shape=(
            jax.ShapeDtypeStruct(master_weight.shape, F32),
            jax.ShapeDtypeStruct(master_weight.shape, BF16),
            jax.ShapeDtypeStruct(m_scale.shape, F32),
            jax.ShapeDtypeStruct(master_weight.shape, BF16),
            jax.ShapeDtypeStruct(m_scale.shape, F32),
        ),
        compiler_params=params("arbitrary", "arbitrary"),
        cost_estimate=cost(40 * master_weight.size, 18 * master_weight.size),
    )(master_weight, grad, m_code, m_scale, v_code, v_scale)


def exchange(buffer, groups):
    places, width = buffer.shape
    parts = buffer.reshape(groups, places // groups, width)
    moved = lax.all_to_all(parts, "grp", split_axis=0, concat_axis=0, tiled=True)
    return moved.reshape(places, width)


def per_device(master_weight, m_code, m_scale, v_code, v_scale, placement, route, x_rows, y_cot):
    local_count = master_weight.shape[0]
    row_count = x_rows.shape[0]
    expert_count = placement.shape[0]
    groups = lax.axis_size("grp")
    replicas = lax.axis_size("rep")
    grad_factor = float(row_count * groups * replicas // expert_count) ** (-0.5)
    capacity = max(2, (3 * row_count + 2 * expert_count - 1) // (2 * expert_count))
    places = expert_count * capacity

    weight_slice = master_weight.astype(BF16)
    weight = lax.all_gather(weight_slice, "rep", axis=1, tiled=True)

    send_x, target = dispatch_x(route, placement, x_rows, capacity)
    send_g = dispatch_g(target, y_cot, places)
    local_x = exchange(send_x, groups)
    local_g = exchange(send_g, groups)

    back_y = forward(local_x, weight, capacity)
    home_y = exchange(back_y, groups)

    part_grad = gradient(local_x, local_g, capacity, local_count, grad_factor)
    grad = lax.psum_scatter(part_grad, "rep", scatter_dimension=1, tiled=True)
    back_dx = backward(local_g, weight, capacity)
    home_dx = exchange(back_dx, groups)

    x_grad = collect(target, home_dx)
    updated = adam(master_weight, grad, m_code, m_scale, v_code, v_scale)
    y_rows = collect(target, home_y)
    return (y_rows, x_grad) + tuple(updated)


def solution(mesh):
    return jax.shard_map(
        per_device,
        mesh=mesh,
        in_specs=(
            P("grp", "rep", None),
            P("grp", "rep", None),
            P("grp", "rep", None),
            P("grp", "rep", None),
            P("grp", "rep", None),
            P(),
            P(("rep", "grp")),
            P(("rep", "grp"), None),
            P(("rep", "grp"), None),
        ),
        out_specs=(
            P(("rep", "grp"), None),
            P(("rep", "grp"), None),
            P("grp", "rep", None),
            P("grp", "rep", None),
            P("grp", "rep", None),
            P("grp", "rep", None),
            P("grp", "rep", None),
        ),
        check_vma=False,
    )
```

time: 220 us -> 156 us (0.71)
  waiting for transfers between devices: 95.6 us -> 46.7 us
  Pallas kernels: 0 us -> 25.5 us
  other arithmetic: 15.8 us -> 2.49 us
  matrix products: 12.4 us -> 0 us
  local copies, waits for them, and re-layouts: 24.3 us -> 11.9 us
  starting transfers between devices: 17.3 us -> 14.6 us
    reduce_scatter x1, waiting for transfers between devices: 28.6 us -> 0.01 us  [per_device(): grad = lax.psum_scatter(part_grad, 'rep', scatter_dimension=1, tiled=True)]
    all_gather x1, waiting for transfers between devices: 26 us -> 0.02 us  [per_device(): weight = lax.all_gather(weight_slice, 'rep', axis=1, tiled=True)]
    pallas_call x0 -> x8, Pallas kernels: none -> 25.5 us  [the longest x1 9.12 us: adam(): pl.pallas_call(adam_kernel, grid=(members, rows // tile), in_specs=[big,...]
    dot_general x8 -> x0, matrix products: 12.4 us -> none  [the longest x1 3.56 us: per_device(): jnp.einsum('esd,end->esn', local_g, weight_rows, preferred_element_type=j...]
    unnamed x22 -> x36, local copies, waits for them, and re-layouts: 3.29 us -> 11.8 us
    mul x4 -> x0, local copies, waits for them, and re-layouts: 7.58 us -> none  [the longest x2 4.44 us: adam_update(): v_code.astype(jnp.float32).reshape(blocked) * v_scale[..., None]]
    sub x1 -> x0, other arithmetic: 6.69 us -> none  [adam_update(): master_next = master_weight - learn_rate * step_size]
    div x4 -> x0, local copies, waits for them, and re-layouts: 6.03 us -> none  [the longest x2 4.17 us: adam_update(): v_blocks / v_scale_next[..., None]]
  transfers between devices with their start and end apart: 5 -> 5, of which waited for: 5 -> 3; matrix products, arithmetic and copies ran while one was open for 12% -> 1% of each run, Pallas kernels for 0% -> 11%
where the time goes in v1:
time: 156 us; the launch traced here: 155 us
  waiting for transfers between devices  46.7 us (30%)
  blocking collectives  40 us (26%)
  Pallas kernels  25.5 us (16%)
  starting transfers between devices  14.6 us (9%)
  between operations  14.2 us (9%)
  local copies, waits for them, and re-layouts  11.9 us (8%)
  other arithmetic  2.49 us (2%)
    all_to_all x3, waiting for transfers between devices, exchange(): lax.all_to_all(parts, 'grp', split_axis=0, concat_axis=0, tiled=True)  46.7 us
    all_to_all x1, blocking collectives, exchange(): lax.all_to_all(parts, 'grp', split_axis=0, concat_axis=0, tiled=True)  40 us
    all_to_all x3, starting transfers between devices, exchange(): lax.all_to_all(parts, 'grp', split_axis=0, concat_axis=0, tiled=True)  14.6 us
    unnamed x36, local copies, waits for them, and re-layouts  11.8 us
    pallas_call x1, Pallas kernels, adam(): pl.pallas_call(adam_kernel, grid=(members, rows // tile), in_specs=[big,...  9.12 us
    pallas_call x1, Pallas kernels, backward(): pl.pallas_call(functools.partial(backward_kernel, capacity, local_count),...  3.73 us
    pallas_call x2, Pallas kernels, collect(): pl.pallas_call(collect_kernel, grid=(width // tile,), in_specs=[pl.BlockS...  3.49 us
    pallas_call x1, Pallas kernels, forward(): pl.pallas_call(functools.partial(forward_kernel, capacity, local_count),...  3.43 us
  transfers between devices with their start and end apart: 5, of which 3 were waited for; matrix products, arithmetic and copies ran while one was open for 1% of the time, Pallas kernels for 11%

profile of v1, /device:TPU:0, one launch (start us, length us, event | category | flops | bytes accessed | tf_op | source)
XLA Modules:
  0.0 155.5 jit_solution(6278347306758327336)
XLA Ops:
  7.2 0.0 copy-start.15
  7.2 0.0 copy-start.12
  7.2 0.0 copy-start.11
  7.2 0.0 copy-start.6
  7.2 0.0 all-gather.2.cloned.1.call-start
  7.3 2.5 %convert_element_type.3 = bf16[2,96,2048]{2,1,0:T(8,128)(2,1)} convert(f32[2,96,2048]{2,1,0:T(8,128)} %master_ref.1) | non-fusion elementwise | flops 393216 | bytes 2359296 | tf_op jit(solution)/shard_map/convert_element_type | solution.py:303
  9.7 0.0 all-gather.2.cloned.1.call-update
  9.8 0.0 copy-done.15
  9.8 0.1 copy.16.placement_ref
  9.9 0.0 copy-done.12
  9.9 0.0 copy-done.11
  9.9 1.2 shard_map.144
  11.0 7.3 %all-to-all-start = ((bf16[8,48,384]{2,1,0:T(8,128)(2,1)}), bf16[8,48,384]{2,1,0:T(8,128)(2,1)S(1)}, u32[]{:S(2)}, u32[]{:S(2)}) async-start(bf16[8,48,384]{2,1,0:T(8,128)(2,1)} %bitcast.2), calls=%async_computation | async-start | bytes 589824 | tf_op jit(solution)/shard_map/all_to_all | solution.py:289
  18.3 0.0 reduce-scatter.2.cloned.1.call-start
  18.3 0.0 copy-done.6
  18.3 1.3 shard_map.147
  19.6 8.3 %all-to-all-done = bf16[8,48,384]{2,1,0:T(8,128)(2,1)S(1)} async-done(((bf16[8,48,384]{2,1,0:T(8,128)(2,1)}), bf16[8,48,384]{2,1,0:T(8,128)(2,1)S(1)}, u32[]{:S(2)}, u32[]{:S(2)}) %all-to-all-start) | async-done | bytes 294944 | tf_op jit(solution)/shard_map/all_to_all | solution.py:289
  27.9 40.0 %all_to_all.20 = bf16[8,48,2048]{2,1,0:T(8,128)(2,1)S(1)} all-to-all(bf16[8,48,2048]{2,1,0:T(8,128)(2,1)S(1)} %bitcast.13), channel_id=1, replica_groups=mesh['rep'=4,'grp'=8] {'grp'}, dimensions={0} | all-to-all | bytes 3145728 | tf_op jit(solution)/shard_map/all_to_all | solution.py:289
  67.9 3.3 %shard_map.150 = bf16[2,384,2048]{2,1,0:T(8,128)(2,1)S(1)} custom-call(bf16[384,384]{1,0:T(8,128)(2,1)S(1)} %bitcast.14, bf16[384,2048]{1,0:T(8,128)(2,1)S(1)} %bitcast.10), custom_call_target="tpu_custom_call" | custom-call | flops 1207959552 | bytes 4718592 | tf_op jit(solution)/shard_map/pallas_call | solution.py:167
  71.3 0.0 copy-start.2
  71.3 1.7 %copy-done.2 = bf16[2,384,2048]{2,1,0:T(8,128)(2,1)} copy-done((bf16[2,384,2048]{2,1,0:T(8,128)(2,1)}, bf16[2,384,2048]{2,1,0:T(8,128)(2,1)S(1)}, u32[]{:S(2)}) %copy-start.2) | copy-done | bytes 3145752
  73.0 0.0 reduce-scatter.2.cloned.1.call-update
  73.0 0.0 all-gather.2.cloned.1.call-done.w_ref
  73.0 0.0 copy-start
  73.0 1.9 %copy-done = bf16[2,384,2048]{2,1,0:T(8,128)(2,1)S(1)} copy-done((bf16[2,384,2048]{2,1,0:T(8,128)(2,1)S(1)}, bf16[2,384,2048]{2,1,0:T(8,128)(2,1)}, u32[]{:S(2)}) %copy-start) | copy-done | bytes 3145752
  74.9 3.7 %shard_map.148 = bf16[384,384]{1,0:T(8,128)(2,1)} custom-call(bf16[384,2048]{1,0:T(8,128)(2,1)S(1)} %bitcast.11, bf16[2,384,2048]{2,1,0:T(8,128)(2,1)S(1)} %copy-done), custom_call_target="tpu_custom_call" | custom-call | flops 1207959552 | bytes 4718592 | tf_op jit(solution)/shard_map/pallas_call | solution.py:213
  78.6 3.5 %all-to-all-start.3 = ((bf16[8,48,384]{2,1,0:T(8,128)(2,1)}), bf16[8,48,384]{2,1,0:T(8,128)(2,1)S(1)}, u32[]{:S(2)}, u32[]{:S(2)}) async-start(bf16[8,48,384]{2,1,0:T(8,128)(2,1)} %bitcast.8), calls=%async_computation.3 | async-start | bytes 589824 | tf_op jit(solution)/shard_map/all_to_all | solution.py:289
  82.2 0.0 copy-start.1
  82.2 1.9 %copy-done.1 = bf16[2,384,2048]{2,1,0:T(8,128)(2,1)S(1)} copy-done((bf16[2,384,2048]{2,1,0:T(8,128)(2,1)S(1)}, bf16[2,384,2048]{2,1,0:T(8,128)(2,1)}, u32[]{:S(2)}) %copy-start.1) | copy-done | bytes 3145752
  84.1 3.4 %shard_map.145 = bf16[384,2048]{1,0:T(8,128)(2,1)} custom-call(bf16[384,384]{1,0:T(8,128)(2,1)S(1)} %bitcast.15, bf16[2,384,2048]{2,1,0:T(8,128)(2,1)S(1)} %copy-done.1), custom_call_target="tpu_custom_call" | custom-call | flops 1207959552 | bytes 4718592 | tf_op jit(solution)/shard_map/pallas_call | solution.py:138
  87.6 3.7 %all-to-all-done.3 = bf16[8,48,384]{2,1,0:T(8,128)(2,1)S(1)} async-done(((bf16[8,48,384]{2,1,0:T(8,128)(2,1)}), bf16[8,48,384]{2,1,0:T(8,128)(2,1)S(1)}, u32[]{:S(2)}, u32[]{:S(2)}) %all-to-all-start.3) | async-done | bytes 294944 | tf_op jit(solution)/shard_map/all_to_all | solution.py:289
  91.3 0.0 copy-start.4
  91.3 0.7 copy-done.4
  92.0 0.0 copy-start.13
  92.0 0.0 copy-start.14
  92.0 0.0 copy-start.5
  92.0 3.8 %all-to-all-start.1 = ((bf16[8,48,2048]{2,1,0:T(8,128)(2,1)}), bf16[8,48,2048]{2,1,0:T(8,128)(2,1)S(1)}, u32[]{:S(2)}, u32[]{:S(2)}) async-start(bf16[8,48,2048]{2,1,0:T(8,128)(2,1)} %bitcast.4), calls=%async_computation.1 | async-start | bytes 3145728 | tf_op jit(solution)/shard_map/all_to_all | solution.py:289
  95.8 0.0 copy-done.13
  95.8 0.1 copy.17.ms_ref
  95.9 0.0 copy-done.14
  95.9 0.7 copy.18.vs_ref
  96.6 0.0 copy-start.3
  96.6 0.0 copy-done.5
  96.6 1.0 shard_map.149
  97.6 0.0 copy-start.10
  97.6 34.7 %all-to-all-done.1 = bf16[8,48,2048]{2,1,0:T(8,128)(2,1)S(1)} async-done(((bf16[8,48,2048]{2,1,0:T(8,128)(2,1)}), bf16[8,48,2048]{2,1,0:T(8,128)(2,1)S(1)}, u32[]{:S(2)}, u32[]{:S(2)}) %all-to-all-start.1) | async-done | bytes 1572896 | tf_op jit(solution)/shard_map/all_to_all | solution.py:289
  132.2 2.5 %shard_map.146 = bf16[256,2048]{1,0:T(8,128)(2,1)} custom-call(s32[1,256]{1,0:T(1,128)S(1)} %get-tuple-element.14.target_ref, bf16[384,2048]{1,0:T(8,128)(2,1)S(1)} %bitcast.12), custom_call_target="tpu_custom_call" | custom-call | flops 402653184 | bytes 2621440 | tf_op jit(solution)/shard_map/pallas_call | solution.py:103
  134.7 0.0 reduce-scatter.2.cloned.1.call-done.grad_ref
  134.8 0.0 copy-done.3
  134.8 0.0 copy-done.10
  134.8 0.0 copy-start.7
  134.8 1.1 copy-done.7
  135.9 0.0 copy-start.8
  135.9 1.1 copy-done.8
  137.0 0.0 copy-start.9
  137.0 1.1 copy-done.9
  138.2 9.1 %shard_map.151 = (f32[2,96,2048]{2,1,0:T(8,128)}, bf16[2,96,2048]{2,1,0:T(8,128)(2,1)}, f32[2,96,16]{2,1,0:T(8,128)S(1)}, bf16[2,96,2048]{2,1,0:T(8,128)(2,1)}, f32[2,96,16]{2,1,0:T(8,128)S(1)}) custom-call(f32[2,96,2048]{2,1,0:T(8,128)S(1)} %copy-done.3, bf16[2,96,2048]{2,1,0:T(8,128)(2,1)S(1)} %copy-done.9, bf16[2,96,2048]{2,1,0:T(8,128)(2,1)S(1)} %copy-done.7, ...), custom_call_target="tpu_custom_call" | custom-call | flops 15728640 | bytes 7077888 | tf_op jit(solution)/shard_map/pallas_call | solution.py:269
  147.3 0.7 copy.19
  148.0 0.7 copy.20
Async XLA Ops:
  7.2 2.6 %copy-start.15 = (s32[16]{0:T(128)S(1)}, s32[16]{0:T(128)}, u32[]{:S(2)}) copy-start(s32[16]{0:T(128)} %param.14) | copy-start | bytes 196
  7.2 2.7 %copy-start.12 = (s32[256]{0:T(256)S(1)}, s32[256]{0:T(256)}, u32[]{:S(2)}) copy-start(s32[256]{0:T(256)} %param.15) | copy-start | bytes 3076
  7.2 2.7 %copy-start.11 = (bf16[256,384]{1,0:T(8,128)(2,1)S(1)}, bf16[256,384]{1,0:T(8,128)(2,1)}, u32[]{:S(2)}) copy-start(bf16[256,384]{1,0:T(8,128)(2,1)} %x_ref.1) | copy-start | bytes 589828
  7.2 11.1 %copy-start.6 = (bf16[256,2048]{1,0:T(8,128)(2,1)S(1)}, bf16[256,2048]{1,0:T(8,128)(2,1)}, u32[]{:S(2)}) copy-start(bf16[256,2048]{1,0:T(8,128)(2,1)} %g_ref.1) | copy-start | bytes 3145732
  7.2 65.8 %all-gather.2.cloned.1.call-start = ((), (), s32[]{:S(2)}) async-start(), calls=%async_computation.5 | async-start | bytes 3932160 | tf_op jit(solution)/shard_map/all_gather | solution.py:304
  11.0 16.9 %all-to-all-start = ((bf16[8,48,384]{2,1,0:T(8,128)(2,1)}), bf16[8,48,384]{2,1,0:T(8,128)(2,1)S(1)}, u32[]{:S(2)}, u32[]{:S(2)}) async-start(bf16[8,48,384]{2,1,0:T(8,128)(2,1)} %bitcast.2), calls=%async_computation | async-start | bytes 589824 | tf_op jit(solution)/shard_map/all_to_all | solution.py:289
  18.3 116.5 %reduce-scatter.2.cloned.1.call-start = ((), (), s32[]{:S(2)}) async-start(), calls=%async_computation.6 | async-start | bytes 3932160 | tf_op jit(solution)/shard_map/reduce_scatter | solution.py:315
  71.3 1.7 %copy-start.2 = (bf16[2,384,2048]{2,1,0:T(8,128)(2,1)}, bf16[2,384,2048]{2,1,0:T(8,128)(2,1)S(1)}, u32[]{:S(2)}) copy-start(bf16[2,384,2048]{2,1,0:T(8,128)(2,1)S(1)} %shard_map.150) | copy-start | bytes 9437188
  73.0 1.9 %copy-start = (bf16[2,384,2048]{2,1,0:T(8,128)(2,1)S(1)}, bf16[2,384,2048]{2,1,0:T(8,128)(2,1)}, u32[]{:S(2)}) copy-start(bf16[2,384,2048]{2,1,0:T(8,128)(2,1)} %all-gather.2.cloned.1.call-done.w_ref) | copy-start | bytes 9437188
  78.6 12.6 %all-to-all-start.3 = ((bf16[8,48,384]{2,1,0:T(8,128)(2,1)}), bf16[8,48,384]{2,1,0:T(8,128)(2,1)S(1)}, u32[]{:S(2)}, u32[]{:S(2)}) async-start(bf16[8,48,384]{2,1,0:T(8,128)(2,1)} %bitcast.8), calls=%async_computation.3 | async-start | bytes 589824 | tf_op jit(solution)/shard_map/all_to_all | solution.py:289
  82.2 1.9 %copy-start.1 = (bf16[2,384,2048]{2,1,0:T(8,128)(2,1)S(1)}, bf16[2,384,2048]{2,1,0:T(8,128)(2,1)}, u32[]{:S(2)}) copy-start(bf16[2,384,2048]{2,1,0:T(8,128)(2,1)} %all-gather.2.cloned.1.call-done.w_ref) | copy-start | bytes 9437188
  91.3 0.7 copy-start.4
  92.0 3.8 %copy-start.13 = (f32[2,96,16]{1,2,0:T(8,128)S(1)}, f32[2,96,16]{1,2,0:T(8,128)}, u32[]{:S(2)}) copy-start(f32[2,96,16]{1,2,0:T(8,128)} %param.11) | copy-start | bytes 36868
  92.0 3.9 %copy-start.14 = (f32[2,96,16]{1,2,0:T(8,128)S(1)}, f32[2,96,16]{1,2,0:T(8,128)}, u32[]{:S(2)}) copy-start(f32[2,96,16]{1,2,0:T(8,128)} %param.13) | copy-start | bytes 36868
  92.0 4.6 %copy-start.5 = (bf16[8,48,384]{2,1,0:T(8,128)(2,1)S(1)}, bf16[8,48,384]{2,1,0:T(8,128)(2,1)}, u32[]{:S(2)}) copy-start(bf16[8,48,384]{2,1,0:T(8,128)(2,1)} %copy-done.4) | copy-start | bytes 884740
  92.0 40.3 %all-to-all-start.1 = ((bf16[8,48,2048]{2,1,0:T(8,128)(2,1)}), bf16[8,48,2048]{2,1,0:T(8,128)(2,1)S(1)}, u32[]{:S(2)}, u32[]{:S(2)}) async-start(bf16[8,48,2048]{2,1,0:T(8,128)(2,1)} %bitcast.4), calls=%async_computation.1 | async-start | bytes 3145728 | tf_op jit(solution)/shard_map/all_to_all | solution.py:289
  96.6 38.2 %copy-start.3 = (f32[2,96,2048]{2,1,0:T(8,128)S(1)}, f32[2,96,2048]{2,1,0:T(8,128)}, u32[]{:S(2)}) copy-start(f32[2,96,2048]{2,1,0:T(8,128)} %master_ref.1) | copy-start | bytes 4718596
  97.6 37.2 %copy-start.10 = (f32[2,96,16]{2,1,0:T(8,128)S(1)}, f32[2,96,16]{2,1,0:T(8,128)}, u32[]{:S(2)}) copy-start(f32[2,96,16]{2,1,0:T(8,128)} %copy.18.vs_ref) | copy-start | bytes 36868
  134.8 1.1 copy-start.7
  135.9 1.1 copy-start.8
  137.0 1.1 copy-start.9
Sparse Core Ops, SparseCore 0:
  10.2 31.2 all-gather.1
  73.1 36.9 reduce-scatter.1

commit v2 on v1

v2 whole, which is shorter than its diff:
```python
import functools

import jax
import jax.numpy as jnp
from jax import lax
from jax.experimental import pallas as pl
from jax.experimental.pallas import tpu as pltpu
from jax.sharding import PartitionSpec as P

BLOCK = 128
ADAM_STEP = 100

beta_one = 0.9
beta_two = 0.95
learn_rate = 0.01

VMEM_LIMIT = 40 * 1024 * 1024
F32 = jnp.float32
BF16 = jnp.bfloat16


def cost(flops, nbytes):
    return pl.CostEstimate(flops=int(flops), bytes_accessed=int(nbytes), transcendentals=0)


def params(*semantics):
    if semantics:
        return pltpu.CompilerParams(vmem_limit_bytes=VMEM_LIMIT, dimension_semantics=semantics)
    return pltpu.CompilerParams(vmem_limit_bytes=VMEM_LIMIT)


def is_power_of_two(n):
    return n & (n - 1) == 0


def row_targets(route_row, placement_col, capacity, local_count, relative):
    expert_count = placement_col.shape[0]
    row_count = route_row.shape[1]
    hot = (placement_col == route_row).astype(F32)
    earlier = lax.broadcasted_iota(jnp.int32, (row_count, row_count), 0)
    later = lax.broadcasted_iota(jnp.int32, (row_count, row_count), 1)
    before = (earlier < later).astype(F32).astype(BF16)
    position = jnp.dot(hot.astype(BF16), before, preferred_element_type=F32)
    slot = lax.broadcasted_iota(jnp.int32, (expert_count, row_count), 0)
    chunk = slot // local_count
    if relative:
        chunk = jnp.bitwise_xor(chunk, lax.axis_index("grp"))
    start = (chunk * local_count + lax.rem(slot, local_count)) * capacity
    return jnp.sum(hot * (start.astype(F32) + position), axis=0, keepdims=True).astype(jnp.int32)


def place_matrix(target, places):
    slots = lax.broadcasted_iota(jnp.int32, (places, target.shape[1]), 0)
    return (slots == target).astype(F32).astype(BF16)


def write_chunks(refs, value):
    rows = refs[0].shape[0]
    for k, ref in enumerate(refs):
        ref[...] = value[k * rows : (k + 1) * rows]


def read_chunks(refs):
    if len(refs) == 1:
        return refs[0][...]
    return jnp.concatenate([ref[...] for ref in refs], axis=0)


def dispatch_x_kernel(capacity, local_count, relative, route_ref, placement_ref, x_ref, *out_refs):
    target_ref, chunk_refs = out_refs[0], out_refs[1:]
    target = row_targets(route_ref[...], placement_ref[...], capacity, local_count, relative)
    target_ref[...] = target
    places = place_matrix(target, len(chunk_refs) * chunk_refs[0].shape[0])
    write_chunks(
        chunk_refs, jnp.dot(places, x_ref[...], preferred_element_type=F32).astype(BF16)
    )


def dispatch_x(route, placement, x_rows, capacity, local_count, chunks):
    row_count, hidden = x_rows.shape
    places = placement.shape[0] * capacity
    out = pl.pallas_call(
        functools.partial(dispatch_x_kernel, capacity, local_count, chunks > 1),
        out_shape=(jax.ShapeDtypeStruct((1, row_count), jnp.int32),)
        + (jax.ShapeDtypeStruct((places // chunks, hidden), BF16),) * chunks,
        compiler_params=params(),
        cost_estimate=cost(2 * places * row_count * hidden, 2 * (places + row_count) * hidden),
        name="dispatch_x",
    )(route.reshape(1, row_count), placement.reshape(-1, 1), x_rows)
    return out[0], list(out[1:])


def dispatch_g_kernel(target_ref, g_ref, *chunk_refs):
    places = place_matrix(target_ref[...], len(chunk_refs) * chunk_refs[0].shape[0])
    write_chunks(
        chunk_refs, jnp.dot(places, g_ref[...], preferred_element_type=F32).astype(BF16)
    )


def dispatch_g(target, y_cot, places, chunks):
    row_count, width = y_cot.shape
    tile = min(width, 512)
    rows = places // chunks
    return list(pl.pallas_call(
        dispatch_g_kernel,
        grid=(width // tile,),
        in_specs=[
            pl.BlockSpec((1, row_count), lambda j: (0, 0)),
            pl.BlockSpec((row_count, tile), lambda j: (0, j)),
        ],
        out_specs=(pl.BlockSpec((rows, tile), lambda j: (0, j)),) * chunks,
        out_shape=(jax.ShapeDtypeStruct((rows, width), BF16),) * chunks,
        compiler_params=params("arbitrary"),
        cost_estimate=cost(2 * places * row_count * width, 2 * (places + row_count) * width),
        name="dispatch_g",
    )(target, y_cot))


def collect_kernel(target_ref, *refs):
    chunk_refs, out_ref = refs[:-1], refs[-1]
    home = read_chunks(chunk_refs)
    places = place_matrix(target_ref[...], home.shape[0])
    out_ref[...] = lax.dot_general(
        places, home, (((0,), (0,)), ((), ())), preferred_element_type=F32
    ).astype(BF16)


def collect(target, home, name):
    rows, width = home[0].shape
    places = rows * len(home)
    row_count = target.shape[1]
    tile = min(width, 512)
    return pl.pallas_call(
        collect_kernel,
        grid=(width // tile,),
        in_specs=[pl.BlockSpec((1, row_count), lambda j: (0, 0))]
        + [pl.BlockSpec((rows, tile), lambda j: (0, j))] * len(home),
        out_specs=pl.BlockSpec((row_count, tile), lambda j: (0, j)),
        out_shape=jax.ShapeDtypeStruct((row_count, width), BF16),
        compiler_params=params("arbitrary"),
        cost_estimate=cost(2 * places * row_count * width, 2 * (places + row_count) * width),
        name=name,
    )(target, *home)


def member_rows(rows, capacity, local_count):
    index = lax.broadcasted_iota(jnp.int32, (rows, 1), 0)
    return lax.rem(index, capacity * local_count) // capacity


def spread(x, capacity, local_count):
    member = member_rows(x.shape[0], capacity, local_count)
    zero = jnp.zeros_like(x)
    return jnp.concatenate([jnp.where(member == e, x, zero) for e in range(local_count)], axis=1)


def join_weight(piece_refs, joined_ref):
    local_count, rows, width = piece_refs[0].shape
    if len(piece_refs) == 1:
        return piece_refs[0][...].reshape(local_count * rows, width)
    here = lax.axis_index("rep")
    for i, ref in enumerate(piece_refs):
        owner = jnp.bitwise_xor(here, i)
        for e in range(local_count):
            joined_ref[e, owner] = ref[e]
    return joined_ref[...].reshape(local_count * len(piece_refs) * rows, width)


def joined_scratch(pieces, tile):
    local_count, rows, _ = pieces[0].shape
    return pltpu.VMEM((local_count, len(pieces), rows, tile), BF16)


def forward_kernel(capacity, local_count, chunks, pieces, *refs):
    x_refs, w_refs = refs[:chunks], refs[chunks : chunks + pieces]
    y_refs, joined_ref = refs[chunks + pieces : -1], refs[-1]
    wide = spread(read_chunks(x_refs), capacity, local_count)
    weight = join_weight(w_refs, joined_ref)
    write_chunks(y_refs, jnp.dot(wide, weight, preferred_element_type=F32).astype(BF16))


def forward(x, weight, capacity):
    rows, hidden = x[0].shape
    local_count, slice_rows, width = weight[0].shape
    tile = min(width, 512)
    total = rows * len(x)
    return list(pl.pallas_call(
        functools.partial(forward_kernel, capacity, local_count, len(x), len(weight)),
        grid=(width // tile,),
        in_specs=[pl.BlockSpec((rows, hidden), lambda j: (0, 0))] * len(x)
        + [pl.BlockSpec((local_count, slice_rows, tile), lambda j: (0, 0, j))] * len(weight),
        out_specs=(pl.BlockSpec((rows, tile), lambda j: (0, j)),) * len(x),
        out_shape=(jax.ShapeDtypeStruct((rows, width), BF16),) * len(x),
        scratch_shapes=[joined_scratch(weight, tile)],
        compiler_params=params("arbitrary"),
        cost_estimate=cost(
            2 * total * local_count * hidden * width,
            2 * (local_count * hidden + total) * width,
        ),
        name="forward",
    )(*x, *weight))


def gradient_kernel(capacity, local_count, chunks, parts, factor, *refs):
    x_refs, g_refs = refs[:chunks], refs[chunks : 2 * chunks]
    wide = spread(read_chunks(x_refs), capacity, local_count)
    outer = lax.dot_general(
        wide, read_chunks(g_refs), (((0,), (0,)), ((), ())), preferred_element_type=F32
    )
    low = (outer * factor).astype(BF16)
    if parts == 1:
        out_ref = refs[-1]
        out_ref[...] = low.reshape(out_ref.shape)
        return
    out_refs, split_ref = refs[2 * chunks : -1], refs[-1]
    split_ref[...] = low.reshape(split_ref.shape)
    here = lax.axis_index("rep")
    for i, out_ref in enumerate(out_refs):
        owner = jnp.bitwise_xor(here, i)
        for e in range(local_count):
            out_ref[e] = split_ref[e, owner]


def gradient(x, g, capacity, local_count, parts, factor):
    rows, hidden = x[0].shape
    width = g[0].shape[1]
    tile = min(width, 512)
    total = rows * len(x)
    slice_rows = hidden // parts
    return list(pl.pallas_call(
        functools.partial(gradient_kernel, capacity, local_count, len(x), parts, factor),
        grid=(width // tile,),
        in_specs=[pl.BlockSpec((rows, hidden), lambda j: (0, 0))] * len(x)
        + [pl.BlockSpec((rows, tile), lambda j: (0, j))] * len(g),
        out_specs=(pl.BlockSpec((local_count, slice_rows, tile), lambda j: (0, 0, j)),) * parts,
        out_shape=(jax.ShapeDtypeStruct((local_count, slice_rows, width), BF16),) * parts,
        scratch_shapes=[pltpu.VMEM((local_count, parts, slice_rows, tile), BF16)]
        if parts > 1
        else [],
        compiler_params=params("arbitrary"),
        cost_estimate=cost(
            2 * total * local_count * hidden * width,
            2 * (local_count * hidden + total) * width,
        ),
        name="gradient",
    )(*x, *g))


def backward_kernel(capacity, local_count, chunks, pieces, *refs):
    g_refs, w_refs = refs[:chunks], refs[chunks : chunks + pieces]
    dx_refs, joined_ref, total_ref = refs[chunks + pieces : -2], refs[-2], refs[-1]
    step = pl.program_id(0)
    hidden = dx_refs[0].shape[1]
    part = lax.dot_general(
        read_chunks(g_refs), join_weight(w_refs, joined_ref), (((1,), (1,)), ((), ())),
        preferred_element_type=F32,
    )

    @pl.when(step == 0)
    def _():
        total_ref[...] = part

    @pl.when(step > 0)
    def _():
        total_ref[...] += part

    @pl.when(step == pl.num_programs(0) - 1)
    def _():
        member = member_rows(total_ref.shape[0], capacity, local_count)
        picked = total_ref[:, :hidden]
        for e in range(1, local_count):
            picked = jnp.where(member == e, total_ref[:, e * hidden : (e + 1) * hidden], picked)
        write_chunks(dx_refs, picked.astype(BF16))


def backward(g, weight, capacity):
    rows, width = g[0].shape
    local_count, slice_rows, _ = weight[0].shape
    hidden = slice_rows * len(weight)
    tile = min(width, 512)
    total = rows * len(g)
    return list(pl.pallas_call(
        functools.partial(backward_kernel, capacity, local_count, len(g), len(weight)),
        grid=(width // tile,),
        in_specs=[pl.BlockSpec((rows, tile), lambda j: (0, j))] * len(g)
        + [pl.BlockSpec((local_count, slice_rows, tile), lambda j: (0, 0, j))] * len(weight),
        out_specs=(pl.BlockSpec((rows, hidden), lambda j: (0, 0)),) * len(g),
        out_shape=(jax.ShapeDtypeStruct((rows, hidden), BF16),) * len(g),
        scratch_shapes=[
            joined_scratch(weight, tile),
            pltpu.VMEM((total, local_count * hidden), F32),
        ],
        compiler_params=params("arbitrary"),
        cost_estimate=cost(
            2 * total * local_count * hidden * width,
            2 * (local_count * hidden + total) * width,
        ),
        name="backward",
    )(*g, *weight))


def cast_kernel(w_ref, out_ref):
    out_ref[...] = w_ref[...].astype(BF16)


def cast_weight(weight):
    members, rows, width = weight.shape
    tile = min(width, 512)
    spec = pl.BlockSpec((members, rows, tile), lambda j: (0, 0, j))
    return pl.pallas_call(
        cast_kernel,
        grid=(width // tile,),
        in_specs=[spec],
        out_specs=spec,
        out_shape=jax.ShapeDtypeStruct(weight.shape, BF16),
        compiler_params=params("arbitrary"),
        cost_estimate=cost(weight.size, 6 * weight.size),
        name="cast_weight",
    )(weight)


def add_kernel(a_ref, b_ref, out_ref):
    out_ref[...] = (a_ref[...].astype(F32) + b_ref[...].astype(F32)).astype(BF16)


def add_parts(a, b):
    members, rows, width = a.shape
    tile = min(width, 1024)
    spec = pl.BlockSpec((members, rows, tile), lambda j: (0, 0, j))
    return pl.pallas_call(
        add_kernel,
        grid=(width // tile,),
        in_specs=[spec, spec],
        out_specs=spec,
        out_shape=jax.ShapeDtypeStruct(a.shape, BF16),
        compiler_params=params("arbitrary"),
        cost_estimate=cost(a.size, 6 * a.size),
        name="add_parts",
    )(a, b)


def adam_kernel(
    parts, master_ref, mc_ref, ms_ref, vc_ref, vs_ref, *refs
):
    grad_refs = refs[:parts]
    master_out, mc_out, ms_out, vc_out, vs_out = refs[parts:]
    blocks = ms_ref.shape[1]
    rows = ms_ref.shape[2]
    corr_one = 1.0 - beta_one**ADAM_STEP
    corr_two = 1.0 - beta_two**ADAM_STEP
    m_scales = (ms_ref[0] * beta_one).T
    v_scales = (vs_ref[0] * beta_two).T
    lane = lax.broadcasted_iota(jnp.int32, (rows, blocks), 1)
    m_tops = jnp.zeros((rows, blocks), F32)
    v_tops = jnp.zeros((rows, blocks), F32)
    for b in range(blocks):
        cols = slice(b * BLOCK, (b + 1) * BLOCK)
        grad = grad_refs[0][0, :, cols].astype(F32)
        for ref in grad_refs[1:]:
            grad = grad + ref[0, :, cols].astype(F32)
        m_next = mc_ref[0, :, cols].astype(F32) * m_scales[:, b : b + 1] + (1.0 - beta_one) * grad
        v_next = vc_ref[0, :, cols].astype(F32) * v_scales[:, b : b + 1] + (
            1.0 - beta_two
        ) * (grad * grad)
        v_hat = v_next * (1.0 / corr_two)
        root = v_hat * lax.rsqrt(v_hat) + 1e-08
        master_out[0, :, cols] = master_ref[0, :, cols] - (learn_rate / corr_one) * m_next / root
        m_top = jnp.max(jnp.abs(m_next), axis=-1, keepdims=True) + 1e-06
        v_top = jnp.max(v_next, axis=-1, keepdims=True) + 1e-06
        mc_out[0, :, cols] = (m_next * (1.0 / m_top)).astype(BF16)
        vc_out[0, :, cols] = (v_next * (1.0 / v_top)).astype(BF16)
        m_tops = jnp.where(lane == b, m_top, m_tops)
        v_tops = jnp.where(lane == b, v_top, v_tops)
    ms_out[0] = m_tops.T
    vs_out[0] = v_tops.T


def adam(master_weight, grads, m_code, m_scale, v_code, v_scale):
    members, rows, width = master_weight.shape
    blocks = m_scale.shape[-1]
    count = 8 if blocks % 8 == 0 else blocks
    big = pl.BlockSpec((1, rows, count * BLOCK), lambda e, j: (e, 0, j))
    small = pl.BlockSpec((1, count, rows), lambda e, j: (e, j, 0))
    scales = jax.ShapeDtypeStruct((members, blocks, rows), F32)
    master_next, m_code_next, m_scale_next, v_code_next, v_scale_next = pl.pallas_call(
        functools.partial(adam_kernel, len(grads)),
        grid=(members, blocks // count),
        in_specs=[big, big, small, big, small] + [big] * len(grads),
        out_specs=(big, big, small, big, small),
        out_shape=(
            jax.ShapeDtypeStruct(master_weight.shape, F32),
            jax.ShapeDtypeStruct(master_weight.shape, BF16),
            scales,
            jax.ShapeDtypeStruct(master_weight.shape, BF16),
            scales,
        ),
        compiler_params=params("arbitrary", "arbitrary"),
        cost_estimate=cost(40 * master_weight.size, 18 * master_weight.size),
        name="adam",
    )(master_weight, m_code, jnp.swapaxes(m_scale, 1, 2), v_code, jnp.swapaxes(v_scale, 1, 2), *grads)
    return (
        master_next,
        m_code_next,
        jnp.swapaxes(m_scale_next, 1, 2),
        v_code_next,
        jnp.swapaxes(v_scale_next, 1, 2),
    )


def swap(array, axis, offset):
    size = lax.axis_size(axis)
    return lax.ppermute(array, axis, [(i, i ^ offset) for i in range(size)])


def exchange(chunks, groups):
    if len(chunks) > 1:
        order = sorted(range(1, len(chunks)), reverse=True)
        moved = {k: swap(chunks[k], "grp", k) for k in order}
        return [chunks[0]] + [moved[k] for k in range(1, len(chunks))]
    places, width = chunks[0].shape
    parts = chunks[0].reshape(groups, places // groups, width)
    moved = lax.all_to_all(parts, "grp", split_axis=0, concat_axis=0, tiled=True)
    return [moved.reshape(places, width)]


def gather_weight(weight_slice, replicas):
    if replicas != 4:
        return [lax.all_gather(weight_slice, "rep", axis=1, tiled=True)]
    far = swap(weight_slice, "rep", 2)
    near = swap(weight_slice, "rep", 1)
    return [weight_slice, near, far, swap(far, "rep", 1)]


def sum_gradient(parts):
    if len(parts) != 4:
        return [lax.psum_scatter(parts[0], "rep", scatter_dimension=1, tiled=True)]
    far = swap(parts[3], "rep", 1)
    near = swap(parts[1], "rep", 1)
    return [parts[0], near, swap(add_parts(parts[2], far), "rep", 2)]


def per_device(master_weight, m_code, m_scale, v_code, v_scale, placement, route, x_rows, y_cot):
    local_count, slice_rows, _ = master_weight.shape
    row_count = x_rows.shape[0]
    expert_count = placement.shape[0]
    groups = lax.axis_size("grp")
    replicas = lax.axis_size("rep")
    grad_factor = float(row_count * groups * replicas // expert_count) ** (-0.5)
    capacity = max(2, (3 * row_count + 2 * expert_count - 1) // (2 * expert_count))
    places = expert_count * capacity
    chunks = groups if is_power_of_two(groups) and (places // groups) % 16 == 0 else 1

    target, send_x = dispatch_x(route, placement, x_rows, capacity, local_count, chunks)
    local_x = exchange(send_x, groups)
    send_g = dispatch_g(target, y_cot, places, chunks)
    local_g = exchange(send_g, groups)
    weight = gather_weight(cast_weight(master_weight), replicas)

    back_y = forward(local_x, weight, capacity)
    home_y = exchange(back_y, groups)

    parts = replicas if replicas == 4 else 1
    grads = sum_gradient(gradient(local_x, local_g, capacity, local_count, parts, grad_factor))
    back_dx = backward(local_g, weight, capacity)
    home_dx = exchange(back_dx, groups)

    updated = adam(master_weight, grads, m_code, m_scale, v_code, v_scale)
    x_grad = collect(target, home_dx, "collect_dx")
    y_rows = collect(target, home_y, "collect_y")
    return (y_rows, x_grad) + tuple(updated)


def solution(mesh):
    return jax.shard_map(
        per_device,
        mesh=mesh,
        in_specs=(
            P("grp", "rep", None),
            P("grp", "rep", None),
            P("grp", "rep", None),
            P("grp", "rep", None),
            P("grp", "rep", None),
            P(),
            P(("rep", "grp")),
            P(("rep", "grp"), None),
            P(("rep", "grp"), None),
        ),
        out_specs=(
            P(("rep", "grp"), None),
            P(("rep", "grp"), None),
            P("grp", "rep", None),
            P("grp", "rep", None),
            P("grp", "rep", None),
            P("grp", "rep", None),
            P("grp", "rep", None),
        ),
        check_vma=False,
    )
```

time: 156 us -> 142 us (0.910)
  the two profiles are of different devices: /device:TPU:0 before, /device:TPU:16 now
where the time goes in v2:
time: 142 us
  waiting for transfers between devices  66.3 us (47%)
  starting transfers between devices  48.8 us (34%)
  Pallas kernels  22.1 us (16%)
  local copies, waits for them, and re-layouts  3.69 us (3%)
    ppermute x34, waiting for transfers between devices, swap(): return lax.ppermute(array, axis, [(i, i ^ offset) for i in range(size)])  66.3 us
    ppermute x34, starting transfers between devices, swap(): return lax.ppermute(array, axis, [(i, i ^ offset) for i in range(size)])  48.8 us
    pallas_call x1, Pallas kernels, adam(): pl.pallas_call(functools.partial(adam_kernel, len(grads)), grid=(members,...  6.19 us
    pallas_call x1, Pallas kernels, gradient(): pl.pallas_call(functools.partial(gradient_kernel, capacity, local_count,...  3.61 us
    pallas_call x2, Pallas kernels, collect(): pl.pallas_call(collect_kernel, grid=(width // tile,), in_specs=[pl.BlockS...  3.53 us
    pallas_call x1, Pallas kernels, backward(): pl.pallas_call(functools.partial(backward_kernel, capacity, local_count,...  3.45 us
    pallas_call x1, Pallas kernels, forward(): pl.pallas_call(functools.partial(forward_kernel, capacity, local_count, l...  2.88 us
    unnamed x16, local copies, waits for them, and re-layouts  2.84 us
  transfers between devices with their start and end apart: 34, of which 19 were waited for; matrix products, arithmetic and copies ran while one was open for 0% of the time, Pallas kernels for 13%

profile of v2, /device:TPU:16, one launch (start us, length us, event | category | flops | bytes accessed | tf_op | source)
XLA Modules:
  0.0 141.7 jit_solution(4826045312322206566)
XLA Ops:
  0.6 0.8 copy.16.placement_ref
  1.5 0.9 copy-done.6
  2.4 0.7 copy-done.7
  3.1 0.5 dispatch_x.1
  3.6 1.2 copy-done.5
  4.8 1.3 dispatch_g.1
  6.1 1.6 %collective-permute-start.17 = (bf16[48,2048]{1,0:T(8,128)(2,1)S(1)}, bf16[48,2048]{1,0:T(8,128)(2,1)S(1)}, u32[]{:S(2)}, u32[]{:S(2)}) collective-permute-start(bf16[48,2048]{1,0:T(8,128)(2,1)S(1)} %get-tuple-element.67), channel_id=1, source_target_pairs={{0,1},{1,0},{2,3},{3,2},{4,5},{5,4},{6,7},{7,6},{8,9},{9,8},{10,11... | collective-permute-start | bytes 589832 | tf_op jit(solution)/shard_map/ppermute | solution.py:412
  7.7 1.6 %collective-permute-start.18 = (bf16[48,2048]{1,0:T(8,128)(2,1)S(1)}, bf16[48,2048]{1,0:T(8,128)(2,1)S(1)}, u32[]{:S(2)}, u32[]{:S(2)}) collective-permute-start(bf16[48,2048]{1,0:T(8,128)(2,1)S(1)} %get-tuple-element.68), channel_id=1, source_target_pairs={{0,2},{1,3},{2,0},{3,1},{4,6},{5,7},{6,4},{7,5},{8,10},{9,11},{10,... | collective-permute-start | bytes 589832 | tf_op jit(solution)/shard_map/ppermute | solution.py:412
  9.2 0.4 collective-permute-start.19
  9.7 1.5 %collective-permute-start = (bf16[48,384]{1,0:T(8,128)(2,1)S(1)}, bf16[48,384]{1,0:T(8,128)(2,1)S(1)}, u32[]{:S(2)}, u32[]{:S(2)}) collective-permute-start(bf16[48,384]{1,0:T(8,128)(2,1)S(1)} %get-tuple-element.51), channel_id=1, source_target_pairs={{0,1},{1,0},{2,3},{3,2},{4,5},{5,4},{6,7},{7,6},{8,9},{9,8},{10,11... | collective-permute-start | bytes 110600 | tf_op jit(solution)/shard_map/ppermute | solution.py:412
  11.2 1.6 %collective-permute-start.1 = (bf16[48,384]{1,0:T(8,128)(2,1)S(1)}, bf16[48,384]{1,0:T(8,128)(2,1)S(1)}, u32[]{:S(2)}, u32[]{:S(2)}) collective-permute-start(bf16[48,384]{1,0:T(8,128)(2,1)S(1)} %get-tuple-element.52), channel_id=1, source_target_pairs={{0,2},{1,3},{2,0},{3,1},{4,6},{5,7},{6,4},{7,5},{8,10},{9,11},{10,... | collective-permute-start | bytes 110600 | tf_op jit(solution)/shard_map/ppermute | solution.py:412
  12.7 2.0 %collective-permute-done.refs_1_ = bf16[48,384]{1,0:T(8,128)(2,1)S(1)} collective-permute-done((bf16[48,384]{1,0:T(8,128)(2,1)S(1)}, bf16[48,384]{1,0:T(8,128)(2,1)S(1)}, u32[]{:S(2)}, u32[]{:S(2)}) %collective-permute-start) | collective-permute-done | bytes 36896 | tf_op jit(solution)/shard_map/ppermute | solution.py:412
  14.7 2.5 %collective-permute-start.2 = (bf16[48,384]{1,0:T(8,128)(2,1)S(1)}, bf16[48,384]{1,0:T(8,128)(2,1)S(1)}, u32[]{:S(2)}, u32[]{:S(2)}) collective-permute-start(bf16[48,384]{1,0:T(8,128)(2,1)S(1)} %get-tuple-element.53), channel_id=1, source_target_pairs={{0,3},{1,2},{2,1},{3,0},{4,7},{5,6},{6,5},{7,4},{8,11},{9,10},{10,... | collective-permute-start | bytes 110600 | tf_op jit(solution)/shard_map/ppermute | solution.py:412
  17.2 2.2 %collective-permute-done.1.refs_2_ = bf16[48,384]{1,0:T(8,128)(2,1)S(1)} collective-permute-done((bf16[48,384]{1,0:T(8,128)(2,1)S(1)}, bf16[48,384]{1,0:T(8,128)(2,1)S(1)}, u32[]{:S(2)}, u32[]{:S(2)}) %collective-permute-start.1) | collective-permute-done | bytes 36896 | tf_op jit(solution)/shard_map/ppermute | solution.py:412
  19.4 0.3 collective-permute-start.3
  19.8 2.5 %collective-permute-start.4 = (bf16[48,384]{1,0:T(8,128)(2,1)S(1)}, bf16[48,384]{1,0:T(8,128)(2,1)S(1)}, u32[]{:S(2)}, u32[]{:S(2)}) collective-permute-start(bf16[48,384]{1,0:T(8,128)(2,1)S(1)} %get-tuple-element.55), channel_id=1, source_target_pairs={{0,5},{1,4},{2,7},{3,6},{4,1},{5,0},{6,3},{7,2},{8,13},{9,12},{10,... | collective-permute-start | bytes 110600 | tf_op jit(solution)/shard_map/ppermute | solution.py:412
  22.3 2.0 %collective-permute-done.3.refs_4_ = bf16[48,384]{1,0:T(8,128)(2,1)S(1)} collective-permute-done((bf16[48,384]{1,0:T(8,128)(2,1)S(1)}, bf16[48,384]{1,0:T(8,128)(2,1)S(1)}, u32[]{:S(2)}, u32[]{:S(2)}) %collective-permute-start.3) | collective-permute-done | bytes 36896 | tf_op jit(solution)/shard_map/ppermute | solution.py:412
  24.3 0.4 collective-permute-start.5
  24.7 0.3 cast_weight.1.refs_8_
  25.1 0.5 collective-permute-done.4.refs_5_
  25.6 1.5 %collective-permute-start.8 = (bf16[2,96,2048]{2,1,0:T(8,128)(2,1)S(1)}, bf16[2,96,2048]{2,1,0:T(8,128)(2,1)S(1)}, u32[]{:S(2)}, u32[]{:S(2)}) collective-permute-start(bf16[2,96,2048]{2,1,0:T(8,128)(2,1)S(1)} %cast_weight.1.refs_8_), channel_id=1, source_target_pairs={{0,16},{8,24},{16,0},{24,8},{1,17},{9,25},{17,1},{25,9},{2,18},{10... | collective-permute-start | bytes 2359304 | tf_op jit(solution)/shard_map/ppermute | solution.py:412
  27.1 1.6 %collective-permute-done.5.refs_6_ = bf16[48,384]{1,0:T(8,128)(2,1)S(1)} collective-permute-done((bf16[48,384]{1,0:T(8,128)(2,1)S(1)}, bf16[48,384]{1,0:T(8,128)(2,1)S(1)}, u32[]{:S(2)}, u32[]{:S(2)}) %collective-permute-start.5) | collective-permute-done | bytes 36896 | tf_op jit(solution)/shard_map/ppermute | solution.py:412
  28.7 1.1 collective-permute-start.6
  29.7 5.9 %collective-permute-done.6.refs_7_ = bf16[48,384]{1,0:T(8,128)(2,1)S(1)} collective-permute-done((bf16[48,384]{1,0:T(8,128)(2,1)S(1)}, bf16[48,384]{1,0:T(8,128)(2,1)S(1)}, u32[]{:S(2)}, u32[]{:S(2)}) %collective-permute-start.6) | collective-permute-done | bytes 36896 | tf_op jit(solution)/shard_map/ppermute | solution.py:412
  35.6 2.4 %collective-permute-start.20 = (bf16[48,2048]{1,0:T(8,128)(2,1)S(1)}, bf16[48,2048]{1,0:T(8,128)(2,1)S(1)}, u32[]{:S(2)}, u32[]{:S(2)}) collective-permute-start(bf16[48,2048]{1,0:T(8,128)(2,1)S(1)} %get-tuple-element.70), channel_id=1, source_target_pairs={{0,4},{1,5},{2,6},{3,7},{4,0},{5,1},{6,2},{7,3},{8,12},{9,13},{10,... | collective-permute-start | bytes 589832 | tf_op jit(solution)/shard_map/ppermute | solution.py:412
  38.0 2.9 %collective-permute-start.22 = (bf16[48,2048]{1,0:T(8,128)(2,1)S(1)}, bf16[48,2048]{1,0:T(8,128)(2,1)S(1)}, u32[]{:S(2)}, u32[]{:S(2)}) collective-permute-start(bf16[48,2048]{1,0:T(8,128)(2,1)S(1)} %get-tuple-element.72), channel_id=1, source_target_pairs={{0,6},{1,7},{2,4},{3,5},{4,2},{5,3},{6,0},{7,1},{8,14},{9,15},{10,... | collective-permute-start | bytes 589832 | tf_op jit(solution)/shard_map/ppermute | solution.py:412
  40.9 0.9 collective-permute-start.23
  41.8 13.0 %collective-permute-done.20.refs_4_.refs_12_ = bf16[48,2048]{1,0:T(8,128)(2,1)S(1)} collective-permute-done((bf16[48,2048]{1,0:T(8,128)(2,1)S(1)}, bf16[48,2048]{1,0:T(8,128)(2,1)S(1)}, u32[]{:S(2)}, u32[]{:S(2)}) %collective-permute-start.20) | collective-permute-done | bytes 196640 | tf_op jit(solution)/shard_map/ppermute | solution.py:412
  54.8 4.2 %collective-permute-done.21.refs_5_.refs_13_ = bf16[48,2048]{1,0:T(8,128)(2,1)S(1)} collective-permute-done((bf16[48,2048]{1,0:T(8,128)(2,1)S(1)}, bf16[48,2048]{1,0:T(8,128)(2,1)S(1)}, u32[]{:S(2)}, u32[]{:S(2)}) %collective-permute-start.21) | collective-permute-done | bytes 196640 | tf_op jit(solution)/shard_map/ppermute | solution.py:412
  59.0 5.3 %collective-permute-done.22.refs_6_.refs_14_ = bf16[48,2048]{1,0:T(8,128)(2,1)S(1)} collective-permute-done((bf16[48,2048]{1,0:T(8,128)(2,1)S(1)}, bf16[48,2048]{1,0:T(8,128)(2,1)S(1)}, u32[]{:S(2)}, u32[]{:S(2)}) %collective-permute-start.22) | collective-permute-done | bytes 196640 | tf_op jit(solution)/shard_map/ppermute | solution.py:412
  64.4 3.3 %collective-permute-done.23.refs_7_.refs_15_ = bf16[48,2048]{1,0:T(8,128)(2,1)S(1)} collective-permute-done((bf16[48,2048]{1,0:T(8,128)(2,1)S(1)}, bf16[48,2048]{1,0:T(8,128)(2,1)S(1)}, u32[]{:S(2)}, u32[]{:S(2)}) %collective-permute-start.23) | collective-permute-done | bytes 196640 | tf_op jit(solution)/shard_map/ppermute | solution.py:412
  67.6 3.6 %gradient.1 = (bf16[2,96,2048]{2,1,0:T(8,128)(2,1)S(1)}, bf16[2,96,2048]{2,1,0:T(8,128)(2,1)S(1)}, bf16[2,96,2048]{2,1,0:T(8,128)(2,1)S(1)}, bf16[2,96,2048]{2,1,0:T(8,128)(2,1)S(1)}) custom-call(bf16[48,384]{1,0:T(8,128)(2,1)S(1)} %get-tuple-element.50.refs_0_, bf16[48,384]{1,0:T(8,128)(2,1)S(1)} %collective-permute-done.refs_1_, ...), custom_call_target="tpu_custom_call" | custom-call | flops 1207959552 | bytes 4718592 | tf_op jit(solution)/shard_map/gradient/pallas_call | solution.py:230
  71.3 0.5 collective-permute-start.7
  71.8 0.1 collective-permute-start.9
  71.9 0.4 collective-permute-start.31
  72.3 1.3 collective-permute-done.32.b_ref
  73.6 0.4 add_parts.1
  74.0 1.6 %collective-permute-start.33 = (bf16[2,96,2048]{2,1,0:T(8,128)(2,1)S(1)}, bf16[2,96,2048]{2,1,0:T(8,128)(2,1)S(1)}, u32[]{:S(2)}, u32[]{:S(2)}) collective-permute-start(bf16[2,96,2048]{2,1,0:T(8,128)(2,1)S(1)} %add_parts.1), channel_id=1, source_target_pairs={{0,16},{8,24},{16,0},{24,8},{1,17},{9,25},{17,1},{25,9},{2,18},{10... | collective-permute-start | bytes 2359304 | tf_op jit(solution)/shard_map/ppermute | solution.py:412
  75.6 0.2 collective-permute-done.9.refs_11_
  75.8 2.9 %forward.1 = (bf16[48,2048]{1,0:T(8,128)(2,1)S(1)}, bf16[48,2048]{1,0:T(8,128)(2,1)S(1)}, bf16[48,2048]{1,0:T(8,128)(2,1)S(1)}, bf16[48,2048]{1,0:T(8,128)(2,1)S...) custom-call(bf16[48,384]{1,0:T(8,128)(2,1)S(1)} %get-tuple-element.5, ...), custom_call_target="tpu_custom_call" | custom-call | flops 1207959552 | bytes 4718592 | tf_op jit(solution)/shard_map/forward/pallas_call | solution.py:187
  78.7 1.4 collective-permute-start.10
  80.1 0.1 collective-permute-start.11
  80.2 3.4 %backward.1 = (bf16[48,384]{1,0:T(8,128)(2,1)S(1)}, bf16[48,384]{1,0:T(8,128)(2,1)S(1)}, bf16[48,384]{1,0:T(8,128)(2,1)S(1)}, bf16[48,384]{1,0:T(8,128)(2,1)S(1)...) custom-call(bf16[48,2048]{1,0:T(8,128)(2,1)S(1)} %get-tuple-element., ...), custom_call_target="tpu_custom_call" | custom-call | flops 1207959552 | bytes 4718592 | tf_op jit(solution)/shard_map/backward/pallas_call | solution.py:282
  83.7 0.8 collective-permute-start.24
  84.4 2.0 %collective-permute-start.25 = (bf16[48,384]{1,0:T(8,128)(2,1)S(1)}, bf16[48,384]{1,0:T(8,128)(2,1)S(1)}, u32[]{:S(2)}, u32[]{:S(2)}) collective-permute-start(bf16[48,384]{1,0:T(8,128)(2,1)S(1)} %get-tuple-element.76), channel_id=1, source_target_pairs={{0,2},{1,3},{2,0},{3,1},{4,6},{5,7},{6,4},{7,5},{8,10},{9,11},{10,... | collective-permute-start | bytes 110600 | tf_op jit(solution)/shard_map/ppermute | solution.py:412
  86.4 1.3 collective-permute-done.24.refs_1_
  87.7 2.1 %collective-permute-start.26 = (bf16[48,384]{1,0:T(8,128)(2,1)S(1)}, bf16[48,384]{1,0:T(8,128)(2,1)S(1)}, u32[]{:S(2)}, u32[]{:S(2)}) collective-permute-start(bf16[48,384]{1,0:T(8,128)(2,1)S(1)} %get-tuple-element.77), channel_id=1, source_target_pairs={{0,3},{1,2},{2,1},{3,0},{4,7},{5,6},{6,5},{7,4},{8,11},{9,10},{10,... | collective-permute-start | bytes 110600 | tf_op jit(solution)/shard_map/ppermute | solution.py:412
  89.8 1.5 %collective-permute-start.27 = (bf16[48,384]{1,0:T(8,128)(2,1)S(1)}, bf16[48,384]{1,0:T(8,128)(2,1)S(1)}, u32[]{:S(2)}, u32[]{:S(2)}) collective-permute-start(bf16[48,384]{1,0:T(8,128)(2,1)S(1)} %get-tuple-element.78), channel_id=1, source_target_pairs={{0,4},{1,5},{2,6},{3,7},{4,0},{5,1},{6,2},{7,3},{8,12},{9,13},{10,... | collective-permute-start | bytes 110600 | tf_op jit(solution)/shard_map/ppermute | solution.py:412
  91.3 1.3 collective-permute-done.26.refs_3_
  92.6 3.0 %collective-permute-start.28 = (bf16[48,384]{1,0:T(8,128)(2,1)S(1)}, bf16[48,384]{1,0:T(8,128)(2,1)S(1)}, u32[]{:S(2)}, u32[]{:S(2)}) collective-permute-start(bf16[48,384]{1,0:T(8,128)(2,1)S(1)} %get-tuple-element.79), channel_id=1, source_target_pairs={{0,5},{1,4},{2,7},{3,6},{4,1},{5,0},{6,3},{7,2},{8,13},{9,12},{10,... | collective-permute-start | bytes 110600 | tf_op jit(solution)/shard_map/ppermute | solution.py:412
  95.6 0.9 collective-permute-start.29
  96.5 1.8 %collective-permute-done.28.refs_5_ = bf16[48,384]{1,0:T(8,128)(2,1)S(1)} collective-permute-done((bf16[48,384]{1,0:T(8,128)(2,1)S(1)}, bf16[48,384]{1,0:T(8,128)(2,1)S(1)}, u32[]{:S(2)}, u32[]{:S(2)}) %collective-permute-start.28) | collective-permute-done | bytes 36896 | tf_op jit(solution)/shard_map/ppermute | solution.py:412
  98.4 1.6 %collective-permute-start.30 = (bf16[48,384]{1,0:T(8,128)(2,1)S(1)}, bf16[48,384]{1,0:T(8,128)(2,1)S(1)}, u32[]{:S(2)}, u32[]{:S(2)}) collective-permute-start(bf16[48,384]{1,0:T(8,128)(2,1)S(1)} %get-tuple-element.81), channel_id=1, source_target_pairs={{0,7},{1,6},{2,5},{3,4},{4,3},{5,2},{6,1},{7,0},{8,15},{9,14},{10,... | collective-permute-start | bytes 110600 | tf_op jit(solution)/shard_map/ppermute | solution.py:412
  100.0 3.8 %collective-permute-start.12 = (bf16[48,2048]{1,0:T(8,128)(2,1)S(1)}, bf16[48,2048]{1,0:T(8,128)(2,1)S(1)}, u32[]{:S(2)}, u32[]{:S(2)}) collective-permute-start(bf16[48,2048]{1,0:T(8,128)(2,1)S(1)} %get-tuple-element.61), channel_id=1, source_target_pairs={{0,3},{1,2},{2,1},{3,0},{4,7},{5,6},{6,5},{7,4},{8,11},{9,10},{10,... | collective-permute-start | bytes 589832 | tf_op jit(solution)/shard_map/ppermute | solution.py:412
  103.8 4.8 %collective-permute-start.13 = (bf16[48,2048]{1,0:T(8,128)(2,1)S(1)}, bf16[48,2048]{1,0:T(8,128)(2,1)S(1)}, u32[]{:S(2)}, u32[]{:S(2)}) collective-permute-start(bf16[48,2048]{1,0:T(8,128)(2,1)S(1)} %get-tuple-element.62), channel_id=1, source_target_pairs={{0,4},{1,5},{2,6},{3,7},{4,0},{5,1},{6,2},{7,3},{8,12},{9,13},{10,... | collective-permute-start | bytes 589832 | tf_op jit(solution)/shard_map/ppermute | solution.py:412
  108.6 0.4 collective-permute-start.15
  109.1 2.5 %collective-permute-start.16 = (bf16[48,2048]{1,0:T(8,128)(2,1)S(1)}, bf16[48,2048]{1,0:T(8,128)(2,1)S(1)}, u32[]{:S(2)}, u32[]{:S(2)}) collective-permute-start(bf16[48,2048]{1,0:T(8,128)(2,1)S(1)} %get-tuple-element.65), channel_id=1, source_target_pairs={{0,7},{1,6},{2,5},{3,4},{4,3},{5,2},{6,1},{7,0},{8,15},{9,14},{10,... | collective-permute-start | bytes 589832 | tf_op jit(solution)/shard_map/ppermute | solution.py:412
  111.6 1.0 collect_dx.1
  112.6 6.2 %adam.1 = (f32[2,96,2048]{2,1,0:T(8,128)}, bf16[2,96,2048]{2,1,0:T(8,128)(2,1)}, f32[2,16,96]{2,1,0:T(8,128)}, bf16[2,96,2048]{2,1,0:T(8,128)(2,1)}, f32[2,16,96]{2,1,0:T(8,128)}) custom-call(f32[2,96,2048]{2,1,0:T(8,128)S(1)} %copy-done, bf16[2,96,2048]{2,1,0:T(8,128)(2,1)S(1)} %copy-done.1, f32[2,16,96]{2,1,0:T(8,128)S(1)} %bitcast.6, ...), custom_call_target="tpu_custom_call" | custom-call | flops 15728640 | bytes 7077888 | tf_op jit(solution)/shard_map/adam/pallas_call | solution.py:385
  118.8 7.4 %collective-permute-done.13.refs_4_ = bf16[48,2048]{1,0:T(8,128)(2,1)S(1)} collective-permute-done((bf16[48,2048]{1,0:T(8,128)(2,1)S(1)}, bf16[48,2048]{1,0:T(8,128)(2,1)S(1)}, u32[]{:S(2)}, u32[]{:S(2)}) %collective-permute-start.13) | collective-permute-done | bytes 196640 | tf_op jit(solution)/shard_map/ppermute | solution.py:412
  126.1 4.2 %collective-permute-done.14.refs_5_ = bf16[48,2048]{1,0:T(8,128)(2,1)S(1)} collective-permute-done((bf16[48,2048]{1,0:T(8,128)(2,1)S(1)}, bf16[48,2048]{1,0:T(8,128)(2,1)S(1)}, u32[]{:S(2)}, u32[]{:S(2)}) %collective-permute-start.14) | collective-permute-done | bytes 196640 | tf_op jit(solution)/shard_map/ppermute | solution.py:412
  130.3 6.0 %collective-permute-done.15.refs_6_ = bf16[48,2048]{1,0:T(8,128)(2,1)S(1)} collective-permute-done((bf16[48,2048]{1,0:T(8,128)(2,1)S(1)}, bf16[48,2048]{1,0:T(8,128)(2,1)S(1)}, u32[]{:S(2)}, u32[]{:S(2)}) %collective-permute-start.15) | collective-permute-done | bytes 196640 | tf_op jit(solution)/shard_map/ppermute | solution.py:412
  136.3 2.8 %collective-permute-done.16.refs_7_ = bf16[48,2048]{1,0:T(8,128)(2,1)S(1)} collective-permute-done((bf16[48,2048]{1,0:T(8,128)(2,1)S(1)}, bf16[48,2048]{1,0:T(8,128)(2,1)S(1)}, u32[]{:S(2)}, u32[]{:S(2)}) %collective-permute-start.16) | collective-permute-done | bytes 196640 | tf_op jit(solution)/shard_map/ppermute | solution.py:412
  139.1 2.5 %collect_y.1 = bf16[256,2048]{1,0:T(8,128)(2,1)} custom-call(s32[1,256]{1,0:T(1,128)S(1)} %get-tuple-element.49.target_ref, bf16[48,2048]{1,0:T(8,128)(2,1)S(1)} %get-tuple-element.58.refs_0_, bf16[48,2048]{1,0:T(8,128)(2,1)S(1)} %collective-permute-done.10.refs_1_, bf16[48,2048]{1,0:T(8,128)(2,1)S(1)} %collective-permute-done.11.refs_2_, ...), custom_call_target="tpu_custom_call" | custom-call | flops 402653184 | bytes 2621440 | tf_op jit(solution)/shard_map/collect_y/pallas_call | solution.py:133
  (31 shorter events, 0.2 us)
Async XLA Ops:
  0.6 24.1 %copy-start = (f32[2,96,2048]{2,1,0:T(8,128)S(1)}, f32[2,96,2048]{2,1,0:T(8,128)}, u32[]{:S(2)}) copy-start(f32[2,96,2048]{2,1,0:T(8,128)} %master_ref.1) | copy-start | bytes 4718596
  1.5 0.9 copy-start.6
  2.4 0.7 copy-start.7
  3.6 1.2 copy-start.5
  6.1 31.9 %collective-permute-start.17 = (bf16[48,2048]{1,0:T(8,128)(2,1)S(1)}, bf16[48,2048]{1,0:T(8,128)(2,1)S(1)}, u32[]{:S(2)}, u32[]{:S(2)}) collective-permute-start(bf16[48,2048]{1,0:T(8,128)(2,1)S(1)} %get-tuple-element.67), channel_id=1, source_target_pairs={{0,1},{1,0},{2,3},{3,2},{4,5},{5,4},{6,7},{7,6},{8,9},{9,8},{10,11... | collective-permute-start | bytes 589832 | tf_op jit(solution)/shard_map/ppermute | solution.py:412
  7.7 30.3 %collective-permute-start.18 = (bf16[48,2048]{1,0:T(8,128)(2,1)S(1)}, bf16[48,2048]{1,0:T(8,128)(2,1)S(1)}, u32[]{:S(2)}, u32[]{:S(2)}) collective-permute-start(bf16[48,2048]{1,0:T(8,128)(2,1)S(1)} %get-tuple-element.68), channel_id=1, source_target_pairs={{0,2},{1,3},{2,0},{3,1},{4,6},{5,7},{6,4},{7,5},{8,10},{9,11},{10,... | collective-permute-start | bytes 589832 | tf_op jit(solution)/shard_map/ppermute | solution.py:412
  9.2 31.7 %collective-permute-start.19 = (bf16[48,2048]{1,0:T(8,128)(2,1)S(1)}, bf16[48,2048]{1,0:T(8,128)(2,1)S(1)}, u32[]{:S(2)}, u32[]{:S(2)}) collective-permute-start(bf16[48,2048]{1,0:T(8,128)(2,1)S(1)} %get-tuple-element.69), channel_id=1, source_target_pairs={{0,3},{1,2},{2,1},{3,0},{4,7},{5,6},{6,5},{7,4},{8,11},{9,10},{10,... | collective-permute-start | bytes 589832 | tf_op jit(solution)/shard_map/ppermute | solution.py:412
  9.7 5.0 %collective-permute-start = (bf16[48,384]{1,0:T(8,128)(2,1)S(1)}, bf16[48,384]{1,0:T(8,128)(2,1)S(1)}, u32[]{:S(2)}, u32[]{:S(2)}) collective-permute-start(bf16[48,384]{1,0:T(8,128)(2,1)S(1)} %get-tuple-element.51), channel_id=1, source_target_pairs={{0,1},{1,0},{2,3},{3,2},{4,5},{5,4},{6,7},{7,6},{8,9},{9,8},{10,11... | collective-permute-start | bytes 110600 | tf_op jit(solution)/shard_map/ppermute | solution.py:412
  11.2 8.3 %collective-permute-start.1 = (bf16[48,384]{1,0:T(8,128)(2,1)S(1)}, bf16[48,384]{1,0:T(8,128)(2,1)S(1)}, u32[]{:S(2)}, u32[]{:S(2)}) collective-permute-start(bf16[48,384]{1,0:T(8,128)(2,1)S(1)} %get-tuple-element.52), channel_id=1, source_target_pairs={{0,2},{1,3},{2,0},{3,1},{4,6},{5,7},{6,4},{7,5},{8,10},{9,11},{10,... | collective-permute-start | bytes 110600 | tf_op jit(solution)/shard_map/ppermute | solution.py:412
  14.7 5.1 %collective-permute-start.2 = (bf16[48,384]{1,0:T(8,128)(2,1)S(1)}, bf16[48,384]{1,0:T(8,128)(2,1)S(1)}, u32[]{:S(2)}, u32[]{:S(2)}) collective-permute-start(bf16[48,384]{1,0:T(8,128)(2,1)S(1)} %get-tuple-element.53), channel_id=1, source_target_pairs={{0,3},{1,2},{2,1},{3,0},{4,7},{5,6},{6,5},{7,4},{8,11},{9,10},{10,... | collective-permute-start | bytes 110600 | tf_op jit(solution)/shard_map/ppermute | solution.py:412
  19.4 4.9 %collective-permute-start.3 = (bf16[48,384]{1,0:T(8,128)(2,1)S(1)}, bf16[48,384]{1,0:T(8,128)(2,1)S(1)}, u32[]{:S(2)}, u32[]{:S(2)}) collective-permute-start(bf16[48,384]{1,0:T(8,128)(2,1)S(1)} %get-tuple-element.54), channel_id=1, source_target_pairs={{0,4},{1,5},{2,6},{3,7},{4,0},{5,1},{6,2},{7,3},{8,12},{9,13},{10,... | collective-permute-start | bytes 110600 | tf_op jit(solution)/shard_map/ppermute | solution.py:412
  19.8 5.8 %collective-permute-start.4 = (bf16[48,384]{1,0:T(8,128)(2,1)S(1)}, bf16[48,384]{1,0:T(8,128)(2,1)S(1)}, u32[]{:S(2)}, u32[]{:S(2)}) collective-permute-start(bf16[48,384]{1,0:T(8,128)(2,1)S(1)} %get-tuple-element.55), channel_id=1, source_target_pairs={{0,5},{1,4},{2,7},{3,6},{4,1},{5,0},{6,3},{7,2},{8,13},{9,12},{10,... | collective-permute-start | bytes 110600 | tf_op jit(solution)/shard_map/ppermute | solution.py:412
  24.3 4.3 %collective-permute-start.5 = (bf16[48,384]{1,0:T(8,128)(2,1)S(1)}, bf16[48,384]{1,0:T(8,128)(2,1)S(1)}, u32[]{:S(2)}, u32[]{:S(2)}) collective-permute-start(bf16[48,384]{1,0:T(8,128)(2,1)S(1)} %get-tuple-element.56), channel_id=1, source_target_pairs={{0,6},{1,7},{2,4},{3,5},{4,2},{5,3},{6,0},{7,1},{8,14},{9,15},{10,... | collective-permute-start | bytes 110600 | tf_op jit(solution)/shard_map/ppermute | solution.py:412
  25.6 46.3 %collective-permute-start.8 = (bf16[2,96,2048]{2,1,0:T(8,128)(2,1)S(1)}, bf16[2,96,2048]{2,1,0:T(8,128)(2,1)S(1)}, u32[]{:S(2)}, u32[]{:S(2)}) collective-permute-start(bf16[2,96,2048]{2,1,0:T(8,128)(2,1)S(1)} %cast_weight.1.refs_8_), channel_id=1, source_target_pairs={{0,16},{8,24},{16,0},{24,8},{1,17},{9,25},{17,1},{25,9},{2,18},{10... | collective-permute-start | bytes 2359304 | tf_op jit(solution)/shard_map/ppermute | solution.py:412
  28.7 7.0 %collective-permute-start.6 = (bf16[48,384]{1,0:T(8,128)(2,1)S(1)}, bf16[48,384]{1,0:T(8,128)(2,1)S(1)}, u32[]{:S(2)}, u32[]{:S(2)}) collective-permute-start(bf16[48,384]{1,0:T(8,128)(2,1)S(1)} %get-tuple-element.57), channel_id=1, source_target_pairs={{0,7},{1,6},{2,5},{3,4},{4,3},{5,2},{6,1},{7,0},{8,15},{9,14},{10,... | collective-permute-start | bytes 110600 | tf_op jit(solution)/shard_map/ppermute | solution.py:412
  35.6 19.2 %collective-permute-start.20 = (bf16[48,2048]{1,0:T(8,128)(2,1)S(1)}, bf16[48,2048]{1,0:T(8,128)(2,1)S(1)}, u32[]{:S(2)}, u32[]{:S(2)}) collective-permute-start(bf16[48,2048]{1,0:T(8,128)(2,1)S(1)} %get-tuple-element.70), channel_id=1, source_target_pairs={{0,4},{1,5},{2,6},{3,7},{4,0},{5,1},{6,2},{7,3},{8,12},{9,13},{10,... | collective-permute-start | bytes 589832 | tf_op jit(solution)/shard_map/ppermute | solution.py:412
  38.0 21.1 %collective-permute-start.21 = (bf16[48,2048]{1,0:T(8,128)(2,1)S(1)}, bf16[48,2048]{1,0:T(8,128)(2,1)S(1)}, u32[]{:S(2)}, u32[]{:S(2)}) collective-permute-start(bf16[48,2048]{1,0:T(8,128)(2,1)S(1)} %get-tuple-element.71), channel_id=1, source_target_pairs={{0,5},{1,4},{2,7},{3,6},{4,1},{5,0},{6,3},{7,2},{8,13},{9,12},{10,... | collective-permute-start | bytes 589832 | tf_op jit(solution)/shard_map/ppermute | solution.py:412
  38.0 26.4 %collective-permute-start.22 = (bf16[48,2048]{1,0:T(8,128)(2,1)S(1)}, bf16[48,2048]{1,0:T(8,128)(2,1)S(1)}, u32[]{:S(2)}, u32[]{:S(2)}) collective-permute-start(bf16[48,2048]{1,0:T(8,128)(2,1)S(1)} %get-tuple-element.72), channel_id=1, source_target_pairs={{0,6},{1,7},{2,4},{3,5},{4,2},{5,3},{6,0},{7,1},{8,14},{9,15},{10,... | collective-permute-start | bytes 589832 | tf_op jit(solution)/shard_map/ppermute | solution.py:412
  40.9 26.7 %collective-permute-start.23 = (bf16[48,2048]{1,0:T(8,128)(2,1)S(1)}, bf16[48,2048]{1,0:T(8,128)(2,1)S(1)}, u32[]{:S(2)}, u32[]{:S(2)}) collective-permute-start(bf16[48,2048]{1,0:T(8,128)(2,1)S(1)} %get-tuple-element.73), channel_id=1, source_target_pairs={{0,7},{1,6},{2,5},{3,4},{4,3},{5,2},{6,1},{7,0},{8,15},{9,14},{10,... | collective-permute-start | bytes 589832 | tf_op jit(solution)/shard_map/ppermute | solution.py:412
  71.2 2.4 %collective-permute-start.32 = (bf16[2,96,2048]{2,1,0:T(8,128)(2,1)S(1)}, bf16[2,96,2048]{2,1,0:T(8,128)(2,1)S(1)}, u32[]{:S(2)}, u32[]{:S(2)}) collective-permute-start(bf16[2,96,2048]{2,1,0:T(8,128)(2,1)S(1)} %get-tuple-element.85), channel_id=1, source_target_pairs={{0,8},{8,0},{16,24},{24,16},{1,9},{9,1},{17,25},{25,17},{2,10},{10... | collective-permute-start | bytes 2359304 | tf_op jit(solution)/shard_map/ppermute | solution.py:412
  71.3 4.3 %collective-permute-start.7 = (bf16[2,96,2048]{2,1,0:T(8,128)(2,1)S(1)}, bf16[2,96,2048]{2,1,0:T(8,128)(2,1)S(1)}, u32[]{:S(2)}, u32[]{:S(2)}) collective-permute-start(bf16[2,96,2048]{2,1,0:T(8,128)(2,1)S(1)} %cast_weight.1.refs_8_), channel_id=1, source_target_pairs={{0,8},{8,0},{16,24},{24,16},{1,9},{9,1},{17,25},{25,17},{2,10},{10... | collective-permute-start | bytes 2359304 | tf_op jit(solution)/shard_map/ppermute | solution.py:412
  71.8 4.0 %collective-permute-start.9 = (bf16[2,96,2048]{2,1,0:T(8,128)(2,1)S(1)}, bf16[2,96,2048]{2,1,0:T(8,128)(2,1)S(1)}, u32[]{:S(2)}, u32[]{:S(2)}) collective-permute-start(bf16[2,96,2048]{2,1,0:T(8,128)(2,1)S(1)} %collective-permute-done.8.refs_10_), channel_id=1, source_target_pairs={{0,8},{8,0},{16,24},{24,16},{1,9},{9,1},{17,25},{25,17},{2,10},{10... | collective-permute-start | bytes 2359304 | tf_op jit(solution)/shard_map/ppermute | solution.py:412
  71.9 12.5 %collective-permute-start.31 = (bf16[2,96,2048]{2,1,0:T(8,128)(2,1)S(1)}, bf16[2,96,2048]{2,1,0:T(8,128)(2,1)S(1)}, u32[]{:S(2)}, u32[]{:S(2)}) collective-permute-start(bf16[2,96,2048]{2,1,0:T(8,128)(2,1)S(1)} %get-tuple-element.83), channel_id=1, source_target_pairs={{0,8},{8,0},{16,24},{24,16},{1,9},{9,1},{17,25},{25,17},{2,10},{10... | collective-permute-start | bytes 2359304 | tf_op jit(solution)/shard_map/ppermute | solution.py:412
  74.0 35.1 %collective-permute-start.33 = (bf16[2,96,2048]{2,1,0:T(8,128)(2,1)S(1)}, bf16[2,96,2048]{2,1,0:T(8,128)(2,1)S(1)}, u32[]{:S(2)}, u32[]{:S(2)}) collective-permute-start(bf16[2,96,2048]{2,1,0:T(8,128)(2,1)S(1)} %add_parts.1), channel_id=1, source_target_pairs={{0,16},{8,24},{16,0},{24,8},{1,17},{9,25},{17,1},{25,9},{2,18},{10... | collective-permute-start | bytes 2359304 | tf_op jit(solution)/shard_map/ppermute | solution.py:412
  78.7 29.9 %collective-permute-start.10 = (bf16[48,2048]{1,0:T(8,128)(2,1)S(1)}, bf16[48,2048]{1,0:T(8,128)(2,1)S(1)}, u32[]{:S(2)}, u32[]{:S(2)}) collective-permute-start(bf16[48,2048]{1,0:T(8,128)(2,1)S(1)} %get-tuple-element.59), channel_id=1, source_target_pairs={{0,1},{1,0},{2,3},{3,2},{4,5},{5,4},{6,7},{7,6},{8,9},{9,8},{10,11... | collective-permute-start | bytes 589832 | tf_op jit(solution)/shard_map/ppermute | solution.py:412
  80.1 32.4 %copy-start.1 = (bf16[2,96,2048]{2,1,0:T(8,128)(2,1)S(1)}, bf16[2,96,2048]{2,1,0:T(8,128)(2,1)}, u32[]{:S(2)}) copy-start(bf16[2,96,2048]{2,1,0:T(8,128)(2,1)} %mc_ref.1) | copy-start | bytes 2359300
  80.1 32.4 %copy-start.2 = (bf16[2,96,2048]{2,1,0:T(8,128)(2,1)S(1)}, bf16[2,96,2048]{2,1,0:T(8,128)(2,1)}, u32[]{:S(2)}) copy-start(bf16[2,96,2048]{2,1,0:T(8,128)(2,1)} %vc_ref.1) | copy-start | bytes 2359300
  80.1 32.4 %copy-start.3 = (f32[2,96,16]{1,2,0:T(8,128)S(1)}, f32[2,96,16]{1,2,0:T(8,128)}, u32[]{:S(2)}) copy-start(f32[2,96,16]{1,2,0:T(8,128)} %param.11) | copy-start | bytes 36868
  80.1 32.5 %copy-start.4 = (f32[2,96,16]{1,2,0:T(8,128)S(1)}, f32[2,96,16]{1,2,0:T(8,128)}, u32[]{:S(2)}) copy-start(f32[2,96,16]{1,2,0:T(8,128)} %param.13) | copy-start | bytes 36868
  80.1 28.5 %collective-permute-start.11 = (bf16[48,2048]{1,0:T(8,128)(2,1)S(1)}, bf16[48,2048]{1,0:T(8,128)(2,1)S(1)}, u32[]{:S(2)}, u32[]{:S(2)}) collective-permute-start(bf16[48,2048]{1,0:T(8,128)(2,1)S(1)} %get-tuple-element.60), channel_id=1, source_target_pairs={{0,2},{1,3},{2,0},{3,1},{4,6},{5,7},{6,4},{7,5},{8,10},{9,11},{10,... | collective-permute-start | bytes 589832 | tf_op jit(solution)/shard_map/ppermute | solution.py:412
  83.7 4.0 %collective-permute-start.24 = (bf16[48,384]{1,0:T(8,128)(2,1)S(1)}, bf16[48,384]{1,0:T(8,128)(2,1)S(1)}, u32[]{:S(2)}, u32[]{:S(2)}) collective-permute-start(bf16[48,384]{1,0:T(8,128)(2,1)S(1)} %get-tuple-element.75), channel_id=1, source_target_pairs={{0,1},{1,0},{2,3},{3,2},{4,5},{5,4},{6,7},{7,6},{8,9},{9,8},{10,11... | collective-permute-start | bytes 110600 | tf_op jit(solution)/shard_map/ppermute | solution.py:412
  84.4 5.4 %collective-permute-start.25 = (bf16[48,384]{1,0:T(8,128)(2,1)S(1)}, bf16[48,384]{1,0:T(8,128)(2,1)S(1)}, u32[]{:S(2)}, u32[]{:S(2)}) collective-permute-start(bf16[48,384]{1,0:T(8,128)(2,1)S(1)} %get-tuple-element.76), channel_id=1, source_target_pairs={{0,2},{1,3},{2,0},{3,1},{4,6},{5,7},{6,4},{7,5},{8,10},{9,11},{10,... | collective-permute-start | bytes 110600 | tf_op jit(solution)/shard_map/ppermute | solution.py:412
  87.7 4.9 %collective-permute-start.26 = (bf16[48,384]{1,0:T(8,128)(2,1)S(1)}, bf16[48,384]{1,0:T(8,128)(2,1)S(1)}, u32[]{:S(2)}, u32[]{:S(2)}) collective-permute-start(bf16[48,384]{1,0:T(8,128)(2,1)S(1)} %get-tuple-element.77), channel_id=1, source_target_pairs={{0,3},{1,2},{2,1},{3,0},{4,7},{5,6},{6,5},{7,4},{8,11},{9,10},{10,... | collective-permute-start | bytes 110600 | tf_op jit(solution)/shard_map/ppermute | solution.py:412
  89.8 5.8 %collective-permute-start.27 = (bf16[48,384]{1,0:T(8,128)(2,1)S(1)}, bf16[48,384]{1,0:T(8,128)(2,1)S(1)}, u32[]{:S(2)}, u32[]{:S(2)}) collective-permute-start(bf16[48,384]{1,0:T(8,128)(2,1)S(1)} %get-tuple-element.78), channel_id=1, source_target_pairs={{0,4},{1,5},{2,6},{3,7},{4,0},{5,1},{6,2},{7,3},{8,12},{9,13},{10,... | collective-permute-start | bytes 110600 | tf_op jit(solution)/shard_map/ppermute | solution.py:412
  92.6 5.8 %collective-permute-start.28 = (bf16[48,384]{1,0:T(8,128)(2,1)S(1)}, bf16[48,384]{1,0:T(8,128)(2,1)S(1)}, u32[]{:S(2)}, u32[]{:S(2)}) collective-permute-start(bf16[48,384]{1,0:T(8,128)(2,1)S(1)} %get-tuple-element.79), channel_id=1, source_target_pairs={{0,5},{1,4},{2,7},{3,6},{4,1},{5,0},{6,3},{7,2},{8,13},{9,12},{10,... | collective-permute-start | bytes 110600 | tf_op jit(solution)/shard_map/ppermute | solution.py:412
  95.6 4.4 %collective-permute-start.29 = (bf16[48,384]{1,0:T(8,128)(2,1)S(1)}, bf16[48,384]{1,0:T(8,128)(2,1)S(1)}, u32[]{:S(2)}, u32[]{:S(2)}) collective-permute-start(bf16[48,384]{1,0:T(8,128)(2,1)S(1)} %get-tuple-element.80), channel_id=1, source_target_pairs={{0,6},{1,7},{2,4},{3,5},{4,2},{5,3},{6,0},{7,1},{8,14},{9,15},{10,... | collective-permute-start | bytes 110600 | tf_op jit(solution)/shard_map/ppermute | solution.py:412
  98.4 5.4 %collective-permute-start.30 = (bf16[48,384]{1,0:T(8,128)(2,1)S(1)}, bf16[48,384]{1,0:T(8,128)(2,1)S(1)}, u32[]{:S(2)}, u32[]{:S(2)}) collective-permute-start(bf16[48,384]{1,0:T(8,128)(2,1)S(1)} %get-tuple-element.81), channel_id=1, source_target_pairs={{0,7},{1,6},{2,5},{3,4},{4,3},{5,2},{6,1},{7,0},{8,15},{9,14},{10,... | collective-permute-start | bytes 110600 | tf_op jit(solution)/shard_map/ppermute | solution.py:412
  100.0 18.8 %collective-permute-start.12 = (bf16[48,2048]{1,0:T(8,128)(2,1)S(1)}, bf16[48,2048]{1,0:T(8,128)(2,1)S(1)}, u32[]{:S(2)}, u32[]{:S(2)}) collective-permute-start(bf16[48,2048]{1,0:T(8,128)(2,1)S(1)} %get-tuple-element.61), channel_id=1, source_target_pairs={{0,3},{1,2},{2,1},{3,0},{4,7},{5,6},{6,5},{7,4},{8,11},{9,10},{10,... | collective-permute-start | bytes 589832 | tf_op jit(solution)/shard_map/ppermute | solution.py:412
  103.8 22.3 %collective-permute-start.13 = (bf16[48,2048]{1,0:T(8,128)(2,1)S(1)}, bf16[48,2048]{1,0:T(8,128)(2,1)S(1)}, u32[]{:S(2)}, u32[]{:S(2)}) collective-permute-start(bf16[48,2048]{1,0:T(8,128)(2,1)S(1)} %get-tuple-element.62), channel_id=1, source_target_pairs={{0,4},{1,5},{2,6},{3,7},{4,0},{5,1},{6,2},{7,3},{8,12},{9,13},{10,... | collective-permute-start | bytes 589832 | tf_op jit(solution)/shard_map/ppermute | solution.py:412
  108.6 21.7 %collective-permute-start.14 = (bf16[48,2048]{1,0:T(8,128)(2,1)S(1)}, bf16[48,2048]{1,0:T(8,128)(2,1)S(1)}, u32[]{:S(2)}, u32[]{:S(2)}) collective-permute-start(bf16[48,2048]{1,0:T(8,128)(2,1)S(1)} %get-tuple-element.63), channel_id=1, source_target_pairs={{0,5},{1,4},{2,7},{3,6},{4,1},{5,0},{6,3},{7,2},{8,13},{9,12},{10,... | collective-permute-start | bytes 589832 | tf_op jit(solution)/shard_map/ppermute | solution.py:412
  108.6 27.7 %collective-permute-start.15 = (bf16[48,2048]{1,0:T(8,128)(2,1)S(1)}, bf16[48,2048]{1,0:T(8,128)(2,1)S(1)}, u32[]{:S(2)}, u32[]{:S(2)}) collective-permute-start(bf16[48,2048]{1,0:T(8,128)(2,1)S(1)} %get-tuple-element.64), channel_id=1, source_target_pairs={{0,6},{1,7},{2,4},{3,5},{4,2},{5,3},{6,0},{7,1},{8,14},{9,15},{10,... | collective-permute-start | bytes 589832 | tf_op jit(solution)/shard_map/ppermute | solution.py:412
  109.1 30.1 %collective-permute-start.16 = (bf16[48,2048]{1,0:T(8,128)(2,1)S(1)}, bf16[48,2048]{1,0:T(8,128)(2,1)S(1)}, u32[]{:S(2)}, u32[]{:S(2)}) collective-permute-start(bf16[48,2048]{1,0:T(8,128)(2,1)S(1)} %get-tuple-element.65), channel_id=1, source_target_pairs={{0,7},{1,6},{2,5},{3,4},{4,3},{5,2},{6,1},{7,0},{8,15},{9,14},{10,... | collective-permute-start | bytes 589832 | tf_op jit(solution)/shard_map/ppermute | solution.py:412

commit v3 on v2

v3 whole, which is shorter than its diff:
```python
import functools

import jax
import jax.numpy as jnp
from jax import lax
from jax.experimental import pallas as pl
from jax.experimental.pallas import tpu as pltpu
from jax.sharding import PartitionSpec as P

BLOCK = 128
ADAM_STEP = 100

beta_one = 0.9
beta_two = 0.95
learn_rate = 0.01

VMEM_LIMIT = 40 * 1024 * 1024
LARGE_LIMIT = 56 * 1024 * 1024
F32 = jnp.float32
BF16 = jnp.bfloat16


def cost(flops, nbytes):
    return pl.CostEstimate(flops=int(flops), bytes_accessed=int(nbytes), transcendentals=0)


def params(*semantics):
    if semantics:
        return pltpu.CompilerParams(vmem_limit_bytes=VMEM_LIMIT, dimension_semantics=semantics)
    return pltpu.CompilerParams(vmem_limit_bytes=VMEM_LIMIT)


def row_targets(route_row, placement_row, capacity):
    expert_count = placement_row.shape[1]
    row_count = route_row.shape[1]
    diagonal = lax.broadcasted_iota(jnp.int32, (expert_count, expert_count), 0) == (
        lax.broadcasted_iota(jnp.int32, (expert_count, expert_count), 1)
    )
    placement_col = jnp.sum(
        jnp.where(diagonal, placement_row, 0).astype(F32), axis=1, keepdims=True
    )
    hot = (placement_col == route_row.astype(F32)).astype(F32)
    earlier = lax.broadcasted_iota(jnp.int32, (row_count, row_count), 0)
    later = lax.broadcasted_iota(jnp.int32, (row_count, row_count), 1)
    before = (earlier < later).astype(F32).astype(BF16)
    position = jnp.dot(hot.astype(BF16), before, preferred_element_type=F32)
    slot = lax.broadcasted_iota(jnp.int32, (expert_count, row_count), 0)
    start = (slot * capacity).astype(F32)
    return jnp.sum(hot * (start + position), axis=0, keepdims=True).astype(jnp.int32)


def place_matrix(target, places):
    slots = lax.broadcasted_iota(jnp.int32, (places, target.shape[1]), 0)
    return (slots == target).astype(F32).astype(BF16)


def dispatch_kernel(
    capacity, route_ref, placement_ref, x_hbm, g_hbm, sent_hbm, target_ref,
    x_ref, g_ref, sent_ref, in_sems, out_sems,
):
    tiles, _, tile = g_ref.shape
    width = tiles * tile
    hidden = x_ref.shape[1]
    loads = [
        pltpu.make_async_copy(
            g_hbm.at[:, pl.ds(j * tile, tile)], g_ref.at[j], in_sems.at[j]
        )
        for j in range(tiles)
    ]
    loads.append(pltpu.make_async_copy(x_hbm, x_ref, in_sems.at[tiles]))
    for load in loads:
        load.start()
    target = row_targets(route_ref[...], placement_ref[...], capacity)
    target_ref[...] = target
    places = place_matrix(target, sent_ref.shape[0])
    stores = []
    for j in range(tiles + 1):
        loads[j].wait()
        columns = pl.ds(j * tile, tile if j < tiles else hidden)
        rows = g_ref[j] if j < tiles else x_ref[...]
        sent_ref[:, columns] = jnp.dot(places, rows, preferred_element_type=F32).astype(BF16)
        store = pltpu.make_async_copy(
            sent_ref.at[:, columns], sent_hbm.at[:, columns], out_sems.at[j]
        )
        store.start()
        stores.append(store)
    for store in stores:
        store.wait()


def dispatch(route, placement, x_rows, y_cot, capacity):
    row_count, hidden = x_rows.shape
    width = y_cot.shape[1]
    tile = min(width, 512)
    tiles = width // tile
    places = placement.shape[0] * capacity
    whole = pl.BlockSpec(memory_space=pltpu.VMEM)
    hbm = pl.BlockSpec(memory_space=pl.ANY)
    return pl.pallas_call(
        functools.partial(dispatch_kernel, capacity),
        in_specs=[whole, whole, hbm, hbm],
        out_specs=(hbm, whole),
        out_shape=(
            jax.ShapeDtypeStruct((places, width + hidden), BF16),
            jax.ShapeDtypeStruct((1, row_count), jnp.int32),
        ),
        scratch_shapes=[
            pltpu.VMEM((row_count, hidden), BF16),
            pltpu.VMEM((tiles, row_count, tile), BF16),
            pltpu.VMEM((places, width + hidden), BF16),
            pltpu.SemaphoreType.DMA((tiles + 1,)),
            pltpu.SemaphoreType.DMA((tiles + 1,)),
        ],
        compiler_params=pltpu.CompilerParams(vmem_limit_bytes=LARGE_LIMIT),
        cost_estimate=cost(
            2 * places * row_count * (hidden + width), 2 * (places + row_count) * (hidden + width)
        ),
        name="dispatch",
    )(route.reshape(1, row_count), placement.reshape(1, -1), x_rows, y_cot)


def home_places_kernel(target_ref, out_ref):
    target = target_ref[...]
    slots = lax.broadcasted_iota(jnp.int32, (out_ref.shape[1], target.shape[1]), 0)
    out_ref[...] = (slots == target).astype(F32).T.astype(BF16)


def home_places(target, places):
    return pl.pallas_call(
        home_places_kernel,
        out_shape=jax.ShapeDtypeStruct((target.shape[1], places), BF16),
        compiler_params=params(),
        cost_estimate=cost(places * target.shape[1], 2 * places * target.shape[1]),
        name="home_places",
    )(target)


def hidden_specs(rows, hidden, width):
    return [
        pl.BlockSpec((rows, BLOCK), functools.partial(lambda k, j: (0, k), width // BLOCK + i))
        for i in range(hidden // BLOCK)
    ]


def read_columns(refs):
    return jnp.concatenate([ref[...] for ref in refs], axis=1)


def collect_kernel(places_ref, home_ref, *refs):
    hidden_refs, y_ref, dx_ref = refs[:-2], refs[-2], refs[-1]
    places = places_ref[...]
    y_ref[...] = jnp.dot(places, home_ref[...], preferred_element_type=F32).astype(BF16)

    @pl.when(pl.program_id(0) == 0)
    def _():
        dx_ref[...] = jnp.dot(
            places, read_columns(hidden_refs), preferred_element_type=F32
        ).astype(BF16)


def collect(places, home, hidden):
    total, width = home.shape
    width -= hidden
    row_count = places.shape[0]
    tile = min(width, 512)
    specs = hidden_specs(total, hidden, width)
    return pl.pallas_call(
        collect_kernel,
        grid=(width // tile,),
        in_specs=[
            pl.BlockSpec((row_count, total), lambda j: (0, 0)),
            pl.BlockSpec((total, tile), lambda j: (0, j)),
        ]
        + specs,
        out_specs=(
            pl.BlockSpec((row_count, tile), lambda j: (0, j)),
            pl.BlockSpec((row_count, hidden), lambda j: (0, 0)),
        ),
        out_shape=(
            jax.ShapeDtypeStruct((row_count, width), BF16),
            jax.ShapeDtypeStruct((row_count, hidden), BF16),
        ),
        compiler_params=params("arbitrary"),
        cost_estimate=cost(
            2 * total * row_count * (hidden + width), 2 * (total + row_count) * (hidden + width)
        ),
        name="collect",
    )(places, *([home] * (1 + len(specs))))


def member_rows(rows, capacity, local_count):
    index = lax.broadcasted_iota(jnp.int32, (rows, 1), 0)
    return lax.rem(index, capacity * local_count) // capacity


def spread(x, capacity, local_count):
    member = member_rows(x.shape[0], capacity, local_count)
    zero = jnp.zeros_like(x)
    return jnp.concatenate([jnp.where(member == e, x, zero) for e in range(local_count)], axis=1)


def products_kernel(capacity, local_count, g_ref, w_ref, *refs):
    x_refs, out_ref, wide_ref, total_ref = refs[:-3], refs[-3], refs[-2], refs[-1]
    step = pl.program_id(0)
    tile = g_ref.shape[1]
    width = tile * pl.num_programs(0)
    weight = w_ref[...].reshape(wide_ref.shape[1], tile)

    @pl.when(step == 0)
    def _():
        wide_ref[...] = spread(read_columns(x_refs), capacity, local_count)
        total_ref[...] = jnp.zeros_like(total_ref)

    columns = pl.ds(pl.multiple_of(step * tile, tile), tile)
    out_ref[:, columns] = jnp.dot(
        wide_ref[...], weight, preferred_element_type=F32
    ).astype(BF16)
    total_ref[...] += lax.dot_general(
        g_ref[...], weight, (((1,), (1,)), ((), ())), preferred_element_type=F32
    )

    @pl.when(step == pl.num_programs(0) - 1)
    def _():
        hidden = wide_ref.shape[1] // local_count
        member = member_rows(total_ref.shape[0], capacity, local_count)
        picked = total_ref[:, :hidden]
        for e in range(1, local_count):
            picked = jnp.where(member == e, total_ref[:, e * hidden : (e + 1) * hidden], picked)
        out_ref[:, out_ref.shape[1] - hidden :] = picked.astype(BF16)


def products(local, weight, capacity):
    local_count, hidden, width = weight.shape
    total = local.shape[0]
    tile = min(width, 512)
    specs = hidden_specs(total, hidden, width)
    return pl.pallas_call(
        functools.partial(products_kernel, capacity, local_count),
        grid=(width // tile,),
        in_specs=[
            pl.BlockSpec((total, tile), lambda j: (0, j)),
            pl.BlockSpec((local_count, hidden, tile), lambda j: (0, 0, j)),
        ]
        + specs,
        out_specs=pl.BlockSpec(local.shape, lambda j: (0, 0)),
        out_shape=jax.ShapeDtypeStruct(local.shape, BF16),
        scratch_shapes=[
            pltpu.VMEM((total, local_count * hidden), BF16),
            pltpu.VMEM((total, local_count * hidden), F32),
        ],
        compiler_params=params("arbitrary"),
        cost_estimate=cost(
            4 * total * local_count * hidden * width,
            2 * (local_count * hidden + 2 * total) * width,
        ),
        name="products",
    )(local, weight, *([local] * len(specs)))


def gradient_kernel(capacity, local_count, parts, factor, g_ref, *refs):
    blocks = len(refs) - 2 - (parts if parts > 1 else 0)
    x_refs, wide_ref = refs[:blocks], refs[-1]
    out_refs = refs[blocks:-2] if parts > 1 else refs[blocks:-1]

    @pl.when(pl.program_id(0) == 0)
    def _():
        wide_ref[...] = spread(read_columns(x_refs), capacity, local_count)

    outer = lax.dot_general(
        wide_ref[...], g_ref[...], (((0,), (0,)), ((), ())), preferred_element_type=F32
    )
    low = (outer * factor).astype(BF16)
    if parts == 1:
        out_refs[0][...] = low.reshape(out_refs[0].shape)
        return
    split_ref = refs[-2]
    split_ref[...] = low.reshape(split_ref.shape)
    here = lax.axis_index("rep")
    for i, out_ref in enumerate(out_refs):
        owner = jnp.bitwise_xor(here, i)
        for e in range(local_count):
            out_ref[e] = split_ref[e, owner]


def gradient(local, hidden, capacity, local_count, parts, factor):
    total, width = local.shape
    width -= hidden
    tile = min(width, 512)
    slice_rows = hidden // parts
    specs = hidden_specs(total, hidden, width)
    split = [pltpu.VMEM((local_count, parts, slice_rows, tile), BF16)] if parts > 1 else []
    return list(pl.pallas_call(
        functools.partial(gradient_kernel, capacity, local_count, parts, factor),
        grid=(width // tile,),
        in_specs=[pl.BlockSpec((total, tile), lambda j: (0, j))] + specs,
        out_specs=(pl.BlockSpec((local_count, slice_rows, tile), lambda j: (0, 0, j)),) * parts,
        out_shape=(jax.ShapeDtypeStruct((local_count, slice_rows, width), BF16),) * parts,
        scratch_shapes=split + [pltpu.VMEM((total, local_count * hidden), BF16)],
        compiler_params=params("arbitrary"),
        cost_estimate=cost(
            2 * total * local_count * hidden * width,
            2 * (local_count * hidden + total) * width,
        ),
        name="gradient",
    )(*([local] * (1 + len(specs)))))


def join_kernel(*refs):
    piece_refs, out_ref = refs[:-1], refs[-1]
    here = lax.axis_index("rep")
    for i, ref in enumerate(piece_refs):
        owner = jnp.bitwise_xor(here, i)
        for e in range(out_ref.shape[0]):
            out_ref[e, owner] = ref[e]


def join_weight(pieces):
    if len(pieces) == 1:
        return pieces[0]
    local_count, rows, width = pieces[0].shape
    count = len(pieces)
    tile = min(width, 512)
    joined = pl.pallas_call(
        join_kernel,
        grid=(width // tile,),
        in_specs=[pl.BlockSpec((local_count, rows, tile), lambda j: (0, 0, j))] * count,
        out_specs=pl.BlockSpec((local_count, count, rows, tile), lambda j: (0, 0, 0, j)),
        out_shape=jax.ShapeDtypeStruct((local_count, count, rows, width), BF16),
        compiler_params=params("arbitrary"),
        cost_estimate=cost(0, 4 * local_count * count * rows * width),
        name="join_weight",
    )(*pieces)
    return joined.reshape(local_count, count * rows, width)


def cast_kernel(w_ref, out_ref):
    out_ref[...] = w_ref[...].astype(BF16)


def cast_weight(weight):
    members, rows, width = weight.shape
    tile = min(width, 512)
    spec = pl.BlockSpec((members, rows, tile), lambda j: (0, 0, j))
    return pl.pallas_call(
        cast_kernel,
        grid=(width // tile,),
        in_specs=[spec],
        out_specs=spec,
        out_shape=jax.ShapeDtypeStruct(weight.shape, BF16),
        compiler_params=params("arbitrary"),
        cost_estimate=cost(weight.size, 6 * weight.size),
        name="cast_weight",
    )(weight)


def add_kernel(a_ref, b_ref, out_ref):
    out_ref[...] = (a_ref[...].astype(F32) + b_ref[...].astype(F32)).astype(BF16)


def add_parts(a, b):
    members, rows, width = a.shape
    tile = min(width, 1024)
    spec = pl.BlockSpec((members, rows, tile), lambda j: (0, 0, j))
    return pl.pallas_call(
        add_kernel,
        grid=(width // tile,),
        in_specs=[spec, spec],
        out_specs=spec,
        out_shape=jax.ShapeDtypeStruct(a.shape, BF16),
        compiler_params=params("arbitrary"),
        cost_estimate=cost(a.size, 6 * a.size),
        name="add_parts",
    )(a, b)


def adam_kernel(
    parts, master_ref, mc_ref, ms_ref, vc_ref, vs_ref, *refs
):
    grad_refs = refs[:parts]
    master_out, mc_out, ms_out, vc_out, vs_out = refs[parts:]
    blocks = ms_ref.shape[1]
    rows = ms_ref.shape[2]
    corr_one = 1.0 - beta_one**ADAM_STEP
    corr_two = 1.0 - beta_two**ADAM_STEP
    m_scales = (ms_ref[0] * beta_one).T
    v_scales = (vs_ref[0] * beta_two).T
    lane = lax.broadcasted_iota(jnp.int32, (rows, blocks), 1)
    m_tops = jnp.zeros((rows, blocks), F32)
    v_tops = jnp.zeros((rows, blocks), F32)
    for b in range(blocks):
        cols = slice(b * BLOCK, (b + 1) * BLOCK)
        grad = grad_refs[0][0, :, cols].astype(F32)
        for ref in grad_refs[1:]:
            grad = grad + ref[0, :, cols].astype(F32)
        m_next = mc_ref[0, :, cols].astype(F32) * m_scales[:, b : b + 1] + (1.0 - beta_one) * grad
        v_next = vc_ref[0, :, cols].astype(F32) * v_scales[:, b : b + 1] + (
            1.0 - beta_two
        ) * (grad * grad)
        v_hat = v_next * (1.0 / corr_two)
        root = v_hat * lax.rsqrt(v_hat) + 1e-08
        master_out[0, :, cols] = master_ref[0, :, cols] - (learn_rate / corr_one) * m_next / root
        m_top = jnp.max(jnp.abs(m_next), axis=-1, keepdims=True) + 1e-06
        v_top = jnp.max(v_next, axis=-1, keepdims=True) + 1e-06
        mc_out[0, :, cols] = (m_next * (1.0 / m_top)).astype(BF16)
        vc_out[0, :, cols] = (v_next * (1.0 / v_top)).astype(BF16)
        m_tops = jnp.where(lane == b, m_top, m_tops)
        v_tops = jnp.where(lane == b, v_top, v_tops)
    ms_out[0] = m_tops.T
    vs_out[0] = v_tops.T


def adam(master_weight, grads, m_code, m_scale, v_code, v_scale):
    members, rows, width = master_weight.shape
    blocks = m_scale.shape[-1]
    count = 8 if blocks % 8 == 0 else blocks
    big = pl.BlockSpec((1, rows, count * BLOCK), lambda e, j: (e, 0, j))
    small = pl.BlockSpec((1, count, rows), lambda e, j: (e, j, 0))
    scales = jax.ShapeDtypeStruct((members, blocks, rows), F32)
    master_next, m_code_next, m_scale_next, v_code_next, v_scale_next = pl.pallas_call(
        functools.partial(adam_kernel, len(grads)),
        grid=(members, blocks // count),
        in_specs=[big, big, small, big, small] + [big] * len(grads),
        out_specs=(big, big, small, big, small),
        out_shape=(
            jax.ShapeDtypeStruct(master_weight.shape, F32),
            jax.ShapeDtypeStruct(master_weight.shape, BF16),
            scales,
            jax.ShapeDtypeStruct(master_weight.shape, BF16),
            scales,
        ),
        compiler_params=params("arbitrary", "arbitrary"),
        cost_estimate=cost(40 * master_weight.size, 18 * master_weight.size),
        name="adam",
    )(master_weight, m_code, jnp.swapaxes(m_scale, 1, 2), v_code, jnp.swapaxes(v_scale, 1, 2), *grads)
    return (
        master_next,
        m_code_next,
        jnp.swapaxes(m_scale_next, 1, 2),
        v_code_next,
        jnp.swapaxes(v_scale_next, 1, 2),
    )


def swap(array, axis, offset):
    size = lax.axis_size(axis)
    return lax.ppermute(array, axis, [(i, i ^ offset) for i in range(size)])


def exchange(buffer, groups):
    places, width = buffer.shape
    parts = buffer.reshape(groups, places // groups, width)
    moved = lax.all_to_all(parts, "grp", split_axis=0, concat_axis=0, tiled=True)
    return moved.reshape(places, width)


def gather_weight(weight_slice, replicas):
    if replicas != 4:
        return [lax.all_gather(weight_slice, "rep", axis=1, tiled=True)]
    far = swap(weight_slice, "rep", 2)
    near = swap(weight_slice, "rep", 1)
    return [weight_slice, near, far, swap(far, "rep", 1)]


def sum_gradient(parts):
    if len(parts) != 4:
        return [lax.psum_scatter(parts[0], "rep", scatter_dimension=1, tiled=True)]
    far = swap(parts[3], "rep", 1)
    near = swap(parts[1], "rep", 1)
    return [parts[0], near, swap(add_parts(parts[2], far), "rep", 2)]


def per_device(master_weight, m_code, m_scale, v_code, v_scale, placement, route, x_rows, y_cot):
    local_count = master_weight.shape[0]
    row_count = x_rows.shape[0]
    expert_count = placement.shape[0]
    groups = lax.axis_size("grp")
    replicas = lax.axis_size("rep")
    grad_factor = float(row_count * groups * replicas // expert_count) ** (-0.5)
    capacity = max(2, (3 * row_count + 2 * expert_count - 1) // (2 * expert_count))
    places = expert_count * capacity
    sent, target = dispatch(route, placement, x_rows, y_cot, capacity)
    local = exchange(sent, groups)
    early_master, target = lax.optimization_barrier((master_weight, target))
    weight = join_weight(gather_weight(cast_weight(early_master), replicas))
    results = products(local, weight, capacity)
    local, results = lax.optimization_barrier((local, results))
    home = exchange(results, groups)

    parts = replicas if replicas == 4 else 1
    hidden = x_rows.shape[1]
    grads = sum_gradient(gradient(local, hidden, capacity, local_count, parts, grad_factor))
    updated = adam(master_weight, grads, m_code, m_scale, v_code, v_scale)
    y_rows, x_grad = collect(home_places(target, places), home, hidden)
    return (y_rows, x_grad) + tuple(updated)


def solution(mesh):
    return jax.shard_map(
        per_device,
        mesh=mesh,
        in_specs=(
            P("grp", "rep", None),
            P("grp", "rep", None),
            P("grp", "rep", None),
            P("grp", "rep", None),
            P("grp", "rep", None),
            P(),
            P(("rep", "grp")),
            P(("rep", "grp"), None),
            P(("rep", "grp"), None),
        ),
        out_specs=(
            P(("rep", "grp"), None),
            P(("rep", "grp"), None),
            P("grp", "rep", None),
            P("grp", "rep", None),
            P("grp", "rep", None),
            P("grp", "rep", None),
            P("grp", "rep", None),
        ),
        check_vma=False,
    )
```

time: 142 us -> 115 us (0.81)
  the two profiles are of different devices: /device:TPU:16 before, /device:TPU:0 now
where the time goes in v3:
time: 115 us
  waiting for transfers between devices  69.4 us (60%)
  Pallas kernels  24.7 us (21%)
  starting transfers between devices  15.4 us (13%)
  local copies, waits for them, and re-layouts  4.79 us (4%)
    ppermute x6, waiting for transfers between devices, swap(): return lax.ppermute(array, axis, [(i, i ^ offset) for i in range(size)])  39.5 us
    all_to_all x2, waiting for transfers between devices, exchange(): lax.all_to_all(parts, 'grp', split_axis=0, concat_axis=0, tiled=True)  29.9 us
    all_to_all x2, starting transfers between devices, exchange(): lax.all_to_all(parts, 'grp', split_axis=0, concat_axis=0, tiled=True)  11.7 us
    pallas_call x1, Pallas kernels, adam(): pl.pallas_call(functools.partial(adam_kernel, len(grads)), grid=(members,...  6.19 us
    unnamed x18, local copies, waits for them, and re-layouts  4.79 us
    pallas_call x1, Pallas kernels, collect(): pl.pallas_call(collect_kernel, grid=(width // tile,), in_specs=[pl.BlockS...  4.46 us
    pallas_call x1, Pallas kernels, products(): pl.pallas_call(functools.partial(products_kernel, capacity, local_count),...  4.44 us
    pallas_call x1, Pallas kernels, dispatch(): pl.pallas_call(functools.partial(dispatch_kernel, capacity), in_specs=[wh...  4.4 us
  transfers between devices with their start and end apart: 8, of which 6 were waited for; matrix products, arithmetic and copies ran while one was open for 0% of the time, Pallas kernels for 10%

profile of v3, /device:TPU:0, one launch (start us, length us, event | category | flops | bytes accessed | tf_op | source)
XLA Modules:
  0.0 115.1 jit_solution(4451524005166378871)
XLA Ops:
  0.6 4.4 %dispatch.1 = (bf16[384,2432]{1,0:T(8,128)(2,1)}, s32[1,256]{1,0:T(1,128)}) custom-call(s32[1,256]{1,0:T(1,128)} %bitcast.26, s32[1,16]{1,0:T(1,128)} %bitcast.27, bf16[256,384]{1,0:T(8,128)(2,1)} %x_hbm.1, bf16[256,2048]{1,0:T(8,128)(2,1)} %g_hbm.1), custom_call_target="tpu_custom_call" | custom-call | flops 478150656 | bytes 3112960 | tf_op jit(solution)/shard_map/dispatch/pallas_call | solution.py:99
  5.0 0.0 copy-start.3
  5.1 7.4 %all-to-all-start = ((bf16[8,48,2432]{2,1,0:T(8,128)(2,1)}), bf16[8,48,2432]{2,1,0:T(8,128)(2,1)S(1)}, u32[]{:S(2)}, u32[]{:S(2)}) async-start(bf16[8,48,2432]{2,1,0:T(8,128)(2,1)} %bitcast.23), calls=%async_computation | async-start | bytes 3735552 | tf_op jit(solution)/shard_map/all_to_all | solution.py:452
  12.4 0.0 copy-done.3
  12.4 0.3 cast_weight.1.refs_0_
  12.8 1.6 %collective-permute-start.1 = (bf16[2,96,2048]{2,1,0:T(8,128)(2,1)S(1)}, bf16[2,96,2048]{2,1,0:T(8,128)(2,1)S(1)}, u32[]{:S(2)}, u32[]{:S(2)}) collective-permute-start(bf16[2,96,2048]{2,1,0:T(8,128)(2,1)S(1)} %cast_weight.1.refs_0_), channel_id=1, source_target_pairs={{0,16},{8,24},{16,0},{24,8},{1,17},{9,25},{17,1},{25,9},{2,18},{10... | collective-permute-start | bytes 2359304 | tf_op jit(solution)/shard_map/ppermute | solution.py:446
  14.4 0.0 collective-permute-start
  14.4 17.5 %collective-permute-done.1.refs_2_ = bf16[2,96,2048]{2,1,0:T(8,128)(2,1)S(1)} collective-permute-done((bf16[2,96,2048]{2,1,0:T(8,128)(2,1)S(1)}, bf16[2,96,2048]{2,1,0:T(8,128)(2,1)S(1)}, u32[]{:S(2)}, u32[]{:S(2)}) %collective-permute-start.1) | collective-permute-done | bytes 786464 | tf_op jit(solution)/shard_map/ppermute | solution.py:446
  31.9 0.0 collective-permute-start.2
  31.9 0.0 collective-permute-done.refs_1_
  31.9 2.3 %collective-permute-done.2.refs_3_ = bf16[2,96,2048]{2,1,0:T(8,128)(2,1)S(1)} collective-permute-done((bf16[2,96,2048]{2,1,0:T(8,128)(2,1)S(1)}, bf16[2,96,2048]{2,1,0:T(8,128)(2,1)S(1)}, u32[]{:S(2)}, u32[]{:S(2)}) %collective-permute-start.2) | collective-permute-done | bytes 786464 | tf_op jit(solution)/shard_map/ppermute | solution.py:446
  34.2 0.8 join_weight.1
  35.0 0.0 copy-start
  35.0 1.6 %copy-done = bf16[2,4,96,2048]{3,2,1,0:T(8,128)(2,1)} copy-done((bf16[2,4,96,2048]{3,2,1,0:T(8,128)(2,1)}, bf16[2,4,96,2048]{3,2,1,0:T(8,128)(2,1)S(1)}, u32[]{:S(2)}) %copy-start) | copy-done | bytes 3145752
  36.6 19.2 %all-to-all-done = bf16[8,48,2432]{2,1,0:T(8,128)(2,1)S(1)} async-done(((bf16[8,48,2432]{2,1,0:T(8,128)(2,1)}), bf16[8,48,2432]{2,1,0:T(8,128)(2,1)S(1)}, u32[]{:S(2)}, u32[]{:S(2)}) %all-to-all-start) | async-done | bytes 1867808 | tf_op jit(solution)/shard_map/all_to_all | solution.py:452
  55.8 0.0 copy-start.1
  55.8 1.9 %copy-done.1 = bf16[2,4,96,2048]{3,2,1,0:T(8,128)(2,1)S(1)} copy-done((bf16[2,4,96,2048]{3,2,1,0:T(8,128)(2,1)S(1)}, bf16[2,4,96,2048]{3,2,1,0:T(8,128)(2,1)}, u32[]{:S(2)}) %copy-start.1) | copy-done | bytes 3145752
  57.7 4.4 %products.1 = bf16[384,2432]{1,0:T(8,128)(2,1)S(1)} custom-call(bf16[384,2432]{1,0:T(8,128)(2,1)S(1)} %bitcast.11, bf16[2,384,2048]{2,1,0:T(8,128)(2,1)S(1)} %bitcast.19, bf16[384,2432]{1,0:T(8,128)(2,1)S(1)} %bitcast.12, bf16[384,2432]{1,0:T(8,128)(2,1)S(1)} %bitcast.13, bf16[384,2432]{1,0:T(8,128)(2,1)S(1)} %bitcast.14), custom_call_target="tpu_custom_call" | custom-call | flops 2415919104 | bytes 6291456 | tf_op jit(solution)/shard_map/products/pallas_call | solution.py:237
  62.1 0.0 copy-start.2
  62.1 1.2 %copy-done.2 = bf16[384,2432]{1,0:T(8,128)(2,1)} copy-done((bf16[384,2432]{1,0:T(8,128)(2,1)}, bf16[384,2432]{1,0:T(8,128)(2,1)S(1)}, u32[]{:S(2)}) %copy-start.2) | copy-done | bytes 1867800
  63.4 4.3 %all-to-all-start.1 = ((bf16[8,48,2432]{2,1,0:T(8,128)(2,1)}), bf16[8,48,2432]{2,1,0:T(8,128)(2,1)}, u32[]{:S(2)}, u32[]{:S(2)}) async-start(bf16[8,48,2432]{2,1,0:T(8,128)(2,1)} %bitcast.20), calls=%async_computation.1 | async-start | bytes 3735552 | tf_op jit(solution)/shard_map/all_to_all | solution.py:452
  67.7 3.5 %gradient.1 = (bf16[2,96,2048]{2,1,0:T(8,128)(2,1)S(1)}, bf16[2,96,2048]{2,1,0:T(8,128)(2,1)S(1)}, bf16[2,96,2048]{2,1,0:T(8,128)(2,1)S(1)}, bf16[2,96,2048]{2,1,0:T(8,128)(2,1)S(1)}) custom-call(bf16[384,2432]{1,0:T(8,128)(2,1)S(1)} %bitcast.15, bf16[384,2432]{1,0:T(8,128)(2,1)S(1)} %bitcast.16, bf16[384,2432]{1,0:T(8,128)(2,1)S(1)} %bitcast.17, ...), custom_call_target="tpu_custom_call" | custom-call | flops 1207959552 | bytes 4718592 | tf_op jit(solution)/shard_map/gradient/pallas_call | solution.py:292
  71.2 0.0 copy-start.8
  71.2 0.0 copy-start.4
  71.2 0.0 copy-start.5
  71.2 0.0 copy-start.6
  71.3 0.0 copy-start.7
  71.3 0.1 collective-permute-start.4
  71.3 0.5 collective-permute-start.3
  71.8 1.8 %collective-permute-done.4.b_ref = bf16[2,96,2048]{2,1,0:T(8,128)(2,1)S(1)} collective-permute-done((bf16[2,96,2048]{2,1,0:T(8,128)(2,1)S(1)}, bf16[2,96,2048]{2,1,0:T(8,128)(2,1)S(1)}, u32[]{:S(2)}, u32[]{:S(2)}) %collective-permute-start.4) | collective-permute-done | bytes 786464 | tf_op jit(solution)/shard_map/ppermute | solution.py:446
  73.6 0.4 add_parts.1
  74.0 1.6 %collective-permute-start.5 = (bf16[2,96,2048]{2,1,0:T(8,128)(2,1)S(1)}, bf16[2,96,2048]{2,1,0:T(8,128)(2,1)S(1)}, u32[]{:S(2)}, u32[]{:S(2)}) collective-permute-start(bf16[2,96,2048]{2,1,0:T(8,128)(2,1)S(1)} %add_parts.1), channel_id=1, source_target_pairs={{0,16},{8,24},{16,0},{24,8},{1,17},{9,25},{17,1},{25,9},{2,18},{10... | collective-permute-start | bytes 2359304 | tf_op jit(solution)/shard_map/ppermute | solution.py:446
  75.6 0.0 copy-done.8
  75.6 0.1 home_places.1.places_ref
  75.7 0.0 collective-permute-done.3.refs_1_
  75.7 17.9 %collective-permute-done.5.refs_2_ = bf16[2,96,2048]{2,1,0:T(8,128)(2,1)S(1)} collective-permute-done((bf16[2,96,2048]{2,1,0:T(8,128)(2,1)S(1)}, bf16[2,96,2048]{2,1,0:T(8,128)(2,1)S(1)}, u32[]{:S(2)}, u32[]{:S(2)}) %collective-permute-start.5) | collective-permute-done | bytes 786464 | tf_op jit(solution)/shard_map/ppermute | solution.py:446
  93.7 0.0 copy-done.4
  93.7 0.0 copy-done.5
  93.7 0.0 copy-done.6
  93.7 0.0 copy-done.7
  93.7 6.2 %adam.1 = (f32[2,96,2048]{2,1,0:T(8,128)}, bf16[2,96,2048]{2,1,0:T(8,128)(2,1)}, f32[2,16,96]{2,1,0:T(8,128)}, bf16[2,96,2048]{2,1,0:T(8,128)(2,1)}, f32[2,16,96]{2,1,0:T(8,128)}) custom-call(f32[2,96,2048]{2,1,0:T(8,128)S(1)} %copy-done.3, bf16[2,96,2048]{2,1,0:T(8,128)(2,1)S(1)} %copy-done.4, f32[2,16,96]{2,1,0:T(8,128)S(1)} %bitcast.21, ...), custom_call_target="tpu_custom_call" | custom-call | flops 15728640 | bytes 7077888 | tf_op jit(solution)/shard_map/adam/pallas_call | solution.py:419
  99.9 10.7 %all-to-all-done.1 = bf16[8,48,2432]{2,1,0:T(8,128)(2,1)} async-done(((bf16[8,48,2432]{2,1,0:T(8,128)(2,1)}), bf16[8,48,2432]{2,1,0:T(8,128)(2,1)}, u32[]{:S(2)}, u32[]{:S(2)}) %all-to-all-start.1) | async-done | bytes 1867808 | tf_op jit(solution)/shard_map/all_to_all | solution.py:452
  110.6 4.5 %collect.1 = (bf16[256,2048]{1,0:T(8,128)(2,1)}, bf16[256,384]{1,0:T(8,128)(2,1)}) custom-call(bf16[256,384]{1,0:T(8,128)(2,1)S(1)} %home_places.1.places_ref, bf16[384,2432]{1,0:T(8,128)(2,1)} %bitcast.6.home_ref.refs_0_.refs_1_.refs_2_, bf16[384,2432]{1,0:T(8,128)(2,1)} %bitcast.6.home_ref.refs_0_.refs_1_.refs_2_, ...), custom_call_target="tpu_custom_call" | custom-call | flops 478150656 | bytes 3112960 | tf_op jit(solution)/shard_map/collect/pallas_call | solution.py:167
Async XLA Ops:
  5.0 7.4 %copy-start.3 = (f32[2,96,2048]{2,1,0:T(8,128)S(1)}, f32[2,96,2048]{2,1,0:T(8,128)}, u32[]{:S(2)}) copy-start(f32[2,96,2048]{2,1,0:T(8,128)} %master_ref.1) | copy-start | bytes 4718596
  5.1 50.7 %all-to-all-start = ((bf16[8,48,2432]{2,1,0:T(8,128)(2,1)}), bf16[8,48,2432]{2,1,0:T(8,128)(2,1)S(1)}, u32[]{:S(2)}, u32[]{:S(2)}) async-start(bf16[8,48,2432]{2,1,0:T(8,128)(2,1)} %bitcast.23), calls=%async_computation | async-start | bytes 3735552 | tf_op jit(solution)/shard_map/all_to_all | solution.py:452
  12.8 19.1 %collective-permute-start.1 = (bf16[2,96,2048]{2,1,0:T(8,128)(2,1)S(1)}, bf16[2,96,2048]{2,1,0:T(8,128)(2,1)S(1)}, u32[]{:S(2)}, u32[]{:S(2)}) collective-permute-start(bf16[2,96,2048]{2,1,0:T(8,128)(2,1)S(1)} %cast_weight.1.refs_0_), channel_id=1, source_target_pairs={{0,16},{8,24},{16,0},{24,8},{1,17},{9,25},{17,1},{25,9},{2,18},{10... | collective-permute-start | bytes 2359304 | tf_op jit(solution)/shard_map/ppermute | solution.py:446
  14.4 17.5 %collective-permute-start = (bf16[2,96,2048]{2,1,0:T(8,128)(2,1)S(1)}, bf16[2,96,2048]{2,1,0:T(8,128)(2,1)S(1)}, u32[]{:S(2)}, u32[]{:S(2)}) collective-permute-start(bf16[2,96,2048]{2,1,0:T(8,128)(2,1)S(1)} %cast_weight.1.refs_0_), channel_id=1, source_target_pairs={{0,8},{8,0},{16,24},{24,16},{1,9},{9,1},{17,25},{25,17},{2,10},{10... | collective-permute-start | bytes 2359304 | tf_op jit(solution)/shard_map/ppermute | solution.py:446
  31.9 2.3 %collective-permute-start.2 = (bf16[2,96,2048]{2,1,0:T(8,128)(2,1)S(1)}, bf16[2,96,2048]{2,1,0:T(8,128)(2,1)S(1)}, u32[]{:S(2)}, u32[]{:S(2)}) collective-permute-start(bf16[2,96,2048]{2,1,0:T(8,128)(2,1)S(1)} %collective-permute-done.1.refs_2_), channel_id=1, source_target_pairs={{0,8},{8,0},{16,24},{24,16},{1,9},{9,1},{17,25},{25,17},{2,10},{10... | collective-permute-start | bytes 2359304 | tf_op jit(solution)/shard_map/ppermute | solution.py:446
  35.0 1.6 %copy-start = (bf16[2,4,96,2048]{3,2,1,0:T(8,128)(2,1)}, bf16[2,4,96,2048]{3,2,1,0:T(8,128)(2,1)S(1)}, u32[]{:S(2)}) copy-start(bf16[2,4,96,2048]{3,2,1,0:T(8,128)(2,1)S(1)} %join_weight.1) | copy-start | bytes 9437188
  55.8 1.9 %copy-start.1 = (bf16[2,4,96,2048]{3,2,1,0:T(8,128)(2,1)S(1)}, bf16[2,4,96,2048]{3,2,1,0:T(8,128)(2,1)}, u32[]{:S(2)}) copy-start(bf16[2,4,96,2048]{3,2,1,0:T(8,128)(2,1)} %copy-done) | copy-start | bytes 9437188
  62.1 1.2 %copy-start.2 = (bf16[384,2432]{1,0:T(8,128)(2,1)}, bf16[384,2432]{1,0:T(8,128)(2,1)S(1)}, u32[]{:S(2)}) copy-start(bf16[384,2432]{1,0:T(8,128)(2,1)S(1)} %products.1) | copy-start | bytes 5603332
  63.4 47.3 %all-to-all-start.1 = ((bf16[8,48,2432]{2,1,0:T(8,128)(2,1)}), bf16[8,48,2432]{2,1,0:T(8,128)(2,1)}, u32[]{:S(2)}, u32[]{:S(2)}) async-start(bf16[8,48,2432]{2,1,0:T(8,128)(2,1)} %bitcast.20), calls=%async_computation.1 | async-start | bytes 3735552 | tf_op jit(solution)/shard_map/all_to_all | solution.py:452
  71.2 4.4 %copy-start.8 = (s32[1,256]{1,0:T(1,128)S(1)}, s32[1,256]{1,0:T(1,128)}, u32[]{:S(2)}) copy-start(s32[1,256]{1,0:T(1,128)} %get-tuple-element.25.target_ref) | copy-start | bytes 3076
  71.2 22.4 %copy-start.4 = (bf16[2,96,2048]{2,1,0:T(8,128)(2,1)S(1)}, bf16[2,96,2048]{2,1,0:T(8,128)(2,1)}, u32[]{:S(2)}) copy-start(bf16[2,96,2048]{2,1,0:T(8,128)(2,1)} %mc_ref.1) | copy-start | bytes 2359300
  71.2 22.4 %copy-start.5 = (bf16[2,96,2048]{2,1,0:T(8,128)(2,1)S(1)}, bf16[2,96,2048]{2,1,0:T(8,128)(2,1)}, u32[]{:S(2)}) copy-start(bf16[2,96,2048]{2,1,0:T(8,128)(2,1)} %vc_ref.1) | copy-start | bytes 2359300
  71.2 22.4 %copy-start.6 = (f32[2,96,16]{1,2,0:T(8,128)S(1)}, f32[2,96,16]{1,2,0:T(8,128)}, u32[]{:S(2)}) copy-start(f32[2,96,16]{1,2,0:T(8,128)} %param.11) | copy-start | bytes 36868
  71.3 22.4 %copy-start.7 = (f32[2,96,16]{1,2,0:T(8,128)S(1)}, f32[2,96,16]{1,2,0:T(8,128)}, u32[]{:S(2)}) copy-start(f32[2,96,16]{1,2,0:T(8,128)} %param.13) | copy-start | bytes 36868
  71.3 2.4 %collective-permute-start.4 = (bf16[2,96,2048]{2,1,0:T(8,128)(2,1)S(1)}, bf16[2,96,2048]{2,1,0:T(8,128)(2,1)S(1)}, u32[]{:S(2)}, u32[]{:S(2)}) collective-permute-start(bf16[2,96,2048]{2,1,0:T(8,128)(2,1)S(1)} %get-tuple-element.35), channel_id=1, source_target_pairs={{0,8},{8,0},{16,24},{24,16},{1,9},{9,1},{17,25},{25,17},{2,10},{10... | collective-permute-start | bytes 2359304 | tf_op jit(solution)/shard_map/ppermute | solution.py:446
  71.3 4.4 %collective-permute-start.3 = (bf16[2,96,2048]{2,1,0:T(8,128)(2,1)S(1)}, bf16[2,96,2048]{2,1,0:T(8,128)(2,1)S(1)}, u32[]{:S(2)}, u32[]{:S(2)}) collective-permute-start(bf16[2,96,2048]{2,1,0:T(8,128)(2,1)S(1)} %get-tuple-element.33), channel_id=1, source_target_pairs={{0,8},{8,0},{16,24},{24,16},{1,9},{9,1},{17,25},{25,17},{2,10},{10... | collective-permute-start | bytes 2359304 | tf_op jit(solution)/shard_map/ppermute | solution.py:446
  74.0 19.6 %collective-permute-start.5 = (bf16[2,96,2048]{2,1,0:T(8,128)(2,1)S(1)}, bf16[2,96,2048]{2,1,0:T(8,128)(2,1)S(1)}, u32[]{:S(2)}, u32[]{:S(2)}) collective-permute-start(bf16[2,96,2048]{2,1,0:T(8,128)(2,1)S(1)} %add_parts.1), channel_id=1, source_target_pairs={{0,16},{8,24},{16,0},{24,8},{1,17},{9,25},{17,1},{25,9},{2,18},{10... | collective-permute-start | bytes 2359304 | tf_op jit(solution)/shard_map/ppermute | solution.py:446

commit v4 on v3

--- a/solution.py
+++ b/solution.py
@@ -55,12 +55,15 @@
 
 
 def dispatch_kernel(
-    capacity, route_ref, placement_ref, x_hbm, g_hbm, sent_hbm, target_ref,
-    x_ref, g_ref, sent_ref, in_sems, out_sems,
+    capacity, route_hbm, placement_hbm, x_hbm, g_hbm, sent_hbm, target_hbm,
+    route_ref, placement_ref, target_ref, x_ref, g_ref, sent_ref, key_sems, in_sems, out_sems,
 ):
     tiles, _, tile = g_ref.shape
-    width = tiles * tile
     hidden = x_ref.shape[1]
+    keys = [
+        pltpu.make_async_copy(route_hbm, route_ref, key_sems.at[0]),
+        pltpu.make_async_copy(placement_hbm, placement_ref, key_sems.at[1]),
+    ]
     loads = [
         pltpu.make_async_copy(
             g_hbm.at[:, pl.ds(j * tile, tile)], g_ref.at[j], in_sems.at[j]
@@ -68,12 +71,15 @@
         for j in range(tiles)
     ]
     loads.append(pltpu.make_async_copy(x_hbm, x_ref, in_sems.at[tiles]))
-    for load in loads:
+    for load in keys + loads:
         load.start()
+    for load in keys:
+        load.wait()
     target = row_targets(route_ref[...], placement_ref[...], capacity)
     target_ref[...] = target
+    stores = [pltpu.make_async_copy(target_ref, target_hbm, key_sems.at[2])]
+    stores[0].start()
     places = place_matrix(target, sent_ref.shape[0])
-    stores = []
     for j in range(tiles + 1):
         loads[j].wait()
         columns = pl.ds(j * tile, tile if j < tiles else hidden)
@@ -91,23 +97,27 @@
 def dispatch(route, placement, x_rows, y_cot, capacity):
     row_count, hidden = x_rows.shape
     width = y_cot.shape[1]
+    expert_count = placement.shape[0]
     tile = min(width, 512)
     tiles = width // tile
-    places = placement.shape[0] * capacity
-    whole = pl.BlockSpec(memory_space=pltpu.VMEM)
+    places = expert_count * capacity
     hbm = pl.BlockSpec(memory_space=pl.ANY)
     return pl.pallas_call(
         functools.partial(dispatch_kernel, capacity),
-        in_specs=[whole, whole, hbm, hbm],
-        out_specs=(hbm, whole),
+        in_specs=[hbm, hbm, hbm, hbm],
+        out_specs=(hbm, hbm),
         out_shape=(
             jax.ShapeDtypeStruct((places, width + hidden), BF16),
             jax.ShapeDtypeStruct((1, row_count), jnp.int32),
         ),
         scratch_shapes=[
+            pltpu.VMEM((1, row_count), jnp.int32),
+            pltpu.VMEM((1, expert_count), jnp.int32),
+            pltpu.VMEM((1, row_count), jnp.int32),
             pltpu.VMEM((row_count, hidden), BF16),
             pltpu.VMEM((tiles, row_count, tile), BF16),
             pltpu.VMEM((places, width + hidden), BF16),
+            pltpu.SemaphoreType.DMA((3,)),
             pltpu.SemaphoreType.DMA((tiles + 1,)),
             pltpu.SemaphoreType.DMA((tiles + 1,)),
         ],
@@ -146,46 +156,65 @@
     return jnp.concatenate([ref[...] for ref in refs], axis=1)
 
 
-def collect_kernel(places_ref, home_ref, *refs):
-    hidden_refs, y_ref, dx_ref = refs[:-2], refs[-2], refs[-1]
+def collect_kernel(
+    places_ref, home_hbm, y_hbm, dx_hbm, home_ref, y_ref, dx_ref, in_sems, out_sems
+):
+    hidden = dx_ref.shape[1]
+    width = y_ref.shape[1]
+    tiles = in_sems.shape[0] - 1
+    tile = width // tiles
+    spans = [pl.ds(j * tile, tile) for j in range(tiles)] + [pl.ds(width, hidden)]
+    loads = [
+        pltpu.make_async_copy(home_hbm.at[:, span], home_ref.at[:, span], in_sems.at[j])
+        for j, span in enumerate(spans)
+    ]
+    for load in loads:
+        load.start()
     places = places_ref[...]
-    y_ref[...] = jnp.dot(places, home_ref[...], preferred_element_type=F32).astype(BF16)
-
-    @pl.when(pl.program_id(0) == 0)
-    def _():
-        dx_ref[...] = jnp.dot(
-            places, read_columns(hidden_refs), preferred_element_type=F32
-        ).astype(BF16)
+    stores = []
+    for j, span in enumerate(spans):
+        loads[j].wait()
+        rows = jnp.dot(places, home_ref[:, span], preferred_element_type=F32).astype(BF16)
+        if j < tiles:
+            y_ref[:, span] = rows
+            store = pltpu.make_async_copy(y_ref.at[:, span], y_hbm.at[:, span], out_sems.at[j])
+        else:
+            dx_ref[...] = rows
+            store = pltpu.make_async_copy(dx_ref, dx_hbm, out_sems.at[j])
+        store.start()
+        stores.append(store)
+    for store in stores:
+        store.wait()
 
 
 def collect(places, home, hidden):
     total, width = home.shape
     width -= hidden
     row_count = places.shape[0]
-    tile = min(width, 512)
-    specs = hidden_specs(total, hidden, width)
+    tiles = width // min(width, 512)
+    whole = pl.BlockSpec(memory_space=pltpu.VMEM)
+    hbm = pl.BlockSpec(memory_space=pl.ANY)
     return pl.pallas_call(
         collect_kernel,
-        grid=(width // tile,),
-        in_specs=[
-            pl.BlockSpec((row_count, total), lambda j: (0, 0)),
-            pl.BlockSpec((total, tile), lambda j: (0, j)),
-        ]
-        + specs,
-        out_specs=(
-            pl.BlockSpec((row_count, tile), lambda j: (0, j)),
-            pl.BlockSpec((row_count, hidden), lambda j: (0, 0)),
-        ),
+        in_specs=[whole, hbm],
+        out_specs=(hbm, hbm),
         out_shape=(
             jax.ShapeDtypeStruct((row_count, width), BF16),
             jax.ShapeDtypeStruct((row_count, hidden), BF16),
         ),
-        compiler_params=params("arbitrary"),
+        scratch_shapes=[
+            pltpu.VMEM((total, width + hidden), BF16),
+            pltpu.VMEM((row_count, width), BF16),
+            pltpu.VMEM((row_count, hidden), BF16),
+            pltpu.SemaphoreType.DMA((tiles + 1,)),
+            pltpu.SemaphoreType.DMA((tiles + 1,)),
+        ],
+        compiler_params=params(),
         cost_estimate=cost(
             2 * total * row_count * (hidden + width), 2 * (total + row_count) * (hidden + width)
         ),
         name="collect",
-    )(places, *([home] * (1 + len(specs))))
+    )(places, home)
 
 
 def member_rows(rows, capacity, local_count):
@@ -199,62 +228,92 @@
     return jnp.concatenate([jnp.where(member == e, x, zero) for e in range(local_count)], axis=1)
 
 
-def products_kernel(capacity, local_count, g_ref, w_ref, *refs):
-    x_refs, out_ref, wide_ref, total_ref = refs[:-3], refs[-3], refs[-2], refs[-1]
-    step = pl.program_id(0)
-    tile = g_ref.shape[1]
-    width = tile * pl.num_programs(0)
-    weight = w_ref[...].reshape(wide_ref.shape[1], tile)
-
-    @pl.when(step == 0)
-    def _():
-        wide_ref[...] = spread(read_columns(x_refs), capacity, local_count)
-        total_ref[...] = jnp.zeros_like(total_ref)
-
-    columns = pl.ds(pl.multiple_of(step * tile, tile), tile)
-    out_ref[:, columns] = jnp.dot(
-        wide_ref[...], weight, preferred_element_type=F32
-    ).astype(BF16)
-    total_ref[...] += lax.dot_general(
-        g_ref[...], weight, (((1,), (1,)), ((), ())), preferred_element_type=F32
-    )
-
-    @pl.when(step == pl.num_programs(0) - 1)
-    def _():
-        hidden = wide_ref.shape[1] // local_count
-        member = member_rows(total_ref.shape[0], capacity, local_count)
-        picked = total_ref[:, :hidden]
-        for e in range(1, local_count):
-            picked = jnp.where(member == e, total_ref[:, e * hidden : (e + 1) * hidden], picked)
-        out_ref[:, out_ref.shape[1] - hidden :] = picked.astype(BF16)
+def products_kernel(capacity, pieces, local_hbm, *refs):
+    w_hbm, out_hbm = refs[:pieces], refs[pieces]
+    x_ref, g_ref, w_ref, out_ref, x_sem, g_sems, w_sems, out_sems = refs[pieces + 1 :]
+    tiles, local_count, _, _, tile = w_ref.shape
+    total, hidden = x_ref.shape
+    width = tiles * tile
+    here = lax.axis_index("rep") if pieces > 1 else 0
+    x_load = pltpu.make_async_copy(local_hbm.at[:, pl.ds(width, hidden)], x_ref, x_sem)
+    x_load.start()
+    loads = []
+    for j in range(tiles):
+        span = pl.ds(j * tile, tile)
+        loads.append([])
+        for i, piece in enumerate(w_hbm):
+            owner = jnp.bitwise_xor(here, i) if pieces > 1 else 0
+            for e in range(local_count):
+                loads[j].append(
+                    pltpu.make_async_copy(
+                        piece.at[e, :, span], w_ref.at[j, e, owner], w_sems.at[j, i, e]
+                    )
+                )
+        loads[j].append(
+            pltpu.make_async_copy(local_hbm.at[:, span], g_ref.at[j], g_sems.at[j])
+        )
+        for load in loads[j]:
+            load.start()
+    x_load.wait()
+    wide = spread(x_ref[...], capacity, local_count)
+    sums = None
+    stores = []
+    for j in range(tiles):
+        span = pl.ds(j * tile, tile)
+        for load in loads[j]:
+            load.wait()
+        weight = w_ref[j].reshape(local_count * hidden, tile)
+        out_ref[:, span] = jnp.dot(wide, weight, preferred_element_type=F32).astype(BF16)
+        store = pltpu.make_async_copy(out_ref.at[:, span], out_hbm.at[:, span], out_sems.at[j])
+        store.start()
+        stores.append(store)
+        part = lax.dot_general(
+            g_ref[j], weight, (((1,), (1,)), ((), ())), preferred_element_type=F32
+        )
+        sums = part if sums is None else sums + part
+    member = member_rows(total, capacity, local_count)
+    picked = sums[:, :hidden]
+    for e in range(1, local_count):
+        picked = jnp.where(member == e, sums[:, e * hidden : (e + 1) * hidden], picked)
+    span = pl.ds(width, hidden)
+    out_ref[:, span] = picked.astype(BF16)
+    store = pltpu.make_async_copy(out_ref.at[:, span], out_hbm.at[:, span], out_sems.at[tiles])
+    store.start()
+    stores.append(store)
+    for store in stores:
+        store.wait()
 
 
 def products(local, weight, capacity):
-    local_count, hidden, width = weight.shape
+    local_count, slice_rows, width = weight[0].shape
+    pieces = len(weight)
+    hidden = slice_rows * pieces
     total = local.shape[0]
     tile = min(width, 512)
-    specs = hidden_specs(total, hidden, width)
+    tiles = width // tile
+    hbm = pl.BlockSpec(memory_space=pl.ANY)
     return pl.pallas_call(
-        functools.partial(products_kernel, capacity, local_count),
-        grid=(width // tile,),
-        in_specs=[
-            pl.BlockSpec((total, tile), lambda j: (0, j)),
-            pl.BlockSpec((local_count, hidden, tile), lambda j: (0, 0, j)),
-        ]
-        + specs,
-        out_specs=pl.BlockSpec(local.shape, lambda j: (0, 0)),
+        functools.partial(products_kernel, capacity, pieces),
+        in_specs=[hbm] * (1 + pieces),
+        out_specs=hbm,
         out_shape=jax.ShapeDtypeStruct(local.shape, BF16),
         scratch_shapes=[
-            pltpu.VMEM((total, local_count * hidden), BF16),
-            pltpu.VMEM((total, local_count * hidden), F32),
+            pltpu.VMEM((total, hidden), BF16),
+            pltpu.VMEM((tiles, total, tile), BF16),
+            pltpu.VMEM((tiles, local_count, pieces, slice_rows, tile), BF16),
+            pltpu.VMEM(local.shape, BF16),
+            pltpu.SemaphoreType.DMA,
+            pltpu.SemaphoreType.DMA((tiles,)),
+            pltpu.SemaphoreType.DMA((tiles, pieces, local_count)),
+            pltpu.SemaphoreType.DMA((tiles + 1,)),
         ],
-        compiler_params=params("arbitrary"),
+        compiler_params=pltpu.CompilerParams(vmem_limit_bytes=LARGE_LIMIT),
         cost_estimate=cost(
             4 * total * local_count * hidden * width,
             2 * (local_count * hidden + 2 * total) * width,
         ),
         name="products",
-    )(local, weight, *([local] * len(specs)))
+    )(local, *weight)
 
 
 def gradient_kernel(capacity, local_count, parts, factor, g_ref, *refs):
@@ -303,34 +362,6 @@
         ),
         name="gradient",
     )(*([local] * (1 + len(specs)))))
-
-
-def join_kernel(*refs):
-    piece_refs, out_ref = refs[:-1], refs[-1]
-    here = lax.axis_index("rep")
-    for i, ref in enumerate(piece_refs):
-        owner = jnp.bitwise_xor(here, i)
-        for e in range(out_ref.shape[0]):
-            out_ref[e, owner] = ref[e]
-
-
-def join_weight(pieces):
-    if len(pieces) == 1:
-        return pieces[0]
-    local_count, rows, width = pieces[0].shape
-    count = len(pieces)
-    tile = min(width, 512)
-    joined = pl.pallas_call(
-        join_kernel,
-        grid=(width // tile,),
-        in_specs=[pl.BlockSpec((local_count, rows, tile), lambda j: (0, 0, j))] * count,
-        out_specs=pl.BlockSpec((local_count, count, rows, tile), lambda j: (0, 0, 0, j)),
-        out_shape=jax.ShapeDtypeStruct((local_count, count, rows, width), BF16),
-        compiler_params=params("arbitrary"),
-        cost_estimate=cost(0, 4 * local_count * count * rows * width),
-        name="join_weight",
-    )(*pieces)
-    return joined.reshape(local_count, count * rows, width)
 
 
 def cast_kernel(w_ref, out_ref):
@@ -481,7 +512,7 @@
     sent, target = dispatch(route, placement, x_rows, y_cot, capacity)
     local = exchange(sent, groups)
     early_master, target = lax.optimization_barrier((master_weight, target))
-    weight = join_weight(gather_weight(cast_weight(early_master), replicas))
+    weight = gather_weight(cast_weight(early_master), replicas)
     results = products(local, weight, capacity)
     local, results = lax.optimization_barrier((local, results))
     home = exchange(results, groups)

time: 115 us -> 114 us (level)
  local copies, waits for them, and re-layouts: 4.79 us -> 3.05 us
    all_to_all x2, waiting for transfers between devices: 29.9 us -> 32.2 us  [exchange(): lax.all_to_all(parts, 'grp', split_axis=0, concat_axis=0, tiled=True)]
    unnamed x18 -> x22, local copies, waits for them, and re-layouts: 4.79 us -> 3.05 us
    ppermute x6, waiting for transfers between devices: 39.5 us -> 37.8 us  [swap(): return lax.ppermute(array, axis, [(i, i ^ offset) for i in range(size)])]
    pallas_call x4 -> x3, Pallas kernels: 14.1 us -> 14.1 us  [the longest x1 7.35 us: products(): pl.pallas_call(functools.partial(products_kernel, capacity, pieces), in_s...]
  transfers between devices with their start and end apart: 8 -> 8, of which waited for: 6 -> 6; matrix products, arithmetic and copies ran while one was open for 0% -> 0% of each run, Pallas kernels for 10% -> 9%
where the time goes in v4:
time: 114 us
  waiting for transfers between devices  70 us (61%)
  Pallas kernels  24.6 us (22%)
  starting transfers between devices  15.6 us (14%)
  local copies, waits for them, and re-layouts  3.05 us (3%)
    ppermute x6, waiting for transfers between devices, swap(): return lax.ppermute(array, axis, [(i, i ^ offset) for i in range(size)])  37.8 us
    all_to_all x2, waiting for transfers between devices, exchange(): lax.all_to_all(parts, 'grp', split_axis=0, concat_axis=0, tiled=True)  32.2 us
    all_to_all x2, starting transfers between devices, exchange(): lax.all_to_all(parts, 'grp', split_axis=0, concat_axis=0, tiled=True)  11.8 us
    pallas_call x1, Pallas kernels, products(): pl.pallas_call(functools.partial(products_kernel, capacity, pieces), in_s...  7.35 us
    pallas_call x1, Pallas kernels, adam(): pl.pallas_call(functools.partial(adam_kernel, len(grads)), grid=(members,...  6.19 us
    ppermute x6, starting transfers between devices, swap(): return lax.ppermute(array, axis, [(i, i ^ offset) for i in range(size)])  3.74 us
    pallas_call x1, Pallas kernels, gradient(): pl.pallas_call(functools.partial(gradient_kernel, capacity, local_count,...  3.52 us
    pallas_call x1, Pallas kernels, dispatch(): pl.pallas_call(functools.partial(dispatch_kernel, capacity), in_specs=[hb...  3.43 us
  transfers between devices with their start and end apart: 8, of which 6 were waited for; matrix products, arithmetic and copies ran while one was open for 0% of the time, Pallas kernels for 9%

profile of v4, /device:TPU:0, one launch (start us, length us, event | category | flops | bytes accessed | tf_op | source)
XLA Modules:
  0.0 114.1 jit_solution(10917686765930018924)
XLA Ops:
  0.6 3.4 %dispatch.1 = (bf16[384,2432]{1,0:T(8,128)(2,1)}, s32[1,256]{1,0:T(1,128)}) custom-call(s32[1,256]{1,0:T(1,128)} %bitcast.21, s32[1,16]{1,0:T(1,128)} %bitcast.22, bf16[256,384]{1,0:T(8,128)(2,1)} %x_hbm.1, bf16[256,2048]{1,0:T(8,128)(2,1)} %g_hbm.1), custom_call_target="tpu_custom_call" | custom-call | flops 478150656 | bytes 3112960 | tf_op jit(solution)/shard_map/dispatch/pallas_call | solution.py:105
  4.1 0.0 copy-start.2
  4.1 7.4 %all-to-all-start = ((bf16[8,48,2432]{2,1,0:T(8,128)(2,1)}), bf16[8,48,2432]{2,1,0:T(8,128)(2,1)S(1)}, u32[]{:S(2)}, u32[]{:S(2)}) async-start(bf16[8,48,2432]{2,1,0:T(8,128)(2,1)} %bitcast.18), calls=%async_computation | async-start | bytes 3735552 | tf_op jit(solution)/shard_map/all_to_all | solution.py:483
  11.5 0.0 copy-done.2
  11.5 0.3 cast_weight.1.refs_0_
  11.8 0.0 copy-start.3
  11.8 1.6 %collective-permute-start.1 = (bf16[2,96,2048]{2,1,0:T(8,128)(2,1)S(1)}, bf16[2,96,2048]{2,1,0:T(8,128)(2,1)S(1)}, u32[]{:S(2)}, u32[]{:S(2)}) collective-permute-start(bf16[2,96,2048]{2,1,0:T(8,128)(2,1)S(1)} %cast_weight.1.refs_0_), channel_id=1, source_target_pairs={{0,16},{8,24},{16,0},{24,8},{1,17},{9,25},{17,1},{25,9},{2,18},{10... | collective-permute-start | bytes 2359304 | tf_op jit(solution)/shard_map/ppermute | solution.py:477
  13.4 0.0 collective-permute-start
  13.4 17.5 %collective-permute-done.1.refs_2_ = bf16[2,96,2048]{2,1,0:T(8,128)(2,1)S(1)} collective-permute-done((bf16[2,96,2048]{2,1,0:T(8,128)(2,1)S(1)}, bf16[2,96,2048]{2,1,0:T(8,128)(2,1)S(1)}, u32[]{:S(2)}, u32[]{:S(2)}) %collective-permute-start.1) | collective-permute-done | bytes 786464 | tf_op jit(solution)/shard_map/ppermute | solution.py:477
  30.9 0.0 copy-start.9
  30.9 0.0 collective-permute-start.2
  30.9 0.0 collective-permute-done.refs_1_
  30.9 0.0 copy-done.3
  30.9 0.9 copy-done.9
  31.8 0.0 copy-start.10
  31.8 0.9 copy-done.10
  32.7 0.7 collective-permute-done.2.refs_3_
  33.3 21.5 %all-to-all-done = bf16[8,48,2432]{2,1,0:T(8,128)(2,1)S(1)} async-done(((bf16[8,48,2432]{2,1,0:T(8,128)(2,1)}), bf16[8,48,2432]{2,1,0:T(8,128)(2,1)S(1)}, u32[]{:S(2)}, u32[]{:S(2)}) %all-to-all-start) | async-done | bytes 1867808 | tf_op jit(solution)/shard_map/all_to_all | solution.py:483
  54.8 0.0 copy-start
  54.8 1.3 %copy-done = bf16[8,48,2432]{2,1,0:T(8,128)(2,1)} copy-done((bf16[8,48,2432]{2,1,0:T(8,128)(2,1)}, bf16[8,48,2432]{2,1,0:T(8,128)(2,1)S(1)}, u32[]{:S(2)}) %copy-start) | copy-done | bytes 1867800
  56.1 7.4 %products.1 = bf16[384,2432]{1,0:T(8,128)(2,1)} custom-call(bf16[384,2432]{1,0:T(8,128)(2,1)} %bitcast.10, bf16[2,96,2048]{2,1,0:T(8,128)(2,1)} %copy-done.3, bf16[2,96,2048]{2,1,0:T(8,128)(2,1)} %copy-done.10, bf16[2,96,2048]{2,1,0:T(8,128)(2,1)} %copy-done.9, bf16[2,96,2048]{2,1,0:T(8,128)(2,1)} %collective-permute-done.2.refs_3_), custom_call_target="tpu_custom_call" | custom-call | flops 2415919104 | bytes 6291456 | tf_op jit(solution)/shard_map/products/pallas_call | solution.py:295
  63.4 0.0 copy-start.1
  63.4 4.5 %all-to-all-start.1 = ((bf16[8,48,2432]{2,1,0:T(8,128)(2,1)}), bf16[8,48,2432]{2,1,0:T(8,128)(2,1)}, u32[]{:S(2)}, u32[]{:S(2)}) async-start(bf16[8,48,2432]{2,1,0:T(8,128)(2,1)} %bitcast.17), calls=%async_computation.1 | async-start | bytes 3735552 | tf_op jit(solution)/shard_map/all_to_all | solution.py:483
  67.9 0.0 copy-done.1
  67.9 3.5 %gradient.1 = (bf16[2,96,2048]{2,1,0:T(8,128)(2,1)S(1)}, bf16[2,96,2048]{2,1,0:T(8,128)(2,1)S(1)}, bf16[2,96,2048]{2,1,0:T(8,128)(2,1)S(1)}, bf16[2,96,2048]{2,1,0:T(8,128)(2,1)S(1)}) custom-call(bf16[384,2432]{1,0:T(8,128)(2,1)S(1)} %bitcast.11, bf16[384,2432]{1,0:T(8,128)(2,1)S(1)} %bitcast.12, bf16[384,2432]{1,0:T(8,128)(2,1)S(1)} %bitcast.13, ...), custom_call_target="tpu_custom_call" | custom-call | flops 1207959552 | bytes 4718592 | tf_op jit(solution)/shard_map/gradient/pallas_call | solution.py:351
  71.4 0.0 copy-start.8
  71.4 0.0 copy-start.4
  71.5 0.0 copy-start.5
  71.5 0.0 copy-start.6
  71.5 0.0 copy-start.7
  71.5 0.1 collective-permute-start.4
  71.6 0.5 collective-permute-start.3
  72.1 1.8 %collective-permute-done.4.b_ref = bf16[2,96,2048]{2,1,0:T(8,128)(2,1)S(1)} collective-permute-done((bf16[2,96,2048]{2,1,0:T(8,128)(2,1)S(1)}, bf16[2,96,2048]{2,1,0:T(8,128)(2,1)S(1)}, u32[]{:S(2)}, u32[]{:S(2)}) %collective-permute-start.4) | collective-permute-done | bytes 786464 | tf_op jit(solution)/shard_map/ppermute | solution.py:477
  73.8 0.4 add_parts.1
  74.2 1.6 %collective-permute-start.5 = (bf16[2,96,2048]{2,1,0:T(8,128)(2,1)S(1)}, bf16[2,96,2048]{2,1,0:T(8,128)(2,1)S(1)}, u32[]{:S(2)}, u32[]{:S(2)}) collective-permute-start(bf16[2,96,2048]{2,1,0:T(8,128)(2,1)S(1)} %add_parts.1), channel_id=1, source_target_pairs={{0,16},{8,24},{16,0},{24,8},{1,17},{9,25},{17,1},{25,9},{2,18},{10... | collective-permute-start | bytes 2359304 | tf_op jit(solution)/shard_map/ppermute | solution.py:477
  75.8 0.0 copy-done.8
  75.8 0.1 home_places.1.places_ref
  76.0 0.0 collective-permute-done.3.refs_1_
  76.0 17.9 %collective-permute-done.5.refs_2_ = bf16[2,96,2048]{2,1,0:T(8,128)(2,1)S(1)} collective-permute-done((bf16[2,96,2048]{2,1,0:T(8,128)(2,1)S(1)}, bf16[2,96,2048]{2,1,0:T(8,128)(2,1)S(1)}, u32[]{:S(2)}, u32[]{:S(2)}) %collective-permute-start.5) | collective-permute-done | bytes 786464 | tf_op jit(solution)/shard_map/ppermute | solution.py:477
  93.9 0.0 copy-done.4
  93.9 0.0 copy-done.5
  93.9 0.0 copy-done.6
  93.9 0.0 copy-done.7
  93.9 6.2 %adam.1 = (f32[2,96,2048]{2,1,0:T(8,128)}, bf16[2,96,2048]{2,1,0:T(8,128)(2,1)}, f32[2,16,96]{2,1,0:T(8,128)}, bf16[2,96,2048]{2,1,0:T(8,128)(2,1)}, f32[2,16,96]{2,1,0:T(8,128)}) custom-call(f32[2,96,2048]{2,1,0:T(8,128)S(1)} %copy-done.2, bf16[2,96,2048]{2,1,0:T(8,128)(2,1)S(1)} %copy-done.4, f32[2,16,96]{2,1,0:T(8,128)S(1)} %bitcast.15, ...), custom_call_target="tpu_custom_call" | custom-call | flops 15728640 | bytes 7077888 | tf_op jit(solution)/shard_map/adam/pallas_call | solution.py:450
  100.1 10.7 %all-to-all-done.1 = bf16[8,48,2432]{2,1,0:T(8,128)(2,1)} async-done(((bf16[8,48,2432]{2,1,0:T(8,128)(2,1)}), bf16[8,48,2432]{2,1,0:T(8,128)(2,1)}, u32[]{:S(2)}, u32[]{:S(2)}) %all-to-all-start.1) | async-done | bytes 1867808 | tf_op jit(solution)/shard_map/all_to_all | solution.py:483
  110.8 3.3 %collect.1 = (bf16[256,2048]{1,0:T(8,128)(2,1)}, bf16[256,384]{1,0:T(8,128)(2,1)}) custom-call(bf16[256,384]{1,0:T(8,128)(2,1)S(1)} %home_places.1.places_ref, bf16[384,2432]{1,0:T(8,128)(2,1)} %bitcast.5.home_hbm), custom_call_target="tpu_custom_call" | custom-call | flops 478150656 | bytes 3112960 | tf_op jit(solution)/shard_map/collect/pallas_call | solution.py:197
Async XLA Ops:
  4.1 7.4 %copy-start.2 = (f32[2,96,2048]{2,1,0:T(8,128)S(1)}, f32[2,96,2048]{2,1,0:T(8,128)}, u32[]{:S(2)}) copy-start(f32[2,96,2048]{2,1,0:T(8,128)} %master_ref.1) | copy-start | bytes 4718596
  4.1 50.7 %all-to-all-start = ((bf16[8,48,2432]{2,1,0:T(8,128)(2,1)}), bf16[8,48,2432]{2,1,0:T(8,128)(2,1)S(1)}, u32[]{:S(2)}, u32[]{:S(2)}) async-start(bf16[8,48,2432]{2,1,0:T(8,128)(2,1)} %bitcast.18), calls=%async_computation | async-start | bytes 3735552 | tf_op jit(solution)/shard_map/all_to_all | solution.py:483
  11.8 19.1 %copy-start.3 = (bf16[2,96,2048]{2,1,0:T(8,128)(2,1)}, bf16[2,96,2048]{2,1,0:T(8,128)(2,1)S(1)}, u32[]{:S(2)}) copy-start(bf16[2,96,2048]{2,1,0:T(8,128)(2,1)S(1)} %cast_weight.1.refs_0_) | copy-start | bytes 2359300
  11.8 19.1 %collective-permute-start.1 = (bf16[2,96,2048]{2,1,0:T(8,128)(2,1)S(1)}, bf16[2,96,2048]{2,1,0:T(8,128)(2,1)S(1)}, u32[]{:S(2)}, u32[]{:S(2)}) collective-permute-start(bf16[2,96,2048]{2,1,0:T(8,128)(2,1)S(1)} %cast_weight.1.refs_0_), channel_id=1, source_target_pairs={{0,16},{8,24},{16,0},{24,8},{1,17},{9,25},{17,1},{25,9},{2,18},{10... | collective-permute-start | bytes 2359304 | tf_op jit(solution)/shard_map/ppermute | solution.py:477
  13.4 17.5 %collective-permute-start = (bf16[2,96,2048]{2,1,0:T(8,128)(2,1)S(1)}, bf16[2,96,2048]{2,1,0:T(8,128)(2,1)S(1)}, u32[]{:S(2)}, u32[]{:S(2)}) collective-permute-start(bf16[2,96,2048]{2,1,0:T(8,128)(2,1)S(1)} %cast_weight.1.refs_0_), channel_id=1, source_target_pairs={{0,8},{8,0},{16,24},{24,16},{1,9},{9,1},{17,25},{25,17},{2,10},{10... | collective-permute-start | bytes 2359304 | tf_op jit(solution)/shard_map/ppermute | solution.py:477
  30.9 0.9 copy-start.9
  30.9 2.4 %collective-permute-start.2 = (bf16[2,96,2048]{2,1,0:T(8,128)(2,1)S(1)}, bf16[2,96,2048]{2,1,0:T(8,128)(2,1)}, u32[]{:S(2)}, u32[]{:S(2)}) collective-permute-start(bf16[2,96,2048]{2,1,0:T(8,128)(2,1)S(1)} %collective-permute-done.1.refs_2_), channel_id=1, source_target_pairs={{0,8},{8,0},{16,24},{24,16},{1,9},{9,1},{17,25},{25,17},{2,10},{10... | collective-permute-start | bytes 2359304 | tf_op jit(solution)/shard_map/ppermute | solution.py:477
  31.8 0.9 copy-start.10
  54.8 1.3 %copy-start = (bf16[8,48,2432]{2,1,0:T(8,128)(2,1)}, bf16[8,48,2432]{2,1,0:T(8,128)(2,1)S(1)}, u32[]{:S(2)}) copy-start(bf16[8,48,2432]{2,1,0:T(8,128)(2,1)S(1)} %all-to-all-done) | copy-start | bytes 5603332
  63.4 4.5 %copy-start.1 = (bf16[8,48,2432]{2,1,0:T(8,128)(2,1)S(1)}, bf16[8,48,2432]{2,1,0:T(8,128)(2,1)}, u32[]{:S(2)}) copy-start(bf16[8,48,2432]{2,1,0:T(8,128)(2,1)} %copy-done) | copy-start | bytes 5603332
  63.4 47.4 %all-to-all-start.1 = ((bf16[8,48,2432]{2,1,0:T(8,128)(2,1)}), bf16[8,48,2432]{2,1,0:T(8,128)(2,1)}, u32[]{:S(2)}, u32[]{:S(2)}) async-start(bf16[8,48,2432]{2,1,0:T(8,128)(2,1)} %bitcast.17), calls=%async_computation.1 | async-start | bytes 3735552 | tf_op jit(solution)/shard_map/all_to_all | solution.py:483
  71.4 4.4 %copy-start.8 = (s32[1,256]{1,0:T(1,128)S(1)}, s32[1,256]{1,0:T(1,128)}, u32[]{:S(2)}) copy-start(s32[1,256]{1,0:T(1,128)} %get-tuple-element.25.target_ref) | copy-start | bytes 3076
  71.4 22.4 %copy-start.4 = (bf16[2,96,2048]{2,1,0:T(8,128)(2,1)S(1)}, bf16[2,96,2048]{2,1,0:T(8,128)(2,1)}, u32[]{:S(2)}) copy-start(bf16[2,96,2048]{2,1,0:T(8,128)(2,1)} %mc_ref.1) | copy-start | bytes 2359300
  71.5 22.4 %copy-start.5 = (bf16[2,96,2048]{2,1,0:T(8,128)(2,1)S(1)}, bf16[2,96,2048]{2,1,0:T(8,128)(2,1)}, u32[]{:S(2)}) copy-start(bf16[2,96,2048]{2,1,0:T(8,128)(2,1)} %vc_ref.1) | copy-start | bytes 2359300
  71.5 22.4 %copy-start.6 = (f32[2,96,16]{1,2,0:T(8,128)S(1)}, f32[2,96,16]{1,2,0:T(8,128)}, u32[]{:S(2)}) copy-start(f32[2,96,16]{1,2,0:T(8,128)} %param.11) | copy-start | bytes 36868
  71.5 22.4 %copy-start.7 = (f32[2,96,16]{1,2,0:T(8,128)S(1)}, f32[2,96,16]{1,2,0:T(8,128)}, u32[]{:S(2)}) copy-start(f32[2,96,16]{1,2,0:T(8,128)} %param.13) | copy-start | bytes 36868
  71.5 2.4 %collective-permute-start.4 = (bf16[2,96,2048]{2,1,0:T(8,128)(2,1)S(1)}, bf16[2,96,2048]{2,1,0:T(8,128)(2,1)S(1)}, u32[]{:S(2)}, u32[]{:S(2)}) collective-permute-start(bf16[2,96,2048]{2,1,0:T(8,128)(2,1)S(1)} %get-tuple-element.35), channel_id=1, source_target_pairs={{0,8},{8,0},{16,24},{24,16},{1,9},{9,1},{17,25},{25,17},{2,10},{10... | collective-permute-start | bytes 2359304 | tf_op jit(solution)/shard_map/ppermute | solution.py:477
  71.6 4.4 %collective-permute-start.3 = (bf16[2,96,2048]{2,1,0:T(8,128)(2,1)S(1)}, bf16[2,96,2048]{2,1,0:T(8,128)(2,1)S(1)}, u32[]{:S(2)}, u32[]{:S(2)}) collective-permute-start(bf16[2,96,2048]{2,1,0:T(8,128)(2,1)S(1)} %get-tuple-element.33), channel_id=1, source_target_pairs={{0,8},{8,0},{16,24},{24,16},{1,9},{9,1},{17,25},{25,17},{2,10},{10... | collective-permute-start | bytes 2359304 | tf_op jit(solution)/shard_map/ppermute | solution.py:477
  74.2 19.6 %collective-permute-start.5 = (bf16[2,96,2048]{2,1,0:T(8,128)(2,1)S(1)}, bf16[2,96,2048]{2,1,0:T(8,128)(2,1)S(1)}, u32[]{:S(2)}, u32[]{:S(2)}) collective-permute-start(bf16[2,96,2048]{2,1,0:T(8,128)(2,1)S(1)} %add_parts.1), channel_id=1, source_target_pairs={{0,16},{8,24},{16,0},{24,8},{1,17},{9,25},{17,1},{25,9},{2,18},{10... | collective-permute-start | bytes 2359304 | tf_op jit(solution)/shard_map/ppermute | solution.py:477

commit v5 on v4

--- a/solution.py
+++ b/solution.py
@@ -55,11 +55,10 @@
 
 
 def dispatch_kernel(
-    capacity, route_hbm, placement_hbm, x_hbm, g_hbm, sent_hbm, target_hbm,
-    route_ref, placement_ref, target_ref, x_ref, g_ref, sent_ref, key_sems, in_sems, out_sems,
+    capacity, route_hbm, placement_hbm, g_hbm, sent_hbm, target_hbm,
+    route_ref, placement_ref, target_ref, g_ref, sent_ref, key_sems, in_sems, out_sems,
 ):
     tiles, _, tile = g_ref.shape
-    hidden = x_ref.shape[1]
     keys = [
         pltpu.make_async_copy(route_hbm, route_ref, key_sems.at[0]),
         pltpu.make_async_copy(placement_hbm, placement_ref, key_sems.at[1]),
@@ -70,7 +69,6 @@
         )
         for j in range(tiles)
     ]
-    loads.append(pltpu.make_async_copy(x_hbm, x_ref, in_sems.at[tiles]))
     for load in keys + loads:
         load.start()
     for load in keys:
@@ -80,23 +78,19 @@
     stores = [pltpu.make_async_copy(target_ref, target_hbm, key_sems.at[2])]
     stores[0].start()
     places = place_matrix(target, sent_ref.shape[0])
-    for j in range(tiles + 1):
+    for j in range(tiles):
         loads[j].wait()
-        columns = pl.ds(j * tile, tile if j < tiles else hidden)
-        rows = g_ref[j] if j < tiles else x_ref[...]
-        sent_ref[:, columns] = jnp.dot(places, rows, preferred_element_type=F32).astype(BF16)
-        store = pltpu.make_async_copy(
-            sent_ref.at[:, columns], sent_hbm.at[:, columns], out_sems.at[j]
-        )
+        span = pl.ds(j * tile, tile)
+        sent_ref[:, span] = jnp.dot(places, g_ref[j], preferred_element_type=F32).astype(BF16)
+        store = pltpu.make_async_copy(sent_ref.at[:, span], sent_hbm.at[:, span], out_sems.at[j])
         store.start()
         stores.append(store)
     for store in stores:
         store.wait()
 
 
-def dispatch(route, placement, x_rows, y_cot, capacity):
-    row_count, hidden = x_rows.shape
-    width = y_cot.shape[1]
+def dispatch(route, placement, y_cot, capacity):
+    row_count, width = y_cot.shape
     expert_count = placement.shape[0]
     tile = min(width, 512)
     tiles = width // tile
@@ -104,29 +98,70 @@
     hbm = pl.BlockSpec(memory_space=pl.ANY)
     return pl.pallas_call(
         functools.partial(dispatch_kernel, capacity),
-        in_specs=[hbm, hbm, hbm, hbm],
+        in_specs=[hbm, hbm, hbm],
         out_specs=(hbm, hbm),
         out_shape=(
-            jax.ShapeDtypeStruct((places, width + hidden), BF16),
+            jax.ShapeDtypeStruct((places, width), BF16),
             jax.ShapeDtypeStruct((1, row_count), jnp.int32),
         ),
         scratch_shapes=[
             pltpu.VMEM((1, row_count), jnp.int32),
             pltpu.VMEM((1, expert_count), jnp.int32),
             pltpu.VMEM((1, row_count), jnp.int32),
-            pltpu.VMEM((row_count, hidden), BF16),
             pltpu.VMEM((tiles, row_count, tile), BF16),
-            pltpu.VMEM((places, width + hidden), BF16),
+            pltpu.VMEM((places, width), BF16),
             pltpu.SemaphoreType.DMA((3,)),
-            pltpu.SemaphoreType.DMA((tiles + 1,)),
-            pltpu.SemaphoreType.DMA((tiles + 1,)),
+            pltpu.SemaphoreType.DMA((tiles,)),
+            pltpu.SemaphoreType.DMA((tiles,)),
         ],
         compiler_params=pltpu.CompilerParams(vmem_limit_bytes=LARGE_LIMIT),
-        cost_estimate=cost(
-            2 * places * row_count * (hidden + width), 2 * (places + row_count) * (hidden + width)
-        ),
+        cost_estimate=cost(2 * places * row_count * width, 2 * (places + row_count) * width),
         name="dispatch",
-    )(route.reshape(1, row_count), placement.reshape(1, -1), x_rows, y_cot)
+    )(route.reshape(1, row_count), placement.reshape(1, -1), y_cot)
+
+
+def chunk_owner(k):
+    return jnp.bitwise_xor(lax.axis_index("grp"), k)
+
+
+def split_chunks(refs, rows, held_ref):
+    if len(refs) == 1:
+        refs[0][...] = rows
+        return
+    held_ref[...] = rows.reshape(held_ref.shape)
+    for k, ref in enumerate(refs):
+        ref[...] = held_ref[chunk_owner(k)]
+
+
+def join_chunks(refs, held_ref):
+    if len(refs) == 1:
+        return refs[0][...]
+    for k, ref in enumerate(refs):
+        held_ref[chunk_owner(k)] = ref[...]
+    return held_ref[...].reshape(len(refs) * refs[0].shape[0], refs[0].shape[1])
+
+
+def held_scratch(chunks, rows, hidden):
+    return pltpu.VMEM((chunks, rows, hidden), BF16)
+
+
+def dispatch_x_kernel(chunks, target_ref, x_ref, *refs):
+    places = place_matrix(target_ref[...], chunks * refs[0].shape[0])
+    rows = jnp.dot(places, x_ref[...], preferred_element_type=F32).astype(BF16)
+    split_chunks(refs[:chunks], rows, refs[-1])
+
+
+def dispatch_x(target, x_rows, places, chunks):
+    row_count, hidden = x_rows.shape
+    rows = places // chunks
+    return list(pl.pallas_call(
+        functools.partial(dispatch_x_kernel, chunks),
+        out_shape=(jax.ShapeDtypeStruct((rows, hidden), BF16),) * chunks,
+        scratch_shapes=[held_scratch(chunks, rows, hidden)],
+        compiler_params=params(),
+        cost_estimate=cost(2 * places * row_count * hidden, 2 * (places + row_count) * hidden),
+        name="dispatch_x",
+    )(target, x_rows))
 
 
 def home_places_kernel(target_ref, out_ref):
@@ -145,25 +180,12 @@
     )(target)
 
 
-def hidden_specs(rows, hidden, width):
-    return [
-        pl.BlockSpec((rows, BLOCK), functools.partial(lambda k, j: (0, k), width // BLOCK + i))
-        for i in range(hidden // BLOCK)
-    ]
-
-
-def read_columns(refs):
-    return jnp.concatenate([ref[...] for ref in refs], axis=1)
-
-
-def collect_kernel(
-    places_ref, home_hbm, y_hbm, dx_hbm, home_ref, y_ref, dx_ref, in_sems, out_sems
-):
-    hidden = dx_ref.shape[1]
-    width = y_ref.shape[1]
-    tiles = in_sems.shape[0] - 1
-    tile = width // tiles
-    spans = [pl.ds(j * tile, tile) for j in range(tiles)] + [pl.ds(width, hidden)]
+def collect_kernel(chunks, places_ref, home_hbm, *refs):
+    dx_refs, y_hbm, x_grad_hbm = refs[:chunks], refs[chunks], refs[chunks + 1]
+    home_ref, held_ref, y_ref, x_grad_ref, in_sems, out_sems = refs[chunks + 2 :]
+    tiles = in_sems.shape[0]
+    tile = y_ref.shape[1] // tiles
+    spans = [pl.ds(j * tile, tile) for j in range(tiles)]
     loads = [
         pltpu.make_async_copy(home_hbm.at[:, span], home_ref.at[:, span], in_sems.at[j])
         for j, span in enumerate(spans)
@@ -171,42 +193,45 @@
     for load in loads:
         load.start()
     places = places_ref[...]
-    stores = []
+    x_grad_ref[...] = jnp.dot(
+        places, join_chunks(dx_refs, held_ref), preferred_element_type=F32
+    ).astype(BF16)
+    stores = [pltpu.make_async_copy(x_grad_ref, x_grad_hbm, out_sems.at[tiles])]
+    stores[0].start()
     for j, span in enumerate(spans):
         loads[j].wait()
-        rows = jnp.dot(places, home_ref[:, span], preferred_element_type=F32).astype(BF16)
-        if j < tiles:
-            y_ref[:, span] = rows
-            store = pltpu.make_async_copy(y_ref.at[:, span], y_hbm.at[:, span], out_sems.at[j])
-        else:
-            dx_ref[...] = rows
-            store = pltpu.make_async_copy(dx_ref, dx_hbm, out_sems.at[j])
+        y_ref[:, span] = jnp.dot(
+            places, home_ref[:, span], preferred_element_type=F32
+        ).astype(BF16)
+        store = pltpu.make_async_copy(y_ref.at[:, span], y_hbm.at[:, span], out_sems.at[j])
         store.start()
         stores.append(store)
     for store in stores:
         store.wait()
 
 
-def collect(places, home, hidden):
-    total, width = home.shape
-    width -= hidden
+def collect(places, home_y, home_dx):
+    total, width = home_y.shape
+    rows, hidden = home_dx[0].shape
+    chunks = len(home_dx)
     row_count = places.shape[0]
     tiles = width // min(width, 512)
     whole = pl.BlockSpec(memory_space=pltpu.VMEM)
     hbm = pl.BlockSpec(memory_space=pl.ANY)
     return pl.pallas_call(
-        collect_kernel,
-        in_specs=[whole, hbm],
+        functools.partial(collect_kernel, chunks),
+        in_specs=[whole, hbm] + [whole] * chunks,
         out_specs=(hbm, hbm),
         out_shape=(
             jax.ShapeDtypeStruct((row_count, width), BF16),
             jax.ShapeDtypeStruct((row_count, hidden), BF16),
         ),
         scratch_shapes=[
-            pltpu.VMEM((total, width + hidden), BF16),
+            pltpu.VMEM((total, width), BF16),
+            held_scratch(chunks, rows, hidden),
             pltpu.VMEM((row_count, width), BF16),
             pltpu.VMEM((row_count, hidden), BF16),
-            pltpu.SemaphoreType.DMA((tiles + 1,)),
+            pltpu.SemaphoreType.DMA((tiles,)),
             pltpu.SemaphoreType.DMA((tiles + 1,)),
         ],
         compiler_params=params(),
@@ -214,7 +239,7 @@
             2 * total * row_count * (hidden + width), 2 * (total + row_count) * (hidden + width)
         ),
         name="collect",
-    )(places, home)
+    )(places, home_y, *home_dx)
 
 
 def member_rows(rows, capacity, local_count):
@@ -228,140 +253,153 @@
     return jnp.concatenate([jnp.where(member == e, x, zero) for e in range(local_count)], axis=1)
 
 
-def products_kernel(capacity, pieces, local_hbm, *refs):
-    w_hbm, out_hbm = refs[:pieces], refs[pieces]
-    x_ref, g_ref, w_ref, out_ref, x_sem, g_sems, w_sems, out_sems = refs[pieces + 1 :]
-    tiles, local_count, _, _, tile = w_ref.shape
-    total, hidden = x_ref.shape
-    width = tiles * tile
-    here = lax.axis_index("rep") if pieces > 1 else 0
-    x_load = pltpu.make_async_copy(local_hbm.at[:, pl.ds(width, hidden)], x_ref, x_sem)
-    x_load.start()
-    loads = []
-    for j in range(tiles):
-        span = pl.ds(j * tile, tile)
-        loads.append([])
-        for i, piece in enumerate(w_hbm):
-            owner = jnp.bitwise_xor(here, i) if pieces > 1 else 0
-            for e in range(local_count):
-                loads[j].append(
-                    pltpu.make_async_copy(
-                        piece.at[e, :, span], w_ref.at[j, e, owner], w_sems.at[j, i, e]
-                    )
-                )
-        loads[j].append(
-            pltpu.make_async_copy(local_hbm.at[:, span], g_ref.at[j], g_sems.at[j])
-        )
-        for load in loads[j]:
-            load.start()
-    x_load.wait()
-    wide = spread(x_ref[...], capacity, local_count)
-    sums = None
-    stores = []
-    for j in range(tiles):
-        span = pl.ds(j * tile, tile)
-        for load in loads[j]:
-            load.wait()
-        weight = w_ref[j].reshape(local_count * hidden, tile)
-        out_ref[:, span] = jnp.dot(wide, weight, preferred_element_type=F32).astype(BF16)
-        store = pltpu.make_async_copy(out_ref.at[:, span], out_hbm.at[:, span], out_sems.at[j])
-        store.start()
-        stores.append(store)
-        part = lax.dot_general(
-            g_ref[j], weight, (((1,), (1,)), ((), ())), preferred_element_type=F32
-        )
-        sums = part if sums is None else sums + part
-    member = member_rows(total, capacity, local_count)
-    picked = sums[:, :hidden]
-    for e in range(1, local_count):
-        picked = jnp.where(member == e, sums[:, e * hidden : (e + 1) * hidden], picked)
-    span = pl.ds(width, hidden)
-    out_ref[:, span] = picked.astype(BF16)
-    store = pltpu.make_async_copy(out_ref.at[:, span], out_hbm.at[:, span], out_sems.at[tiles])
-    store.start()
-    stores.append(store)
-    for store in stores:
-        store.wait()
-
-
-def products(local, weight, capacity):
-    local_count, slice_rows, width = weight[0].shape
-    pieces = len(weight)
-    hidden = slice_rows * pieces
-    total = local.shape[0]
-    tile = min(width, 512)
-    tiles = width // tile
-    hbm = pl.BlockSpec(memory_space=pl.ANY)
-    return pl.pallas_call(
-        functools.partial(products_kernel, capacity, pieces),
-        in_specs=[hbm] * (1 + pieces),
-        out_specs=hbm,
-        out_shape=jax.ShapeDtypeStruct(local.shape, BF16),
-        scratch_shapes=[
-            pltpu.VMEM((total, hidden), BF16),
-            pltpu.VMEM((tiles, total, tile), BF16),
-            pltpu.VMEM((tiles, local_count, pieces, slice_rows, tile), BF16),
-            pltpu.VMEM(local.shape, BF16),
-            pltpu.SemaphoreType.DMA,
-            pltpu.SemaphoreType.DMA((tiles,)),
-            pltpu.SemaphoreType.DMA((tiles, pieces, local_count)),
-            pltpu.SemaphoreType.DMA((tiles + 1,)),
-        ],
-        compiler_params=pltpu.CompilerParams(vmem_limit_bytes=LARGE_LIMIT),
-        cost_estimate=cost(
-            4 * total * local_count * hidden * width,
-            2 * (local_count * hidden + 2 * total) * width,
-        ),
-        name="products",
-    )(local, *weight)
-
-
-def gradient_kernel(capacity, local_count, parts, factor, g_ref, *refs):
-    blocks = len(refs) - 2 - (parts if parts > 1 else 0)
-    x_refs, wide_ref = refs[:blocks], refs[-1]
-    out_refs = refs[blocks:-2] if parts > 1 else refs[blocks:-1]
+def join_weight(piece_refs, joined_ref):
+    local_count, rows, width = piece_refs[0].shape
+    if len(piece_refs) == 1:
+        return piece_refs[0][...].reshape(local_count * rows, width)
+    here = lax.axis_index("rep")
+    for i, ref in enumerate(piece_refs):
+        owner = jnp.bitwise_xor(here, i)
+        for e in range(local_count):
+            joined_ref[e, owner] = ref[e]
+    return joined_ref[...].reshape(local_count * len(piece_refs) * rows, width)
+
+
+def joined_scratch(pieces, tile):
+    local_count, rows, _ = pieces[0].shape
+    return pltpu.VMEM((local_count, len(pieces), rows, tile), BF16)
+
+
+def forward_kernel(capacity, local_count, chunks, pieces, *refs):
+    x_refs, w_refs = refs[:chunks], refs[chunks : chunks + pieces]
+    y_ref, wide_ref, held_ref, joined_ref = refs[chunks + pieces :]
 
     @pl.when(pl.program_id(0) == 0)
     def _():
-        wide_ref[...] = spread(read_columns(x_refs), capacity, local_count)
-
+        wide_ref[...] = spread(join_chunks(x_refs, held_ref), capacity, local_count)
+
+    y_ref[...] = jnp.dot(
+        wide_ref[...], join_weight(w_refs, joined_ref), preferred_element_type=F32
+    ).astype(BF16)
+
+
+def forward(x, weight, capacity):
+    rows, hidden = x[0].shape
+    local_count, slice_rows, width = weight[0].shape
+    tile = min(width, 512)
+    total = rows * len(x)
+    wide = local_count * hidden
+    return pl.pallas_call(
+        functools.partial(forward_kernel, capacity, local_count, len(x), len(weight)),
+        grid=(width // tile,),
+        in_specs=[pl.BlockSpec((rows, hidden), lambda j: (0, 0))] * len(x)
+        + [pl.BlockSpec((local_count, slice_rows, tile), lambda j: (0, 0, j))] * len(weight),
+        out_specs=(
+            pl.BlockSpec((total, tile), lambda j: (0, j)),
+            pl.BlockSpec((total, wide), lambda j: (0, 0)),
+        ),
+        out_shape=(
+            jax.ShapeDtypeStruct((total, width), BF16),
+            jax.ShapeDtypeStruct((total, wide), BF16),
+        ),
+        scratch_shapes=[held_scratch(len(x), rows, hidden), joined_scratch(weight, tile)],
+        compiler_params=params("arbitrary"),
+        cost_estimate=cost(2 * total * wide * width, 2 * (wide + total) * width),
+        name="forward",
+    )(*x, *weight)
+
+
+def backward_kernel(capacity, local_count, chunks, pieces, g_ref, *refs):
+    w_refs, dx_refs = refs[:pieces], refs[pieces : pieces + chunks]
+    held_ref, joined_ref, total_ref = refs[pieces + chunks :]
+    step = pl.program_id(0)
+    hidden = dx_refs[0].shape[1]
+    part = lax.dot_general(
+        g_ref[...], join_weight(w_refs, joined_ref), (((1,), (1,)), ((), ())),
+        preferred_element_type=F32,
+    )
+
+    @pl.when(step == 0)
+    def _():
+        total_ref[...] = part
+
+    @pl.when(step > 0)
+    def _():
+        total_ref[...] += part
+
+    @pl.when(step == pl.num_programs(0) - 1)
+    def _():
+        member = member_rows(total_ref.shape[0], capacity, local_count)
+        picked = total_ref[:, :hidden]
+        for e in range(1, local_count):
+            picked = jnp.where(member == e, total_ref[:, e * hidden : (e + 1) * hidden], picked)
+        split_chunks(dx_refs, picked.astype(BF16), held_ref)
+
+
+def backward(g, weight, capacity, chunks):
+    total, width = g.shape
+    local_count, slice_rows, _ = weight[0].shape
+    hidden = slice_rows * len(weight)
+    rows = total // chunks
+    tile = min(width, 512)
+    return list(pl.pallas_call(
+        functools.partial(backward_kernel, capacity, local_count, chunks, len(weight)),
+        grid=(width // tile,),
+        in_specs=[pl.BlockSpec((total, tile), lambda j: (0, j))]
+        + [pl.BlockSpec((local_count, slice_rows, tile), lambda j: (0, 0, j))] * len(weight),
+        out_specs=(pl.BlockSpec((rows, hidden), lambda j: (0, 0)),) * chunks,
+        out_shape=(jax.ShapeDtypeStruct((rows, hidden), BF16),) * chunks,
+        scratch_shapes=[
+            held_scratch(chunks, rows, hidden),
+            joined_scratch(weight, tile),
+            pltpu.VMEM((total, local_count * hidden), F32),
+        ],
+        compiler_params=params("arbitrary"),
+        cost_estimate=cost(
+            2 * total * local_count * hidden * width,
+            2 * (local_count * hidden + total) * width,
+        ),
+        name="backward",
+    )(g, *weight))
+
+
+def gradient_kernel(parts, factor, wide_ref, g_ref, *refs):
     outer = lax.dot_general(
         wide_ref[...], g_ref[...], (((0,), (0,)), ((), ())), preferred_element_type=F32
     )
     low = (outer * factor).astype(BF16)
     if parts == 1:
-        out_refs[0][...] = low.reshape(out_refs[0].shape)
+        refs[0][...] = low.reshape(refs[0].shape)
         return
-    split_ref = refs[-2]
+    out_refs, split_ref = refs[:-1], refs[-1]
     split_ref[...] = low.reshape(split_ref.shape)
     here = lax.axis_index("rep")
     for i, out_ref in enumerate(out_refs):
         owner = jnp.bitwise_xor(here, i)
-        for e in range(local_count):
+        for e in range(split_ref.shape[0]):
             out_ref[e] = split_ref[e, owner]
 
 
-def gradient(local, hidden, capacity, local_count, parts, factor):
-    total, width = local.shape
-    width -= hidden
+def gradient(wide, g, local_count, parts, factor):
+    total, width = g.shape
     tile = min(width, 512)
-    slice_rows = hidden // parts
-    specs = hidden_specs(total, hidden, width)
+    columns = wide.shape[1]
+    slice_rows = columns // local_count // parts
     split = [pltpu.VMEM((local_count, parts, slice_rows, tile), BF16)] if parts > 1 else []
     return list(pl.pallas_call(
-        functools.partial(gradient_kernel, capacity, local_count, parts, factor),
+        functools.partial(gradient_kernel, parts, factor),
         grid=(width // tile,),
-        in_specs=[pl.BlockSpec((total, tile), lambda j: (0, j))] + specs,
+        in_specs=[
+            pl.BlockSpec((total, columns), lambda j: (0, 0)),
+            pl.BlockSpec((total, tile), lambda j: (0, j)),
+        ],
         out_specs=(pl.BlockSpec((local_count, slice_rows, tile), lambda j: (0, 0, j)),) * parts,
         out_shape=(jax.ShapeDtypeStruct((local_count, slice_rows, width), BF16),) * parts,
-        scratch_shapes=split + [pltpu.VMEM((total, local_count * hidden), BF16)],
+        scratch_shapes=split,
         compiler_params=params("arbitrary"),
-        cost_estimate=cost(
-            2 * total * local_count * hidden * width,
-            2 * (local_count * hidden + total) * width,
-        ),
+        cost_estimate=cost(2 * total * columns * width, 2 * (columns + total) * width),
         name="gradient",
-    )(*([local] * (1 + len(specs)))))
+    )(wide, g))
 
 
 def cast_kernel(w_ref, out_ref):
@@ -484,6 +522,12 @@
     return moved.reshape(places, width)
 
 
+def exchange_chunks(chunks, groups):
+    if len(chunks) == 1:
+        return [exchange(chunks[0], groups)]
+    return [chunks[0]] + [swap(chunk, "grp", k) for k, chunk in enumerate(chunks) if k > 0]
+
+
 def gather_weight(weight_slice, replicas):
     if replicas != 4:
         return [lax.all_gather(weight_slice, "rep", axis=1, tiled=True)]
@@ -509,19 +553,23 @@
     grad_factor = float(row_count * groups * replicas // expert_count) ** (-0.5)
     capacity = max(2, (3 * row_count + 2 * expert_count - 1) // (2 * expert_count))
     places = expert_count * capacity
-    sent, target = dispatch(route, placement, x_rows, y_cot, capacity)
-    local = exchange(sent, groups)
-    early_master, target = lax.optimization_barrier((master_weight, target))
+    few = groups <= 8 and groups & (groups - 1) == 0 and places // groups % 16 == 0
+    chunks = groups if few else 1
+    parts = replicas if replicas == 4 else 1
+
+    sent_g, target = dispatch(route, placement, y_cot, capacity)
+    local_g = exchange(sent_g, groups)
+
+    early_master, early_x, target = lax.optimization_barrier((master_weight, x_rows, target))
     weight = gather_weight(cast_weight(early_master), replicas)
-    results = products(local, weight, capacity)
-    local, results = lax.optimization_barrier((local, results))
-    home = exchange(results, groups)
-
-    parts = replicas if replicas == 4 else 1
-    hidden = x_rows.shape[1]
-    grads = sum_gradient(gradient(local, hidden, capacity, local_count, parts, grad_factor))
+    local_x = exchange_chunks(dispatch_x(target, early_x, places, chunks), groups)
+    back_y, wide = forward(local_x, weight, capacity)
+    home_y = exchange(back_y, groups)
+
+    grads = sum_gradient(gradient(wide, local_g, local_count, parts, grad_factor))
+    home_dx = exchange_chunks(backward(local_g, weight, capacity, chunks), groups)
     updated = adam(master_weight, grads, m_code, m_scale, v_code, v_scale)
-    y_rows, x_grad = collect(home_places(target, places), home, hidden)
+    y_rows, x_grad = collect(home_places(target, places), home_y, home_dx)
     return (y_rows, x_grad) + tuple(updated)
 
 

time: 114 us -> 121 us (1.061)
  waiting for transfers between devices: 70 us -> 41.8 us
  starting transfers between devices: 15.6 us -> 42.4 us
  local copies, waits for them, and re-layouts: 3.05 us -> 13.3 us
  Pallas kernels: 24.6 us -> 22.1 us
    all_to_all x2, waiting for transfers between devices: 32.2 us -> 0.01 us  [exchange(): lax.all_to_all(parts, 'grp', split_axis=0, concat_axis=0, tiled=True)]
    ppermute x6 -> x20, starting transfers between devices: 3.74 us -> 31.4 us  [swap(): return lax.ppermute(array, axis, [(i, i ^ offset) for i in range(size)])]
    unnamed x22 -> x54, local copies, waits for them, and re-layouts: 3.05 us -> 13.3 us
    ppermute x6 -> x20, waiting for transfers between devices: 37.8 us -> 41.8 us  [swap(): return lax.ppermute(array, axis, [(i, i ^ offset) for i in range(size)])]
    pallas_call x3 -> x5, Pallas kernels: 14.1 us -> 12 us  [the longest x1 3.41 us: backward(): pl.pallas_call(functools.partial(backward_kernel, capacity, local_count,...]
  transfers between devices with their start and end apart: 8 -> 22, of which waited for: 6 -> 9; matrix products, arithmetic and copies ran while one was open for 0% -> 0% of each run, Pallas kernels for 9% -> 14%
where the time goes in v5:
time: 121 us
  starting transfers between devices  42.4 us (35%)
  waiting for transfers between devices  41.8 us (35%)
  Pallas kernels  22.1 us (18%)
  local copies, waits for them, and re-layouts  13.3 us (11%)
    ppermute x20, waiting for transfers between devices, swap(): return lax.ppermute(array, axis, [(i, i ^ offset) for i in range(size)])  41.8 us
    ppermute x20, starting transfers between devices, swap(): return lax.ppermute(array, axis, [(i, i ^ offset) for i in range(size)])  31.4 us
    unnamed x54, local copies, waits for them, and re-layouts  13.3 us
    all_to_all x2, starting transfers between devices, exchange(): lax.all_to_all(parts, 'grp', split_axis=0, concat_axis=0, tiled=True)  11 us
    pallas_call x1, Pallas kernels, adam(): pl.pallas_call(functools.partial(adam_kernel, len(grads)), grid=(members,...  6.19 us
    pallas_call x1, Pallas kernels, backward(): pl.pallas_call(functools.partial(backward_kernel, capacity, local_count,...  3.41 us
    pallas_call x1, Pallas kernels, dispatch(): pl.pallas_call(functools.partial(dispatch_kernel, capacity), in_specs=[hb...  3.08 us
    pallas_call x1, Pallas kernels, gradient(): pl.pallas_call(functools.partial(gradient_kernel, parts, factor), grid=(w...  3.01 us
  transfers between devices with their start and end apart: 22, of which 9 were waited for; matrix products, arithmetic and copies ran while one was open for 0% of the time, Pallas kernels for 14%

profile of v5, /device:TPU:0, one launch (start us, length us, event | category | flops | bytes accessed | tf_op | source)
XLA Modules:
  0.0 120.5 jit_solution(11279665541650586823)
XLA Ops:
  0.6 3.1 %dispatch.1 = (bf16[384,2048]{1,0:T(8,128)(2,1)}, s32[1,256]{1,0:T(1,128)}) custom-call(s32[1,256]{1,0:T(1,128)} %bitcast.19, s32[1,16]{1,0:T(1,128)} %bitcast.20, bf16[256,2048]{1,0:T(8,128)(2,1)} %g_hbm.1), custom_call_target="tpu_custom_call" | custom-call | flops 402653184 | bytes 2621440 | tf_op jit(solution)/shard_map/dispatch/pallas_call | solution.py:99
  3.7 0.0 copy-start
  3.7 7.4 %all-to-all-start.1 = ((bf16[8,48,2048]{2,1,0:T(8,128)(2,1)}), bf16[8,48,2048]{2,1,0:T(8,128)(2,1)S(1)}, u32[]{:S(2)}, u32[]{:S(2)}) async-start(bf16[8,48,2048]{2,1,0:T(8,128)(2,1)} %bitcast.16), calls=%async_computation.1 | async-start | bytes 3145728 | tf_op jit(solution)/shard_map/all_to_all | solution.py:521
  11.1 0.0 copy-start.24
  11.2 0.3 cast_weight.1.refs_8_.refs_0_
  11.5 1.6 %collective-permute-start.8 = (bf16[2,96,2048]{2,1,0:T(8,128)(2,1)S(1)}, bf16[2,96,2048]{2,1,0:T(8,128)(2,1)S(1)}, u32[]{:S(2)}, u32[]{:S(2)}) collective-permute-start(bf16[2,96,2048]{2,1,0:T(8,128)(2,1)S(1)} %cast_weight.1.refs_8_.refs_0_), channel_id=1, source_target_pairs={{0,16},{8,24},{16,0},{24,8},{1,17},{9,25},{17,1},{25,9},{2,18},{10... | collective-permute-start | bytes 2359304 | tf_op jit(solution)/shard_map/ppermute | solution.py:515
  13.1 17.5 %collective-permute-done.8.refs_10_.refs_2_ = bf16[2,96,2048]{2,1,0:T(8,128)(2,1)S(1)} collective-permute-done((bf16[2,96,2048]{2,1,0:T(8,128)(2,1)S(1)}, bf16[2,96,2048]{2,1,0:T(8,128)(2,1)S(1)}, u32[]{:S(2)}, u32[]{:S(2)}) %collective-permute-start.8) | collective-permute-done | bytes 786464 | tf_op jit(solution)/shard_map/ppermute | solution.py:515
  30.6 0.3 dispatch_x.1
  30.9 1.8 %collective-permute-start = (bf16[48,384]{1,0:T(8,128)(2,1)S(1)}, bf16[48,384]{1,0:T(8,128)(2,1)S(1)}, u32[]{:S(2)}, u32[]{:S(2)}) collective-permute-start(bf16[48,384]{1,0:T(8,128)(2,1)S(1)} %get-tuple-element.45), channel_id=1, source_target_pairs={{0,1},{1,0},{2,3},{3,2},{4,5},{5,4},{6,7},{7,6},{8,9},{9,8},{10,11... | collective-permute-start | bytes 110600 | tf_op jit(solution)/shard_map/ppermute | solution.py:515
  32.7 1.5 %collective-permute-start.1 = (bf16[48,384]{1,0:T(8,128)(2,1)S(1)}, bf16[48,384]{1,0:T(8,128)(2,1)S(1)}, u32[]{:S(2)}, u32[]{:S(2)}) collective-permute-start(bf16[48,384]{1,0:T(8,128)(2,1)S(1)} %get-tuple-element.46), channel_id=1, source_target_pairs={{0,2},{1,3},{2,0},{3,1},{4,6},{5,7},{6,4},{7,5},{8,10},{9,11},{10,... | collective-permute-start | bytes 110600 | tf_op jit(solution)/shard_map/ppermute | solution.py:515
  34.1 0.3 collective-permute-start.2
  34.5 2.5 %collective-permute-done.refs_1_ = bf16[48,384]{1,0:T(8,128)(2,1)S(1)} collective-permute-done((bf16[48,384]{1,0:T(8,128)(2,1)S(1)}, bf16[48,384]{1,0:T(8,128)(2,1)S(1)}, u32[]{:S(2)}, u32[]{:S(2)}) %collective-permute-start) | collective-permute-done | bytes 36896 | tf_op jit(solution)/shard_map/ppermute | solution.py:515
  36.9 0.6 collective-permute-start.3
  37.5 1.4 %collective-permute-done.1.refs_2_ = bf16[48,384]{1,0:T(8,128)(2,1)S(1)} collective-permute-done((bf16[48,384]{1,0:T(8,128)(2,1)S(1)}, bf16[48,384]{1,0:T(8,128)(2,1)S(1)}, u32[]{:S(2)}, u32[]{:S(2)}) %collective-permute-start.1) | collective-permute-done | bytes 36896 | tf_op jit(solution)/shard_map/ppermute | solution.py:515
  39.0 4.8 %collective-permute-start.4 = (bf16[48,384]{1,0:T(8,128)(2,1)S(1)}, bf16[48,384]{1,0:T(8,128)(2,1)S(1)}, u32[]{:S(2)}, u32[]{:S(2)}) collective-permute-start(bf16[48,384]{1,0:T(8,128)(2,1)S(1)} %get-tuple-element.49), channel_id=1, source_target_pairs={{0,5},{1,4},{2,7},{3,6},{4,1},{5,0},{6,3},{7,2},{8,13},{9,12},{10,... | collective-permute-start | bytes 110600 | tf_op jit(solution)/shard_map/ppermute | solution.py:515
  43.8 0.3 collective-permute-start.5
  44.1 8.0 %collective-permute-done.3.refs_4_ = bf16[48,384]{1,0:T(8,128)(2,1)S(1)} collective-permute-done((bf16[48,384]{1,0:T(8,128)(2,1)S(1)}, bf16[48,384]{1,0:T(8,128)(2,1)S(1)}, u32[]{:S(2)}, u32[]{:S(2)}) %collective-permute-start.3) | collective-permute-done | bytes 36896 | tf_op jit(solution)/shard_map/ppermute | solution.py:515
  52.1 2.0 %collective-permute-start.6 = (bf16[48,384]{1,0:T(8,128)(2,1)S(1)}, bf16[48,384]{1,0:T(8,128)(2,1)S(1)}, u32[]{:S(2)}, u32[]{:S(2)}) collective-permute-start(bf16[48,384]{1,0:T(8,128)(2,1)S(1)} %get-tuple-element.51), channel_id=1, source_target_pairs={{0,7},{1,6},{2,5},{3,4},{4,3},{5,2},{6,1},{7,0},{8,15},{9,14},{10,... | collective-permute-start | bytes 110600 | tf_op jit(solution)/shard_map/ppermute | solution.py:515
  54.1 4.7 %collective-permute-done.6.refs_7_ = bf16[48,384]{1,0:T(8,128)(2,1)S(1)} collective-permute-done((bf16[48,384]{1,0:T(8,128)(2,1)S(1)}, bf16[48,384]{1,0:T(8,128)(2,1)S(1)}, u32[]{:S(2)}, u32[]{:S(2)}) %collective-permute-start.6) | collective-permute-done | bytes 36896 | tf_op jit(solution)/shard_map/ppermute | solution.py:515
  58.8 2.9 %forward.1 = (bf16[384,2048]{1,0:T(8,128)(2,1)S(1)}, bf16[384,768]{1,0:T(8,128)(2,1)S(1)}) custom-call(bf16[48,384]{1,0:T(8,128)(2,1)S(1)} %get-tuple-element.44.refs_0_, bf16[48,384]{1,0:T(8,128)(2,1)S(1)} %collective-permute-done.refs_1_, bf16[48,384]{1,0:T(8,128)(2,1)S(1)} %collective-permute-done.1.refs_2_, ...), custom_call_target="tpu_custom_call" | custom-call | flops 1207959552 | bytes 4718592 | tf_op jit(solution)/shard_map/forward/pallas_call | solution.py:292
  61.7 0.0 copy-start.4
  61.7 0.9 copy-done.4
  62.6 1.2 copy-done.6
  63.7 0.9 copy-done.7
  64.6 0.9 copy-done.9
  65.5 0.9 copy-done.11
  66.4 0.8 copy-done.25
  67.2 1.1 copy-done.1
  68.3 3.6 %all-to-all-start = ((bf16[8,48,2048]{2,1,0:T(8,128)(2,1)}), bf16[8,48,2048]{2,1,0:T(8,128)(2,1)S(1)}, u32[]{:S(2)}, u32[]{:S(2)}) async-start(bf16[8,48,2048]{2,1,0:T(8,128)(2,1)} %bitcast.13), calls=%async_computation | async-start | bytes 3145728 | tf_op jit(solution)/shard_map/all_to_all | solution.py:521
  71.9 0.0 copy-start.2
  71.9 1.4 %copy-done.2 = bf16[8,48,2048]{2,1,0:T(8,128)(2,1)S(1)} copy-done((bf16[8,48,2048]{2,1,0:T(8,128)(2,1)S(1)}, bf16[8,48,2048]{2,1,0:T(8,128)(2,1)}, u32[]{:S(2)}) %copy-start.2) | copy-done | bytes 1572888
  73.3 1.1 copy-done.26
  74.4 3.0 %gradient.1 = (bf16[2,96,2048]{2,1,0:T(8,128)(2,1)S(1)}, bf16[2,96,2048]{2,1,0:T(8,128)(2,1)S(1)}, bf16[2,96,2048]{2,1,0:T(8,128)(2,1)S(1)}, bf16[2,96,2048]{2,1,0:T(8,128)(2,1)S(1)}) custom-call(bf16[384,768]{1,0:T(8,128)(2,1)S(1)} %copy-done.26, bf16[384,2048]{1,0:T(8,128)(2,1)S(1)} %bitcast.11), custom_call_target="tpu_custom_call" | custom-call | flops 1207959552 | bytes 4718592 | tf_op jit(solution)/shard_map/gradient/pallas_call | solution.py:389
  77.4 0.0 copy-start.3
  77.4 0.0 copy-start.5
  77.5 0.1 collective-permute-start.18
  77.5 0.5 collective-permute-start.17
  78.0 1.8 %collective-permute-done.18.b_ref = bf16[2,96,2048]{2,1,0:T(8,128)(2,1)S(1)} collective-permute-done((bf16[2,96,2048]{2,1,0:T(8,128)(2,1)S(1)}, bf16[2,96,2048]{2,1,0:T(8,128)(2,1)S(1)}, u32[]{:S(2)}, u32[]{:S(2)}) %collective-permute-start.18) | collective-permute-done | bytes 786464 | tf_op jit(solution)/shard_map/ppermute | solution.py:515
  79.8 0.4 add_parts.1
  80.2 0.0 copy-start.13
  80.2 0.0 copy-start.14
  80.2 0.0 copy-start.21
  80.2 0.0 copy-start.22
  80.3 1.6 %collective-permute-start.19 = (bf16[2,96,2048]{2,1,0:T(8,128)(2,1)S(1)}, bf16[2,96,2048]{2,1,0:T(8,128)(2,1)S(1)}, u32[]{:S(2)}, u32[]{:S(2)}) collective-permute-start(bf16[2,96,2048]{2,1,0:T(8,128)(2,1)S(1)} %add_parts.1), channel_id=1, source_target_pairs={{0,16},{8,24},{16,0},{24,8},{1,17},{9,25},{17,1},{25,9},{2,18},{10... | collective-permute-start | bytes 2359304 | tf_op jit(solution)/shard_map/ppermute | solution.py:515
  81.9 3.4 %backward.1 = (bf16[48,384]{1,0:T(8,128)(2,1)S(1)}, bf16[48,384]{1,0:T(8,128)(2,1)S(1)}, bf16[48,384]{1,0:T(8,128)(2,1)S(1)}, bf16[48,384]{1,0:T(8,128)(2,1)S(1)...) custom-call(bf16[384,2048]{1,0:T(8,128)(2,1)S(1)} %bitcast.12, ...), custom_call_target="tpu_custom_call" | custom-call | flops 1207959552 | bytes 4718592 | tf_op jit(solution)/shard_map/backward/pallas_call | solution.py:345
  85.3 2.0 %collective-permute-start.10 = (bf16[48,384]{1,0:T(8,128)(2,1)S(1)}, bf16[48,384]{1,0:T(8,128)(2,1)S(1)}, u32[]{:S(2)}, u32[]{:S(2)}) collective-permute-start(bf16[48,384]{1,0:T(8,128)(2,1)S(1)} %get-tuple-element.56), channel_id=1, source_target_pairs={{0,1},{1,0},{2,3},{3,2},{4,5},{5,4},{6,7},{7,6},{8,9},{9,8},{10,11... | collective-permute-start | bytes 110600 | tf_op jit(solution)/shard_map/ppermute | solution.py:515
  87.3 1.5 %collective-permute-start.11 = (bf16[48,384]{1,0:T(8,128)(2,1)S(1)}, bf16[48,384]{1,0:T(8,128)(2,1)S(1)}, u32[]{:S(2)}, u32[]{:S(2)}) collective-permute-start(bf16[48,384]{1,0:T(8,128)(2,1)S(1)} %get-tuple-element.57), channel_id=1, source_target_pairs={{0,2},{1,3},{2,0},{3,1},{4,6},{5,7},{6,4},{7,5},{8,10},{9,11},{10,... | collective-permute-start | bytes 110600 | tf_op jit(solution)/shard_map/ppermute | solution.py:515
  88.7 0.1 collective-permute-start.12
  88.8 0.8 collective-permute-done.10.refs_1_
  89.6 2.9 %collective-permute-start.13 = (bf16[48,384]{1,0:T(8,128)(2,1)S(1)}, bf16[48,384]{1,0:T(8,128)(2,1)S(1)}, u32[]{:S(2)}, u32[]{:S(2)}) collective-permute-start(bf16[48,384]{1,0:T(8,128)(2,1)S(1)} %get-tuple-element.59), channel_id=1, source_target_pairs={{0,4},{1,5},{2,6},{3,7},{4,0},{5,1},{6,2},{7,3},{8,12},{9,13},{10,... | collective-permute-start | bytes 110600 | tf_op jit(solution)/shard_map/ppermute | solution.py:515
  92.5 5.1 %collective-permute-done.11.refs_2_ = bf16[48,384]{1,0:T(8,128)(2,1)S(1)} collective-permute-done((bf16[48,384]{1,0:T(8,128)(2,1)S(1)}, bf16[48,384]{1,0:T(8,128)(2,1)S(1)}, u32[]{:S(2)}, u32[]{:S(2)}) %collective-permute-start.11) | collective-permute-done | bytes 36896 | tf_op jit(solution)/shard_map/ppermute | solution.py:515
  97.6 6.0 %collective-permute-start.14 = (bf16[48,384]{1,0:T(8,128)(2,1)S(1)}, bf16[48,384]{1,0:T(8,128)(2,1)S(1)}, u32[]{:S(2)}, u32[]{:S(2)}) collective-permute-start(bf16[48,384]{1,0:T(8,128)(2,1)S(1)} %get-tuple-element.60), channel_id=1, source_target_pairs={{0,5},{1,4},{2,7},{3,6},{4,1},{5,0},{6,3},{7,2},{8,13},{9,12},{10,... | collective-permute-start | bytes 110600 | tf_op jit(solution)/shard_map/ppermute | solution.py:515
  103.6 0.2 collective-permute-start.15
  103.7 3.8 %collective-permute-start.16 = (bf16[48,384]{1,0:T(8,128)(2,1)S(1)}, bf16[48,384]{1,0:T(8,128)(2,1)S(1)}, u32[]{:S(2)}, u32[]{:S(2)}) collective-permute-start(bf16[48,384]{1,0:T(8,128)(2,1)S(1)} %get-tuple-element.62), channel_id=1, source_target_pairs={{0,7},{1,6},{2,5},{3,4},{4,3},{5,2},{6,1},{7,0},{8,15},{9,14},{10,... | collective-permute-start | bytes 110600 | tf_op jit(solution)/shard_map/ppermute | solution.py:515
  107.5 0.1 home_places.1.places_ref
  107.7 6.2 %adam.1 = (f32[2,96,2048]{2,1,0:T(8,128)}, bf16[2,96,2048]{2,1,0:T(8,128)(2,1)}, f32[2,16,96]{2,1,0:T(8,128)}, bf16[2,96,2048]{2,1,0:T(8,128)(2,1)}, f32[2,16,96]{2,1,0:T(8,128)}) custom-call(f32[2,96,2048]{2,1,0:T(8,128)S(1)} %copy-done, bf16[2,96,2048]{2,1,0:T(8,128)(2,1)S(1)} %copy-done.13, f32[2,16,96]{2,1,0:T(8,128)S(1)} %bitcast.14, ...), custom_call_target="tpu_custom_call" | custom-call | flops 15728640 | bytes 7077888 | tf_op jit(solution)/shard_map/adam/pallas_call | solution.py:488
  113.9 0.1 collective-permute-done.14.refs_5_
  113.9 0.6 copy-done.15
  114.6 0.6 copy-done.17
  115.2 0.6 copy-done.19
  115.8 0.8 copy-done.16
  116.6 0.8 copy-done.18
  117.3 0.8 copy-done.20
  118.1 2.4 %collect.1 = (bf16[256,2048]{1,0:T(8,128)(2,1)}, bf16[256,384]{1,0:T(8,128)(2,1)}) custom-call(bf16[256,384]{1,0:T(8,128)(2,1)S(1)} %home_places.1.places_ref, bf16[384,2048]{1,0:T(8,128)(2,1)S(1)} %bitcast.10, bf16[48,384]{1,0:T(8,128)(2,1)S(1)} %get-tuple-element.55.refs_0_, bf16[48,384]{1,0:T(8,128)(2,1)S(1)} %collective-permute-done.10.refs_1_, ...), custom_call_target="tpu_custom_call" | custom-call | flops 478150656 | bytes 3112960 | tf_op jit(solution)/shard_map/collect/pallas_call | solution.py:221
  (44 shorter events, 0.1 us)
Async XLA Ops:
  3.7 7.4 %copy-start = (f32[2,96,2048]{2,1,0:T(8,128)S(1)}, f32[2,96,2048]{2,1,0:T(8,128)}, u32[]{:S(2)}) copy-start(f32[2,96,2048]{2,1,0:T(8,128)} %master_ref.1) | copy-start | bytes 4718596
  3.7 63.5 %all-to-all-start.1 = ((bf16[8,48,2048]{2,1,0:T(8,128)(2,1)}), bf16[8,48,2048]{2,1,0:T(8,128)(2,1)S(1)}, u32[]{:S(2)}, u32[]{:S(2)}) async-start(bf16[8,48,2048]{2,1,0:T(8,128)(2,1)} %bitcast.16), calls=%async_computation.1 | async-start | bytes 3145728 | tf_op jit(solution)/shard_map/all_to_all | solution.py:521
  11.1 19.5 %copy-start.23 = (s32[1,256]{1,0:T(1,128)S(1)}, s32[1,256]{1,0:T(1,128)}, u32[]{:S(2)}) copy-start(s32[1,256]{1,0:T(1,128)} %get-tuple-element.42.target_ref) | copy-start | bytes 3076
  11.1 19.5 %copy-start.24 = (bf16[256,384]{1,0:T(8,128)(2,1)S(1)}, bf16[256,384]{1,0:T(8,128)(2,1)}, u32[]{:S(2)}) copy-start(bf16[256,384]{1,0:T(8,128)(2,1)} %x_ref) | copy-start | bytes 589828
  11.5 19.1 %collective-permute-start.8 = (bf16[2,96,2048]{2,1,0:T(8,128)(2,1)S(1)}, bf16[2,96,2048]{2,1,0:T(8,128)(2,1)S(1)}, u32[]{:S(2)}, u32[]{:S(2)}) collective-permute-start(bf16[2,96,2048]{2,1,0:T(8,128)(2,1)S(1)} %cast_weight.1.refs_8_.refs_0_), channel_id=1, source_target_pairs={{0,16},{8,24},{16,0},{24,8},{1,17},{9,25},{17,1},{25,9},{2,18},{10... | collective-permute-start | bytes 2359304 | tf_op jit(solution)/shard_map/ppermute | solution.py:515
  13.1 45.7 %collective-permute-start.7 = (bf16[2,96,2048]{2,1,0:T(8,128)(2,1)S(1)}, bf16[2,96,2048]{2,1,0:T(8,128)(2,1)S(1)}, u32[]{:S(2)}, u32[]{:S(2)}) collective-permute-start(bf16[2,96,2048]{2,1,0:T(8,128)(2,1)S(1)} %cast_weight.1.refs_8_.refs_0_), channel_id=1, source_target_pairs={{0,8},{8,0},{16,24},{24,16},{1,9},{9,1},{17,25},{25,17},{2,10},{10... | collective-permute-start | bytes 2359304 | tf_op jit(solution)/shard_map/ppermute | solution.py:515
  30.6 28.2 %collective-permute-start.9 = (bf16[2,96,2048]{2,1,0:T(8,128)(2,1)S(1)}, bf16[2,96,2048]{2,1,0:T(8,128)(2,1)S(1)}, u32[]{:S(2)}, u32[]{:S(2)}) collective-permute-start(bf16[2,96,2048]{2,1,0:T(8,128)(2,1)S(1)} %collective-permute-done.8.refs_10_.refs_2_), channel_id=1, source_target_pairs={{0,8},{8,0},{16,24},{24,16},{1,9},{9,1},{17,25},{25,17},{2,10},{10... | collective-permute-start | bytes 2359304 | tf_op jit(solution)/shard_map/ppermute | solution.py:515
  30.9 6.0 %collective-permute-start = (bf16[48,384]{1,0:T(8,128)(2,1)S(1)}, bf16[48,384]{1,0:T(8,128)(2,1)S(1)}, u32[]{:S(2)}, u32[]{:S(2)}) collective-permute-start(bf16[48,384]{1,0:T(8,128)(2,1)S(1)} %get-tuple-element.45), channel_id=1, source_target_pairs={{0,1},{1,0},{2,3},{3,2},{4,5},{5,4},{6,7},{7,6},{8,9},{9,8},{10,11... | collective-permute-start | bytes 110600 | tf_op jit(solution)/shard_map/ppermute | solution.py:515
  32.7 6.3 %collective-permute-start.1 = (bf16[48,384]{1,0:T(8,128)(2,1)S(1)}, bf16[48,384]{1,0:T(8,128)(2,1)S(1)}, u32[]{:S(2)}, u32[]{:S(2)}) collective-permute-start(bf16[48,384]{1,0:T(8,128)(2,1)S(1)} %get-tuple-element.46), channel_id=1, source_target_pairs={{0,2},{1,3},{2,0},{3,1},{4,6},{5,7},{6,4},{7,5},{8,10},{9,11},{10,... | collective-permute-start | bytes 110600 | tf_op jit(solution)/shard_map/ppermute | solution.py:515
  34.1 9.6 %collective-permute-start.2 = (bf16[48,384]{1,0:T(8,128)(2,1)S(1)}, bf16[48,384]{1,0:T(8,128)(2,1)S(1)}, u32[]{:S(2)}, u32[]{:S(2)}) collective-permute-start(bf16[48,384]{1,0:T(8,128)(2,1)S(1)} %get-tuple-element.47), channel_id=1, source_target_pairs={{0,3},{1,2},{2,1},{3,0},{4,7},{5,6},{6,5},{7,4},{8,11},{9,10},{10,... | collective-permute-start | bytes 110600 | tf_op jit(solution)/shard_map/ppermute | solution.py:515
  36.9 15.2 %collective-permute-start.3 = (bf16[48,384]{1,0:T(8,128)(2,1)S(1)}, bf16[48,384]{1,0:T(8,128)(2,1)S(1)}, u32[]{:S(2)}, u32[]{:S(2)}) collective-permute-start(bf16[48,384]{1,0:T(8,128)(2,1)S(1)} %get-tuple-element.48), channel_id=1, source_target_pairs={{0,4},{1,5},{2,6},{3,7},{4,0},{5,1},{6,2},{7,3},{8,12},{9,13},{10,... | collective-permute-start | bytes 110600 | tf_op jit(solution)/shard_map/ppermute | solution.py:515
  39.0 15.1 %collective-permute-start.4 = (bf16[48,384]{1,0:T(8,128)(2,1)S(1)}, bf16[48,384]{1,0:T(8,128)(2,1)S(1)}, u32[]{:S(2)}, u32[]{:S(2)}) collective-permute-start(bf16[48,384]{1,0:T(8,128)(2,1)S(1)} %get-tuple-element.49), channel_id=1, source_target_pairs={{0,5},{1,4},{2,7},{3,6},{4,1},{5,0},{6,3},{7,2},{8,13},{9,12},{10,... | collective-permute-start | bytes 110600 | tf_op jit(solution)/shard_map/ppermute | solution.py:515
  43.8 10.3 %collective-permute-start.5 = (bf16[48,384]{1,0:T(8,128)(2,1)S(1)}, bf16[48,384]{1,0:T(8,128)(2,1)S(1)}, u32[]{:S(2)}, u32[]{:S(2)}) collective-permute-start(bf16[48,384]{1,0:T(8,128)(2,1)S(1)} %get-tuple-element.50), channel_id=1, source_target_pairs={{0,6},{1,7},{2,4},{3,5},{4,2},{5,3},{6,0},{7,1},{8,14},{9,15},{10,... | collective-permute-start | bytes 110600 | tf_op jit(solution)/shard_map/ppermute | solution.py:515
  52.1 6.7 %collective-permute-start.6 = (bf16[48,384]{1,0:T(8,128)(2,1)S(1)}, bf16[48,384]{1,0:T(8,128)(2,1)S(1)}, u32[]{:S(2)}, u32[]{:S(2)}) collective-permute-start(bf16[48,384]{1,0:T(8,128)(2,1)S(1)} %get-tuple-element.51), channel_id=1, source_target_pairs={{0,7},{1,6},{2,5},{3,4},{4,3},{5,2},{6,1},{7,0},{8,15},{9,14},{10,... | collective-permute-start | bytes 110600 | tf_op jit(solution)/shard_map/ppermute | solution.py:515
  61.7 0.9 copy-start.4
  62.6 1.2 copy-start.6
  63.7 0.9 copy-start.7
  64.6 0.9 copy-start.9
  65.5 0.9 copy-start.11
  66.4 0.8 copy-start.25
  67.2 1.1 copy-start.1
  68.3 47.4 %all-to-all-start = ((bf16[8,48,2048]{2,1,0:T(8,128)(2,1)}), bf16[8,48,2048]{2,1,0:T(8,128)(2,1)S(1)}, u32[]{:S(2)}, u32[]{:S(2)}) async-start(bf16[8,48,2048]{2,1,0:T(8,128)(2,1)} %bitcast.13), calls=%async_computation | async-start | bytes 3145728 | tf_op jit(solution)/shard_map/all_to_all | solution.py:521
  71.9 1.4 %copy-start.2 = (bf16[8,48,2048]{2,1,0:T(8,128)(2,1)S(1)}, bf16[8,48,2048]{2,1,0:T(8,128)(2,1)}, u32[]{:S(2)}) copy-start(bf16[8,48,2048]{2,1,0:T(8,128)(2,1)} %copy-done.1) | copy-start | bytes 4718596
  73.3 1.1 copy-start.26
  74.4 7.4 %copy-start.8 = (bf16[2,96,2048]{2,1,0:T(8,128)(2,1)S(1)}, bf16[2,96,2048]{2,1,0:T(8,128)(2,1)}, u32[]{:S(2)}) copy-start(bf16[2,96,2048]{2,1,0:T(8,128)(2,1)} %copy-done.7) | copy-start | bytes 2359300
  74.4 7.4 %copy-start.10 = (bf16[2,96,2048]{2,1,0:T(8,128)(2,1)S(1)}, bf16[2,96,2048]{2,1,0:T(8,128)(2,1)}, u32[]{:S(2)}) copy-start(bf16[2,96,2048]{2,1,0:T(8,128)(2,1)} %copy-done.9) | copy-start | bytes 2359300
  74.4 7.4 %copy-start.12 = (bf16[2,96,2048]{2,1,0:T(8,128)(2,1)S(1)}, bf16[2,96,2048]{2,1,0:T(8,128)(2,1)}, u32[]{:S(2)}) copy-start(bf16[2,96,2048]{2,1,0:T(8,128)(2,1)} %copy-done.11) | copy-start | bytes 2359300
  77.4 4.4 %copy-start.3 = (bf16[8,48,2048]{2,1,0:T(8,128)(2,1)S(1)}, bf16[8,48,2048]{2,1,0:T(8,128)(2,1)}, u32[]{:S(2)}) copy-start(bf16[8,48,2048]{2,1,0:T(8,128)(2,1)} %copy-done.1) | copy-start | bytes 4718596
  77.4 4.4 %copy-start.5 = (bf16[2,96,2048]{2,1,0:T(8,128)(2,1)S(1)}, bf16[2,96,2048]{2,1,0:T(8,128)(2,1)}, u32[]{:S(2)}) copy-start(bf16[2,96,2048]{2,1,0:T(8,128)(2,1)} %copy-done.4) | copy-start | bytes 2359300
  77.5 2.4 %collective-permute-start.18 = (bf16[2,96,2048]{2,1,0:T(8,128)(2,1)S(1)}, bf16[2,96,2048]{2,1,0:T(8,128)(2,1)S(1)}, u32[]{:S(2)}, u32[]{:S(2)}) collective-permute-start(bf16[2,96,2048]{2,1,0:T(8,128)(2,1)S(1)} %get-tuple-element.69), channel_id=1, source_target_pairs={{0,8},{8,0},{16,24},{24,16},{1,9},{9,1},{17,25},{25,17},{2,10},{10... | collective-permute-start | bytes 2359304 | tf_op jit(solution)/shard_map/ppermute | solution.py:515
  77.5 26.0 %collective-permute-start.17 = (bf16[2,96,2048]{2,1,0:T(8,128)(2,1)S(1)}, bf16[2,96,2048]{2,1,0:T(8,128)(2,1)S(1)}, u32[]{:S(2)}, u32[]{:S(2)}) collective-permute-start(bf16[2,96,2048]{2,1,0:T(8,128)(2,1)S(1)} %get-tuple-element.67), channel_id=1, source_target_pairs={{0,8},{8,0},{16,24},{24,16},{1,9},{9,1},{17,25},{25,17},{2,10},{10... | collective-permute-start | bytes 2359304 | tf_op jit(solution)/shard_map/ppermute | solution.py:515
  80.2 27.4 %copy-start.13 = (bf16[2,96,2048]{2,1,0:T(8,128)(2,1)S(1)}, bf16[2,96,2048]{2,1,0:T(8,128)(2,1)}, u32[]{:S(2)}) copy-start(bf16[2,96,2048]{2,1,0:T(8,128)(2,1)} %mc_ref.1) | copy-start | bytes 2359300
  80.2 27.4 %copy-start.14 = (bf16[2,96,2048]{2,1,0:T(8,128)(2,1)S(1)}, bf16[2,96,2048]{2,1,0:T(8,128)(2,1)}, u32[]{:S(2)}) copy-start(bf16[2,96,2048]{2,1,0:T(8,128)(2,1)} %vc_ref.1) | copy-start | bytes 2359300
  80.2 27.4 %copy-start.21 = (f32[2,96,16]{1,2,0:T(8,128)S(1)}, f32[2,96,16]{1,2,0:T(8,128)}, u32[]{:S(2)}) copy-start(f32[2,96,16]{1,2,0:T(8,128)} %param.11) | copy-start | bytes 36868
  80.2 27.4 %copy-start.22 = (f32[2,96,16]{1,2,0:T(8,128)S(1)}, f32[2,96,16]{1,2,0:T(8,128)}, u32[]{:S(2)}) copy-start(f32[2,96,16]{1,2,0:T(8,128)} %param.13) | copy-start | bytes 36868
  80.3 23.5 %collective-permute-start.19 = (bf16[2,96,2048]{2,1,0:T(8,128)(2,1)S(1)}, bf16[2,96,2048]{2,1,0:T(8,128)(2,1)S(1)}, u32[]{:S(2)}, u32[]{:S(2)}) collective-permute-start(bf16[2,96,2048]{2,1,0:T(8,128)(2,1)S(1)} %add_parts.1), channel_id=1, source_target_pairs={{0,16},{8,24},{16,0},{24,8},{1,17},{9,25},{17,1},{25,9},{2,18},{10... | collective-permute-start | bytes 2359304 | tf_op jit(solution)/shard_map/ppermute | solution.py:515
  85.3 4.3 %collective-permute-start.10 = (bf16[48,384]{1,0:T(8,128)(2,1)S(1)}, bf16[48,384]{1,0:T(8,128)(2,1)S(1)}, u32[]{:S(2)}, u32[]{:S(2)}) collective-permute-start(bf16[48,384]{1,0:T(8,128)(2,1)S(1)} %get-tuple-element.56), channel_id=1, source_target_pairs={{0,1},{1,0},{2,3},{3,2},{4,5},{5,4},{6,7},{7,6},{8,9},{9,8},{10,11... | collective-permute-start | bytes 110600 | tf_op jit(solution)/shard_map/ppermute | solution.py:515
  87.3 10.3 %collective-permute-start.11 = (bf16[48,384]{1,0:T(8,128)(2,1)S(1)}, bf16[48,384]{1,0:T(8,128)(2,1)S(1)}, u32[]{:S(2)}, u32[]{:S(2)}) collective-permute-start(bf16[48,384]{1,0:T(8,128)(2,1)S(1)} %get-tuple-element.57), channel_id=1, source_target_pairs={{0,2},{1,3},{2,0},{3,1},{4,6},{5,7},{6,4},{7,5},{8,10},{9,11},{10,... | collective-permute-start | bytes 110600 | tf_op jit(solution)/shard_map/ppermute | solution.py:515
  88.7 25.1 %collective-permute-start.12 = (bf16[48,384]{1,0:T(8,128)(2,1)S(1)}, bf16[48,384]{1,0:T(8,128)(2,1)S(1)}, u32[]{:S(2)}, u32[]{:S(2)}) collective-permute-start(bf16[48,384]{1,0:T(8,128)(2,1)S(1)} %get-tuple-element.58), channel_id=1, source_target_pairs={{0,3},{1,2},{2,1},{3,0},{4,7},{5,6},{6,5},{7,4},{8,11},{9,10},{10,... | collective-permute-start | bytes 110600 | tf_op jit(solution)/shard_map/ppermute | solution.py:515
  89.6 24.3 %collective-permute-start.13 = (bf16[48,384]{1,0:T(8,128)(2,1)S(1)}, bf16[48,384]{1,0:T(8,128)(2,1)S(1)}, u32[]{:S(2)}, u32[]{:S(2)}) collective-permute-start(bf16[48,384]{1,0:T(8,128)(2,1)S(1)} %get-tuple-element.59), channel_id=1, source_target_pairs={{0,4},{1,5},{2,6},{3,7},{4,0},{5,1},{6,2},{7,3},{8,12},{9,13},{10,... | collective-permute-start | bytes 110600 | tf_op jit(solution)/shard_map/ppermute | solution.py:515
  97.6 16.3 %collective-permute-start.14 = (bf16[48,384]{1,0:T(8,128)(2,1)S(1)}, bf16[48,384]{1,0:T(8,128)(2,1)S(1)}, u32[]{:S(2)}, u32[]{:S(2)}) collective-permute-start(bf16[48,384]{1,0:T(8,128)(2,1)S(1)} %get-tuple-element.60), channel_id=1, source_target_pairs={{0,5},{1,4},{2,7},{3,6},{4,1},{5,0},{6,3},{7,2},{8,13},{9,12},{10,... | collective-permute-start | bytes 110600 | tf_op jit(solution)/shard_map/ppermute | solution.py:515
  103.6 11.0 %collective-permute-start.15 = (bf16[48,384]{1,0:T(8,128)(2,1)S(1)}, bf16[48,384]{1,0:T(8,128)(2,1)S(1)}, u32[]{:S(2)}, u32[]{:S(2)}) collective-permute-start(bf16[48,384]{1,0:T(8,128)(2,1)S(1)} %get-tuple-element.61), channel_id=1, source_target_pairs={{0,6},{1,7},{2,4},{3,5},{4,2},{5,3},{6,0},{7,1},{8,14},{9,15},{10,... | collective-permute-start | bytes 110600 | tf_op jit(solution)/shard_map/ppermute | solution.py:515
  103.7 11.5 %collective-permute-start.16 = (bf16[48,384]{1,0:T(8,128)(2,1)S(1)}, bf16[48,384]{1,0:T(8,128)(2,1)S(1)}, u32[]{:S(2)}, u32[]{:S(2)}) collective-permute-start(bf16[48,384]{1,0:T(8,128)(2,1)S(1)} %get-tuple-element.62), channel_id=1, source_target_pairs={{0,7},{1,6},{2,5},{3,4},{4,3},{5,2},{6,1},{7,0},{8,15},{9,14},{10,... | collective-permute-start | bytes 110600 | tf_op jit(solution)/shard_map/ppermute | solution.py:515
  113.9 0.6 copy-start.15
  114.6 0.6 copy-start.17
  115.2 0.6 copy-start.19
  115.8 0.8 copy-start.16
  116.6 0.8 copy-start.18
  117.3 0.8 copy-start.20

commit v6 on v5

--- a/solution.py
+++ b/solution.py
@@ -14,8 +14,7 @@
 beta_two = 0.95
 learn_rate = 0.01
 
-VMEM_LIMIT = 40 * 1024 * 1024
-LARGE_LIMIT = 56 * 1024 * 1024
+VMEM_LIMIT = 60 * 1024 * 1024
 F32 = jnp.float32
 BF16 = jnp.bfloat16
 
@@ -114,7 +113,7 @@
             pltpu.SemaphoreType.DMA((tiles,)),
             pltpu.SemaphoreType.DMA((tiles,)),
         ],
-        compiler_params=pltpu.CompilerParams(vmem_limit_bytes=LARGE_LIMIT),
+        compiler_params=pltpu.CompilerParams(vmem_limit_bytes=VMEM_LIMIT),
         cost_estimate=cost(2 * places * row_count * width, 2 * (places + row_count) * width),
         name="dispatch",
     )(route.reshape(1, row_count), placement.reshape(1, -1), y_cot)
@@ -182,7 +181,7 @@
 
 def collect_kernel(chunks, places_ref, home_hbm, *refs):
     dx_refs, y_hbm, x_grad_hbm = refs[:chunks], refs[chunks], refs[chunks + 1]
-    home_ref, held_ref, y_ref, x_grad_ref, in_sems, out_sems = refs[chunks + 2 :]
+    home_ref, held_ref, y_ref, x_grad_ref, in_sems, chunk_sems, out_sems = refs[chunks + 2 :]
     tiles = in_sems.shape[0]
     tile = y_ref.shape[1] // tiles
     spans = [pl.ds(j * tile, tile) for j in range(tiles)]
@@ -190,12 +189,19 @@
         pltpu.make_async_copy(home_hbm.at[:, span], home_ref.at[:, span], in_sems.at[j])
         for j, span in enumerate(spans)
     ]
-    for load in loads:
+    chunk_loads = [
+        pltpu.make_async_copy(
+            ref, held_ref.at[chunk_owner(k) if chunks > 1 else 0], chunk_sems.at[k]
+        )
+        for k, ref in enumerate(dx_refs)
+    ]
+    for load in chunk_loads + loads:
         load.start()
     places = places_ref[...]
-    x_grad_ref[...] = jnp.dot(
-        places, join_chunks(dx_refs, held_ref), preferred_element_type=F32
-    ).astype(BF16)
+    for load in chunk_loads:
+        load.wait()
+    home_dx = held_ref[...].reshape(places.shape[1], x_grad_ref.shape[1])
+    x_grad_ref[...] = jnp.dot(places, home_dx, preferred_element_type=F32).astype(BF16)
     stores = [pltpu.make_async_copy(x_grad_ref, x_grad_hbm, out_sems.at[tiles])]
     stores[0].start()
     for j, span in enumerate(spans):
@@ -220,7 +226,7 @@
     hbm = pl.BlockSpec(memory_space=pl.ANY)
     return pl.pallas_call(
         functools.partial(collect_kernel, chunks),
-        in_specs=[whole, hbm] + [whole] * chunks,
+        in_specs=[whole, hbm] + [hbm] * chunks,
         out_specs=(hbm, hbm),
         out_shape=(
             jax.ShapeDtypeStruct((row_count, width), BF16),
@@ -232,6 +238,7 @@
             pltpu.VMEM((row_count, width), BF16),
             pltpu.VMEM((row_count, hidden), BF16),
             pltpu.SemaphoreType.DMA((tiles,)),
+            pltpu.SemaphoreType.DMA((chunks,)),
             pltpu.SemaphoreType.DMA((tiles + 1,)),
         ],
         compiler_params=params(),
@@ -528,12 +535,15 @@
     return [chunks[0]] + [swap(chunk, "grp", k) for k, chunk in enumerate(chunks) if k > 0]
 
 
-def gather_weight(weight_slice, replicas):
+def gather_weight(weight_slice, replicas, send_between):
     if replicas != 4:
-        return [lax.all_gather(weight_slice, "rep", axis=1, tiled=True)]
+        between = send_between()
+        return [lax.all_gather(weight_slice, "rep", axis=1, tiled=True)], between
+    near = swap(weight_slice, "rep", 1)
     far = swap(weight_slice, "rep", 2)
-    near = swap(weight_slice, "rep", 1)
-    return [weight_slice, near, far, swap(far, "rep", 1)]
+    between = send_between()
+    far, between = lax.optimization_barrier((far, between))
+    return [weight_slice, near, far, swap(far, "rep", 1)], between
 
 
 def sum_gradient(parts):
@@ -561,8 +571,11 @@
     local_g = exchange(sent_g, groups)
 
     early_master, early_x, target = lax.optimization_barrier((master_weight, x_rows, target))
-    weight = gather_weight(cast_weight(early_master), replicas)
-    local_x = exchange_chunks(dispatch_x(target, early_x, places, chunks), groups)
+
+    def send_x():
+        return exchange_chunks(dispatch_x(target, early_x, places, chunks), groups)
+
+    weight, local_x = gather_weight(cast_weight(early_master), replicas, send_x)
     back_y, wide = forward(local_x, weight, capacity)
     home_y = exchange(back_y, groups)
 

time: 121 us -> 120 us (level)
  Pallas kernels: 22.1 us -> 40.8 us
  waiting for transfers between devices: 41.8 us -> 28.9 us
  local copies, waits for them, and re-layouts: 13.3 us -> 3.24 us
  starting transfers between devices: 42.4 us -> 45.3 us
    ppermute x20, waiting for transfers between devices: 41.8 us -> 28.9 us  [swap(): return lax.ppermute(array, axis, [(i, i ^ offset) for i in range(size)])]
    unnamed x54 -> x42, local copies, waits for them, and re-layouts: 13.3 us -> 3.24 us
    ppermute x20, starting transfers between devices: 31.4 us -> 34.5 us  [swap(): return lax.ppermute(array, axis, [(i, i ^ offset) for i in range(size)])]
    pallas_call x1, Pallas kernels: 0.34 us -> 3.42 us  [cast_weight(): pl.pallas_call(cast_kernel, grid=(width // tile,), in_specs=[spec], out_s...]
    pallas_call x1, Pallas kernels: 2.9 us -> 5.54 us  [forward(): pl.pallas_call(functools.partial(forward_kernel, capacity, local_count, l...]
    pallas_call x1, Pallas kernels: 3.01 us -> 5.36 us  [gradient(): pl.pallas_call(functools.partial(gradient_kernel, parts, factor), grid=(w...]
    pallas_call x1, Pallas kernels: 3.41 us -> 5.73 us  [backward(): pl.pallas_call(functools.partial(backward_kernel, capacity, local_count,...]
    pallas_call x1, Pallas kernels: 2.4 us -> 4.5 us  [collect(): pl.pallas_call(functools.partial(collect_kernel, chunks), in_specs=[whole...]
  transfers between devices with their start and end apart: 22 -> 22, of which waited for: 9 -> 9; matrix products, arithmetic and copies ran while one was open for 0% -> 0% of each run, Pallas kernels for 14% -> 28%
where the time goes in v6:
time: 120 us; the launch traced here: 119 us
  starting transfers between devices  45.3 us (38%)
  Pallas kernels  40.8 us (34%)
  waiting for transfers between devices  28.9 us (24%)
  local copies, waits for them, and re-layouts  3.24 us (3%)
    ppermute x20, starting transfers between devices, swap(): return lax.ppermute(array, axis, [(i, i ^ offset) for i in range(size)])  34.5 us
    ppermute x20, waiting for transfers between devices, swap(): return lax.ppermute(array, axis, [(i, i ^ offset) for i in range(size)])  28.9 us
    all_to_all x2, starting transfers between devices, exchange(): lax.all_to_all(parts, 'grp', split_axis=0, concat_axis=0, tiled=True)  10.9 us
    pallas_call x1, Pallas kernels, adam(): pl.pallas_call(functools.partial(adam_kernel, len(grads)), grid=(members,...  7.5 us
    pallas_call x1, Pallas kernels, backward(): pl.pallas_call(functools.partial(backward_kernel, capacity, local_count,...  5.73 us
    pallas_call x1, Pallas kernels, forward(): pl.pallas_call(functools.partial(forward_kernel, capacity, local_count, l...  5.54 us
    pallas_call x1, Pallas kernels, gradient(): pl.pallas_call(functools.partial(gradient_kernel, parts, factor), grid=(w...  5.36 us
    pallas_call x1, Pallas kernels, collect(): pl.pallas_call(functools.partial(collect_kernel, chunks), in_specs=[whole...  4.5 us
  transfers between devices with their start and end apart: 22, of which 9 were waited for; matrix products, arithmetic and copies ran while one was open for 0% of the time, Pallas kernels for 28%

profile of v6, /device:TPU:0, one launch (start us, length us, event | category | flops | bytes accessed | tf_op | source)
XLA Modules:
  0.0 119.1 jit_solution(8042138017306710565)
XLA Ops:
  0.6 3.1 %dispatch.1 = (bf16[384,2048]{1,0:T(8,128)(2,1)}, s32[1,256]{1,0:T(1,128)}) custom-call(s32[1,256]{1,0:T(1,128)} %bitcast.19, s32[1,16]{1,0:T(1,128)} %bitcast.20, bf16[256,2048]{1,0:T(8,128)(2,1)} %g_hbm.1), custom_call_target="tpu_custom_call" | custom-call | flops 402653184 | bytes 2621440 | tf_op jit(solution)/shard_map/dispatch/pallas_call | solution.py:98
  3.7 7.3 %all-to-all-start.1 = ((bf16[8,48,2048]{2,1,0:T(8,128)(2,1)}), bf16[8,48,2048]{2,1,0:T(8,128)(2,1)S(1)}, u32[]{:S(2)}, u32[]{:S(2)}) async-start(bf16[8,48,2048]{2,1,0:T(8,128)(2,1)} %bitcast.14), calls=%async_computation.1 | async-start | bytes 3145728 | tf_op jit(solution)/shard_map/all_to_all | solution.py:528
  11.0 3.4 %cast_weight.1.refs_8_.refs_0_ = bf16[2,96,2048]{2,1,0:T(8,128)(2,1)} custom-call(f32[2,96,2048]{2,1,0:T(8,128)} %master_ref.1), custom_call_target="tpu_custom_call" | custom-call | flops 393216 | bytes 2359296 | tf_op jit(solution)/shard_map/cast_weight/pallas_call | solution.py:420
  14.4 1.5 %collective-permute-start = (bf16[2,96,2048]{2,1,0:T(8,128)(2,1)}, bf16[2,96,2048]{2,1,0:T(8,128)(2,1)S(1)}, u32[]{:S(2)}, u32[]{:S(2)}) collective-permute-start(bf16[2,96,2048]{2,1,0:T(8,128)(2,1)} %cast_weight.1.refs_8_.refs_0_), channel_id=1, source_target_pairs={{0,16},{8,24},{16,0},{24,8},{1,17},{9,25},{17,1},{25,9},{2,18},{10... | collective-permute-start | bytes 2359304 | tf_op jit(solution)/shard_map/ppermute | solution.py:522
  15.9 1.9 %dispatch_x.1 = (bf16[48,384]{1,0:T(8,128)(2,1)}, bf16[48,384]{1,0:T(8,128)(2,1)}, bf16[48,384]{1,0:T(8,128)(2,1)}, bf16[48,384]{1,0:T(8,128)(2,1)}, bf16[48,384...) custom-call(s32[1,256]{1,0:T(1,128)} %get-tuple-element.51.target_ref, ...), custom_call_target="tpu_custom_call" | custom-call | flops 75497472 | bytes 491520 | tf_op jit(solution)/shard_map/dispatch_x/pallas_call | solution.py:156
  17.8 2.0 %collective-permute-start.1 = (bf16[48,384]{1,0:T(8,128)(2,1)}, bf16[48,384]{1,0:T(8,128)(2,1)S(1)}, u32[]{:S(2)}, u32[]{:S(2)}) collective-permute-start(bf16[48,384]{1,0:T(8,128)(2,1)} %get-tuple-element.55), channel_id=1, source_target_pairs={{0,1},{1,0},{2,3},{3,2},{4,5},{5,4},{6,7},{7,6},{8,9},{9,8},{10,11... | collective-permute-start | bytes 110600 | tf_op jit(solution)/shard_map/ppermute | solution.py:522
  19.9 1.5 %collective-permute-start.2 = (bf16[48,384]{1,0:T(8,128)(2,1)}, bf16[48,384]{1,0:T(8,128)(2,1)S(1)}, u32[]{:S(2)}, u32[]{:S(2)}) collective-permute-start(bf16[48,384]{1,0:T(8,128)(2,1)} %get-tuple-element.56), channel_id=1, source_target_pairs={{0,2},{1,3},{2,0},{3,1},{4,6},{5,7},{6,4},{7,5},{8,10},{9,11},{10,... | collective-permute-start | bytes 110600 | tf_op jit(solution)/shard_map/ppermute | solution.py:522
  21.3 0.1 collective-permute-start.3
  21.4 2.9 %collective-permute-start.4 = (bf16[48,384]{1,0:T(8,128)(2,1)}, bf16[48,384]{1,0:T(8,128)(2,1)S(1)}, u32[]{:S(2)}, u32[]{:S(2)}) collective-permute-start(bf16[48,384]{1,0:T(8,128)(2,1)} %get-tuple-element.58), channel_id=1, source_target_pairs={{0,4},{1,5},{2,6},{3,7},{4,0},{5,1},{6,2},{7,3},{8,12},{9,13},{10,... | collective-permute-start | bytes 110600 | tf_op jit(solution)/shard_map/ppermute | solution.py:522
  24.2 0.5 collective-permute-done.1.refs_1_
  24.7 4.4 %collective-permute-start.5 = (bf16[48,384]{1,0:T(8,128)(2,1)}, bf16[48,384]{1,0:T(8,128)(2,1)S(1)}, u32[]{:S(2)}, u32[]{:S(2)}) collective-permute-start(bf16[48,384]{1,0:T(8,128)(2,1)} %get-tuple-element.59), channel_id=1, source_target_pairs={{0,5},{1,4},{2,7},{3,6},{4,1},{5,0},{6,3},{7,2},{8,13},{9,12},{10,... | collective-permute-start | bytes 110600 | tf_op jit(solution)/shard_map/ppermute | solution.py:522
  29.1 10.1 %collective-permute-done.2.refs_2_ = bf16[48,384]{1,0:T(8,128)(2,1)S(1)} collective-permute-done((bf16[48,384]{1,0:T(8,128)(2,1)}, bf16[48,384]{1,0:T(8,128)(2,1)S(1)}, u32[]{:S(2)}, u32[]{:S(2)}) %collective-permute-start.2) | collective-permute-done | bytes 36896 | tf_op jit(solution)/shard_map/ppermute | solution.py:522
  39.3 3.1 %collective-permute-start.6 = (bf16[48,384]{1,0:T(8,128)(2,1)}, bf16[48,384]{1,0:T(8,128)(2,1)S(1)}, u32[]{:S(2)}, u32[]{:S(2)}) collective-permute-start(bf16[48,384]{1,0:T(8,128)(2,1)} %get-tuple-element.60), channel_id=1, source_target_pairs={{0,6},{1,7},{2,4},{3,5},{4,2},{5,3},{6,0},{7,1},{8,14},{9,15},{10,... | collective-permute-start | bytes 110600 | tf_op jit(solution)/shard_map/ppermute | solution.py:522
  42.4 0.0 collective-permute-done.3.refs_3_
  42.4 1.5 %collective-permute-start.7 = (bf16[48,384]{1,0:T(8,128)(2,1)}, bf16[48,384]{1,0:T(8,128)(2,1)S(1)}, u32[]{:S(2)}, u32[]{:S(2)}) collective-permute-start(bf16[48,384]{1,0:T(8,128)(2,1)} %get-tuple-element.61), channel_id=1, source_target_pairs={{0,7},{1,6},{2,5},{3,4},{4,3},{5,2},{6,1},{7,0},{8,15},{9,14},{10,... | collective-permute-start | bytes 110600 | tf_op jit(solution)/shard_map/ppermute | solution.py:522
  43.9 9.3 %collective-permute-done.4.refs_4_ = bf16[48,384]{1,0:T(8,128)(2,1)S(1)} collective-permute-done((bf16[48,384]{1,0:T(8,128)(2,1)}, bf16[48,384]{1,0:T(8,128)(2,1)S(1)}, u32[]{:S(2)}, u32[]{:S(2)}) %collective-permute-start.4) | collective-permute-done | bytes 36896 | tf_op jit(solution)/shard_map/ppermute | solution.py:522
  53.1 0.0 collective-permute-start.8
  53.1 1.2 %collective-permute-done.5.refs_5_ = bf16[48,384]{1,0:T(8,128)(2,1)S(1)} collective-permute-done((bf16[48,384]{1,0:T(8,128)(2,1)}, bf16[48,384]{1,0:T(8,128)(2,1)S(1)}, u32[]{:S(2)}, u32[]{:S(2)}) %collective-permute-start.5) | collective-permute-done | bytes 36896 | tf_op jit(solution)/shard_map/ppermute | solution.py:522
  54.4 0.0 collective-permute-done.6.refs_6_
  54.4 0.0 collective-permute-done.7.refs_7_
  54.4 0.0 collective-permute-done.refs_10_.refs_2_
  54.4 0.1 collective-permute-start.9
  54.5 1.1 collective-permute-done.8.refs_9_.refs_1_
  55.6 1.3 %collective-permute-done.9.refs_11_.refs_3_ = bf16[2,96,2048]{2,1,0:T(8,128)(2,1)} collective-permute-done((bf16[2,96,2048]{2,1,0:T(8,128)(2,1)S(1)}, bf16[2,96,2048]{2,1,0:T(8,128)(2,1)}, u32[]{:S(2)}, u32[]{:S(2)}) %collective-permute-start.9) | collective-permute-done | bytes 786464 | tf_op jit(solution)/shard_map/ppermute | solution.py:522
  56.9 0.0 copy-done.15
  57.0 5.5 %forward.1 = (bf16[384,2048]{1,0:T(8,128)(2,1)}, bf16[384,768]{1,0:T(8,128)(2,1)}) custom-call(bf16[48,384]{1,0:T(8,128)(2,1)} %get-tuple-element.62.refs_0_, bf16[48,384]{1,0:T(8,128)(2,1)} %copy-done.14, bf16[48,384]{1,0:T(8,128)(2,1)} %copy-done.15, bf16[48,384]{1,0:T(8,128)(2,1)} %copy-done.16, bf16[48,384]{1,0:T(8,128)(2,1)} %copy-done.17, ...), custom_call_target="tpu_custom_call" | custom-call | flops 1207959552 | bytes 4718592 | tf_op jit(solution)/shard_map/forward/pallas_call | solution.py:299
  62.5 0.0 all-to-all-done.1
  62.5 0.0 copy-start.1
  62.5 1.1 copy-done.1
  63.7 3.6 %all-to-all-start = ((bf16[8,48,2048]{2,1,0:T(8,128)(2,1)}), bf16[8,48,2048]{2,1,0:T(8,128)(2,1)S(1)}, u32[]{:S(2)}, u32[]{:S(2)}) async-start(bf16[8,48,2048]{2,1,0:T(8,128)(2,1)} %bitcast.13), calls=%async_computation | async-start | bytes 3145728 | tf_op jit(solution)/shard_map/all_to_all | solution.py:528
  67.3 5.4 %gradient.1 = (bf16[2,96,2048]{2,1,0:T(8,128)(2,1)}, bf16[2,96,2048]{2,1,0:T(8,128)(2,1)}, bf16[2,96,2048]{2,1,0:T(8,128)(2,1)}, bf16[2,96,2048]{2,1,0:T(8,128)(2,1)}) custom-call(bf16[384,768]{1,0:T(8,128)(2,1)} %get-tuple-element.83.wide_ref, bf16[384,2048]{1,0:T(8,128)(2,1)} %bitcast.11), custom_call_target="tpu_custom_call" | custom-call | flops 1207959552 | bytes 4718592 | tf_op jit(solution)/shard_map/gradient/pallas_call | solution.py:396
  72.6 0.1 collective-permute-start.18
  72.8 0.4 collective-permute-start.17
  73.1 2.0 %collective-permute-done.18.b_ref = bf16[2,96,2048]{2,1,0:T(8,128)(2,1)S(1)} collective-permute-done((bf16[2,96,2048]{2,1,0:T(8,128)(2,1)}, bf16[2,96,2048]{2,1,0:T(8,128)(2,1)S(1)}, u32[]{:S(2)}, u32[]{:S(2)}) %collective-permute-start.18) | collective-permute-done | bytes 786464 | tf_op jit(solution)/shard_map/ppermute | solution.py:522
  75.1 0.9 copy-done.4
  76.0 2.2 %add_parts.1 = bf16[2,96,2048]{2,1,0:T(8,128)(2,1)} custom-call(bf16[2,96,2048]{2,1,0:T(8,128)(2,1)} %get-tuple-element.86.a_ref, bf16[2,96,2048]{2,1,0:T(8,128)(2,1)} %copy-done.4), custom_call_target="tpu_custom_call" | custom-call | flops 393216 | bytes 2359296 | tf_op jit(solution)/shard_map/add_parts/pallas_call | solution.py:440
  78.2 1.5 %collective-permute-start.19 = (bf16[2,96,2048]{2,1,0:T(8,128)(2,1)}, bf16[2,96,2048]{2,1,0:T(8,128)(2,1)S(1)}, u32[]{:S(2)}, u32[]{:S(2)}) collective-permute-start(bf16[2,96,2048]{2,1,0:T(8,128)(2,1)} %add_parts.1), channel_id=1, source_target_pairs={{0,16},{8,24},{16,0},{24,8},{1,17},{9,25},{17,1},{25,9},{2,18},{10... | collective-permute-start | bytes 2359304 | tf_op jit(solution)/shard_map/ppermute | solution.py:522
  79.7 5.7 %backward.1 = (bf16[48,384]{1,0:T(8,128)(2,1)}, bf16[48,384]{1,0:T(8,128)(2,1)}, bf16[48,384]{1,0:T(8,128)(2,1)}, bf16[48,384]{1,0:T(8,128)(2,1)}, bf16[48,384]{...) custom-call(bf16[384,2048]{1,0:T(8,128)(2,1)} %bitcast.12, ...), custom_call_target="tpu_custom_call" | custom-call | flops 1207959552 | bytes 4718592 | tf_op jit(solution)/shard_map/backward/pallas_call | solution.py:352
  85.5 2.0 %collective-permute-start.10 = (bf16[48,384]{1,0:T(8,128)(2,1)}, bf16[48,384]{1,0:T(8,128)(2,1)S(1)}, u32[]{:S(2)}, u32[]{:S(2)}) collective-permute-start(bf16[48,384]{1,0:T(8,128)(2,1)} %get-tuple-element.74), channel_id=1, source_target_pairs={{0,1},{1,0},{2,3},{3,2},{4,5},{5,4},{6,7},{7,6},{8,9},{9,8},{10,11... | collective-permute-start | bytes 110600 | tf_op jit(solution)/shard_map/ppermute | solution.py:522
  87.4 1.5 %collective-permute-start.11 = (bf16[48,384]{1,0:T(8,128)(2,1)}, bf16[48,384]{1,0:T(8,128)(2,1)S(1)}, u32[]{:S(2)}, u32[]{:S(2)}) collective-permute-start(bf16[48,384]{1,0:T(8,128)(2,1)} %get-tuple-element.75), channel_id=1, source_target_pairs={{0,2},{1,3},{2,0},{3,1},{4,6},{5,7},{6,4},{7,5},{8,10},{9,11},{10,... | collective-permute-start | bytes 110600 | tf_op jit(solution)/shard_map/ppermute | solution.py:522
  88.9 0.1 collective-permute-start.12
  89.0 1.1 collective-permute-done.10.refs_1_
  90.1 3.6 %collective-permute-start.13 = (bf16[48,384]{1,0:T(8,128)(2,1)}, bf16[48,384]{1,0:T(8,128)(2,1)S(1)}, u32[]{:S(2)}, u32[]{:S(2)}) collective-permute-start(bf16[48,384]{1,0:T(8,128)(2,1)} %get-tuple-element.77), channel_id=1, source_target_pairs={{0,4},{1,5},{2,6},{3,7},{4,0},{5,1},{6,2},{7,3},{8,12},{9,13},{10,... | collective-permute-start | bytes 110600 | tf_op jit(solution)/shard_map/ppermute | solution.py:522
  93.6 2.3 %collective-permute-done.11.refs_2_ = bf16[48,384]{1,0:T(8,128)(2,1)S(1)} collective-permute-done((bf16[48,384]{1,0:T(8,128)(2,1)}, bf16[48,384]{1,0:T(8,128)(2,1)S(1)}, u32[]{:S(2)}, u32[]{:S(2)}) %collective-permute-start.11) | collective-permute-done | bytes 36896 | tf_op jit(solution)/shard_map/ppermute | solution.py:522
  95.9 4.5 %collective-permute-start.14 = (bf16[48,384]{1,0:T(8,128)(2,1)}, bf16[48,384]{1,0:T(8,128)(2,1)S(1)}, u32[]{:S(2)}, u32[]{:S(2)}) collective-permute-start(bf16[48,384]{1,0:T(8,128)(2,1)} %get-tuple-element.78), channel_id=1, source_target_pairs={{0,5},{1,4},{2,7},{3,6},{4,1},{5,0},{6,3},{7,2},{8,13},{9,12},{10,... | collective-permute-start | bytes 110600 | tf_op jit(solution)/shard_map/ppermute | solution.py:522
  100.4 0.0 collective-permute-done.17.refs_1_
  100.4 1.1 collective-permute-start.15
  101.6 0.0 collective-permute-done.19.refs_2_
  101.6 2.7 %collective-permute-start.16 = (bf16[48,384]{1,0:T(8,128)(2,1)}, bf16[48,384]{1,0:T(8,128)(2,1)S(1)}, u32[]{:S(2)}, u32[]{:S(2)}) collective-permute-start(bf16[48,384]{1,0:T(8,128)(2,1)} %get-tuple-element.80), channel_id=1, source_target_pairs={{0,7},{1,6},{2,5},{3,4},{4,3},{5,2},{6,1},{7,0},{8,15},{9,14},{10,... | collective-permute-start | bytes 110600 | tf_op jit(solution)/shard_map/ppermute | solution.py:522
  104.3 1.5 %home_places.1.places_ref = bf16[256,384]{1,0:T(8,128)(2,1)} custom-call(s32[1,256]{1,0:T(1,128)} %get-tuple-element.51.target_ref), custom_call_target="tpu_custom_call" | custom-call | flops 98304 | bytes 196608 | tf_op jit(solution)/shard_map/home_places/pallas_call | solution.py:173
  105.8 7.5 %adam.1 = (f32[2,96,2048]{2,1,0:T(8,128)}, bf16[2,96,2048]{2,1,0:T(8,128)(2,1)}, f32[2,16,96]{2,1,0:T(8,128)}, bf16[2,96,2048]{2,1,0:T(8,128)(2,1)}, f32[2,16,96]{2,1,0:T(8,128)}) custom-call(f32[2,96,2048]{2,1,0:T(8,128)} %master_ref.1, bf16[2,96,2048]{2,1,0:T(8,128)(2,1)} %mc_ref.1, f32[2,16,96]{2,1,0:T(8,128)} %bitcast.15, bf16[2,96,2048]{2,1,0:T(8,128)(2,1)} %vc_ref.1, ...), custom_call_target="tpu_custom_call" | custom-call | flops 15728640 | bytes 7077888 | tf_op jit(solution)/shard_map/adam/pallas_call | solution.py:495
  113.3 0.0 collective-permute-done.12.refs_3_
  113.3 0.0 collective-permute-done.13.refs_4_
  113.4 0.0 collective-permute-done.14.refs_5_
  113.4 0.0 collective-permute-done.15.refs_6_
  113.4 0.0 collective-permute-done.16.refs_7_
  113.4 0.0 all-to-all-done
  113.4 0.5 copy-done.9
  113.9 0.0 copy-done.10
  114.0 0.0 copy-done.11
  114.0 0.0 copy-done.12
  114.0 0.0 copy-done.13
  114.0 0.6 copy-done
  114.6 4.5 %collect.1 = (bf16[256,2048]{1,0:T(8,128)(2,1)}, bf16[256,384]{1,0:T(8,128)(2,1)}) custom-call(bf16[256,384]{1,0:T(8,128)(2,1)} %home_places.1.places_ref, bf16[384,2048]{1,0:T(8,128)(2,1)} %bitcast.10, bf16[48,384]{1,0:T(8,128)(2,1)} %get-tuple-element.73.refs_0_, bf16[48,384]{1,0:T(8,128)(2,1)} %copy-done.7, bf16[48,384]{1,0:T(8,128)(2,1)} %copy-done.8, ...), custom_call_target="tpu_custom_call" | custom-call | flops 478150656 | bytes 3112960 | tf_op jit(solution)/shard_map/collect/pallas_call | solution.py:227
  (32 shorter events, 0.1 us)
Async XLA Ops:
  3.7 58.8 %all-to-all-start.1 = ((bf16[8,48,2048]{2,1,0:T(8,128)(2,1)}), bf16[8,48,2048]{2,1,0:T(8,128)(2,1)S(1)}, u32[]{:S(2)}, u32[]{:S(2)}) async-start(bf16[8,48,2048]{2,1,0:T(8,128)(2,1)} %bitcast.14), calls=%async_computation.1 | async-start | bytes 3145728 | tf_op jit(solution)/shard_map/all_to_all | solution.py:528
  14.4 40.0 %collective-permute-start = (bf16[2,96,2048]{2,1,0:T(8,128)(2,1)}, bf16[2,96,2048]{2,1,0:T(8,128)(2,1)S(1)}, u32[]{:S(2)}, u32[]{:S(2)}) collective-permute-start(bf16[2,96,2048]{2,1,0:T(8,128)(2,1)} %cast_weight.1.refs_8_.refs_0_), channel_id=1, source_target_pairs={{0,16},{8,24},{16,0},{24,8},{1,17},{9,25},{17,1},{25,9},{2,18},{10... | collective-permute-start | bytes 2359304 | tf_op jit(solution)/shard_map/ppermute | solution.py:522
  17.8 6.9 %collective-permute-start.1 = (bf16[48,384]{1,0:T(8,128)(2,1)}, bf16[48,384]{1,0:T(8,128)(2,1)S(1)}, u32[]{:S(2)}, u32[]{:S(2)}) collective-permute-start(bf16[48,384]{1,0:T(8,128)(2,1)} %get-tuple-element.55), channel_id=1, source_target_pairs={{0,1},{1,0},{2,3},{3,2},{4,5},{5,4},{6,7},{7,6},{8,9},{9,8},{10,11... | collective-permute-start | bytes 110600 | tf_op jit(solution)/shard_map/ppermute | solution.py:522
  19.9 19.4 %collective-permute-start.2 = (bf16[48,384]{1,0:T(8,128)(2,1)}, bf16[48,384]{1,0:T(8,128)(2,1)S(1)}, u32[]{:S(2)}, u32[]{:S(2)}) collective-permute-start(bf16[48,384]{1,0:T(8,128)(2,1)} %get-tuple-element.56), channel_id=1, source_target_pairs={{0,2},{1,3},{2,0},{3,1},{4,6},{5,7},{6,4},{7,5},{8,10},{9,11},{10,... | collective-permute-start | bytes 110600 | tf_op jit(solution)/shard_map/ppermute | solution.py:522
  21.3 21.1 %collective-permute-start.3 = (bf16[48,384]{1,0:T(8,128)(2,1)}, bf16[48,384]{1,0:T(8,128)(2,1)S(1)}, u32[]{:S(2)}, u32[]{:S(2)}) collective-permute-start(bf16[48,384]{1,0:T(8,128)(2,1)} %get-tuple-element.57), channel_id=1, source_target_pairs={{0,3},{1,2},{2,1},{3,0},{4,7},{5,6},{6,5},{7,4},{8,11},{9,10},{10,... | collective-permute-start | bytes 110600 | tf_op jit(solution)/shard_map/ppermute | solution.py:522
  21.4 31.8 %collective-permute-start.4 = (bf16[48,384]{1,0:T(8,128)(2,1)}, bf16[48,384]{1,0:T(8,128)(2,1)S(1)}, u32[]{:S(2)}, u32[]{:S(2)}) collective-permute-start(bf16[48,384]{1,0:T(8,128)(2,1)} %get-tuple-element.58), channel_id=1, source_target_pairs={{0,4},{1,5},{2,6},{3,7},{4,0},{5,1},{6,2},{7,3},{8,12},{9,13},{10,... | collective-permute-start | bytes 110600 | tf_op jit(solution)/shard_map/ppermute | solution.py:522
  24.7 32.2 %copy-start.14 = (bf16[48,384]{1,0:T(8,128)(2,1)}, bf16[48,384]{1,0:T(8,128)(2,1)S(1)}, u32[]{:S(2)}) copy-start(bf16[48,384]{1,0:T(8,128)(2,1)S(1)} %collective-permute-done.1.refs_1_) | copy-start | bytes 110596
  24.7 29.6 %collective-permute-start.5 = (bf16[48,384]{1,0:T(8,128)(2,1)}, bf16[48,384]{1,0:T(8,128)(2,1)S(1)}, u32[]{:S(2)}, u32[]{:S(2)}) collective-permute-start(bf16[48,384]{1,0:T(8,128)(2,1)} %get-tuple-element.59), channel_id=1, source_target_pairs={{0,5},{1,4},{2,7},{3,6},{4,1},{5,0},{6,3},{7,2},{8,13},{9,12},{10,... | collective-permute-start | bytes 110600 | tf_op jit(solution)/shard_map/ppermute | solution.py:522
  39.3 17.6 %copy-start.15 = (bf16[48,384]{1,0:T(8,128)(2,1)}, bf16[48,384]{1,0:T(8,128)(2,1)S(1)}, u32[]{:S(2)}) copy-start(bf16[48,384]{1,0:T(8,128)(2,1)S(1)} %collective-permute-done.2.refs_2_) | copy-start | bytes 110596
  39.3 15.1 %collective-permute-start.6 = (bf16[48,384]{1,0:T(8,128)(2,1)}, bf16[48,384]{1,0:T(8,128)(2,1)S(1)}, u32[]{:S(2)}, u32[]{:S(2)}) collective-permute-start(bf16[48,384]{1,0:T(8,128)(2,1)} %get-tuple-element.60), channel_id=1, source_target_pairs={{0,6},{1,7},{2,4},{3,5},{4,2},{5,3},{6,0},{7,1},{8,14},{9,15},{10,... | collective-permute-start | bytes 110600 | tf_op jit(solution)/shard_map/ppermute | solution.py:522
  42.4 14.5 %copy-start.16 = (bf16[48,384]{1,0:T(8,128)(2,1)}, bf16[48,384]{1,0:T(8,128)(2,1)S(1)}, u32[]{:S(2)}) copy-start(bf16[48,384]{1,0:T(8,128)(2,1)S(1)} %collective-permute-done.3.refs_3_) | copy-start | bytes 110596
  42.4 12.0 %collective-permute-start.7 = (bf16[48,384]{1,0:T(8,128)(2,1)}, bf16[48,384]{1,0:T(8,128)(2,1)S(1)}, u32[]{:S(2)}, u32[]{:S(2)}) collective-permute-start(bf16[48,384]{1,0:T(8,128)(2,1)} %get-tuple-element.61), channel_id=1, source_target_pairs={{0,7},{1,6},{2,5},{3,4},{4,3},{5,2},{6,1},{7,0},{8,15},{9,14},{10,... | collective-permute-start | bytes 110600 | tf_op jit(solution)/shard_map/ppermute | solution.py:522
  53.1 3.8 %copy-start.17 = (bf16[48,384]{1,0:T(8,128)(2,1)}, bf16[48,384]{1,0:T(8,128)(2,1)S(1)}, u32[]{:S(2)}) copy-start(bf16[48,384]{1,0:T(8,128)(2,1)S(1)} %collective-permute-done.4.refs_4_) | copy-start | bytes 110596
  53.1 2.5 %collective-permute-start.8 = (bf16[2,96,2048]{2,1,0:T(8,128)(2,1)}, bf16[2,96,2048]{2,1,0:T(8,128)(2,1)S(1)}, u32[]{:S(2)}, u32[]{:S(2)}) collective-permute-start(bf16[2,96,2048]{2,1,0:T(8,128)(2,1)} %cast_weight.1.refs_8_.refs_0_), channel_id=1, source_target_pairs={{0,8},{8,0},{16,24},{24,16},{1,9},{9,1},{17,25},{25,17},{2,10},{10... | collective-permute-start | bytes 2359304 | tf_op jit(solution)/shard_map/ppermute | solution.py:522
  54.4 2.5 %copy-start.18 = (bf16[48,384]{1,0:T(8,128)(2,1)}, bf16[48,384]{1,0:T(8,128)(2,1)S(1)}, u32[]{:S(2)}) copy-start(bf16[48,384]{1,0:T(8,128)(2,1)S(1)} %collective-permute-done.5.refs_5_) | copy-start | bytes 110596
  54.4 2.6 %copy-start.19 = (bf16[48,384]{1,0:T(8,128)(2,1)}, bf16[48,384]{1,0:T(8,128)(2,1)S(1)}, u32[]{:S(2)}) copy-start(bf16[48,384]{1,0:T(8,128)(2,1)S(1)} %collective-permute-done.6.refs_6_) | copy-start | bytes 110596
  54.4 2.6 %copy-start.20 = (bf16[48,384]{1,0:T(8,128)(2,1)}, bf16[48,384]{1,0:T(8,128)(2,1)S(1)}, u32[]{:S(2)}) copy-start(bf16[48,384]{1,0:T(8,128)(2,1)S(1)} %collective-permute-done.7.refs_7_) | copy-start | bytes 110596
  54.4 2.5 %copy-start.2 = (bf16[2,96,2048]{2,1,0:T(8,128)(2,1)}, bf16[2,96,2048]{2,1,0:T(8,128)(2,1)S(1)}, u32[]{:S(2)}) copy-start(bf16[2,96,2048]{2,1,0:T(8,128)(2,1)S(1)} %collective-permute-done.refs_10_.refs_2_) | copy-start | bytes 2359300
  54.4 2.5 %collective-permute-start.9 = (bf16[2,96,2048]{2,1,0:T(8,128)(2,1)S(1)}, bf16[2,96,2048]{2,1,0:T(8,128)(2,1)}, u32[]{:S(2)}, u32[]{:S(2)}) collective-permute-start(bf16[2,96,2048]{2,1,0:T(8,128)(2,1)S(1)} %collective-permute-done.refs_10_.refs_2_), channel_id=1, source_target_pairs={{0,8},{8,0},{16,24},{24,16},{1,9},{9,1},{17,25},{25,17},{2,10},{10... | collective-permute-start | bytes 2359304 | tf_op jit(solution)/shard_map/ppermute | solution.py:522
  55.6 1.3 %copy-start.3 = (bf16[2,96,2048]{2,1,0:T(8,128)(2,1)}, bf16[2,96,2048]{2,1,0:T(8,128)(2,1)S(1)}, u32[]{:S(2)}) copy-start(bf16[2,96,2048]{2,1,0:T(8,128)(2,1)S(1)} %collective-permute-done.8.refs_9_.refs_1_) | copy-start | bytes 2359300
  62.5 1.1 copy-start.1
  63.7 49.7 %all-to-all-start = ((bf16[8,48,2048]{2,1,0:T(8,128)(2,1)}), bf16[8,48,2048]{2,1,0:T(8,128)(2,1)S(1)}, u32[]{:S(2)}, u32[]{:S(2)}) async-start(bf16[8,48,2048]{2,1,0:T(8,128)(2,1)} %bitcast.13), calls=%async_computation | async-start | bytes 3145728 | tf_op jit(solution)/shard_map/all_to_all | solution.py:528
  72.6 2.5 %collective-permute-start.18 = (bf16[2,96,2048]{2,1,0:T(8,128)(2,1)}, bf16[2,96,2048]{2,1,0:T(8,128)(2,1)S(1)}, u32[]{:S(2)}, u32[]{:S(2)}) collective-permute-start(bf16[2,96,2048]{2,1,0:T(8,128)(2,1)} %get-tuple-element.87), channel_id=1, source_target_pairs={{0,8},{8,0},{16,24},{24,16},{1,9},{9,1},{17,25},{25,17},{2,10},{10... | collective-permute-start | bytes 2359304 | tf_op jit(solution)/shard_map/ppermute | solution.py:522
  72.8 27.7 %collective-permute-start.17 = (bf16[2,96,2048]{2,1,0:T(8,128)(2,1)}, bf16[2,96,2048]{2,1,0:T(8,128)(2,1)S(1)}, u32[]{:S(2)}, u32[]{:S(2)}) collective-permute-start(bf16[2,96,2048]{2,1,0:T(8,128)(2,1)} %get-tuple-element.85), channel_id=1, source_target_pairs={{0,8},{8,0},{16,24},{24,16},{1,9},{9,1},{17,25},{25,17},{2,10},{10... | collective-permute-start | bytes 2359304 | tf_op jit(solution)/shard_map/ppermute | solution.py:522
  75.1 0.9 copy-start.4
  78.2 23.4 %collective-permute-start.19 = (bf16[2,96,2048]{2,1,0:T(8,128)(2,1)}, bf16[2,96,2048]{2,1,0:T(8,128)(2,1)S(1)}, u32[]{:S(2)}, u32[]{:S(2)}) collective-permute-start(bf16[2,96,2048]{2,1,0:T(8,128)(2,1)} %add_parts.1), channel_id=1, source_target_pairs={{0,16},{8,24},{16,0},{24,8},{1,17},{9,25},{17,1},{25,9},{2,18},{10... | collective-permute-start | bytes 2359304 | tf_op jit(solution)/shard_map/ppermute | solution.py:522
  85.5 4.6 %collective-permute-start.10 = (bf16[48,384]{1,0:T(8,128)(2,1)}, bf16[48,384]{1,0:T(8,128)(2,1)S(1)}, u32[]{:S(2)}, u32[]{:S(2)}) collective-permute-start(bf16[48,384]{1,0:T(8,128)(2,1)} %get-tuple-element.74), channel_id=1, source_target_pairs={{0,1},{1,0},{2,3},{3,2},{4,5},{5,4},{6,7},{7,6},{8,9},{9,8},{10,11... | collective-permute-start | bytes 110600 | tf_op jit(solution)/shard_map/ppermute | solution.py:522
  87.4 8.5 %collective-permute-start.11 = (bf16[48,384]{1,0:T(8,128)(2,1)}, bf16[48,384]{1,0:T(8,128)(2,1)S(1)}, u32[]{:S(2)}, u32[]{:S(2)}) collective-permute-start(bf16[48,384]{1,0:T(8,128)(2,1)} %get-tuple-element.75), channel_id=1, source_target_pairs={{0,2},{1,3},{2,0},{3,1},{4,6},{5,7},{6,4},{7,5},{8,10},{9,11},{10,... | collective-permute-start | bytes 110600 | tf_op jit(solution)/shard_map/ppermute | solution.py:522
  88.9 24.4 %collective-permute-start.12 = (bf16[48,384]{1,0:T(8,128)(2,1)}, bf16[48,384]{1,0:T(8,128)(2,1)S(1)}, u32[]{:S(2)}, u32[]{:S(2)}) collective-permute-start(bf16[48,384]{1,0:T(8,128)(2,1)} %get-tuple-element.76), channel_id=1, source_target_pairs={{0,3},{1,2},{2,1},{3,0},{4,7},{5,6},{6,5},{7,4},{8,11},{9,10},{10,... | collective-permute-start | bytes 110600 | tf_op jit(solution)/shard_map/ppermute | solution.py:522
  90.1 23.2 %copy-start.7 = (bf16[48,384]{1,0:T(8,128)(2,1)}, bf16[48,384]{1,0:T(8,128)(2,1)S(1)}, u32[]{:S(2)}) copy-start(bf16[48,384]{1,0:T(8,128)(2,1)S(1)} %collective-permute-done.10.refs_1_) | copy-start | bytes 110596
  90.1 23.3 %collective-permute-start.13 = (bf16[48,384]{1,0:T(8,128)(2,1)}, bf16[48,384]{1,0:T(8,128)(2,1)S(1)}, u32[]{:S(2)}, u32[]{:S(2)}) collective-permute-start(bf16[48,384]{1,0:T(8,128)(2,1)} %get-tuple-element.77), channel_id=1, source_target_pairs={{0,4},{1,5},{2,6},{3,7},{4,0},{5,1},{6,2},{7,3},{8,12},{9,13},{10,... | collective-permute-start | bytes 110600 | tf_op jit(solution)/shard_map/ppermute | solution.py:522
  95.9 17.4 %copy-start.8 = (bf16[48,384]{1,0:T(8,128)(2,1)}, bf16[48,384]{1,0:T(8,128)(2,1)S(1)}, u32[]{:S(2)}) copy-start(bf16[48,384]{1,0:T(8,128)(2,1)S(1)} %collective-permute-done.11.refs_2_) | copy-start | bytes 110596
  95.9 17.4 %collective-permute-start.14 = (bf16[48,384]{1,0:T(8,128)(2,1)}, bf16[48,384]{1,0:T(8,128)(2,1)S(1)}, u32[]{:S(2)}, u32[]{:S(2)}) collective-permute-start(bf16[48,384]{1,0:T(8,128)(2,1)} %get-tuple-element.78), channel_id=1, source_target_pairs={{0,5},{1,4},{2,7},{3,6},{4,1},{5,0},{6,3},{7,2},{8,13},{9,12},{10,... | collective-permute-start | bytes 110600 | tf_op jit(solution)/shard_map/ppermute | solution.py:522
  100.4 5.4 %copy-start.5 = (bf16[2,96,2048]{2,1,0:T(8,128)(2,1)}, bf16[2,96,2048]{2,1,0:T(8,128)(2,1)S(1)}, u32[]{:S(2)}) copy-start(bf16[2,96,2048]{2,1,0:T(8,128)(2,1)S(1)} %collective-permute-done.17.refs_1_) | copy-start | bytes 2359300
  100.4 12.9 %collective-permute-start.15 = (bf16[48,384]{1,0:T(8,128)(2,1)}, bf16[48,384]{1,0:T(8,128)(2,1)S(1)}, u32[]{:S(2)}, u32[]{:S(2)}) collective-permute-start(bf16[48,384]{1,0:T(8,128)(2,1)} %get-tuple-element.79), channel_id=1, source_target_pairs={{0,6},{1,7},{2,4},{3,5},{4,2},{5,3},{6,0},{7,1},{8,14},{9,15},{10,... | collective-permute-start | bytes 110600 | tf_op jit(solution)/shard_map/ppermute | solution.py:522
  101.6 4.2 %copy-start.6 = (bf16[2,96,2048]{2,1,0:T(8,128)(2,1)}, bf16[2,96,2048]{2,1,0:T(8,128)(2,1)S(1)}, u32[]{:S(2)}) copy-start(bf16[2,96,2048]{2,1,0:T(8,128)(2,1)S(1)} %collective-permute-done.19.refs_2_) | copy-start | bytes 2359300
  101.6 11.8 %collective-permute-start.16 = (bf16[48,384]{1,0:T(8,128)(2,1)}, bf16[48,384]{1,0:T(8,128)(2,1)S(1)}, u32[]{:S(2)}, u32[]{:S(2)}) collective-permute-start(bf16[48,384]{1,0:T(8,128)(2,1)} %get-tuple-element.80), channel_id=1, source_target_pairs={{0,7},{1,6},{2,5},{3,4},{4,3},{5,2},{6,1},{7,0},{8,15},{9,14},{10,... | collective-permute-start | bytes 110600 | tf_op jit(solution)/shard_map/ppermute | solution.py:522
  113.3 0.6 copy-start.9
  113.3 0.6 copy-start.10
  113.4 0.6 copy-start.11
  113.4 0.6 copy-start.12
  113.4 0.6 copy-start.13
  113.4 1.2 copy-start

commit v7 on v4

--- a/solution.py
+++ b/solution.py
@@ -30,7 +30,14 @@
     return pltpu.CompilerParams(vmem_limit_bytes=VMEM_LIMIT)
 
 
-def row_targets(route_row, placement_row, capacity):
+def order_of(device, groups):
+    if groups % 2:
+        return device
+    half = groups // 2
+    return device % half * 2 + device // half
+
+
+def row_targets(route_row, placement_row, capacity, groups):
     expert_count = placement_row.shape[1]
     row_count = route_row.shape[1]
     diagonal = lax.broadcasted_iota(jnp.int32, (expert_count, expert_count), 0) == (
@@ -45,7 +52,9 @@
     before = (earlier < later).astype(F32).astype(BF16)
     position = jnp.dot(hot.astype(BF16), before, preferred_element_type=F32)
     slot = lax.broadcasted_iota(jnp.int32, (expert_count, row_count), 0)
-    start = (slot * capacity).astype(F32)
+    local_count = expert_count // groups
+    order = order_of(slot // local_count, groups)
+    start = ((order * local_count + slot % local_count) * capacity).astype(F32)
     return jnp.sum(hot * (start + position), axis=0, keepdims=True).astype(jnp.int32)
 
 
@@ -55,7 +64,7 @@
 
 
 def dispatch_kernel(
-    capacity, route_hbm, placement_hbm, x_hbm, g_hbm, sent_hbm, target_hbm,
+    capacity, groups, route_hbm, placement_hbm, x_hbm, g_hbm, sent_hbm, target_hbm,
     route_ref, placement_ref, target_ref, x_ref, g_ref, sent_ref, key_sems, in_sems, out_sems,
 ):
     tiles, _, tile = g_ref.shape
@@ -75,7 +84,7 @@
         load.start()
     for load in keys:
         load.wait()
-    target = row_targets(route_ref[...], placement_ref[...], capacity)
+    target = row_targets(route_ref[...], placement_ref[...], capacity, groups)
     target_ref[...] = target
     stores = [pltpu.make_async_copy(target_ref, target_hbm, key_sems.at[2])]
     stores[0].start()
@@ -94,7 +103,7 @@
         store.wait()
 
 
-def dispatch(route, placement, x_rows, y_cot, capacity):
+def dispatch(route, placement, x_rows, y_cot, capacity, groups):
     row_count, hidden = x_rows.shape
     width = y_cot.shape[1]
     expert_count = placement.shape[0]
@@ -103,7 +112,7 @@
     places = expert_count * capacity
     hbm = pl.BlockSpec(memory_space=pl.ANY)
     return pl.pallas_call(
-        functools.partial(dispatch_kernel, capacity),
+        functools.partial(dispatch_kernel, capacity, groups),
         in_specs=[hbm, hbm, hbm, hbm],
         out_specs=(hbm, hbm),
         out_shape=(
@@ -228,60 +237,58 @@
     return jnp.concatenate([jnp.where(member == e, x, zero) for e in range(local_count)], axis=1)
 
 
-def products_kernel(capacity, pieces, local_hbm, *refs):
-    w_hbm, out_hbm = refs[:pieces], refs[pieces]
-    x_ref, g_ref, w_ref, out_ref, x_sem, g_sems, w_sems, out_sems = refs[pieces + 1 :]
-    tiles, local_count, _, _, tile = w_ref.shape
-    total, hidden = x_ref.shape
-    width = tiles * tile
-    here = lax.axis_index("rep") if pieces > 1 else 0
-    x_load = pltpu.make_async_copy(local_hbm.at[:, pl.ds(width, hidden)], x_ref, x_sem)
-    x_load.start()
-    loads = []
-    for j in range(tiles):
-        span = pl.ds(j * tile, tile)
-        loads.append([])
-        for i, piece in enumerate(w_hbm):
-            owner = jnp.bitwise_xor(here, i) if pieces > 1 else 0
-            for e in range(local_count):
-                loads[j].append(
-                    pltpu.make_async_copy(
-                        piece.at[e, :, span], w_ref.at[j, e, owner], w_sems.at[j, i, e]
-                    )
-                )
-        loads[j].append(
-            pltpu.make_async_copy(local_hbm.at[:, span], g_ref.at[j], g_sems.at[j])
-        )
-        for load in loads[j]:
-            load.start()
-    x_load.wait()
-    wide = spread(x_ref[...], capacity, local_count)
-    sums = None
-    stores = []
-    for j in range(tiles):
-        span = pl.ds(j * tile, tile)
-        for load in loads[j]:
-            load.wait()
-        weight = w_ref[j].reshape(local_count * hidden, tile)
-        out_ref[:, span] = jnp.dot(wide, weight, preferred_element_type=F32).astype(BF16)
-        store = pltpu.make_async_copy(out_ref.at[:, span], out_hbm.at[:, span], out_sems.at[j])
-        store.start()
-        stores.append(store)
-        part = lax.dot_general(
-            g_ref[j], weight, (((1,), (1,)), ((), ())), preferred_element_type=F32
-        )
-        sums = part if sums is None else sums + part
-    member = member_rows(total, capacity, local_count)
-    picked = sums[:, :hidden]
-    for e in range(1, local_count):
-        picked = jnp.where(member == e, sums[:, e * hidden : (e + 1) * hidden], picked)
-    span = pl.ds(width, hidden)
-    out_ref[:, span] = picked.astype(BF16)
-    store = pltpu.make_async_copy(out_ref.at[:, span], out_hbm.at[:, span], out_sems.at[tiles])
-    store.start()
-    stores.append(store)
-    for store in stores:
-        store.wait()
+def join_weight(piece_refs, joined_ref):
+    local_count, rows, width = piece_refs[0].shape
+    if len(piece_refs) == 1:
+        return piece_refs[0][...].reshape(local_count * rows, width)
+    here = lax.axis_index("rep")
+    for i, ref in enumerate(piece_refs):
+        owner = jnp.bitwise_xor(here, i)
+        for e in range(local_count):
+            joined_ref[e, owner] = ref[e]
+    return joined_ref[...].reshape(local_count * len(piece_refs) * rows, width)
+
+
+def products_kernel(capacity, local_count, pieces, g_ref, *refs):
+    w_refs = refs[:pieces]
+    x_refs, out_hbm = refs[pieces:-6], refs[-6]
+    joined_ref, wide_ref, total_ref, out_ref, out_sems = refs[-5:]
+    step = pl.program_id(0)
+    steps = out_sems.shape[0] - 1
+    tile = g_ref.shape[1]
+    hidden = wide_ref.shape[1] // local_count
+    columns = pl.ds(pl.multiple_of(step * tile, tile), tile)
+
+    @pl.when(step == 0)
+    def _():
+        wide_ref[...] = spread(read_columns(x_refs), capacity, local_count)
+        total_ref[...] = jnp.zeros_like(total_ref)
+
+    weight = join_weight(w_refs, joined_ref)
+    out_ref[:, columns] = jnp.dot(
+        wide_ref[...], weight, preferred_element_type=F32
+    ).astype(BF16)
+    pltpu.make_async_copy(
+        out_ref.at[:, columns], out_hbm.at[:, columns], out_sems.at[step]
+    ).start()
+    total_ref[...] += lax.dot_general(
+        g_ref[...], weight, (((1,), (1,)), ((), ())), preferred_element_type=F32
+    )
+
+    @pl.when(step == steps - 1)
+    def _():
+        member = member_rows(total_ref.shape[0], capacity, local_count)
+        picked = total_ref[:, :hidden]
+        for e in range(1, local_count):
+            picked = jnp.where(member == e, total_ref[:, e * hidden : (e + 1) * hidden], picked)
+        last = pl.ds(steps * tile, hidden)
+        out_ref[:, last] = picked.astype(BF16)
+        final = pltpu.make_async_copy(out_ref.at[:, last], out_hbm.at[:, last], out_sems.at[steps])
+        final.start()
+        for j in range(steps):
+            span = pl.ds(j * tile, tile)
+            pltpu.make_async_copy(out_ref.at[:, span], out_hbm.at[:, span], out_sems.at[j]).wait()
+        final.wait()
 
 
 def products(local, weight, capacity):
@@ -291,29 +298,31 @@
     total = local.shape[0]
     tile = min(width, 512)
     tiles = width // tile
-    hbm = pl.BlockSpec(memory_space=pl.ANY)
+    specs = hidden_specs(total, hidden, width)
     return pl.pallas_call(
-        functools.partial(products_kernel, capacity, pieces),
-        in_specs=[hbm] * (1 + pieces),
-        out_specs=hbm,
+        functools.partial(products_kernel, capacity, local_count, pieces),
+        grid=(tiles,),
+        in_specs=[pl.BlockSpec((total, tile), lambda j: (0, j))]
+        + [pl.BlockSpec((local_count, slice_rows, tile), lambda j: (0, 0, j))] * pieces
+        + specs,
+        out_specs=pl.BlockSpec(memory_space=pl.ANY),
         out_shape=jax.ShapeDtypeStruct(local.shape, BF16),
         scratch_shapes=[
-            pltpu.VMEM((total, hidden), BF16),
-            pltpu.VMEM((tiles, total, tile), BF16),
-            pltpu.VMEM((tiles, local_count, pieces, slice_rows, tile), BF16),
+            pltpu.VMEM((local_count, pieces, slice_rows, tile), BF16),
+            pltpu.VMEM((total, local_count * hidden), BF16),
+            pltpu.VMEM((total, local_count * hidden), F32),
             pltpu.VMEM(local.shape, BF16),
-            pltpu.SemaphoreType.DMA,
-            pltpu.SemaphoreType.DMA((tiles,)),
-            pltpu.SemaphoreType.DMA((tiles, pieces, local_count)),
             pltpu.SemaphoreType.DMA((tiles + 1,)),
         ],
-        compiler_params=pltpu.CompilerParams(vmem_limit_bytes=LARGE_LIMIT),
+        compiler_params=pltpu.CompilerParams(
+            vmem_limit_bytes=LARGE_LIMIT, dimension_semantics=("arbitrary",)
+        ),
         cost_estimate=cost(
             4 * total * local_count * hidden * width,
             2 * (local_count * hidden + 2 * total) * width,
         ),
         name="products",
-    )(local, *weight)
+    )(local, *weight, *([local] * len(specs)))
 
 
 def gradient_kernel(capacity, local_count, parts, factor, g_ref, *refs):
@@ -355,7 +364,9 @@
         out_specs=(pl.BlockSpec((local_count, slice_rows, tile), lambda j: (0, 0, j)),) * parts,
         out_shape=(jax.ShapeDtypeStruct((local_count, slice_rows, width), BF16),) * parts,
         scratch_shapes=split + [pltpu.VMEM((total, local_count * hidden), BF16)],
-        compiler_params=params("arbitrary"),
+        compiler_params=pltpu.CompilerParams(
+            vmem_limit_bytes=LARGE_LIMIT, dimension_semantics=("arbitrary",)
+        ),
         cost_estimate=cost(
             2 * total * local_count * hidden * width,
             2 * (local_count * hidden + total) * width,
@@ -480,7 +491,10 @@
 def exchange(buffer, groups):
     places, width = buffer.shape
     parts = buffer.reshape(groups, places // groups, width)
-    moved = lax.all_to_all(parts, "grp", split_axis=0, concat_axis=0, tiled=True)
+    members = sorted(range(groups), key=lambda device: order_of(device, groups))
+    moved = lax.all_to_all(
+        parts, "grp", split_axis=0, concat_axis=0, tiled=True, axis_index_groups=[members]
+    )
     return moved.reshape(places, width)
 
 
@@ -509,7 +523,7 @@
     grad_factor = float(row_count * groups * replicas // expert_count) ** (-0.5)
     capacity = max(2, (3 * row_count + 2 * expert_count - 1) // (2 * expert_count))
     places = expert_count * capacity
-    sent, target = dispatch(route, placement, x_rows, y_cot, capacity)
+    sent, target = dispatch(route, placement, x_rows, y_cot, capacity, groups)
     local = exchange(sent, groups)
     early_master, target = lax.optimization_barrier((master_weight, target))
     weight = gather_weight(cast_weight(early_master), replicas)

time: 114 us -> 111 us (0.974); the launches traced: 114 us -> 109 us
  waiting for transfers between devices: 70 us -> 61.6 us
  starting transfers between devices: 15.6 us -> 17.9 us
    all_to_all x2, waiting for transfers between devices: 32.2 us -> 23.3 us  [exchange(): lax.all_to_all(parts, 'grp', split_axis=0, concat_axis=0, tiled=True, axi...]
    all_to_all x2, starting transfers between devices: 11.8 us -> 14.2 us  [exchange(): lax.all_to_all(parts, 'grp', split_axis=0, concat_axis=0, tiled=True, axi...]
    pallas_call x1, Pallas kernels: 3.52 us -> 5.64 us  [gradient(): pl.pallas_call(functools.partial(gradient_kernel, capacity, local_count,...]
    unnamed x22 -> x26, local copies, waits for them, and re-layouts: 3.05 us -> 3.68 us
  transfers between devices with their start and end apart: 8 -> 8, of which waited for: 6 -> 6; matrix products, arithmetic and copies ran while one was open for 0% -> 0% of each run, Pallas kernels for 9% -> 12%
where the time goes in v7:
time: 111 us; the launch traced here: 109 us
  waiting for transfers between devices  61.6 us (55%)
  Pallas kernels  25.2 us (23%)
  starting transfers between devices  17.9 us (16%)
  local copies, waits for them, and re-layouts  3.68 us (3%)
    ppermute x6, waiting for transfers between devices, swap(): return lax.ppermute(array, axis, [(i, i ^ offset) for i in range(size)])  38.2 us
    all_to_all x2, waiting for transfers between devices, exchange(): lax.all_to_all(parts, 'grp', split_axis=0, concat_axis=0, tiled=True, axi...  23.3 us
    all_to_all x2, starting transfers between devices, exchange(): lax.all_to_all(parts, 'grp', split_axis=0, concat_axis=0, tiled=True, axi...  14.2 us
    pallas_call x1, Pallas kernels, products(): pl.pallas_call(functools.partial(products_kernel, capacity, local_count,...  6.63 us
    pallas_call x1, Pallas kernels, adam(): pl.pallas_call(functools.partial(adam_kernel, len(grads)), grid=(members,...  6.19 us
    pallas_call x1, Pallas kernels, gradient(): pl.pallas_call(functools.partial(gradient_kernel, capacity, local_count,...  5.64 us
    ppermute x6, starting transfers between devices, swap(): return lax.ppermute(array, axis, [(i, i ^ offset) for i in range(size)])  3.7 us
    unnamed x26, local copies, waits for them, and re-layouts  3.68 us
  transfers between devices with their start and end apart: 8, of which 6 were waited for; matrix products, arithmetic and copies ran while one was open for 0% of the time, Pallas kernels for 12%

profile of v7, /device:TPU:0, one launch (start us, length us, event | category | flops | bytes accessed | tf_op | source)
XLA Modules:
  0.0 109.1 jit_solution(14928014618477372534)
XLA Ops:
  0.6 3.5 %dispatch.1 = (bf16[384,2432]{1,0:T(8,128)(2,1)}, s32[1,256]{1,0:T(1,128)}) custom-call(s32[1,256]{1,0:T(1,128)} %bitcast.17, s32[1,16]{1,0:T(1,128)} %bitcast.18, bf16[256,384]{1,0:T(8,128)(2,1)} %x_hbm.1, bf16[256,2048]{1,0:T(8,128)(2,1)} %g_hbm.1), custom_call_target="tpu_custom_call" | custom-call | flops 478150656 | bytes 3112960 | tf_op jit(solution)/shard_map/dispatch/pallas_call | solution.py:114
  4.1 0.0 copy-start
  4.1 7.4 %all-to-all-start = ((bf16[8,48,2432]{2,1,0:T(8,128)(2,1)}), bf16[8,48,2432]{2,1,0:T(8,128)(2,1)}, u32[]{:S(2)}, u32[]{:S(2)}) async-start(bf16[8,48,2432]{2,1,0:T(8,128)(2,1)} %bitcast.14), calls=%async_computation | async-start | bytes 3735552 | tf_op jit(solution)/shard_map/all_to_all | solution.py:495
  11.5 0.0 copy-done
  11.5 0.3 cast_weight.1.refs_0_
  11.9 0.0 copy-start.1
  11.9 1.6 %collective-permute-start.1 = (bf16[2,96,2048]{2,1,0:T(8,128)(2,1)S(1)}, bf16[2,96,2048]{2,1,0:T(8,128)(2,1)S(1)}, u32[]{:S(2)}, u32[]{:S(2)}) collective-permute-start(bf16[2,96,2048]{2,1,0:T(8,128)(2,1)S(1)} %cast_weight.1.refs_0_), channel_id=1, source_target_pairs={{0,16},{8,24},{16,0},{24,8},{1,17},{9,25},{17,1},{25,9},{2,18},{10... | collective-permute-start | bytes 2359304 | tf_op jit(solution)/shard_map/ppermute | solution.py:488
  13.5 0.0 collective-permute-start
  13.5 17.5 %collective-permute-done.1.refs_2_ = bf16[2,96,2048]{2,1,0:T(8,128)(2,1)S(1)} collective-permute-done((bf16[2,96,2048]{2,1,0:T(8,128)(2,1)S(1)}, bf16[2,96,2048]{2,1,0:T(8,128)(2,1)S(1)}, u32[]{:S(2)}, u32[]{:S(2)}) %collective-permute-start.1) | collective-permute-done | bytes 786464 | tf_op jit(solution)/shard_map/ppermute | solution.py:488
  30.9 0.0 copy-start.11
  30.9 0.0 collective-permute-start.2
  30.9 0.0 collective-permute-done.refs_1_
  30.9 0.0 copy-start.12
  31.0 0.9 copy-done.12
  31.9 1.5 %collective-permute-done.2.refs_3_ = bf16[2,96,2048]{2,1,0:T(8,128)(2,1)} collective-permute-done((bf16[2,96,2048]{2,1,0:T(8,128)(2,1)S(1)}, bf16[2,96,2048]{2,1,0:T(8,128)(2,1)}, u32[]{:S(2)}, u32[]{:S(2)}) %collective-permute-start.2) | collective-permute-done | bytes 786464 | tf_op jit(solution)/shard_map/ppermute | solution.py:488
  33.4 18.5 %all-to-all-done = bf16[8,48,2432]{2,1,0:T(8,128)(2,1)} async-done(((bf16[8,48,2432]{2,1,0:T(8,128)(2,1)}), bf16[8,48,2432]{2,1,0:T(8,128)(2,1)}, u32[]{:S(2)}, u32[]{:S(2)}) %all-to-all-start) | async-done | bytes 1867808 | tf_op jit(solution)/shard_map/all_to_all | solution.py:495
  51.9 0.0 copy-done.1
  51.9 0.0 copy-done.11
  51.9 6.6 %products.1 = bf16[384,2432]{1,0:T(8,128)(2,1)} custom-call(bf16[384,2432]{1,0:T(8,128)(2,1)} %bitcast.3.g_ref.refs_4_.refs_5_.refs_6_.refs_0_.refs_1_.refs_2_, bf16[2,96,2048]{2,1,0:T(8,128)(2,1)} %copy-done.1, bf16[2,96,2048]{2,1,0:T(8,128)(2,1)} %copy-done.12, bf16[2,96,2048]{2,1,0:T(8,128)(2,1)} %copy-done.11, ...), custom_call_target="tpu_custom_call" | custom-call | flops 2415919104 | bytes 6291456 | tf_op jit(solution)/shard_map/products/pallas_call | solution.py:302
  58.5 6.8 %all-to-all-start.1 = ((bf16[8,48,2432]{2,1,0:T(8,128)(2,1)}), bf16[8,48,2432]{2,1,0:T(8,128)(2,1)S(1)}, u32[]{:S(2)}, u32[]{:S(2)}) async-start(bf16[8,48,2432]{2,1,0:T(8,128)(2,1)} %bitcast.13), calls=%async_computation.1 | async-start | bytes 3735552 | tf_op jit(solution)/shard_map/all_to_all | solution.py:495
  65.3 0.0 copy-start.3
  65.3 0.0 copy-start.4
  65.3 0.0 copy-start.8
  65.3 0.0 copy-start.9
  65.4 5.6 %gradient.1 = (bf16[2,96,2048]{2,1,0:T(8,128)(2,1)}, bf16[2,96,2048]{2,1,0:T(8,128)(2,1)}, bf16[2,96,2048]{2,1,0:T(8,128)(2,1)}, bf16[2,96,2048]{2,1,0:T(8,128)(2,1)}) custom-call(bf16[384,2432]{1,0:T(8,128)(2,1)} %bitcast.3.g_ref.refs_4_.refs_5_.refs_6_.refs_0_.refs_1_.refs_2_, ...), custom_call_target="tpu_custom_call" | custom-call | flops 1207959552 | bytes 4718592 | tf_op jit(solution)/shard_map/gradient/pallas_call | solution.py:360
  71.0 0.0 copy-start.10
  71.0 0.0 collective-permute-start.4
  71.0 0.5 collective-permute-start.3
  71.5 2.0 %collective-permute-done.4.b_ref = bf16[2,96,2048]{2,1,0:T(8,128)(2,1)S(1)} collective-permute-done((bf16[2,96,2048]{2,1,0:T(8,128)(2,1)}, bf16[2,96,2048]{2,1,0:T(8,128)(2,1)S(1)}, u32[]{:S(2)}, u32[]{:S(2)}) %collective-permute-start.4) | collective-permute-done | bytes 786464 | tf_op jit(solution)/shard_map/ppermute | solution.py:488
  73.5 0.0 copy-start.2
  73.5 1.1 %copy-done.2 = bf16[2,96,2048]{2,1,0:T(8,128)(2,1)S(1)} copy-done((bf16[2,96,2048]{2,1,0:T(8,128)(2,1)S(1)}, bf16[2,96,2048]{2,1,0:T(8,128)(2,1)}, u32[]{:S(2)}) %copy-start.2) | copy-done | bytes 786456
  74.7 0.0 copy-start.5
  74.7 0.4 add_parts.1
  75.1 1.6 %collective-permute-start.5 = (bf16[2,96,2048]{2,1,0:T(8,128)(2,1)S(1)}, bf16[2,96,2048]{2,1,0:T(8,128)(2,1)S(1)}, u32[]{:S(2)}, u32[]{:S(2)}) collective-permute-start(bf16[2,96,2048]{2,1,0:T(8,128)(2,1)S(1)} %add_parts.1), channel_id=1, source_target_pairs={{0,16},{8,24},{16,0},{24,8},{1,17},{9,25},{17,1},{25,9},{2,18},{10... | collective-permute-start | bytes 2359304 | tf_op jit(solution)/shard_map/ppermute | solution.py:488
  76.6 0.0 copy-done.10
  76.6 0.1 home_places.1.places_ref
  76.8 0.0 copy-start.6
  76.8 0.7 copy-done.6
  77.5 0.0 collective-permute-done.3.refs_1_
  77.5 17.2 %collective-permute-done.5.refs_2_ = bf16[2,96,2048]{2,1,0:T(8,128)(2,1)S(1)} collective-permute-done((bf16[2,96,2048]{2,1,0:T(8,128)(2,1)S(1)}, bf16[2,96,2048]{2,1,0:T(8,128)(2,1)S(1)}, u32[]{:S(2)}, u32[]{:S(2)}) %collective-permute-start.5) | collective-permute-done | bytes 786464 | tf_op jit(solution)/shard_map/ppermute | solution.py:488
  94.7 0.0 copy-done.3
  94.7 0.0 copy-done.4
  94.7 0.0 copy-done.8
  94.7 0.0 copy-done.9
  94.7 0.0 copy-done.5
  94.7 6.2 %adam.1 = (f32[2,96,2048]{2,1,0:T(8,128)}, bf16[2,96,2048]{2,1,0:T(8,128)(2,1)}, f32[2,16,96]{2,1,0:T(8,128)}, bf16[2,96,2048]{2,1,0:T(8,128)(2,1)}, f32[2,16,96]{2,1,0:T(8,128)}) custom-call(f32[2,96,2048]{2,1,0:T(8,128)S(1)} %copy-done, bf16[2,96,2048]{2,1,0:T(8,128)(2,1)S(1)} %copy-done.3, f32[2,16,96]{2,1,0:T(8,128)S(1)} %bitcast.11, ...), custom_call_target="tpu_custom_call" | custom-call | flops 15728640 | bytes 7077888 | tf_op jit(solution)/shard_map/adam/pallas_call | solution.py:461
  100.9 4.8 %all-to-all-done.1 = bf16[8,48,2432]{2,1,0:T(8,128)(2,1)S(1)} async-done(((bf16[8,48,2432]{2,1,0:T(8,128)(2,1)}), bf16[8,48,2432]{2,1,0:T(8,128)(2,1)S(1)}, u32[]{:S(2)}, u32[]{:S(2)}) %all-to-all-start.1) | async-done | bytes 1867808 | tf_op jit(solution)/shard_map/all_to_all | solution.py:495
  105.7 0.0 copy-start.7
  105.7 0.9 copy-done.7
  106.7 2.4 %collect.1 = (bf16[256,2048]{1,0:T(8,128)(2,1)}, bf16[256,384]{1,0:T(8,128)(2,1)}) custom-call(bf16[256,384]{1,0:T(8,128)(2,1)S(1)} %copy-done.7, bf16[384,2432]{1,0:T(8,128)(2,1)S(1)} %bitcast.10), custom_call_target="tpu_custom_call" | custom-call | flops 478150656 | bytes 3112960 | tf_op jit(solution)/shard_map/collect/pallas_call | solution.py:206
Async XLA Ops:
  4.1 7.4 %copy-start = (f32[2,96,2048]{2,1,0:T(8,128)S(1)}, f32[2,96,2048]{2,1,0:T(8,128)}, u32[]{:S(2)}) copy-start(f32[2,96,2048]{2,1,0:T(8,128)} %master_ref.1) | copy-start | bytes 4718596
  4.1 47.8 %all-to-all-start = ((bf16[8,48,2432]{2,1,0:T(8,128)(2,1)}), bf16[8,48,2432]{2,1,0:T(8,128)(2,1)}, u32[]{:S(2)}, u32[]{:S(2)}) async-start(bf16[8,48,2432]{2,1,0:T(8,128)(2,1)} %bitcast.14), calls=%async_computation | async-start | bytes 3735552 | tf_op jit(solution)/shard_map/all_to_all | solution.py:495
  11.9 40.0 %copy-start.1 = (bf16[2,96,2048]{2,1,0:T(8,128)(2,1)}, bf16[2,96,2048]{2,1,0:T(8,128)(2,1)S(1)}, u32[]{:S(2)}) copy-start(bf16[2,96,2048]{2,1,0:T(8,128)(2,1)S(1)} %cast_weight.1.refs_0_) | copy-start | bytes 2359300
  11.9 19.1 %collective-permute-start.1 = (bf16[2,96,2048]{2,1,0:T(8,128)(2,1)S(1)}, bf16[2,96,2048]{2,1,0:T(8,128)(2,1)S(1)}, u32[]{:S(2)}, u32[]{:S(2)}) collective-permute-start(bf16[2,96,2048]{2,1,0:T(8,128)(2,1)S(1)} %cast_weight.1.refs_0_), channel_id=1, source_target_pairs={{0,16},{8,24},{16,0},{24,8},{1,17},{9,25},{17,1},{25,9},{2,18},{10... | collective-permute-start | bytes 2359304 | tf_op jit(solution)/shard_map/ppermute | solution.py:488
  13.5 17.5 %collective-permute-start = (bf16[2,96,2048]{2,1,0:T(8,128)(2,1)S(1)}, bf16[2,96,2048]{2,1,0:T(8,128)(2,1)S(1)}, u32[]{:S(2)}, u32[]{:S(2)}) collective-permute-start(bf16[2,96,2048]{2,1,0:T(8,128)(2,1)S(1)} %cast_weight.1.refs_0_), channel_id=1, source_target_pairs={{0,8},{8,0},{16,24},{24,16},{1,9},{9,1},{17,25},{25,17},{2,10},{10... | collective-permute-start | bytes 2359304 | tf_op jit(solution)/shard_map/ppermute | solution.py:488
  30.9 20.9 %copy-start.11 = (bf16[2,96,2048]{2,1,0:T(8,128)(2,1)}, bf16[2,96,2048]{2,1,0:T(8,128)(2,1)S(1)}, u32[]{:S(2)}) copy-start(bf16[2,96,2048]{2,1,0:T(8,128)(2,1)S(1)} %collective-permute-done.1.refs_2_) | copy-start | bytes 2359300
  30.9 2.4 %collective-permute-start.2 = (bf16[2,96,2048]{2,1,0:T(8,128)(2,1)S(1)}, bf16[2,96,2048]{2,1,0:T(8,128)(2,1)}, u32[]{:S(2)}, u32[]{:S(2)}) collective-permute-start(bf16[2,96,2048]{2,1,0:T(8,128)(2,1)S(1)} %collective-permute-done.1.refs_2_), channel_id=1, source_target_pairs={{0,8},{8,0},{16,24},{24,16},{1,9},{9,1},{17,25},{25,17},{2,10},{10... | collective-permute-start | bytes 2359304 | tf_op jit(solution)/shard_map/ppermute | solution.py:488
  30.9 0.9 copy-start.12
  58.5 47.2 %all-to-all-start.1 = ((bf16[8,48,2432]{2,1,0:T(8,128)(2,1)}), bf16[8,48,2432]{2,1,0:T(8,128)(2,1)S(1)}, u32[]{:S(2)}, u32[]{:S(2)}) async-start(bf16[8,48,2432]{2,1,0:T(8,128)(2,1)} %bitcast.13), calls=%async_computation.1 | async-start | bytes 3735552 | tf_op jit(solution)/shard_map/all_to_all | solution.py:495
  65.3 29.4 %copy-start.3 = (bf16[2,96,2048]{2,1,0:T(8,128)(2,1)S(1)}, bf16[2,96,2048]{2,1,0:T(8,128)(2,1)}, u32[]{:S(2)}) copy-start(bf16[2,96,2048]{2,1,0:T(8,128)(2,1)} %mc_ref.1) | copy-start | bytes 2359300
  65.3 29.4 %copy-start.4 = (bf16[2,96,2048]{2,1,0:T(8,128)(2,1)S(1)}, bf16[2,96,2048]{2,1,0:T(8,128)(2,1)}, u32[]{:S(2)}) copy-start(bf16[2,96,2048]{2,1,0:T(8,128)(2,1)} %vc_ref.1) | copy-start | bytes 2359300
  65.3 29.4 %copy-start.8 = (f32[2,96,16]{1,2,0:T(8,128)S(1)}, f32[2,96,16]{1,2,0:T(8,128)}, u32[]{:S(2)}) copy-start(f32[2,96,16]{1,2,0:T(8,128)} %param.11) | copy-start | bytes 36868
  65.3 29.4 %copy-start.9 = (f32[2,96,16]{1,2,0:T(8,128)S(1)}, f32[2,96,16]{1,2,0:T(8,128)}, u32[]{:S(2)}) copy-start(f32[2,96,16]{1,2,0:T(8,128)} %param.13) | copy-start | bytes 36868
  71.0 5.6 %copy-start.10 = (s32[1,256]{1,0:T(1,128)S(1)}, s32[1,256]{1,0:T(1,128)}, u32[]{:S(2)}) copy-start(s32[1,256]{1,0:T(1,128)} %get-tuple-element.25.target_ref) | copy-start | bytes 3076
  71.0 2.5 %collective-permute-start.4 = (bf16[2,96,2048]{2,1,0:T(8,128)(2,1)}, bf16[2,96,2048]{2,1,0:T(8,128)(2,1)S(1)}, u32[]{:S(2)}, u32[]{:S(2)}) collective-permute-start(bf16[2,96,2048]{2,1,0:T(8,128)(2,1)} %get-tuple-element.35), channel_id=1, source_target_pairs={{0,8},{8,0},{16,24},{24,16},{1,9},{9,1},{17,25},{25,17},{2,10},{10... | collective-permute-start | bytes 2359304 | tf_op jit(solution)/shard_map/ppermute | solution.py:488
  71.0 6.4 %collective-permute-start.3 = (bf16[2,96,2048]{2,1,0:T(8,128)(2,1)}, bf16[2,96,2048]{2,1,0:T(8,128)(2,1)S(1)}, u32[]{:S(2)}, u32[]{:S(2)}) collective-permute-start(bf16[2,96,2048]{2,1,0:T(8,128)(2,1)} %get-tuple-element.33), channel_id=1, source_target_pairs={{0,8},{8,0},{16,24},{24,16},{1,9},{9,1},{17,25},{25,17},{2,10},{10... | collective-permute-start | bytes 2359304 | tf_op jit(solution)/shard_map/ppermute | solution.py:488
  73.5 1.1 %copy-start.2 = (bf16[2,96,2048]{2,1,0:T(8,128)(2,1)S(1)}, bf16[2,96,2048]{2,1,0:T(8,128)(2,1)}, u32[]{:S(2)}) copy-start(bf16[2,96,2048]{2,1,0:T(8,128)(2,1)} %get-tuple-element.34.a_ref) | copy-start | bytes 2359300
  74.7 20.1 %copy-start.5 = (bf16[2,96,2048]{2,1,0:T(8,128)(2,1)S(1)}, bf16[2,96,2048]{2,1,0:T(8,128)(2,1)}, u32[]{:S(2)}) copy-start(bf16[2,96,2048]{2,1,0:T(8,128)(2,1)} %get-tuple-element.32.refs_0_) | copy-start | bytes 2359300
  75.1 19.6 %collective-permute-start.5 = (bf16[2,96,2048]{2,1,0:T(8,128)(2,1)S(1)}, bf16[2,96,2048]{2,1,0:T(8,128)(2,1)S(1)}, u32[]{:S(2)}, u32[]{:S(2)}) collective-permute-start(bf16[2,96,2048]{2,1,0:T(8,128)(2,1)S(1)} %add_parts.1), channel_id=1, source_target_pairs={{0,16},{8,24},{16,0},{24,8},{1,17},{9,25},{17,1},{25,9},{2,18},{10... | collective-permute-start | bytes 2359304 | tf_op jit(solution)/shard_map/ppermute | solution.py:488
  76.8 0.7 copy-start.6
  105.7 0.9 copy-start.7

commit v8 on v7

--- a/solution.py
+++ b/solution.py
@@ -154,19 +154,9 @@
     )(target)
 
 
-def hidden_specs(rows, hidden, width):
-    return [
-        pl.BlockSpec((rows, BLOCK), functools.partial(lambda k, j: (0, k), width // BLOCK + i))
-        for i in range(hidden // BLOCK)
-    ]
-
-
-def read_columns(refs):
-    return jnp.concatenate([ref[...] for ref in refs], axis=1)
-
-
 def collect_kernel(
-    places_ref, home_hbm, y_hbm, dx_hbm, home_ref, y_ref, dx_ref, in_sems, out_sems
+    places_hbm, home_hbm, y_hbm, dx_hbm,
+    places_ref, home_ref, y_ref, dx_ref, places_sem, in_sems, out_sems,
 ):
     hidden = dx_ref.shape[1]
     width = y_ref.shape[1]
@@ -177,8 +167,10 @@
         pltpu.make_async_copy(home_hbm.at[:, span], home_ref.at[:, span], in_sems.at[j])
         for j, span in enumerate(spans)
     ]
-    for load in loads:
+    places_load = pltpu.make_async_copy(places_hbm, places_ref, places_sem)
+    for load in [places_load] + loads:
         load.start()
+    places_load.wait()
     places = places_ref[...]
     stores = []
     for j, span in enumerate(spans):
@@ -201,20 +193,21 @@
     width -= hidden
     row_count = places.shape[0]
     tiles = width // min(width, 512)
-    whole = pl.BlockSpec(memory_space=pltpu.VMEM)
     hbm = pl.BlockSpec(memory_space=pl.ANY)
     return pl.pallas_call(
         collect_kernel,
-        in_specs=[whole, hbm],
+        in_specs=[hbm, hbm],
         out_specs=(hbm, hbm),
         out_shape=(
             jax.ShapeDtypeStruct((row_count, width), BF16),
             jax.ShapeDtypeStruct((row_count, hidden), BF16),
         ),
         scratch_shapes=[
+            pltpu.VMEM(places.shape, BF16),
             pltpu.VMEM((total, width + hidden), BF16),
             pltpu.VMEM((row_count, width), BF16),
             pltpu.VMEM((row_count, hidden), BF16),
+            pltpu.SemaphoreType.DMA,
             pltpu.SemaphoreType.DMA((tiles + 1,)),
             pltpu.SemaphoreType.DMA((tiles + 1,)),
         ],
@@ -237,34 +230,37 @@
     return jnp.concatenate([jnp.where(member == e, x, zero) for e in range(local_count)], axis=1)
 
 
-def join_weight(piece_refs, joined_ref):
-    local_count, rows, width = piece_refs[0].shape
-    if len(piece_refs) == 1:
-        return piece_refs[0][...].reshape(local_count * rows, width)
-    here = lax.axis_index("rep")
-    for i, ref in enumerate(piece_refs):
-        owner = jnp.bitwise_xor(here, i)
-        for e in range(local_count):
-            joined_ref[e, owner] = ref[e]
-    return joined_ref[...].reshape(local_count * len(piece_refs) * rows, width)
-
-
-def products_kernel(capacity, local_count, pieces, g_ref, *refs):
-    w_refs = refs[:pieces]
-    x_refs, out_hbm = refs[pieces:-6], refs[-6]
-    joined_ref, wide_ref, total_ref, out_ref, out_sems = refs[-5:]
+def products_kernel(capacity, pieces, local_ref, *refs):
+    w_hbm, out_hbm = refs[:pieces], refs[pieces]
+    w_ref, wide_ref, total_ref, out_ref, w_sems, out_sems = refs[pieces + 1 :]
     step = pl.program_id(0)
-    steps = out_sems.shape[0] - 1
-    tile = g_ref.shape[1]
+    steps, local_count, _, _, tile = w_ref.shape
     hidden = wide_ref.shape[1] // local_count
     columns = pl.ds(pl.multiple_of(step * tile, tile), tile)
+    here = lax.axis_index("rep") if pieces > 1 else 0
+
+    def weight_loads(j, span):
+        return [
+            pltpu.make_async_copy(
+                piece.at[e, :, span],
+                w_ref.at[j, e, jnp.bitwise_xor(here, i) if pieces > 1 else 0],
+                w_sems.at[j, i, e],
+            )
+            for i, piece in enumerate(w_hbm)
+            for e in range(local_count)
+        ]
 
     @pl.when(step == 0)
     def _():
-        wide_ref[...] = spread(read_columns(x_refs), capacity, local_count)
+        for j in range(steps):
+            for load in weight_loads(j, pl.ds(j * tile, tile)):
+                load.start()
+        wide_ref[...] = spread(local_ref[:, steps * tile :], capacity, local_count)
         total_ref[...] = jnp.zeros_like(total_ref)
 
-    weight = join_weight(w_refs, joined_ref)
+    for load in weight_loads(step, columns):
+        load.wait()
+    weight = w_ref[step].reshape(local_count * hidden, tile)
     out_ref[:, columns] = jnp.dot(
         wide_ref[...], weight, preferred_element_type=F32
     ).astype(BF16)
@@ -272,7 +268,7 @@
         out_ref.at[:, columns], out_hbm.at[:, columns], out_sems.at[step]
     ).start()
     total_ref[...] += lax.dot_general(
-        g_ref[...], weight, (((1,), (1,)), ((), ())), preferred_element_type=F32
+        local_ref[:, columns], weight, (((1,), (1,)), ((), ())), preferred_element_type=F32
     )
 
     @pl.when(step == steps - 1)
@@ -298,50 +294,50 @@
     total = local.shape[0]
     tile = min(width, 512)
     tiles = width // tile
-    specs = hidden_specs(total, hidden, width)
+    hbm = pl.BlockSpec(memory_space=pltpu.HBM)
     return pl.pallas_call(
-        functools.partial(products_kernel, capacity, local_count, pieces),
+        functools.partial(products_kernel, capacity, pieces),
         grid=(tiles,),
-        in_specs=[pl.BlockSpec((total, tile), lambda j: (0, j))]
-        + [pl.BlockSpec((local_count, slice_rows, tile), lambda j: (0, 0, j))] * pieces
-        + specs,
-        out_specs=pl.BlockSpec(memory_space=pl.ANY),
+        in_specs=[pl.BlockSpec(memory_space=pltpu.VMEM)] + [hbm] * pieces,
+        out_specs=hbm,
         out_shape=jax.ShapeDtypeStruct(local.shape, BF16),
         scratch_shapes=[
-            pltpu.VMEM((local_count, pieces, slice_rows, tile), BF16),
+            pltpu.VMEM((tiles, local_count, pieces, slice_rows, tile), BF16),
             pltpu.VMEM((total, local_count * hidden), BF16),
             pltpu.VMEM((total, local_count * hidden), F32),
             pltpu.VMEM(local.shape, BF16),
+            pltpu.SemaphoreType.DMA((tiles, pieces, local_count)),
             pltpu.SemaphoreType.DMA((tiles + 1,)),
         ],
-        compiler_params=pltpu.CompilerParams(
-            vmem_limit_bytes=LARGE_LIMIT, dimension_semantics=("arbitrary",)
-        ),
+        compiler_params=params("arbitrary"),
         cost_estimate=cost(
             4 * total * local_count * hidden * width,
             2 * (local_count * hidden + 2 * total) * width,
         ),
         name="products",
-    )(local, *weight, *([local] * len(specs)))
-
-
-def gradient_kernel(capacity, local_count, parts, factor, g_ref, *refs):
-    blocks = len(refs) - 2 - (parts if parts > 1 else 0)
-    x_refs, wide_ref = refs[:blocks], refs[-1]
-    out_refs = refs[blocks:-2] if parts > 1 else refs[blocks:-1]
-
-    @pl.when(pl.program_id(0) == 0)
+    )(local, *weight)
+
+
+def gradient_kernel(capacity, local_count, parts, factor, local_ref, *refs):
+    out_refs, wide_ref = refs[:parts], refs[-1]
+    step = pl.program_id(0)
+    tile = out_refs[0].shape[-1]
+    width = local_ref.shape[1] - wide_ref.shape[1] // local_count
+
+    @pl.when(step == 0)
     def _():
-        wide_ref[...] = spread(read_columns(x_refs), capacity, local_count)
-
+        wide_ref[...] = spread(local_ref[:, width:], capacity, local_count)
+
+    columns = pl.ds(pl.multiple_of(step * tile, tile), tile)
     outer = lax.dot_general(
-        wide_ref[...], g_ref[...], (((0,), (0,)), ((), ())), preferred_element_type=F32
+        wide_ref[...], local_ref[:, columns], (((0,), (0,)), ((), ())),
+        preferred_element_type=F32,
     )
     low = (outer * factor).astype(BF16)
     if parts == 1:
         out_refs[0][...] = low.reshape(out_refs[0].shape)
         return
-    split_ref = refs[-2]
+    split_ref = refs[parts]
     split_ref[...] = low.reshape(split_ref.shape)
     here = lax.axis_index("rep")
     for i, out_ref in enumerate(out_refs):
@@ -355,24 +351,21 @@
     width -= hidden
     tile = min(width, 512)
     slice_rows = hidden // parts
-    specs = hidden_specs(total, hidden, width)
     split = [pltpu.VMEM((local_count, parts, slice_rows, tile), BF16)] if parts > 1 else []
     return list(pl.pallas_call(
         functools.partial(gradient_kernel, capacity, local_count, parts, factor),
         grid=(width // tile,),
-        in_specs=[pl.BlockSpec((total, tile), lambda j: (0, j))] + specs,
+        in_specs=[pl.BlockSpec(memory_space=pltpu.VMEM)],
         out_specs=(pl.BlockSpec((local_count, slice_rows, tile), lambda j: (0, 0, j)),) * parts,
         out_shape=(jax.ShapeDtypeStruct((local_count, slice_rows, width), BF16),) * parts,
         scratch_shapes=split + [pltpu.VMEM((total, local_count * hidden), BF16)],
-        compiler_params=pltpu.CompilerParams(
-            vmem_limit_bytes=LARGE_LIMIT, dimension_semantics=("arbitrary",)
-        ),
+        compiler_params=params("arbitrary"),
         cost_estimate=cost(
             2 * total * local_count * hidden * width,
             2 * (local_count * hidden + total) * width,
         ),
         name="gradient",
-    )(*([local] * (1 + len(specs)))))
+    )(local))
 
 
 def cast_kernel(w_ref, out_ref):

time: 111 us -> 117 us (1.054)
  local copies, waits for them, and re-layouts: 3.68 us -> 13 us
  Pallas kernels: 25.2 us -> 22.6 us
    unnamed x26 -> x38, local copies, waits for them, and re-layouts: 3.68 us -> 13 us
    pallas_call x1, Pallas kernels: 5.64 us -> 3.14 us  [gradient(): pl.pallas_call(functools.partial(gradient_kernel, capacity, local_count,...]
    ppermute x6, waiting for transfers between devices: 38.2 us -> 36.1 us  [swap(): return lax.ppermute(array, axis, [(i, i ^ offset) for i in range(size)])]
    all_to_all x2, waiting for transfers between devices: 23.3 us -> 24.8 us  [exchange(): lax.all_to_all(parts, 'grp', split_axis=0, concat_axis=0, tiled=True, axi...]
  transfers between devices with their start and end apart: 8 -> 8, of which waited for: 6 -> 6; matrix products, arithmetic and copies ran while one was open for 0% -> 0% of each run, Pallas kernels for 12% -> 9%
where the time goes in v8:
time: 117 us; the launch traced here: 115 us
  waiting for transfers between devices  60.9 us (52%)
  Pallas kernels  22.6 us (19%)
  starting transfers between devices  17.9 us (15%)
  local copies, waits for them, and re-layouts  13 us (11%)
    ppermute x6, waiting for transfers between devices, swap(): return lax.ppermute(array, axis, [(i, i ^ offset) for i in range(size)])  36.1 us
    all_to_all x2, waiting for transfers between devices, exchange(): lax.all_to_all(parts, 'grp', split_axis=0, concat_axis=0, tiled=True, axi...  24.8 us
    all_to_all x2, starting transfers between devices, exchange(): lax.all_to_all(parts, 'grp', split_axis=0, concat_axis=0, tiled=True, axi...  14.2 us
    unnamed x38, local copies, waits for them, and re-layouts  13 us
    pallas_call x1, Pallas kernels, products(): pl.pallas_call(functools.partial(products_kernel, capacity, pieces), grid...  6.3 us
    pallas_call x1, Pallas kernels, adam(): pl.pallas_call(functools.partial(adam_kernel, len(grads)), grid=(members,...  6.19 us
    ppermute x6, starting transfers between devices, swap(): return lax.ppermute(array, axis, [(i, i ^ offset) for i in range(size)])  3.74 us
    pallas_call x1, Pallas kernels, dispatch(): pl.pallas_call(functools.partial(dispatch_kernel, capacity, groups), in_s...  3.44 us
  transfers between devices with their start and end apart: 8, of which 6 were waited for; matrix products, arithmetic and copies ran while one was open for 0% of the time, Pallas kernels for 9%

profile of v8, /device:TPU:0, one launch (start us, length us, event | category | flops | bytes accessed | tf_op | source)
XLA Modules:
  0.0 115.2 jit_solution(9896300031407968432)
XLA Ops:
  0.6 3.4 %dispatch.1 = (bf16[384,2432]{1,0:T(8,128)(2,1)}, s32[1,256]{1,0:T(1,128)}) custom-call(s32[1,256]{1,0:T(1,128)} %bitcast.19, s32[1,16]{1,0:T(1,128)} %bitcast.20, bf16[256,384]{1,0:T(8,128)(2,1)} %x_hbm.1, bf16[256,2048]{1,0:T(8,128)(2,1)} %g_hbm.1), custom_call_target="tpu_custom_call" | custom-call | flops 478150656 | bytes 3112960 | tf_op jit(solution)/shard_map/dispatch/pallas_call | solution.py:114
  4.1 0.0 copy-start
  4.1 7.4 %all-to-all-start = ((bf16[8,48,2432]{2,1,0:T(8,128)(2,1)}), bf16[8,48,2432]{2,1,0:T(8,128)(2,1)S(1)}, u32[]{:S(2)}, u32[]{:S(2)}) async-start(bf16[8,48,2432]{2,1,0:T(8,128)(2,1)} %bitcast.16), calls=%async_computation | async-start | bytes 3735552 | tf_op jit(solution)/shard_map/all_to_all | solution.py:488
  11.5 0.0 copy-done
  11.5 0.3 cast_weight.1.refs_0_
  11.8 1.6 %collective-permute-start.1 = (bf16[2,96,2048]{2,1,0:T(8,128)(2,1)S(1)}, bf16[2,96,2048]{2,1,0:T(8,128)(2,1)S(1)}, u32[]{:S(2)}, u32[]{:S(2)}) collective-permute-start(bf16[2,96,2048]{2,1,0:T(8,128)(2,1)S(1)} %cast_weight.1.refs_0_), channel_id=1, source_target_pairs={{0,16},{8,24},{16,0},{24,8},{1,17},{9,25},{17,1},{25,9},{2,18},{10... | collective-permute-start | bytes 2359304 | tf_op jit(solution)/shard_map/ppermute | solution.py:481
  13.4 0.0 collective-permute-start
  13.4 0.0 copy-start.4
  13.4 0.9 copy-done.4
  14.3 16.6 %collective-permute-done.1.refs_2_ = bf16[2,96,2048]{2,1,0:T(8,128)(2,1)S(1)} collective-permute-done((bf16[2,96,2048]{2,1,0:T(8,128)(2,1)S(1)}, bf16[2,96,2048]{2,1,0:T(8,128)(2,1)S(1)}, u32[]{:S(2)}, u32[]{:S(2)}) %collective-permute-start.1) | collective-permute-done | bytes 786464 | tf_op jit(solution)/shard_map/ppermute | solution.py:481
  30.9 0.0 collective-permute-start.2
  30.9 0.0 copy-start.13
  30.9 0.9 copy-done.13
  31.8 0.0 collective-permute-done.refs_1_
  31.8 0.0 copy-start.15
  31.8 0.9 copy-done.15
  32.7 0.5 collective-permute-done.2.refs_3_
  33.2 0.0 copy-start.17
  33.2 0.9 copy-done.17
  34.1 17.7 %all-to-all-done = bf16[8,48,2432]{2,1,0:T(8,128)(2,1)S(1)} async-done(((bf16[8,48,2432]{2,1,0:T(8,128)(2,1)}), bf16[8,48,2432]{2,1,0:T(8,128)(2,1)S(1)}, u32[]{:S(2)}, u32[]{:S(2)}) %all-to-all-start) | async-done | bytes 1867808 | tf_op jit(solution)/shard_map/all_to_all | solution.py:488
  51.8 0.0 copy-start.2
  51.8 0.0 copy-start.5
  51.8 1.7 %copy-done.5 = bf16[2,96,2048]{2,1,0:T(8,128)(2,1)S(1)} copy-done((bf16[2,96,2048]{2,1,0:T(8,128)(2,1)S(1)}, bf16[2,96,2048]{2,1,0:T(8,128)(2,1)}, u32[]{:S(2)}) %copy-start.5) | copy-done | bytes 786456
  53.4 0.0 copy-start.14
  53.4 1.1 copy-done.14
  54.6 0.0 copy-start.16
  54.6 1.1 copy-done.16
  55.7 0.0 copy-start.18
  55.7 1.1 copy-done.18
  56.8 6.3 %products.1 = bf16[384,2432]{1,0:T(8,128)(2,1)S(1)} custom-call(bf16[384,2432]{1,0:T(8,128)(2,1)S(1)} %bitcast.12, bf16[2,96,2048]{2,1,0:T(8,128)(2,1)S(1)} %copy-done.5, bf16[2,96,2048]{2,1,0:T(8,128)(2,1)S(1)} %copy-done.16, bf16[2,96,2048]{2,1,0:T(8,128)(2,1)S(1)} %copy-done.14, bf16[2,96,2048]{2,1,0:T(8,128)(2,1)S(1)} %copy-done.18), custom_call_target="tpu_custom_call" | custom-call | flops 2415919104 | bytes 6291456 | tf_op jit(solution)/shard_map/products/pallas_call | solution.py:298
  63.1 0.0 copy-done.2
  63.2 0.0 copy-start.1
  63.2 1.3 %copy-done.1 = bf16[384,2432]{1,0:T(8,128)(2,1)} copy-done((bf16[384,2432]{1,0:T(8,128)(2,1)}, bf16[384,2432]{1,0:T(8,128)(2,1)S(1)}, u32[]{:S(2)}) %copy-start.1) | copy-done | bytes 1867800
  64.4 6.8 %all-to-all-start.1 = ((bf16[8,48,2432]{2,1,0:T(8,128)(2,1)}), bf16[8,48,2432]{2,1,0:T(8,128)(2,1)S(1)}, u32[]{:S(2)}, u32[]{:S(2)}) async-start(bf16[8,48,2432]{2,1,0:T(8,128)(2,1)} %bitcast.11), calls=%async_computation.1 | async-start | bytes 3735552 | tf_op jit(solution)/shard_map/all_to_all | solution.py:488
  71.2 0.0 copy-start.3
  71.2 1.5 %copy-done.3 = bf16[8,48,2432]{2,1,0:T(8,128)(2,1)S(1)} copy-done((bf16[8,48,2432]{2,1,0:T(8,128)(2,1)S(1)}, bf16[8,48,2432]{2,1,0:T(8,128)(2,1)}, u32[]{:S(2)}) %copy-start.3) | copy-done | bytes 1867800
  72.7 3.1 %gradient.1 = (bf16[2,96,2048]{2,1,0:T(8,128)(2,1)S(1)}, bf16[2,96,2048]{2,1,0:T(8,128)(2,1)S(1)}, bf16[2,96,2048]{2,1,0:T(8,128)(2,1)S(1)}, bf16[2,96,2048]{2,1,0:T(8,128)(2,1)S(1)}) custom-call(bf16[384,2432]{1,0:T(8,128)(2,1)S(1)} %bitcast.13), custom_call_target="tpu_custom_call" | custom-call | flops 1207959552 | bytes 4718592 | tf_op jit(solution)/shard_map/gradient/pallas_call | solution.py:355
  75.9 0.0 copy-start.12
  75.9 0.0 copy-start.6
  75.9 0.0 copy-start.7
  75.9 0.0 copy-start.10
  75.9 0.0 copy-start.11
  75.9 0.1 collective-permute-start.4
  76.0 0.5 collective-permute-start.3
  76.5 1.8 %collective-permute-done.4.b_ref = bf16[2,96,2048]{2,1,0:T(8,128)(2,1)S(1)} collective-permute-done((bf16[2,96,2048]{2,1,0:T(8,128)(2,1)S(1)}, bf16[2,96,2048]{2,1,0:T(8,128)(2,1)S(1)}, u32[]{:S(2)}, u32[]{:S(2)}) %collective-permute-start.4) | collective-permute-done | bytes 786464 | tf_op jit(solution)/shard_map/ppermute | solution.py:481
  78.3 0.4 add_parts.1
  78.7 1.6 %collective-permute-start.5 = (bf16[2,96,2048]{2,1,0:T(8,128)(2,1)S(1)}, bf16[2,96,2048]{2,1,0:T(8,128)(2,1)S(1)}, u32[]{:S(2)}, u32[]{:S(2)}) collective-permute-start(bf16[2,96,2048]{2,1,0:T(8,128)(2,1)S(1)} %add_parts.1), channel_id=1, source_target_pairs={{0,16},{8,24},{16,0},{24,8},{1,17},{9,25},{17,1},{25,9},{2,18},{10... | collective-permute-start | bytes 2359304 | tf_op jit(solution)/shard_map/ppermute | solution.py:481
  80.2 0.0 copy-done.12
  80.2 0.1 home_places.1.places_hbm
  80.4 0.0 copy-start.8
  80.4 0.7 copy-done.8
  81.1 0.0 collective-permute-done.3.refs_1_
  81.1 17.2 %collective-permute-done.5.refs_2_ = bf16[2,96,2048]{2,1,0:T(8,128)(2,1)S(1)} collective-permute-done((bf16[2,96,2048]{2,1,0:T(8,128)(2,1)S(1)}, bf16[2,96,2048]{2,1,0:T(8,128)(2,1)S(1)}, u32[]{:S(2)}, u32[]{:S(2)}) %collective-permute-start.5) | collective-permute-done | bytes 786464 | tf_op jit(solution)/shard_map/ppermute | solution.py:481
  98.3 0.0 copy-done.6
  98.3 0.0 copy-done.7
  98.3 0.0 copy-done.10
  98.3 0.0 copy-done.11
  98.3 6.2 %adam.1 = (f32[2,96,2048]{2,1,0:T(8,128)}, bf16[2,96,2048]{2,1,0:T(8,128)(2,1)}, f32[2,16,96]{2,1,0:T(8,128)}, bf16[2,96,2048]{2,1,0:T(8,128)(2,1)}, f32[2,16,96]{2,1,0:T(8,128)}) custom-call(f32[2,96,2048]{2,1,0:T(8,128)S(1)} %copy-done, bf16[2,96,2048]{2,1,0:T(8,128)(2,1)S(1)} %copy-done.6, f32[2,16,96]{2,1,0:T(8,128)S(1)} %bitcast.14, ...), custom_call_target="tpu_custom_call" | custom-call | flops 15728640 | bytes 7077888 | tf_op jit(solution)/shard_map/adam/pallas_call | solution.py:454
  104.5 7.1 %all-to-all-done.1 = bf16[8,48,2432]{2,1,0:T(8,128)(2,1)S(1)} async-done(((bf16[8,48,2432]{2,1,0:T(8,128)(2,1)}), bf16[8,48,2432]{2,1,0:T(8,128)(2,1)S(1)}, u32[]{:S(2)}, u32[]{:S(2)}) %all-to-all-start.1) | async-done | bytes 1867808 | tf_op jit(solution)/shard_map/all_to_all | solution.py:488
  111.6 0.0 copy-start.9
  111.6 0.9 copy-done.9
  112.6 2.7 %collect.1 = (bf16[256,2048]{1,0:T(8,128)(2,1)}, bf16[256,384]{1,0:T(8,128)(2,1)}) custom-call(bf16[256,384]{1,0:T(8,128)(2,1)S(1)} %copy-done.9, bf16[384,2432]{1,0:T(8,128)(2,1)S(1)} %bitcast.10), custom_call_target="tpu_custom_call" | custom-call | flops 478150656 | bytes 3112960 | tf_op jit(solution)/shard_map/collect/pallas_call | solution.py:197
Async XLA Ops:
  4.1 7.4 %copy-start = (f32[2,96,2048]{2,1,0:T(8,128)S(1)}, f32[2,96,2048]{2,1,0:T(8,128)}, u32[]{:S(2)}) copy-start(f32[2,96,2048]{2,1,0:T(8,128)} %master_ref.1) | copy-start | bytes 4718596
  4.1 47.7 %all-to-all-start = ((bf16[8,48,2432]{2,1,0:T(8,128)(2,1)}), bf16[8,48,2432]{2,1,0:T(8,128)(2,1)S(1)}, u32[]{:S(2)}, u32[]{:S(2)}) async-start(bf16[8,48,2432]{2,1,0:T(8,128)(2,1)} %bitcast.16), calls=%async_computation | async-start | bytes 3735552 | tf_op jit(solution)/shard_map/all_to_all | solution.py:488
  11.8 19.1 %collective-permute-start.1 = (bf16[2,96,2048]{2,1,0:T(8,128)(2,1)S(1)}, bf16[2,96,2048]{2,1,0:T(8,128)(2,1)S(1)}, u32[]{:S(2)}, u32[]{:S(2)}) collective-permute-start(bf16[2,96,2048]{2,1,0:T(8,128)(2,1)S(1)} %cast_weight.1.refs_0_), channel_id=1, source_target_pairs={{0,16},{8,24},{16,0},{24,8},{1,17},{9,25},{17,1},{25,9},{2,18},{10... | collective-permute-start | bytes 2359304 | tf_op jit(solution)/shard_map/ppermute | solution.py:481
  13.4 18.4 %collective-permute-start = (bf16[2,96,2048]{2,1,0:T(8,128)(2,1)S(1)}, bf16[2,96,2048]{2,1,0:T(8,128)(2,1)S(1)}, u32[]{:S(2)}, u32[]{:S(2)}) collective-permute-start(bf16[2,96,2048]{2,1,0:T(8,128)(2,1)S(1)} %cast_weight.1.refs_0_), channel_id=1, source_target_pairs={{0,8},{8,0},{16,24},{24,16},{1,9},{9,1},{17,25},{25,17},{2,10},{10... | collective-permute-start | bytes 2359304 | tf_op jit(solution)/shard_map/ppermute | solution.py:481
  13.4 0.9 copy-start.4
  30.9 2.3 %collective-permute-start.2 = (bf16[2,96,2048]{2,1,0:T(8,128)(2,1)S(1)}, bf16[2,96,2048]{2,1,0:T(8,128)(2,1)S(1)}, u32[]{:S(2)}, u32[]{:S(2)}) collective-permute-start(bf16[2,96,2048]{2,1,0:T(8,128)(2,1)S(1)} %collective-permute-done.1.refs_2_), channel_id=1, source_target_pairs={{0,8},{8,0},{16,24},{24,16},{1,9},{9,1},{17,25},{25,17},{2,10},{10... | collective-permute-start | bytes 2359304 | tf_op jit(solution)/shard_map/ppermute | solution.py:481
  30.9 0.9 copy-start.13
  31.8 0.9 copy-start.15
  33.2 0.9 copy-start.17
  51.8 11.4 %copy-start.2 = (bf16[8,48,2432]{2,1,0:T(8,128)(2,1)}, bf16[8,48,2432]{2,1,0:T(8,128)(2,1)S(1)}, u32[]{:S(2)}) copy-start(bf16[8,48,2432]{2,1,0:T(8,128)(2,1)S(1)} %all-to-all-done) | copy-start | bytes 5603332
  51.8 1.7 %copy-start.5 = (bf16[2,96,2048]{2,1,0:T(8,128)(2,1)S(1)}, bf16[2,96,2048]{2,1,0:T(8,128)(2,1)}, u32[]{:S(2)}) copy-start(bf16[2,96,2048]{2,1,0:T(8,128)(2,1)} %copy-done.4) | copy-start | bytes 2359300
  53.4 1.1 copy-start.14
  54.6 1.1 copy-start.16
  55.7 1.1 copy-start.18
  63.2 1.3 %copy-start.1 = (bf16[384,2432]{1,0:T(8,128)(2,1)}, bf16[384,2432]{1,0:T(8,128)(2,1)S(1)}, u32[]{:S(2)}) copy-start(bf16[384,2432]{1,0:T(8,128)(2,1)S(1)} %products.1) | copy-start | bytes 5603332
  64.4 47.2 %all-to-all-start.1 = ((bf16[8,48,2432]{2,1,0:T(8,128)(2,1)}), bf16[8,48,2432]{2,1,0:T(8,128)(2,1)S(1)}, u32[]{:S(2)}, u32[]{:S(2)}) async-start(bf16[8,48,2432]{2,1,0:T(8,128)(2,1)} %bitcast.11), calls=%async_computation.1 | async-start | bytes 3735552 | tf_op jit(solution)/shard_map/all_to_all | solution.py:488
  71.2 1.5 %copy-start.3 = (bf16[8,48,2432]{2,1,0:T(8,128)(2,1)S(1)}, bf16[8,48,2432]{2,1,0:T(8,128)(2,1)}, u32[]{:S(2)}) copy-start(bf16[8,48,2432]{2,1,0:T(8,128)(2,1)} %copy-done.2) | copy-start | bytes 5603332
  75.9 4.4 %copy-start.12 = (s32[1,256]{1,0:T(1,128)S(1)}, s32[1,256]{1,0:T(1,128)}, u32[]{:S(2)}) copy-start(s32[1,256]{1,0:T(1,128)} %get-tuple-element.25.target_ref) | copy-start | bytes 3076
  75.9 22.4 %copy-start.6 = (bf16[2,96,2048]{2,1,0:T(8,128)(2,1)S(1)}, bf16[2,96,2048]{2,1,0:T(8,128)(2,1)}, u32[]{:S(2)}) copy-start(bf16[2,96,2048]{2,1,0:T(8,128)(2,1)} %mc_ref.1) | copy-start | bytes 2359300
  75.9 22.4 %copy-start.7 = (bf16[2,96,2048]{2,1,0:T(8,128)(2,1)S(1)}, bf16[2,96,2048]{2,1,0:T(8,128)(2,1)}, u32[]{:S(2)}) copy-start(bf16[2,96,2048]{2,1,0:T(8,128)(2,1)} %vc_ref.1) | copy-start | bytes 2359300
  75.9 22.4 %copy-start.10 = (f32[2,96,16]{1,2,0:T(8,128)S(1)}, f32[2,96,16]{1,2,0:T(8,128)}, u32[]{:S(2)}) copy-start(f32[2,96,16]{1,2,0:T(8,128)} %param.11) | copy-start | bytes 36868
  75.9 22.4 %copy-start.11 = (f32[2,96,16]{1,2,0:T(8,128)S(1)}, f32[2,96,16]{1,2,0:T(8,128)}, u32[]{:S(2)}) copy-start(f32[2,96,16]{1,2,0:T(8,128)} %param.13) | copy-start | bytes 36868
  75.9 2.4 %collective-permute-start.4 = (bf16[2,96,2048]{2,1,0:T(8,128)(2,1)S(1)}, bf16[2,96,2048]{2,1,0:T(8,128)(2,1)S(1)}, u32[]{:S(2)}, u32[]{:S(2)}) collective-permute-start(bf16[2,96,2048]{2,1,0:T(8,128)(2,1)S(1)} %get-tuple-element.35), channel_id=1, source_target_pairs={{0,8},{8,0},{16,24},{24,16},{1,9},{9,1},{17,25},{25,17},{2,10},{10... | collective-permute-start | bytes 2359304 | tf_op jit(solution)/shard_map/ppermute | solution.py:481
  76.0 5.1 %collective-permute-start.3 = (bf16[2,96,2048]{2,1,0:T(8,128)(2,1)S(1)}, bf16[2,96,2048]{2,1,0:T(8,128)(2,1)S(1)}, u32[]{:S(2)}, u32[]{:S(2)}) collective-permute-start(bf16[2,96,2048]{2,1,0:T(8,128)(2,1)S(1)} %get-tuple-element.33), channel_id=1, source_target_pairs={{0,8},{8,0},{16,24},{24,16},{1,9},{9,1},{17,25},{25,17},{2,10},{10... | collective-permute-start | bytes 2359304 | tf_op jit(solution)/shard_map/ppermute | solution.py:481
  78.7 19.6 %collective-permute-start.5 = (bf16[2,96,2048]{2,1,0:T(8,128)(2,1)S(1)}, bf16[2,96,2048]{2,1,0:T(8,128)(2,1)S(1)}, u32[]{:S(2)}, u32[]{:S(2)}) collective-permute-start(bf16[2,96,2048]{2,1,0:T(8,128)(2,1)S(1)} %add_parts.1), channel_id=1, source_target_pairs={{0,16},{8,24},{16,0},{24,8},{1,17},{9,25},{17,1},{25,9},{2,18},{10... | collective-permute-start | bytes 2359304 | tf_op jit(solution)/shard_map/ppermute | solution.py:481
  80.4 0.7 copy-start.8
  111.6 0.9 copy-start.9

commit v9 on v8

--- a/solution.py
+++ b/solution.py
@@ -138,43 +138,33 @@
     )(route.reshape(1, row_count), placement.reshape(1, -1), x_rows, y_cot)
 
 
-def home_places_kernel(target_ref, out_ref):
-    target = target_ref[...]
-    slots = lax.broadcasted_iota(jnp.int32, (out_ref.shape[1], target.shape[1]), 0)
-    out_ref[...] = (slots == target).astype(F32).T.astype(BF16)
-
-
-def home_places(target, places):
-    return pl.pallas_call(
-        home_places_kernel,
-        out_shape=jax.ShapeDtypeStruct((target.shape[1], places), BF16),
-        compiler_params=params(),
-        cost_estimate=cost(places * target.shape[1], 2 * places * target.shape[1]),
-        name="home_places",
-    )(target)
+def hidden_specs(rows, hidden, width):
+    return [
+        pl.BlockSpec((rows, BLOCK), functools.partial(lambda k, j: (0, k), width // BLOCK + i))
+        for i in range(hidden // BLOCK)
+    ]
+
+
+def read_columns(refs):
+    return jnp.concatenate([ref[...] for ref in refs], axis=1)
 
 
 def collect_kernel(
-    places_hbm, home_hbm, y_hbm, dx_hbm,
-    places_ref, home_ref, y_ref, dx_ref, places_sem, in_sems, out_sems,
+    target_hbm, home_ref, y_hbm, dx_hbm, target_ref, y_ref, dx_ref, target_sem, out_sems
 ):
     hidden = dx_ref.shape[1]
     width = y_ref.shape[1]
-    tiles = in_sems.shape[0] - 1
+    tiles = out_sems.shape[0] - 1
     tile = width // tiles
     spans = [pl.ds(j * tile, tile) for j in range(tiles)] + [pl.ds(width, hidden)]
-    loads = [
-        pltpu.make_async_copy(home_hbm.at[:, span], home_ref.at[:, span], in_sems.at[j])
-        for j, span in enumerate(spans)
-    ]
-    places_load = pltpu.make_async_copy(places_hbm, places_ref, places_sem)
-    for load in [places_load] + loads:
-        load.start()
-    places_load.wait()
-    places = places_ref[...]
+    target_load = pltpu.make_async_copy(target_hbm, target_ref, target_sem)
+    target_load.start()
+    target_load.wait()
+    target = target_ref[...]
+    slots = lax.broadcasted_iota(jnp.int32, (home_ref.shape[0], target.shape[1]), 0)
+    places = (slots == target).astype(F32).T.astype(BF16)
     stores = []
     for j, span in enumerate(spans):
-        loads[j].wait()
         rows = jnp.dot(places, home_ref[:, span], preferred_element_type=F32).astype(BF16)
         if j < tiles:
             y_ref[:, span] = rows
@@ -188,27 +178,25 @@
         store.wait()
 
 
-def collect(places, home, hidden):
+def collect(target, home, hidden):
     total, width = home.shape
     width -= hidden
-    row_count = places.shape[0]
+    row_count = target.shape[1]
     tiles = width // min(width, 512)
     hbm = pl.BlockSpec(memory_space=pl.ANY)
     return pl.pallas_call(
         collect_kernel,
-        in_specs=[hbm, hbm],
+        in_specs=[hbm, pl.BlockSpec(memory_space=pltpu.VMEM)],
         out_specs=(hbm, hbm),
         out_shape=(
             jax.ShapeDtypeStruct((row_count, width), BF16),
             jax.ShapeDtypeStruct((row_count, hidden), BF16),
         ),
         scratch_shapes=[
-            pltpu.VMEM(places.shape, BF16),
-            pltpu.VMEM((total, width + hidden), BF16),
+            pltpu.VMEM(target.shape, jnp.int32),
             pltpu.VMEM((row_count, width), BF16),
             pltpu.VMEM((row_count, hidden), BF16),
             pltpu.SemaphoreType.DMA,
-            pltpu.SemaphoreType.DMA((tiles + 1,)),
             pltpu.SemaphoreType.DMA((tiles + 1,)),
         ],
         compiler_params=params(),
@@ -216,7 +204,7 @@
             2 * total * row_count * (hidden + width), 2 * (total + row_count) * (hidden + width)
         ),
         name="collect",
-    )(places, home)
+    )(target, home)
 
 
 def member_rows(rows, capacity, local_count):
@@ -230,9 +218,9 @@
     return jnp.concatenate([jnp.where(member == e, x, zero) for e in range(local_count)], axis=1)
 
 
-def products_kernel(capacity, pieces, local_ref, *refs):
+def products_kernel(capacity, pieces, local_hbm, *refs):
     w_hbm, out_hbm = refs[:pieces], refs[pieces]
-    w_ref, wide_ref, total_ref, out_ref, w_sems, out_sems = refs[pieces + 1 :]
+    x_ref, g_ref, w_ref, wide_ref, total_ref, out_ref, g_sems, w_sems, out_sems = refs[pieces + 1 :]
     step = pl.program_id(0)
     steps, local_count, _, _, tile = w_ref.shape
     hidden = wide_ref.shape[1] // local_count
@@ -250,12 +238,21 @@
             for e in range(local_count)
         ]
 
+    def row_load(j, span):
+        return pltpu.make_async_copy(local_hbm.at[:, span], g_ref.at[j], g_sems.at[j])
+
     @pl.when(step == 0)
     def _():
+        x_load = pltpu.make_async_copy(
+            local_hbm.at[:, pl.ds(steps * tile, hidden)], x_ref, g_sems.at[steps]
+        )
+        x_load.start()
         for j in range(steps):
-            for load in weight_loads(j, pl.ds(j * tile, tile)):
+            span = pl.ds(j * tile, tile)
+            for load in weight_loads(j, span) + [row_load(j, span)]:
                 load.start()
-        wide_ref[...] = spread(local_ref[:, steps * tile :], capacity, local_count)
+        x_load.wait()
+        wide_ref[...] = spread(x_ref[...], capacity, local_count)
         total_ref[...] = jnp.zeros_like(total_ref)
 
     for load in weight_loads(step, columns):
@@ -267,8 +264,9 @@
     pltpu.make_async_copy(
         out_ref.at[:, columns], out_hbm.at[:, columns], out_sems.at[step]
     ).start()
+    row_load(step, columns).wait()
     total_ref[...] += lax.dot_general(
-        local_ref[:, columns], weight, (((1,), (1,)), ((), ())), preferred_element_type=F32
+        g_ref[step], weight, (((1,), (1,)), ((), ())), preferred_element_type=F32
     )
 
     @pl.when(step == steps - 1)
@@ -294,22 +292,27 @@
     total = local.shape[0]
     tile = min(width, 512)
     tiles = width // tile
-    hbm = pl.BlockSpec(memory_space=pltpu.HBM)
+    hbm = pl.BlockSpec(memory_space=pl.ANY)
     return pl.pallas_call(
         functools.partial(products_kernel, capacity, pieces),
         grid=(tiles,),
-        in_specs=[pl.BlockSpec(memory_space=pltpu.VMEM)] + [hbm] * pieces,
+        in_specs=[hbm] * (1 + pieces),
         out_specs=hbm,
         out_shape=jax.ShapeDtypeStruct(local.shape, BF16),
         scratch_shapes=[
+            pltpu.VMEM((total, hidden), BF16),
+            pltpu.VMEM((tiles, total, tile), BF16),
             pltpu.VMEM((tiles, local_count, pieces, slice_rows, tile), BF16),
             pltpu.VMEM((total, local_count * hidden), BF16),
             pltpu.VMEM((total, local_count * hidden), F32),
             pltpu.VMEM(local.shape, BF16),
+            pltpu.SemaphoreType.DMA((tiles + 1,)),
             pltpu.SemaphoreType.DMA((tiles, pieces, local_count)),
             pltpu.SemaphoreType.DMA((tiles + 1,)),
         ],
-        compiler_params=params("arbitrary"),
+        compiler_params=pltpu.CompilerParams(
+            vmem_limit_bytes=LARGE_LIMIT, dimension_semantics=("arbitrary",)
+        ),
         cost_estimate=cost(
             4 * total * local_count * hidden * width,
             2 * (local_count * hidden + 2 * total) * width,
@@ -318,26 +321,23 @@
     )(local, *weight)
 
 
-def gradient_kernel(capacity, local_count, parts, factor, local_ref, *refs):
-    out_refs, wide_ref = refs[:parts], refs[-1]
-    step = pl.program_id(0)
-    tile = out_refs[0].shape[-1]
-    width = local_ref.shape[1] - wide_ref.shape[1] // local_count
-
-    @pl.when(step == 0)
+def gradient_kernel(capacity, local_count, parts, factor, g_ref, *refs):
+    blocks = len(refs) - 2 - (parts if parts > 1 else 0)
+    x_refs, wide_ref = refs[:blocks], refs[-1]
+    out_refs = refs[blocks:-2] if parts > 1 else refs[blocks:-1]
+
+    @pl.when(pl.program_id(0) == 0)
     def _():
-        wide_ref[...] = spread(local_ref[:, width:], capacity, local_count)
-
-    columns = pl.ds(pl.multiple_of(step * tile, tile), tile)
+        wide_ref[...] = spread(read_columns(x_refs), capacity, local_count)
+
     outer = lax.dot_general(
-        wide_ref[...], local_ref[:, columns], (((0,), (0,)), ((), ())),
-        preferred_element_type=F32,
+        wide_ref[...], g_ref[...], (((0,), (0,)), ((), ())), preferred_element_type=F32
     )
     low = (outer * factor).astype(BF16)
     if parts == 1:
         out_refs[0][...] = low.reshape(out_refs[0].shape)
         return
-    split_ref = refs[parts]
+    split_ref = refs[-2]
     split_ref[...] = low.reshape(split_ref.shape)
     here = lax.axis_index("rep")
     for i, out_ref in enumerate(out_refs):
@@ -351,21 +351,24 @@
     width -= hidden
     tile = min(width, 512)
     slice_rows = hidden // parts
+    specs = hidden_specs(total, hidden, width)
     split = [pltpu.VMEM((local_count, parts, slice_rows, tile), BF16)] if parts > 1 else []
     return list(pl.pallas_call(
         functools.partial(gradient_kernel, capacity, local_count, parts, factor),
         grid=(width // tile,),
-        in_specs=[pl.BlockSpec(memory_space=pltpu.VMEM)],
+        in_specs=[pl.BlockSpec((total, tile), lambda j: (0, j))] + specs,
         out_specs=(pl.BlockSpec((local_count, slice_rows, tile), lambda j: (0, 0, j)),) * parts,
         out_shape=(jax.ShapeDtypeStruct((local_count, slice_rows, width), BF16),) * parts,
         scratch_shapes=split + [pltpu.VMEM((total, local_count * hidden), BF16)],
-        compiler_params=params("arbitrary"),
+        compiler_params=pltpu.CompilerParams(
+            vmem_limit_bytes=LARGE_LIMIT, dimension_semantics=("arbitrary",)
+        ),
         cost_estimate=cost(
             2 * total * local_count * hidden * width,
             2 * (local_count * hidden + total) * width,
         ),
         name="gradient",
-    )(local))
+    )(*([local] * (1 + len(specs)))))
 
 
 def cast_kernel(w_ref, out_ref):
@@ -528,7 +531,7 @@
     hidden = x_rows.shape[1]
     grads = sum_gradient(gradient(local, hidden, capacity, local_count, parts, grad_factor))
     updated = adam(master_weight, grads, m_code, m_scale, v_code, v_scale)
-    y_rows, x_grad = collect(home_places(target, places), home, hidden)
+    y_rows, x_grad = collect(target, home, hidden)
     return (y_rows, x_grad) + tuple(updated)
 
 

time: 117 us -> 111 us (0.949)
  local copies, waits for them, and re-layouts: 13 us -> 2.08 us
  Pallas kernels: 22.6 us -> 26 us
  waiting for transfers between devices: 60.9 us -> 62.4 us
    unnamed x38 -> x22, local copies, waits for them, and re-layouts: 13 us -> 2.08 us
    ppermute x6, waiting for transfers between devices: 36.1 us -> 39 us  [swap(): return lax.ppermute(array, axis, [(i, i ^ offset) for i in range(size)])]
    pallas_call x1, Pallas kernels: 3.14 us -> 5.64 us  [gradient(): pl.pallas_call(functools.partial(gradient_kernel, capacity, local_count,...]
    pallas_call x1, Pallas kernels: 6.3 us -> 8.35 us  [products(): pl.pallas_call(functools.partial(products_kernel, capacity, pieces), grid...]
    all_to_all x2, waiting for transfers between devices: 24.8 us -> 23.4 us  [exchange(): lax.all_to_all(parts, 'grp', split_axis=0, concat_axis=0, tiled=True, axi...]
    pallas_call x2 -> x1, Pallas kernels: 2.8 us -> 1.62 us  [collect(): pl.pallas_call(collect_kernel, in_specs=[hbm, pl.BlockSpec(memory_space=p...]
  transfers between devices with their start and end apart: 8 -> 8, of which waited for: 6 -> 6; matrix products, arithmetic and copies ran while one was open for 0% -> 0% of each run, Pallas kernels for 9% -> 12%
where the time goes in v9:
time: 111 us; the launch traced here: 109 us
  waiting for transfers between devices  62.4 us (56%)
  Pallas kernels  26 us (23%)
  starting transfers between devices  17.9 us (16%)
  local copies, waits for them, and re-layouts  2.08 us (2%)
    ppermute x6, waiting for transfers between devices, swap(): return lax.ppermute(array, axis, [(i, i ^ offset) for i in range(size)])  39 us
    all_to_all x2, waiting for transfers between devices, exchange(): lax.all_to_all(parts, 'grp', split_axis=0, concat_axis=0, tiled=True, axi...  23.4 us
    all_to_all x2, starting transfers between devices, exchange(): lax.all_to_all(parts, 'grp', split_axis=0, concat_axis=0, tiled=True, axi...  14.2 us
    pallas_call x1, Pallas kernels, products(): pl.pallas_call(functools.partial(products_kernel, capacity, pieces), grid...  8.35 us
    pallas_call x1, Pallas kernels, adam(): pl.pallas_call(functools.partial(adam_kernel, len(grads)), grid=(members,...  6.19 us
    pallas_call x1, Pallas kernels, gradient(): pl.pallas_call(functools.partial(gradient_kernel, capacity, local_count,...  5.64 us
    ppermute x6, starting transfers between devices, swap(): return lax.ppermute(array, axis, [(i, i ^ offset) for i in range(size)])  3.68 us
    pallas_call x1, Pallas kernels, dispatch(): pl.pallas_call(functools.partial(dispatch_kernel, capacity, groups), in_s...  3.46 us
  transfers between devices with their start and end apart: 8, of which 6 were waited for; matrix products, arithmetic and copies ran while one was open for 0% of the time, Pallas kernels for 12%

profile of v9, /device:TPU:0, one launch (start us, length us, event | category | flops | bytes accessed | tf_op | source)
XLA Modules:
  0.0 109.1 jit_solution(11513500317945372203)
XLA Ops:
  0.6 3.5 %dispatch.1 = (bf16[384,2432]{1,0:T(8,128)(2,1)}, s32[1,256]{1,0:T(1,128)}) custom-call(s32[1,256]{1,0:T(1,128)} %bitcast.17, s32[1,16]{1,0:T(1,128)} %bitcast.18, bf16[256,384]{1,0:T(8,128)(2,1)} %x_hbm.1, bf16[256,2048]{1,0:T(8,128)(2,1)} %g_hbm.1), custom_call_target="tpu_custom_call" | custom-call | flops 478150656 | bytes 3112960 | tf_op jit(solution)/shard_map/dispatch/pallas_call | solution.py:114
  4.1 0.0 copy-start
  4.1 7.4 %all-to-all-start = ((bf16[8,48,2432]{2,1,0:T(8,128)(2,1)}), bf16[8,48,2432]{2,1,0:T(8,128)(2,1)}, u32[]{:S(2)}, u32[]{:S(2)}) async-start(bf16[8,48,2432]{2,1,0:T(8,128)(2,1)} %bitcast.14), calls=%async_computation | async-start | bytes 3735552 | tf_op jit(solution)/shard_map/all_to_all | solution.py:491
  11.5 0.0 copy-done
  11.5 0.3 cast_weight.1.refs_0_
  11.9 0.0 copy-start.1
  11.9 1.6 %collective-permute-start.1 = (bf16[2,96,2048]{2,1,0:T(8,128)(2,1)S(1)}, bf16[2,96,2048]{2,1,0:T(8,128)(2,1)S(1)}, u32[]{:S(2)}, u32[]{:S(2)}) collective-permute-start(bf16[2,96,2048]{2,1,0:T(8,128)(2,1)S(1)} %cast_weight.1.refs_0_), channel_id=1, source_target_pairs={{0,16},{8,24},{16,0},{24,8},{1,17},{9,25},{17,1},{25,9},{2,18},{10... | collective-permute-start | bytes 2359304 | tf_op jit(solution)/shard_map/ppermute | solution.py:484
  13.5 0.0 collective-permute-start
  13.5 17.5 %collective-permute-done.1.refs_2_ = bf16[2,96,2048]{2,1,0:T(8,128)(2,1)S(1)} collective-permute-done((bf16[2,96,2048]{2,1,0:T(8,128)(2,1)S(1)}, bf16[2,96,2048]{2,1,0:T(8,128)(2,1)S(1)}, u32[]{:S(2)}, u32[]{:S(2)}) %collective-permute-start.1) | collective-permute-done | bytes 786464 | tf_op jit(solution)/shard_map/ppermute | solution.py:484
  30.9 0.0 copy-start.9
  30.9 0.0 collective-permute-start.2
  30.9 0.0 collective-permute-done.refs_1_
  30.9 0.0 copy-start.10
  31.0 0.9 copy-done.10
  31.9 1.5 %collective-permute-done.2.refs_3_ = bf16[2,96,2048]{2,1,0:T(8,128)(2,1)} collective-permute-done((bf16[2,96,2048]{2,1,0:T(8,128)(2,1)S(1)}, bf16[2,96,2048]{2,1,0:T(8,128)(2,1)}, u32[]{:S(2)}, u32[]{:S(2)}) %collective-permute-start.2) | collective-permute-done | bytes 786464 | tf_op jit(solution)/shard_map/ppermute | solution.py:484
  33.4 18.5 %all-to-all-done = bf16[8,48,2432]{2,1,0:T(8,128)(2,1)} async-done(((bf16[8,48,2432]{2,1,0:T(8,128)(2,1)}), bf16[8,48,2432]{2,1,0:T(8,128)(2,1)}, u32[]{:S(2)}, u32[]{:S(2)}) %all-to-all-start) | async-done | bytes 1867808 | tf_op jit(solution)/shard_map/all_to_all | solution.py:491
  51.9 0.0 copy-done.1
  51.9 0.0 copy-done.9
  51.9 8.3 %products.1 = bf16[384,2432]{1,0:T(8,128)(2,1)} custom-call(bf16[384,2432]{1,0:T(8,128)(2,1)} %bitcast.3.local_hbm.g_ref.refs_0_.refs_1_.refs_2_, bf16[2,96,2048]{2,1,0:T(8,128)(2,1)} %copy-done.1, bf16[2,96,2048]{2,1,0:T(8,128)(2,1)} %copy-done.10, bf16[2,96,2048]{2,1,0:T(8,128)(2,1)} %copy-done.9, bf16[2,96,2048]{2,1,0:T(8,128)(2,1)} %collective-permute-done.2.refs_3_), custom_call_target="tpu_custom_call" | custom-call | flops 2415919104 | bytes 6291456 | tf_op jit(solution)/shard_map/products/pallas_call | solution.py:296
  60.2 6.8 %all-to-all-start.1 = ((bf16[8,48,2432]{2,1,0:T(8,128)(2,1)}), bf16[8,48,2432]{2,1,0:T(8,128)(2,1)S(1)}, u32[]{:S(2)}, u32[]{:S(2)}) async-start(bf16[8,48,2432]{2,1,0:T(8,128)(2,1)} %bitcast.13), calls=%async_computation.1 | async-start | bytes 3735552 | tf_op jit(solution)/shard_map/all_to_all | solution.py:491
  67.0 0.0 copy-start.3
  67.0 0.0 copy-start.4
  67.1 0.0 copy-start.6
  67.1 0.0 copy-start.7
  67.1 5.6 %gradient.1 = (bf16[2,96,2048]{2,1,0:T(8,128)(2,1)}, bf16[2,96,2048]{2,1,0:T(8,128)(2,1)}, bf16[2,96,2048]{2,1,0:T(8,128)(2,1)}, bf16[2,96,2048]{2,1,0:T(8,128)(2,1)}) custom-call(bf16[384,2432]{1,0:T(8,128)(2,1)} %bitcast.3.local_hbm.g_ref.refs_0_.refs_1_.refs_2_, bf16[384,2432]{1,0:T(8,128)(2,1)} %bitcast.3.local_hbm.g_ref.refs_0_.refs_1_.refs_2_, ...), custom_call_target="tpu_custom_call" | custom-call | flops 1207959552 | bytes 4718592 | tf_op jit(solution)/shard_map/gradient/pallas_call | solution.py:356
  72.7 0.0 collective-permute-start.4
  72.7 0.5 collective-permute-start.3
  73.2 2.0 %collective-permute-done.4.b_ref = bf16[2,96,2048]{2,1,0:T(8,128)(2,1)S(1)} collective-permute-done((bf16[2,96,2048]{2,1,0:T(8,128)(2,1)}, bf16[2,96,2048]{2,1,0:T(8,128)(2,1)S(1)}, u32[]{:S(2)}, u32[]{:S(2)}) %collective-permute-start.4) | collective-permute-done | bytes 786464 | tf_op jit(solution)/shard_map/ppermute | solution.py:484
  75.2 0.0 copy-start.2
  75.2 1.1 %copy-done.2 = bf16[2,96,2048]{2,1,0:T(8,128)(2,1)S(1)} copy-done((bf16[2,96,2048]{2,1,0:T(8,128)(2,1)S(1)}, bf16[2,96,2048]{2,1,0:T(8,128)(2,1)}, u32[]{:S(2)}) %copy-start.2) | copy-done | bytes 786456
  76.4 0.0 copy-start.5
  76.4 0.4 add_parts.1
  76.8 1.6 %collective-permute-start.5 = (bf16[2,96,2048]{2,1,0:T(8,128)(2,1)S(1)}, bf16[2,96,2048]{2,1,0:T(8,128)(2,1)S(1)}, u32[]{:S(2)}, u32[]{:S(2)}) collective-permute-start(bf16[2,96,2048]{2,1,0:T(8,128)(2,1)S(1)} %add_parts.1), channel_id=1, source_target_pairs={{0,16},{8,24},{16,0},{24,8},{1,17},{9,25},{17,1},{25,9},{2,18},{10... | collective-permute-start | bytes 2359304 | tf_op jit(solution)/shard_map/ppermute | solution.py:484
  78.3 0.0 collective-permute-done.3.refs_1_
  78.3 18.1 %collective-permute-done.5.refs_2_ = bf16[2,96,2048]{2,1,0:T(8,128)(2,1)S(1)} collective-permute-done((bf16[2,96,2048]{2,1,0:T(8,128)(2,1)S(1)}, bf16[2,96,2048]{2,1,0:T(8,128)(2,1)S(1)}, u32[]{:S(2)}, u32[]{:S(2)}) %collective-permute-start.5) | collective-permute-done | bytes 786464 | tf_op jit(solution)/shard_map/ppermute | solution.py:484
  96.4 0.0 copy-done.3
  96.4 0.0 copy-done.4
  96.4 0.0 copy-done.6
  96.4 0.0 copy-done.7
  96.4 0.0 copy-done.5
  96.4 0.0 copy-start.8
  96.4 6.2 %adam.1 = (f32[2,96,2048]{2,1,0:T(8,128)}, bf16[2,96,2048]{2,1,0:T(8,128)(2,1)}, f32[2,16,96]{2,1,0:T(8,128)}, bf16[2,96,2048]{2,1,0:T(8,128)(2,1)}, f32[2,16,96]{2,1,0:T(8,128)}) custom-call(f32[2,96,2048]{2,1,0:T(8,128)S(1)} %copy-done, bf16[2,96,2048]{2,1,0:T(8,128)(2,1)S(1)} %copy-done.3, f32[2,16,96]{2,1,0:T(8,128)S(1)} %bitcast.11, ...), custom_call_target="tpu_custom_call" | custom-call | flops 15728640 | bytes 7077888 | tf_op jit(solution)/shard_map/adam/pallas_call | solution.py:457
  102.6 4.8 %all-to-all-done.1 = bf16[8,48,2432]{2,1,0:T(8,128)(2,1)S(1)} async-done(((bf16[8,48,2432]{2,1,0:T(8,128)(2,1)}), bf16[8,48,2432]{2,1,0:T(8,128)(2,1)S(1)}, u32[]{:S(2)}, u32[]{:S(2)}) %all-to-all-start.1) | async-done | bytes 1867808 | tf_op jit(solution)/shard_map/all_to_all | solution.py:491
  107.5 0.0 copy-done.8
  107.5 1.6 %collect.1 = (bf16[256,2048]{1,0:T(8,128)(2,1)}, bf16[256,384]{1,0:T(8,128)(2,1)}) custom-call(s32[1,256]{1,0:T(1,128)S(1)} %copy-done.8, bf16[384,2432]{1,0:T(8,128)(2,1)S(1)} %bitcast.10), custom_call_target="tpu_custom_call" | custom-call | flops 478150656 | bytes 3112960 | tf_op jit(solution)/shard_map/collect/pallas_call | solution.py:187
Async XLA Ops:
  4.1 7.4 %copy-start = (f32[2,96,2048]{2,1,0:T(8,128)S(1)}, f32[2,96,2048]{2,1,0:T(8,128)}, u32[]{:S(2)}) copy-start(f32[2,96,2048]{2,1,0:T(8,128)} %master_ref.1) | copy-start | bytes 4718596
  4.1 47.8 %all-to-all-start = ((bf16[8,48,2432]{2,1,0:T(8,128)(2,1)}), bf16[8,48,2432]{2,1,0:T(8,128)(2,1)}, u32[]{:S(2)}, u32[]{:S(2)}) async-start(bf16[8,48,2432]{2,1,0:T(8,128)(2,1)} %bitcast.14), calls=%async_computation | async-start | bytes 3735552 | tf_op jit(solution)/shard_map/all_to_all | solution.py:491
  11.9 40.0 %copy-start.1 = (bf16[2,96,2048]{2,1,0:T(8,128)(2,1)}, bf16[2,96,2048]{2,1,0:T(8,128)(2,1)S(1)}, u32[]{:S(2)}) copy-start(bf16[2,96,2048]{2,1,0:T(8,128)(2,1)S(1)} %cast_weight.1.refs_0_) | copy-start | bytes 2359300
  11.9 19.1 %collective-permute-start.1 = (bf16[2,96,2048]{2,1,0:T(8,128)(2,1)S(1)}, bf16[2,96,2048]{2,1,0:T(8,128)(2,1)S(1)}, u32[]{:S(2)}, u32[]{:S(2)}) collective-permute-start(bf16[2,96,2048]{2,1,0:T(8,128)(2,1)S(1)} %cast_weight.1.refs_0_), channel_id=1, source_target_pairs={{0,16},{8,24},{16,0},{24,8},{1,17},{9,25},{17,1},{25,9},{2,18},{10... | collective-permute-start | bytes 2359304 | tf_op jit(solution)/shard_map/ppermute | solution.py:484
  13.5 17.5 %collective-permute-start = (bf16[2,96,2048]{2,1,0:T(8,128)(2,1)S(1)}, bf16[2,96,2048]{2,1,0:T(8,128)(2,1)S(1)}, u32[]{:S(2)}, u32[]{:S(2)}) collective-permute-start(bf16[2,96,2048]{2,1,0:T(8,128)(2,1)S(1)} %cast_weight.1.refs_0_), channel_id=1, source_target_pairs={{0,8},{8,0},{16,24},{24,16},{1,9},{9,1},{17,25},{25,17},{2,10},{10... | collective-permute-start | bytes 2359304 | tf_op jit(solution)/shard_map/ppermute | solution.py:484
  30.9 20.9 %copy-start.9 = (bf16[2,96,2048]{2,1,0:T(8,128)(2,1)}, bf16[2,96,2048]{2,1,0:T(8,128)(2,1)S(1)}, u32[]{:S(2)}) copy-start(bf16[2,96,2048]{2,1,0:T(8,128)(2,1)S(1)} %collective-permute-done.1.refs_2_) | copy-start | bytes 2359300
  30.9 2.4 %collective-permute-start.2 = (bf16[2,96,2048]{2,1,0:T(8,128)(2,1)S(1)}, bf16[2,96,2048]{2,1,0:T(8,128)(2,1)}, u32[]{:S(2)}, u32[]{:S(2)}) collective-permute-start(bf16[2,96,2048]{2,1,0:T(8,128)(2,1)S(1)} %collective-permute-done.1.refs_2_), channel_id=1, source_target_pairs={{0,8},{8,0},{16,24},{24,16},{1,9},{9,1},{17,25},{25,17},{2,10},{10... | collective-permute-start | bytes 2359304 | tf_op jit(solution)/shard_map/ppermute | solution.py:484
  30.9 0.9 copy-start.10
  60.2 47.2 %all-to-all-start.1 = ((bf16[8,48,2432]{2,1,0:T(8,128)(2,1)}), bf16[8,48,2432]{2,1,0:T(8,128)(2,1)S(1)}, u32[]{:S(2)}, u32[]{:S(2)}) async-start(bf16[8,48,2432]{2,1,0:T(8,128)(2,1)} %bitcast.13), calls=%async_computation.1 | async-start | bytes 3735552 | tf_op jit(solution)/shard_map/all_to_all | solution.py:491
  67.0 29.4 %copy-start.3 = (bf16[2,96,2048]{2,1,0:T(8,128)(2,1)S(1)}, bf16[2,96,2048]{2,1,0:T(8,128)(2,1)}, u32[]{:S(2)}) copy-start(bf16[2,96,2048]{2,1,0:T(8,128)(2,1)} %mc_ref.1) | copy-start | bytes 2359300
  67.0 29.4 %copy-start.4 = (bf16[2,96,2048]{2,1,0:T(8,128)(2,1)S(1)}, bf16[2,96,2048]{2,1,0:T(8,128)(2,1)}, u32[]{:S(2)}) copy-start(bf16[2,96,2048]{2,1,0:T(8,128)(2,1)} %vc_ref.1) | copy-start | bytes 2359300
  67.1 29.3 %copy-start.6 = (f32[2,96,16]{1,2,0:T(8,128)S(1)}, f32[2,96,16]{1,2,0:T(8,128)}, u32[]{:S(2)}) copy-start(f32[2,96,16]{1,2,0:T(8,128)} %param.11) | copy-start | bytes 36868
  67.1 29.3 %copy-start.7 = (f32[2,96,16]{1,2,0:T(8,128)S(1)}, f32[2,96,16]{1,2,0:T(8,128)}, u32[]{:S(2)}) copy-start(f32[2,96,16]{1,2,0:T(8,128)} %param.13) | copy-start | bytes 36868
  72.7 2.5 %collective-permute-start.4 = (bf16[2,96,2048]{2,1,0:T(8,128)(2,1)}, bf16[2,96,2048]{2,1,0:T(8,128)(2,1)S(1)}, u32[]{:S(2)}, u32[]{:S(2)}) collective-permute-start(bf16[2,96,2048]{2,1,0:T(8,128)(2,1)} %get-tuple-element.35), channel_id=1, source_target_pairs={{0,8},{8,0},{16,24},{24,16},{1,9},{9,1},{17,25},{25,17},{2,10},{10... | collective-permute-start | bytes 2359304 | tf_op jit(solution)/shard_map/ppermute | solution.py:484
  72.7 5.6 %collective-permute-start.3 = (bf16[2,96,2048]{2,1,0:T(8,128)(2,1)}, bf16[2,96,2048]{2,1,0:T(8,128)(2,1)S(1)}, u32[]{:S(2)}, u32[]{:S(2)}) collective-permute-start(bf16[2,96,2048]{2,1,0:T(8,128)(2,1)} %get-tuple-element.33), channel_id=1, source_target_pairs={{0,8},{8,0},{16,24},{24,16},{1,9},{9,1},{17,25},{25,17},{2,10},{10... | collective-permute-start | bytes 2359304 | tf_op jit(solution)/shard_map/ppermute | solution.py:484
  75.2 1.1 %copy-start.2 = (bf16[2,96,2048]{2,1,0:T(8,128)(2,1)S(1)}, bf16[2,96,2048]{2,1,0:T(8,128)(2,1)}, u32[]{:S(2)}) copy-start(bf16[2,96,2048]{2,1,0:T(8,128)(2,1)} %get-tuple-element.34.a_ref) | copy-start | bytes 2359300
  76.4 20.1 %copy-start.5 = (bf16[2,96,2048]{2,1,0:T(8,128)(2,1)S(1)}, bf16[2,96,2048]{2,1,0:T(8,128)(2,1)}, u32[]{:S(2)}) copy-start(bf16[2,96,2048]{2,1,0:T(8,128)(2,1)} %get-tuple-element.32.refs_0_) | copy-start | bytes 2359300
  76.8 19.6 %collective-permute-start.5 = (bf16[2,96,2048]{2,1,0:T(8,128)(2,1)S(1)}, bf16[2,96,2048]{2,1,0:T(8,128)(2,1)S(1)}, u32[]{:S(2)}, u32[]{:S(2)}) collective-permute-start(bf16[2,96,2048]{2,1,0:T(8,128)(2,1)S(1)} %add_parts.1), channel_id=1, source_target_pairs={{0,16},{8,24},{16,0},{24,8},{1,17},{9,25},{17,1},{25,9},{2,18},{10... | collective-permute-start | bytes 2359304 | tf_op jit(solution)/shard_map/ppermute | solution.py:484
  96.4 11.0 %copy-start.8 = (s32[1,256]{1,0:T(1,128)S(1)}, s32[1,256]{1,0:T(1,128)}, u32[]{:S(2)}) copy-start(s32[1,256]{1,0:T(1,128)} %get-tuple-element.25.target_hbm) | copy-start | bytes 3076

commit v10 on v9

--- a/solution.py
+++ b/solution.py
@@ -67,19 +67,20 @@
     capacity, groups, route_hbm, placement_hbm, x_hbm, g_hbm, sent_hbm, target_hbm,
     route_ref, placement_ref, target_ref, x_ref, g_ref, sent_ref, key_sems, in_sems, out_sems,
 ):
-    tiles, _, tile = g_ref.shape
-    hidden = x_ref.shape[1]
+    row_count, hidden = x_ref.shape
+    width = g_ref.shape[1]
+    tiles = out_sems.shape[0] - 1
+    tile = width // tiles
+    parts = in_sems.shape[0] - 1
     keys = [
         pltpu.make_async_copy(route_hbm, route_ref, key_sems.at[0]),
         pltpu.make_async_copy(placement_hbm, placement_ref, key_sems.at[1]),
     ]
-    loads = [
-        pltpu.make_async_copy(
-            g_hbm.at[:, pl.ds(j * tile, tile)], g_ref.at[j], in_sems.at[j]
-        )
-        for j in range(tiles)
+    bands = [pl.ds(i * (row_count // parts), row_count // parts) for i in range(parts)]
+    loads = [pltpu.make_async_copy(x_hbm, x_ref, in_sems.at[parts])] + [
+        pltpu.make_async_copy(g_hbm.at[band], g_ref.at[band], in_sems.at[i])
+        for i, band in enumerate(bands)
     ]
-    loads.append(pltpu.make_async_copy(x_hbm, x_ref, in_sems.at[tiles]))
     for load in keys + loads:
         load.start()
     for load in keys:
@@ -90,9 +91,10 @@
     stores[0].start()
     places = place_matrix(target, sent_ref.shape[0])
     for j in range(tiles + 1):
-        loads[j].wait()
-        columns = pl.ds(j * tile, tile if j < tiles else hidden)
-        rows = g_ref[j] if j < tiles else x_ref[...]
+        for load in loads[:1] if j == 0 else loads[1:] if j == 1 else []:
+            load.wait()
+        columns = pl.ds((j - 1) * tile, tile) if j else pl.ds(width, hidden)
+        rows = g_ref[:, columns] if j else x_ref[...]
         sent_ref[:, columns] = jnp.dot(places, rows, preferred_element_type=F32).astype(BF16)
         store = pltpu.make_async_copy(
             sent_ref.at[:, columns], sent_hbm.at[:, columns], out_sems.at[j]
@@ -109,6 +111,7 @@
     expert_count = placement.shape[0]
     tile = min(width, 512)
     tiles = width // tile
+    parts = 4 if row_count % 64 == 0 else 1
     places = expert_count * capacity
     hbm = pl.BlockSpec(memory_space=pl.ANY)
     return pl.pallas_call(
@@ -124,10 +127,10 @@
             pltpu.VMEM((1, expert_count), jnp.int32),
             pltpu.VMEM((1, row_count), jnp.int32),
             pltpu.VMEM((row_count, hidden), BF16),
-            pltpu.VMEM((tiles, row_count, tile), BF16),
+            pltpu.VMEM((row_count, width), BF16),
             pltpu.VMEM((places, width + hidden), BF16),
             pltpu.SemaphoreType.DMA((3,)),
-            pltpu.SemaphoreType.DMA((tiles + 1,)),
+            pltpu.SemaphoreType.DMA((parts + 1,)),
             pltpu.SemaphoreType.DMA((tiles + 1,)),
         ],
         compiler_params=pltpu.CompilerParams(vmem_limit_bytes=LARGE_LIMIT),
@@ -218,55 +221,69 @@
     return jnp.concatenate([jnp.where(member == e, x, zero) for e in range(local_count)], axis=1)
 
 
-def products_kernel(capacity, pieces, local_hbm, *refs):
-    w_hbm, out_hbm = refs[:pieces], refs[pieces]
-    x_ref, g_ref, w_ref, wide_ref, total_ref, out_ref, g_sems, w_sems, out_sems = refs[pieces + 1 :]
+def join_kernel(*refs):
+    piece_refs, out_ref = refs[:-1], refs[-1]
+    pieces = len(piece_refs)
+    here = lax.axis_index("rep") if pieces > 1 else 0
+    for i, ref in enumerate(piece_refs):
+        owner = jnp.bitwise_xor(here, i) if pieces > 1 else 0
+        for e in range(out_ref.shape[1]):
+            out_ref[0, e, owner] = ref[e]
+
+
+def join_weight(weight):
+    local_count, rows, width = weight[0].shape
+    pieces = len(weight)
+    tile = min(width, 512)
+    tiles = width // tile
+    joined = pl.pallas_call(
+        join_kernel,
+        grid=(tiles,),
+        in_specs=[pl.BlockSpec((local_count, rows, tile), lambda j: (0, 0, j))] * pieces,
+        out_specs=pl.BlockSpec((1, local_count, pieces, rows, tile), lambda j: (j, 0, 0, 0, 0)),
+        out_shape=jax.ShapeDtypeStruct((tiles, local_count, pieces, rows, tile), BF16),
+        compiler_params=pltpu.CompilerParams(
+            vmem_limit_bytes=LARGE_LIMIT, dimension_semantics=("arbitrary",)
+        ),
+        cost_estimate=cost(0, 4 * local_count * pieces * rows * width),
+        name="join_weight",
+    )(*weight)
+    return joined.reshape(tiles, local_count * pieces * rows, tile)
+
+
+def products_kernel(
+    capacity, local_count, local_hbm, w_hbm, out_hbm,
+    local_ref, w_ref, wide_ref, total_ref, out_ref, local_sem, w_sems, out_sems,
+):
     step = pl.program_id(0)
-    steps, local_count, _, _, tile = w_ref.shape
+    steps, _, tile = w_ref.shape
     hidden = wide_ref.shape[1] // local_count
     columns = pl.ds(pl.multiple_of(step * tile, tile), tile)
-    here = lax.axis_index("rep") if pieces > 1 else 0
-
-    def weight_loads(j, span):
-        return [
-            pltpu.make_async_copy(
-                piece.at[e, :, span],
-                w_ref.at[j, e, jnp.bitwise_xor(here, i) if pieces > 1 else 0],
-                w_sems.at[j, i, e],
-            )
-            for i, piece in enumerate(w_hbm)
-            for e in range(local_count)
-        ]
-
-    def row_load(j, span):
-        return pltpu.make_async_copy(local_hbm.at[:, span], g_ref.at[j], g_sems.at[j])
+
+    def weight_load(j):
+        return pltpu.make_async_copy(w_hbm.at[j], w_ref.at[j], w_sems.at[j])
 
     @pl.when(step == 0)
     def _():
-        x_load = pltpu.make_async_copy(
-            local_hbm.at[:, pl.ds(steps * tile, hidden)], x_ref, g_sems.at[steps]
-        )
-        x_load.start()
-        for j in range(steps):
-            span = pl.ds(j * tile, tile)
-            for load in weight_loads(j, span) + [row_load(j, span)]:
-                load.start()
-        x_load.wait()
-        wide_ref[...] = spread(x_ref[...], capacity, local_count)
+        local_load = pltpu.make_async_copy(local_hbm, local_ref, local_sem)
+        local_load.start()
+        weight_load(0).start()
         total_ref[...] = jnp.zeros_like(total_ref)
-
-    for load in weight_loads(step, columns):
-        load.wait()
-    weight = w_ref[step].reshape(local_count * hidden, tile)
+        local_load.wait()
+        for j in range(1, steps):
+            weight_load(j).start()
+        wide_ref[...] = spread(local_ref[:, steps * tile :], capacity, local_count)
+
+    weight_load(step).wait()
+    weight = w_ref[step]
     out_ref[:, columns] = jnp.dot(
         wide_ref[...], weight, preferred_element_type=F32
     ).astype(BF16)
     pltpu.make_async_copy(
         out_ref.at[:, columns], out_hbm.at[:, columns], out_sems.at[step]
     ).start()
-    row_load(step, columns).wait()
     total_ref[...] += lax.dot_general(
-        g_ref[step], weight, (((1,), (1,)), ((), ())), preferred_element_type=F32
+        local_ref[:, columns], weight, (((1,), (1,)), ((), ())), preferred_element_type=F32
     )
 
     @pl.when(step == steps - 1)
@@ -285,40 +302,33 @@
         final.wait()
 
 
-def products(local, weight, capacity):
-    local_count, slice_rows, width = weight[0].shape
-    pieces = len(weight)
-    hidden = slice_rows * pieces
+def products(local, weight, capacity, local_count):
+    tiles, wide, tile = weight.shape
+    width = tiles * tile
     total = local.shape[0]
-    tile = min(width, 512)
-    tiles = width // tile
     hbm = pl.BlockSpec(memory_space=pl.ANY)
     return pl.pallas_call(
-        functools.partial(products_kernel, capacity, pieces),
+        functools.partial(products_kernel, capacity, local_count),
         grid=(tiles,),
-        in_specs=[hbm] * (1 + pieces),
+        in_specs=[hbm, hbm],
         out_specs=hbm,
         out_shape=jax.ShapeDtypeStruct(local.shape, BF16),
         scratch_shapes=[
-            pltpu.VMEM((total, hidden), BF16),
-            pltpu.VMEM((tiles, total, tile), BF16),
-            pltpu.VMEM((tiles, local_count, pieces, slice_rows, tile), BF16),
-            pltpu.VMEM((total, local_count * hidden), BF16),
-            pltpu.VMEM((total, local_count * hidden), F32),
             pltpu.VMEM(local.shape, BF16),
-            pltpu.SemaphoreType.DMA((tiles + 1,)),
-            pltpu.SemaphoreType.DMA((tiles, pieces, local_count)),
+            pltpu.VMEM(weight.shape, BF16),
+            pltpu.VMEM((total, wide), BF16),
+            pltpu.VMEM((total, wide), F32),
+            pltpu.VMEM(local.shape, BF16),
+            pltpu.SemaphoreType.DMA,
+            pltpu.SemaphoreType.DMA((tiles,)),
             pltpu.SemaphoreType.DMA((tiles + 1,)),
         ],
         compiler_params=pltpu.CompilerParams(
             vmem_limit_bytes=LARGE_LIMIT, dimension_semantics=("arbitrary",)
         ),
-        cost_estimate=cost(
-            4 * total * local_count * hidden * width,
-            2 * (local_count * hidden + 2 * total) * width,
-        ),
+        cost_estimate=cost(4 * total * wide * width, 2 * (wide + 2 * total) * width),
         name="products",
-    )(local, *weight)
+    )(local, weight)
 
 
 def gradient_kernel(capacity, local_count, parts, factor, g_ref, *refs):
@@ -522,8 +532,8 @@
     sent, target = dispatch(route, placement, x_rows, y_cot, capacity, groups)
     local = exchange(sent, groups)
     early_master, target = lax.optimization_barrier((master_weight, target))
-    weight = gather_weight(cast_weight(early_master), replicas)
-    results = products(local, weight, capacity)
+    weight = join_weight(gather_weight(cast_weight(early_master), replicas))
+    results = products(local, weight, capacity, local_count)
     local, results = lax.optimization_barrier((local, results))
     home = exchange(results, groups)
 

time: 111 us -> 110 us (level)
  waiting for transfers between devices: 62.4 us -> 58 us
  Pallas kernels: 26 us -> 27.7 us
  local copies, waits for them, and re-layouts: 2.08 us -> 3.33 us
    all_to_all x2, waiting for transfers between devices: 23.4 us -> 18.2 us  [exchange(): lax.all_to_all(parts, 'grp', split_axis=0, concat_axis=0, tiled=True, axi...]
    pallas_call x1 -> x2, Pallas kernels: 8.35 us -> 10.4 us  [the longest x1 6.14 us: products(): pl.pallas_call(functools.partial(products_kernel, capacity, local_count),...]
    unnamed x22 -> x26, local copies, waits for them, and re-layouts: 2.08 us -> 3.33 us
  transfers between devices with their start and end apart: 8 -> 8, of which waited for: 6 -> 6; matrix products, arithmetic and copies ran while one was open for 0% -> 0% of each run, Pallas kernels for 12% -> 16%
where the time goes in v10:
time: 110 us; the launch traced here: 108 us
  waiting for transfers between devices  58 us (53%)
  Pallas kernels  27.7 us (25%)
  starting transfers between devices  17.9 us (16%)
  local copies, waits for them, and re-layouts  3.33 us (3%)
    ppermute x6, waiting for transfers between devices, swap(): return lax.ppermute(array, axis, [(i, i ^ offset) for i in range(size)])  39.8 us
    all_to_all x2, waiting for transfers between devices, exchange(): lax.all_to_all(parts, 'grp', split_axis=0, concat_axis=0, tiled=True, axi...  18.2 us
    all_to_all x2, starting transfers between devices, exchange(): lax.all_to_all(parts, 'grp', split_axis=0, concat_axis=0, tiled=True, axi...  14.2 us
    pallas_call x1, Pallas kernels, adam(): pl.pallas_call(functools.partial(adam_kernel, len(grads)), grid=(members,...  6.19 us
    pallas_call x1, Pallas kernels, products(): pl.pallas_call(functools.partial(products_kernel, capacity, local_count),...  6.14 us
    pallas_call x1, Pallas kernels, gradient(): pl.pallas_call(functools.partial(gradient_kernel, capacity, local_count,...  5.64 us
    pallas_call x1, Pallas kernels, join_weight(): pl.pallas_call(join_kernel, grid=(tiles,), in_specs=[pl.BlockSpec((local_...  4.29 us
    ppermute x6, starting transfers between devices, swap(): return lax.ppermute(array, axis, [(i, i ^ offset) for i in range(size)])  3.68 us
  transfers between devices with their start and end apart: 8, of which 6 were waited for; matrix products, arithmetic and copies ran while one was open for 0% of the time, Pallas kernels for 16%

profile of v10, /device:TPU:0, one launch (start us, length us, event | category | flops | bytes accessed | tf_op | source)
XLA Modules:
  0.0 107.7 jit_solution(15171550444884838233)
XLA Ops:
  0.6 3.1 %dispatch.1 = (bf16[384,2432]{1,0:T(8,128)(2,1)}, s32[1,256]{1,0:T(1,128)}) custom-call(s32[1,256]{1,0:T(1,128)} %bitcast.24, s32[1,16]{1,0:T(1,128)} %bitcast.25, bf16[256,384]{1,0:T(8,128)(2,1)} %x_hbm.1, bf16[256,2048]{1,0:T(8,128)(2,1)} %g_hbm.1), custom_call_target="tpu_custom_call" | custom-call | flops 478150656 | bytes 3112960 | tf_op jit(solution)/shard_map/dispatch/pallas_call | solution.py:117
  3.7 0.0 copy-start
  3.7 7.4 %all-to-all-start = ((bf16[8,48,2432]{2,1,0:T(8,128)(2,1)}), bf16[8,48,2432]{2,1,0:T(8,128)(2,1)S(1)}, u32[]{:S(2)}, u32[]{:S(2)}) async-start(bf16[8,48,2432]{2,1,0:T(8,128)(2,1)} %bitcast.21), calls=%async_computation | async-start | bytes 3735552 | tf_op jit(solution)/shard_map/all_to_all | solution.py:501
  11.1 0.0 copy-done
  11.1 0.3 cast_weight.1.refs_0_
  11.5 0.0 copy-start.1
  11.5 1.6 %collective-permute-start.1 = (bf16[2,96,2048]{2,1,0:T(8,128)(2,1)S(1)}, bf16[2,96,2048]{2,1,0:T(8,128)(2,1)S(1)}, u32[]{:S(2)}, u32[]{:S(2)}) collective-permute-start(bf16[2,96,2048]{2,1,0:T(8,128)(2,1)S(1)} %cast_weight.1.refs_0_), channel_id=1, source_target_pairs={{0,16},{8,24},{16,0},{24,8},{1,17},{9,25},{17,1},{25,9},{2,18},{10... | collective-permute-start | bytes 2359304 | tf_op jit(solution)/shard_map/ppermute | solution.py:494
  13.1 0.0 collective-permute-start
  13.1 17.5 %collective-permute-done.1.refs_2_ = bf16[2,96,2048]{2,1,0:T(8,128)(2,1)S(1)} collective-permute-done((bf16[2,96,2048]{2,1,0:T(8,128)(2,1)S(1)}, bf16[2,96,2048]{2,1,0:T(8,128)(2,1)S(1)}, u32[]{:S(2)}, u32[]{:S(2)}) %collective-permute-start.1) | collective-permute-done | bytes 786464 | tf_op jit(solution)/shard_map/ppermute | solution.py:494
  30.6 0.0 copy-start.10
  30.6 0.0 collective-permute-start.2
  30.6 0.0 collective-permute-done.refs_1_
  30.6 0.0 copy-start.11
  30.6 2.3 %collective-permute-done.2.refs_3_ = bf16[2,96,2048]{2,1,0:T(8,128)(2,1)S(1)} collective-permute-done((bf16[2,96,2048]{2,1,0:T(8,128)(2,1)S(1)}, bf16[2,96,2048]{2,1,0:T(8,128)(2,1)S(1)}, u32[]{:S(2)}, u32[]{:S(2)}) %collective-permute-start.2) | collective-permute-done | bytes 786464 | tf_op jit(solution)/shard_map/ppermute | solution.py:494
  32.9 0.0 copy-done.1
  32.9 0.0 copy-done.10
  32.9 0.0 copy-done.11
  32.9 0.0 copy-start.12
  32.9 0.9 copy-done.12
  33.8 4.3 %join_weight.1 = bf16[4,2,4,96,512]{4,3,2,1,0:T(8,128)(2,1)} custom-call(bf16[2,96,2048]{2,1,0:T(8,128)(2,1)} %copy-done.1, bf16[2,96,2048]{2,1,0:T(8,128)(2,1)} %copy-done.11, bf16[2,96,2048]{2,1,0:T(8,128)(2,1)} %copy-done.10, bf16[2,96,2048]{2,1,0:T(8,128)(2,1)} %copy-done.12), custom_call_target="tpu_custom_call" | custom-call | bytes 6291456 | tf_op jit(solution)/shard_map/join_weight/pallas_call | solution.py:239
  38.1 13.4 %all-to-all-done = bf16[8,48,2432]{2,1,0:T(8,128)(2,1)S(1)} async-done(((bf16[8,48,2432]{2,1,0:T(8,128)(2,1)}), bf16[8,48,2432]{2,1,0:T(8,128)(2,1)S(1)}, u32[]{:S(2)}, u32[]{:S(2)}) %all-to-all-start) | async-done | bytes 1867808 | tf_op jit(solution)/shard_map/all_to_all | solution.py:501
  51.4 0.0 copy-start.9
  51.4 1.3 %copy-done.9 = bf16[8,48,2432]{2,1,0:T(8,128)(2,1)} copy-done((bf16[8,48,2432]{2,1,0:T(8,128)(2,1)}, bf16[8,48,2432]{2,1,0:T(8,128)(2,1)S(1)}, u32[]{:S(2)}) %copy-start.9) | copy-done | bytes 1867800
  52.7 6.1 %products.1 = bf16[384,2432]{1,0:T(8,128)(2,1)} custom-call(bf16[384,2432]{1,0:T(8,128)(2,1)} %bitcast.14, bf16[4,768,512]{2,1,0:T(8,128)(2,1)} %bitcast.19), custom_call_target="tpu_custom_call" | custom-call | flops 2415919104 | bytes 6291456 | tf_op jit(solution)/shard_map/products/pallas_call | solution.py:310
  58.8 6.8 %all-to-all-start.1 = ((bf16[8,48,2432]{2,1,0:T(8,128)(2,1)}), bf16[8,48,2432]{2,1,0:T(8,128)(2,1)S(1)}, u32[]{:S(2)}, u32[]{:S(2)}) async-start(bf16[8,48,2432]{2,1,0:T(8,128)(2,1)} %bitcast.20), calls=%async_computation.1 | async-start | bytes 3735552 | tf_op jit(solution)/shard_map/all_to_all | solution.py:501
  65.6 0.0 copy-start.3
  65.6 0.0 copy-start.4
  65.6 0.0 copy-start.6
  65.6 0.0 copy-start.7
  65.7 5.6 %gradient.1 = (bf16[2,96,2048]{2,1,0:T(8,128)(2,1)}, bf16[2,96,2048]{2,1,0:T(8,128)(2,1)}, bf16[2,96,2048]{2,1,0:T(8,128)(2,1)}, bf16[2,96,2048]{2,1,0:T(8,128)(2,1)}) custom-call(bf16[384,2432]{1,0:T(8,128)(2,1)} %bitcast.15, bf16[384,2432]{1,0:T(8,128)(2,1)} %bitcast.16, bf16[384,2432]{1,0:T(8,128)(2,1)} %bitcast.17, bf16[384,2432]{1,0:T(8,128)(2,1)} %bitcast.18), custom_call_target="tpu_custom_call" | custom-call | flops 1207959552 | bytes 4718592 | tf_op jit(solution)/shard_map/gradient/pallas_call | solution.py:366
  71.3 0.0 collective-permute-start.4
  71.3 0.5 collective-permute-start.3
  71.8 2.0 %collective-permute-done.4.b_ref = bf16[2,96,2048]{2,1,0:T(8,128)(2,1)S(1)} collective-permute-done((bf16[2,96,2048]{2,1,0:T(8,128)(2,1)}, bf16[2,96,2048]{2,1,0:T(8,128)(2,1)S(1)}, u32[]{:S(2)}, u32[]{:S(2)}) %collective-permute-start.4) | collective-permute-done | bytes 786464 | tf_op jit(solution)/shard_map/ppermute | solution.py:494
  73.8 0.0 copy-start.2
  73.8 1.1 %copy-done.2 = bf16[2,96,2048]{2,1,0:T(8,128)(2,1)S(1)} copy-done((bf16[2,96,2048]{2,1,0:T(8,128)(2,1)S(1)}, bf16[2,96,2048]{2,1,0:T(8,128)(2,1)}, u32[]{:S(2)}) %copy-start.2) | copy-done | bytes 786456
  74.9 0.0 copy-start.5
  74.9 0.4 add_parts.1
  75.3 1.6 %collective-permute-start.5 = (bf16[2,96,2048]{2,1,0:T(8,128)(2,1)S(1)}, bf16[2,96,2048]{2,1,0:T(8,128)(2,1)S(1)}, u32[]{:S(2)}, u32[]{:S(2)}) collective-permute-start(bf16[2,96,2048]{2,1,0:T(8,128)(2,1)S(1)} %add_parts.1), channel_id=1, source_target_pairs={{0,16},{8,24},{16,0},{24,8},{1,17},{9,25},{17,1},{25,9},{2,18},{10... | collective-permute-start | bytes 2359304 | tf_op jit(solution)/shard_map/ppermute | solution.py:494
  76.9 0.0 collective-permute-done.3.refs_1_
  76.9 18.1 %collective-permute-done.5.refs_2_ = bf16[2,96,2048]{2,1,0:T(8,128)(2,1)S(1)} collective-permute-done((bf16[2,96,2048]{2,1,0:T(8,128)(2,1)S(1)}, bf16[2,96,2048]{2,1,0:T(8,128)(2,1)S(1)}, u32[]{:S(2)}, u32[]{:S(2)}) %collective-permute-start.5) | collective-permute-done | bytes 786464 | tf_op jit(solution)/shard_map/ppermute | solution.py:494
  95.0 0.0 copy-done.3
  95.0 0.0 copy-done.4
  95.0 0.0 copy-done.6
  95.0 0.0 copy-done.7
  95.0 0.0 copy-done.5
  95.0 0.0 copy-start.8
  95.0 6.2 %adam.1 = (f32[2,96,2048]{2,1,0:T(8,128)}, bf16[2,96,2048]{2,1,0:T(8,128)(2,1)}, f32[2,16,96]{2,1,0:T(8,128)}, bf16[2,96,2048]{2,1,0:T(8,128)(2,1)}, f32[2,16,96]{2,1,0:T(8,128)}) custom-call(f32[2,96,2048]{2,1,0:T(8,128)S(1)} %copy-done, bf16[2,96,2048]{2,1,0:T(8,128)(2,1)S(1)} %copy-done.3, f32[2,16,96]{2,1,0:T(8,128)S(1)} %bitcast.12, ...), custom_call_target="tpu_custom_call" | custom-call | flops 15728640 | bytes 7077888 | tf_op jit(solution)/shard_map/adam/pallas_call | solution.py:467
  101.2 4.8 %all-to-all-done.1 = bf16[8,48,2432]{2,1,0:T(8,128)(2,1)S(1)} async-done(((bf16[8,48,2432]{2,1,0:T(8,128)(2,1)}), bf16[8,48,2432]{2,1,0:T(8,128)(2,1)S(1)}, u32[]{:S(2)}, u32[]{:S(2)}) %all-to-all-start.1) | async-done | bytes 1867808 | tf_op jit(solution)/shard_map/all_to_all | solution.py:501
  106.0 0.0 copy-done.8
  106.0 1.6 %collect.1 = (bf16[256,2048]{1,0:T(8,128)(2,1)}, bf16[256,384]{1,0:T(8,128)(2,1)}) custom-call(s32[1,256]{1,0:T(1,128)S(1)} %copy-done.8, bf16[384,2432]{1,0:T(8,128)(2,1)S(1)} %bitcast.11), custom_call_target="tpu_custom_call" | custom-call | flops 478150656 | bytes 3112960 | tf_op jit(solution)/shard_map/collect/pallas_call | solution.py:190
Async XLA Ops:
  3.7 7.4 %copy-start = (f32[2,96,2048]{2,1,0:T(8,128)S(1)}, f32[2,96,2048]{2,1,0:T(8,128)}, u32[]{:S(2)}) copy-start(f32[2,96,2048]{2,1,0:T(8,128)} %master_ref.1) | copy-start | bytes 4718596
  3.7 47.7 %all-to-all-start = ((bf16[8,48,2432]{2,1,0:T(8,128)(2,1)}), bf16[8,48,2432]{2,1,0:T(8,128)(2,1)S(1)}, u32[]{:S(2)}, u32[]{:S(2)}) async-start(bf16[8,48,2432]{2,1,0:T(8,128)(2,1)} %bitcast.21), calls=%async_computation | async-start | bytes 3735552 | tf_op jit(solution)/shard_map/all_to_all | solution.py:501
  11.5 21.4 %copy-start.1 = (bf16[2,96,2048]{2,1,0:T(8,128)(2,1)}, bf16[2,96,2048]{2,1,0:T(8,128)(2,1)S(1)}, u32[]{:S(2)}) copy-start(bf16[2,96,2048]{2,1,0:T(8,128)(2,1)S(1)} %cast_weight.1.refs_0_) | copy-start | bytes 2359300
  11.5 19.1 %collective-permute-start.1 = (bf16[2,96,2048]{2,1,0:T(8,128)(2,1)S(1)}, bf16[2,96,2048]{2,1,0:T(8,128)(2,1)S(1)}, u32[]{:S(2)}, u32[]{:S(2)}) collective-permute-start(bf16[2,96,2048]{2,1,0:T(8,128)(2,1)S(1)} %cast_weight.1.refs_0_), channel_id=1, source_target_pairs={{0,16},{8,24},{16,0},{24,8},{1,17},{9,25},{17,1},{25,9},{2,18},{10... | collective-permute-start | bytes 2359304 | tf_op jit(solution)/shard_map/ppermute | solution.py:494
  13.1 17.5 %collective-permute-start = (bf16[2,96,2048]{2,1,0:T(8,128)(2,1)S(1)}, bf16[2,96,2048]{2,1,0:T(8,128)(2,1)S(1)}, u32[]{:S(2)}, u32[]{:S(2)}) collective-permute-start(bf16[2,96,2048]{2,1,0:T(8,128)(2,1)S(1)} %cast_weight.1.refs_0_), channel_id=1, source_target_pairs={{0,8},{8,0},{16,24},{24,16},{1,9},{9,1},{17,25},{25,17},{2,10},{10... | collective-permute-start | bytes 2359304 | tf_op jit(solution)/shard_map/ppermute | solution.py:494
  30.6 2.3 %copy-start.10 = (bf16[2,96,2048]{2,1,0:T(8,128)(2,1)}, bf16[2,96,2048]{2,1,0:T(8,128)(2,1)S(1)}, u32[]{:S(2)}) copy-start(bf16[2,96,2048]{2,1,0:T(8,128)(2,1)S(1)} %collective-permute-done.1.refs_2_) | copy-start | bytes 2359300
  30.6 2.3 %collective-permute-start.2 = (bf16[2,96,2048]{2,1,0:T(8,128)(2,1)S(1)}, bf16[2,96,2048]{2,1,0:T(8,128)(2,1)S(1)}, u32[]{:S(2)}, u32[]{:S(2)}) collective-permute-start(bf16[2,96,2048]{2,1,0:T(8,128)(2,1)S(1)} %collective-permute-done.1.refs_2_), channel_id=1, source_target_pairs={{0,8},{8,0},{16,24},{24,16},{1,9},{9,1},{17,25},{25,17},{2,10},{10... | collective-permute-start | bytes 2359304 | tf_op jit(solution)/shard_map/ppermute | solution.py:494
  30.6 2.3 %copy-start.11 = (bf16[2,96,2048]{2,1,0:T(8,128)(2,1)}, bf16[2,96,2048]{2,1,0:T(8,128)(2,1)S(1)}, u32[]{:S(2)}) copy-start(bf16[2,96,2048]{2,1,0:T(8,128)(2,1)S(1)} %collective-permute-done.refs_1_) | copy-start | bytes 2359300
  32.9 0.9 copy-start.12
  51.4 1.3 %copy-start.9 = (bf16[8,48,2432]{2,1,0:T(8,128)(2,1)}, bf16[8,48,2432]{2,1,0:T(8,128)(2,1)S(1)}, u32[]{:S(2)}) copy-start(bf16[8,48,2432]{2,1,0:T(8,128)(2,1)S(1)} %all-to-all-done) | copy-start | bytes 5603332
  58.8 47.2 %all-to-all-start.1 = ((bf16[8,48,2432]{2,1,0:T(8,128)(2,1)}), bf16[8,48,2432]{2,1,0:T(8,128)(2,1)S(1)}, u32[]{:S(2)}, u32[]{:S(2)}) async-start(bf16[8,48,2432]{2,1,0:T(8,128)(2,1)} %bitcast.20), calls=%async_computation.1 | async-start | bytes 3735552 | tf_op jit(solution)/shard_map/all_to_all | solution.py:501
  65.6 29.4 %copy-start.3 = (bf16[2,96,2048]{2,1,0:T(8,128)(2,1)S(1)}, bf16[2,96,2048]{2,1,0:T(8,128)(2,1)}, u32[]{:S(2)}) copy-start(bf16[2,96,2048]{2,1,0:T(8,128)(2,1)} %mc_ref.1) | copy-start | bytes 2359300
  65.6 29.4 %copy-start.4 = (bf16[2,96,2048]{2,1,0:T(8,128)(2,1)S(1)}, bf16[2,96,2048]{2,1,0:T(8,128)(2,1)}, u32[]{:S(2)}) copy-start(bf16[2,96,2048]{2,1,0:T(8,128)(2,1)} %vc_ref.1) | copy-start | bytes 2359300
  65.6 29.3 %copy-start.6 = (f32[2,96,16]{1,2,0:T(8,128)S(1)}, f32[2,96,16]{1,2,0:T(8,128)}, u32[]{:S(2)}) copy-start(f32[2,96,16]{1,2,0:T(8,128)} %param.11) | copy-start | bytes 36868
  65.6 29.3 %copy-start.7 = (f32[2,96,16]{1,2,0:T(8,128)S(1)}, f32[2,96,16]{1,2,0:T(8,128)}, u32[]{:S(2)}) copy-start(f32[2,96,16]{1,2,0:T(8,128)} %param.13) | copy-start | bytes 36868
  71.3 2.5 %collective-permute-start.4 = (bf16[2,96,2048]{2,1,0:T(8,128)(2,1)}, bf16[2,96,2048]{2,1,0:T(8,128)(2,1)S(1)}, u32[]{:S(2)}, u32[]{:S(2)}) collective-permute-start(bf16[2,96,2048]{2,1,0:T(8,128)(2,1)} %get-tuple-element.35), channel_id=1, source_target_pairs={{0,8},{8,0},{16,24},{24,16},{1,9},{9,1},{17,25},{25,17},{2,10},{10... | collective-permute-start | bytes 2359304 | tf_op jit(solution)/shard_map/ppermute | solution.py:494
  71.3 5.6 %collective-permute-start.3 = (bf16[2,96,2048]{2,1,0:T(8,128)(2,1)}, bf16[2,96,2048]{2,1,0:T(8,128)(2,1)S(1)}, u32[]{:S(2)}, u32[]{:S(2)}) collective-permute-start(bf16[2,96,2048]{2,1,0:T(8,128)(2,1)} %get-tuple-element.33), channel_id=1, source_target_pairs={{0,8},{8,0},{16,24},{24,16},{1,9},{9,1},{17,25},{25,17},{2,10},{10... | collective-permute-start | bytes 2359304 | tf_op jit(solution)/shard_map/ppermute | solution.py:494
  73.8 1.1 %copy-start.2 = (bf16[2,96,2048]{2,1,0:T(8,128)(2,1)S(1)}, bf16[2,96,2048]{2,1,0:T(8,128)(2,1)}, u32[]{:S(2)}) copy-start(bf16[2,96,2048]{2,1,0:T(8,128)(2,1)} %get-tuple-element.34.a_ref) | copy-start | bytes 2359300
  74.9 20.1 %copy-start.5 = (bf16[2,96,2048]{2,1,0:T(8,128)(2,1)S(1)}, bf16[2,96,2048]{2,1,0:T(8,128)(2,1)}, u32[]{:S(2)}) copy-start(bf16[2,96,2048]{2,1,0:T(8,128)(2,1)} %get-tuple-element.32.refs_0_) | copy-start | bytes 2359300
  75.3 19.6 %collective-permute-start.5 = (bf16[2,96,2048]{2,1,0:T(8,128)(2,1)S(1)}, bf16[2,96,2048]{2,1,0:T(8,128)(2,1)S(1)}, u32[]{:S(2)}, u32[]{:S(2)}) collective-permute-start(bf16[2,96,2048]{2,1,0:T(8,128)(2,1)S(1)} %add_parts.1), channel_id=1, source_target_pairs={{0,16},{8,24},{16,0},{24,8},{1,17},{9,25},{17,1},{25,9},{2,18},{10... | collective-permute-start | bytes 2359304 | tf_op jit(solution)/shard_map/ppermute | solution.py:494
  95.0 11.0 %copy-start.8 = (s32[1,256]{1,0:T(1,128)S(1)}, s32[1,256]{1,0:T(1,128)}, u32[]{:S(2)}) copy-start(s32[1,256]{1,0:T(1,128)} %get-tuple-element.25.target_hbm) | copy-start | bytes 3076

commit v11 on v10

--- a/solution.py
+++ b/solution.py
@@ -15,7 +15,7 @@
 learn_rate = 0.01
 
 VMEM_LIMIT = 40 * 1024 * 1024
-LARGE_LIMIT = 56 * 1024 * 1024
+LARGE_LIMIT = 60 * 1024 * 1024 + 512 * 1024
 F32 = jnp.float32
 BF16 = jnp.bfloat16
 
@@ -251,13 +251,38 @@
     return joined.reshape(tiles, local_count * pieces * rows, tile)
 
 
+def member_parts(value, capacity, local_count):
+    rows, width = value.shape
+    groups = rows // (capacity * local_count)
+    parts = value.astype(F32).reshape(groups, local_count, capacity, width)
+    return [
+        parts[:, e].reshape(groups * capacity, width).astype(BF16) for e in range(local_count)
+    ]
+
+
+def join_members(parts, capacity):
+    groups = parts[0].shape[0] // capacity
+    width = parts[0].shape[1]
+    stacked = [part.reshape(groups, 1, capacity, width) for part in parts]
+    joined = jnp.concatenate(stacked, axis=1)
+    return joined.reshape(groups * len(parts) * capacity, width)
+
+
+def pick_members(totals, capacity):
+    member = member_rows(totals[0].shape[0], capacity, len(totals))
+    picked = totals[0]
+    for e in range(1, len(totals)):
+        picked = jnp.where(member == e, totals[e], picked)
+    return picked
+
+
 def products_kernel(
-    capacity, local_count, local_hbm, w_hbm, out_hbm,
-    local_ref, w_ref, wide_ref, total_ref, out_ref, local_sem, w_sems, out_sems,
+    capacity, apart, local_hbm, w_hbm, out_hbm,
+    local_ref, w_ref, x_ref, total_ref, out_ref, local_sem, w_sems, out_sems,
 ):
     step = pl.program_id(0)
     steps, _, tile = w_ref.shape
-    hidden = wide_ref.shape[1] // local_count
+    local_count, _, hidden = total_ref.shape
     columns = pl.ds(pl.multiple_of(step * tile, tile), tile)
 
     def weight_load(j):
@@ -272,28 +297,32 @@
         local_load.wait()
         for j in range(1, steps):
             weight_load(j).start()
-        wide_ref[...] = spread(local_ref[:, steps * tile :], capacity, local_count)
+        x = local_ref[:, steps * tile :]
+        for e, part in enumerate(member_parts(x, capacity, local_count) if apart else [x]):
+            x_ref[e] = part
 
     weight_load(step).wait()
-    weight = w_ref[step]
-    out_ref[:, columns] = jnp.dot(
-        wide_ref[...], weight, preferred_element_type=F32
-    ).astype(BF16)
+    weights = [w_ref[step, e * hidden : (e + 1) * hidden] for e in range(local_count)]
+    xs = [x_ref[e if apart else 0] for e in range(local_count)]
+    ys = [jnp.dot(x, w, preferred_element_type=F32) for x, w in zip(xs, weights)]
+    y = join_members(ys, capacity) if apart else pick_members(ys, capacity)
+    out_ref[:, columns] = y.astype(BF16)
     pltpu.make_async_copy(
         out_ref.at[:, columns], out_hbm.at[:, columns], out_sems.at[step]
     ).start()
-    total_ref[...] += lax.dot_general(
-        local_ref[:, columns], weight, (((1,), (1,)), ((), ())), preferred_element_type=F32
-    )
+    g = local_ref[:, columns]
+    gs = member_parts(g, capacity, local_count) if apart else [g] * local_count
+    for e in range(local_count):
+        total_ref[e] += lax.dot_general(
+            gs[e], weights[e], (((1,), (1,)), ((), ())), preferred_element_type=F32
+        )
 
     @pl.when(step == steps - 1)
     def _():
-        member = member_rows(total_ref.shape[0], capacity, local_count)
-        picked = total_ref[:, :hidden]
-        for e in range(1, local_count):
-            picked = jnp.where(member == e, total_ref[:, e * hidden : (e + 1) * hidden], picked)
+        totals = [total_ref[e] for e in range(local_count)]
+        dx = join_members(totals, capacity) if apart else pick_members(totals, capacity)
         last = pl.ds(steps * tile, hidden)
-        out_ref[:, last] = picked.astype(BF16)
+        out_ref[:, last] = dx.astype(BF16)
         final = pltpu.make_async_copy(out_ref.at[:, last], out_hbm.at[:, last], out_sems.at[steps])
         final.start()
         for j in range(steps):
@@ -306,9 +335,12 @@
     tiles, wide, tile = weight.shape
     width = tiles * tile
     total = local.shape[0]
+    hidden = wide // local_count
+    apart = capacity % 8 == 0
+    rows = total // local_count if apart else total
     hbm = pl.BlockSpec(memory_space=pl.ANY)
     return pl.pallas_call(
-        functools.partial(products_kernel, capacity, local_count),
+        functools.partial(products_kernel, capacity, apart),
         grid=(tiles,),
         in_specs=[hbm, hbm],
         out_specs=hbm,
@@ -316,8 +348,8 @@
         scratch_shapes=[
             pltpu.VMEM(local.shape, BF16),
             pltpu.VMEM(weight.shape, BF16),
-            pltpu.VMEM((total, wide), BF16),
-            pltpu.VMEM((total, wide), F32),
+            pltpu.VMEM((local_count if apart else 1, rows, hidden), BF16),
+            pltpu.VMEM((local_count, rows, hidden), F32),
             pltpu.VMEM(local.shape, BF16),
             pltpu.SemaphoreType.DMA,
             pltpu.SemaphoreType.DMA((tiles,)),
@@ -326,7 +358,7 @@
         compiler_params=pltpu.CompilerParams(
             vmem_limit_bytes=LARGE_LIMIT, dimension_semantics=("arbitrary",)
         ),
-        cost_estimate=cost(4 * total * wide * width, 2 * (wide + 2 * total) * width),
+        cost_estimate=cost(4 * rows * wide * width, 2 * (wide + 2 * total) * width),
         name="products",
     )(local, weight)
 

time: 110 us -> 108 us (0.982)
  local copies, waits for them, and re-layouts: 3.33 us -> 2.09 us
    unnamed x26 -> x22, local copies, waits for them, and re-layouts: 3.33 us -> 2.09 us
where the time goes in v11:
time: 108 us; the launch traced here: 106 us
  waiting for transfers between devices  58.2 us (54%)
  Pallas kernels  26.9 us (25%)
  starting transfers between devices  17.9 us (17%)
  local copies, waits for them, and re-layouts  2.09 us (2%)
    ppermute x6, waiting for transfers between devices, swap(): return lax.ppermute(array, axis, [(i, i ^ offset) for i in range(size)])  39 us
    all_to_all x2, waiting for transfers between devices, exchange(): lax.all_to_all(parts, 'grp', split_axis=0, concat_axis=0, tiled=True, axi...  19.2 us
    all_to_all x2, starting transfers between devices, exchange(): lax.all_to_all(parts, 'grp', split_axis=0, concat_axis=0, tiled=True, axi...  14.2 us
    pallas_call x1, Pallas kernels, adam(): pl.pallas_call(functools.partial(adam_kernel, len(grads)), grid=(members,...  6.19 us
    pallas_call x1, Pallas kernels, gradient(): pl.pallas_call(functools.partial(gradient_kernel, capacity, local_count,...  5.54 us
    pallas_call x1, Pallas kernels, products(): pl.pallas_call(functools.partial(products_kernel, capacity, apart), grid=...  5.45 us
    pallas_call x1, Pallas kernels, join_weight(): pl.pallas_call(join_kernel, grid=(tiles,), in_specs=[pl.BlockSpec((local_...  4.3 us
    ppermute x6, starting transfers between devices, swap(): return lax.ppermute(array, axis, [(i, i ^ offset) for i in range(size)])  3.69 us
  transfers between devices with their start and end apart: 8, of which 6 were waited for; matrix products, arithmetic and copies ran while one was open for 0% of the time, Pallas kernels for 16%

profile of v11, /device:TPU:0, one launch (start us, length us, event | category | flops | bytes accessed | tf_op | source)
XLA Modules:
  0.0 105.8 jit_solution(2492310584308768223)
XLA Ops:
  0.6 3.1 %dispatch.1 = (bf16[384,2432]{1,0:T(8,128)(2,1)}, s32[1,256]{1,0:T(1,128)}) custom-call(s32[1,256]{1,0:T(1,128)} %bitcast.19, s32[1,16]{1,0:T(1,128)} %bitcast.20, bf16[256,384]{1,0:T(8,128)(2,1)} %x_hbm.1, bf16[256,2048]{1,0:T(8,128)(2,1)} %g_hbm.1), custom_call_target="tpu_custom_call" | custom-call | flops 478150656 | bytes 3112960 | tf_op jit(solution)/shard_map/dispatch/pallas_call | solution.py:117
  3.7 0.0 copy-start
  3.7 7.4 %all-to-all-start = ((bf16[8,48,2432]{2,1,0:T(8,128)(2,1)}), bf16[8,48,2432]{2,1,0:T(8,128)(2,1)}, u32[]{:S(2)}, u32[]{:S(2)}) async-start(bf16[8,48,2432]{2,1,0:T(8,128)(2,1)} %bitcast.16), calls=%async_computation | async-start | bytes 3735552 | tf_op jit(solution)/shard_map/all_to_all | solution.py:533
  11.1 0.0 copy-done
  11.1 0.3 cast_weight.1.refs_0_
  11.5 0.0 copy-start.1
  11.5 1.6 %collective-permute-start.1 = (bf16[2,96,2048]{2,1,0:T(8,128)(2,1)S(1)}, bf16[2,96,2048]{2,1,0:T(8,128)(2,1)S(1)}, u32[]{:S(2)}, u32[]{:S(2)}) collective-permute-start(bf16[2,96,2048]{2,1,0:T(8,128)(2,1)S(1)} %cast_weight.1.refs_0_), channel_id=1, source_target_pairs={{0,16},{8,24},{16,0},{24,8},{1,17},{9,25},{17,1},{25,9},{2,18},{10... | collective-permute-start | bytes 2359304 | tf_op jit(solution)/shard_map/ppermute | solution.py:526
  13.1 0.0 collective-permute-start
  13.1 17.5 %collective-permute-done.1.refs_2_ = bf16[2,96,2048]{2,1,0:T(8,128)(2,1)S(1)} collective-permute-done((bf16[2,96,2048]{2,1,0:T(8,128)(2,1)S(1)}, bf16[2,96,2048]{2,1,0:T(8,128)(2,1)S(1)}, u32[]{:S(2)}, u32[]{:S(2)}) %collective-permute-start.1) | collective-permute-done | bytes 786464 | tf_op jit(solution)/shard_map/ppermute | solution.py:526
  30.6 0.0 copy-start.9
  30.6 0.0 collective-permute-start.2
  30.6 0.0 collective-permute-done.refs_1_
  30.6 0.0 copy-start.10
  30.6 0.9 copy-done.10
  31.5 1.5 %collective-permute-done.2.refs_3_ = bf16[2,96,2048]{2,1,0:T(8,128)(2,1)} collective-permute-done((bf16[2,96,2048]{2,1,0:T(8,128)(2,1)S(1)}, bf16[2,96,2048]{2,1,0:T(8,128)(2,1)}, u32[]{:S(2)}, u32[]{:S(2)}) %collective-permute-start.2) | collective-permute-done | bytes 786464 | tf_op jit(solution)/shard_map/ppermute | solution.py:526
  33.0 0.0 copy-done.1
  33.0 0.0 copy-done.9
  33.0 4.3 %join_weight.1 = bf16[4,2,4,96,512]{4,3,2,1,0:T(8,128)(2,1)} custom-call(bf16[2,96,2048]{2,1,0:T(8,128)(2,1)} %copy-done.1, bf16[2,96,2048]{2,1,0:T(8,128)(2,1)} %copy-done.10, bf16[2,96,2048]{2,1,0:T(8,128)(2,1)} %copy-done.9, bf16[2,96,2048]{2,1,0:T(8,128)(2,1)} %collective-permute-done.2.refs_3_), custom_call_target="tpu_custom_call" | custom-call | bytes 6291456 | tf_op jit(solution)/shard_map/join_weight/pallas_call | solution.py:239
  37.3 14.2 %all-to-all-done = bf16[8,48,2432]{2,1,0:T(8,128)(2,1)} async-done(((bf16[8,48,2432]{2,1,0:T(8,128)(2,1)}), bf16[8,48,2432]{2,1,0:T(8,128)(2,1)}, u32[]{:S(2)}, u32[]{:S(2)}) %all-to-all-start) | async-done | bytes 1867808 | tf_op jit(solution)/shard_map/all_to_all | solution.py:533
  51.5 5.4 %products.1 = bf16[384,2432]{1,0:T(8,128)(2,1)} custom-call(bf16[384,2432]{1,0:T(8,128)(2,1)} %bitcast.3.local_hbm.g_ref.refs_0_.refs_1_.refs_2_, bf16[4,768,512]{2,1,0:T(8,128)(2,1)} %bitcast.14), custom_call_target="tpu_custom_call" | custom-call | flops 1207959552 | bytes 6291456 | tf_op jit(solution)/shard_map/products/pallas_call | solution.py:342
  57.0 6.8 %all-to-all-start.1 = ((bf16[8,48,2432]{2,1,0:T(8,128)(2,1)}), bf16[8,48,2432]{2,1,0:T(8,128)(2,1)S(1)}, u32[]{:S(2)}, u32[]{:S(2)}) async-start(bf16[8,48,2432]{2,1,0:T(8,128)(2,1)} %bitcast.15), calls=%async_computation.1 | async-start | bytes 3735552 | tf_op jit(solution)/shard_map/all_to_all | solution.py:533
  63.8 0.0 copy-start.6
  63.8 0.0 copy-start.7
  63.8 5.5 %gradient.1 = (bf16[2,96,2048]{2,1,0:T(8,128)(2,1)}, bf16[2,96,2048]{2,1,0:T(8,128)(2,1)}, bf16[2,96,2048]{2,1,0:T(8,128)(2,1)}, bf16[2,96,2048]{2,1,0:T(8,128)(2,1)}) custom-call(bf16[384,2432]{1,0:T(8,128)(2,1)} %bitcast.3.local_hbm.g_ref.refs_0_.refs_1_.refs_2_, bf16[384,2432]{1,0:T(8,128)(2,1)} %bitcast.3.local_hbm.g_ref.refs_0_.refs_1_.refs_2_, ...), custom_call_target="tpu_custom_call" | custom-call | flops 1207959552 | bytes 4718592 | tf_op jit(solution)/shard_map/gradient/pallas_call | solution.py:398
  69.3 0.0 collective-permute-start.4
  69.3 0.5 collective-permute-start.3
  69.8 2.0 %collective-permute-done.4.b_ref = bf16[2,96,2048]{2,1,0:T(8,128)(2,1)S(1)} collective-permute-done((bf16[2,96,2048]{2,1,0:T(8,128)(2,1)}, bf16[2,96,2048]{2,1,0:T(8,128)(2,1)S(1)}, u32[]{:S(2)}, u32[]{:S(2)}) %collective-permute-start.4) | collective-permute-done | bytes 786464 | tf_op jit(solution)/shard_map/ppermute | solution.py:526
  71.8 0.0 copy-start.2
  71.8 1.1 %copy-done.2 = bf16[2,96,2048]{2,1,0:T(8,128)(2,1)S(1)} copy-done((bf16[2,96,2048]{2,1,0:T(8,128)(2,1)S(1)}, bf16[2,96,2048]{2,1,0:T(8,128)(2,1)}, u32[]{:S(2)}) %copy-start.2) | copy-done | bytes 786456
  73.0 0.0 copy-start.3
  73.0 0.0 copy-start.4
  73.0 0.0 copy-start.5
  73.0 0.4 add_parts.1
  73.4 1.6 %collective-permute-start.5 = (bf16[2,96,2048]{2,1,0:T(8,128)(2,1)S(1)}, bf16[2,96,2048]{2,1,0:T(8,128)(2,1)S(1)}, u32[]{:S(2)}, u32[]{:S(2)}) collective-permute-start(bf16[2,96,2048]{2,1,0:T(8,128)(2,1)S(1)} %add_parts.1), channel_id=1, source_target_pairs={{0,16},{8,24},{16,0},{24,8},{1,17},{9,25},{17,1},{25,9},{2,18},{10... | collective-permute-start | bytes 2359304 | tf_op jit(solution)/shard_map/ppermute | solution.py:526
  74.9 0.0 collective-permute-done.3.refs_1_
  74.9 18.1 %collective-permute-done.5.refs_2_ = bf16[2,96,2048]{2,1,0:T(8,128)(2,1)S(1)} collective-permute-done((bf16[2,96,2048]{2,1,0:T(8,128)(2,1)S(1)}, bf16[2,96,2048]{2,1,0:T(8,128)(2,1)S(1)}, u32[]{:S(2)}, u32[]{:S(2)}) %collective-permute-start.5) | collective-permute-done | bytes 786464 | tf_op jit(solution)/shard_map/ppermute | solution.py:526
  93.0 0.0 copy-done.6
  93.0 0.0 copy-done.7
  93.0 0.0 copy-done.3
  93.0 0.0 copy-done.4
  93.0 0.0 copy-done.5
  93.0 0.0 copy-start.8
  93.0 6.2 %adam.1 = (f32[2,96,2048]{2,1,0:T(8,128)}, bf16[2,96,2048]{2,1,0:T(8,128)(2,1)}, f32[2,16,96]{2,1,0:T(8,128)}, bf16[2,96,2048]{2,1,0:T(8,128)(2,1)}, f32[2,16,96]{2,1,0:T(8,128)}) custom-call(f32[2,96,2048]{2,1,0:T(8,128)S(1)} %copy-done, bf16[2,96,2048]{2,1,0:T(8,128)(2,1)S(1)} %copy-done.3, f32[2,16,96]{2,1,0:T(8,128)S(1)} %bitcast.12, ...), custom_call_target="tpu_custom_call" | custom-call | flops 15728640 | bytes 7077888 | tf_op jit(solution)/shard_map/adam/pallas_call | solution.py:499
  99.2 5.0 %all-to-all-done.1 = bf16[8,48,2432]{2,1,0:T(8,128)(2,1)S(1)} async-done(((bf16[8,48,2432]{2,1,0:T(8,128)(2,1)}), bf16[8,48,2432]{2,1,0:T(8,128)(2,1)S(1)}, u32[]{:S(2)}, u32[]{:S(2)}) %all-to-all-start.1) | async-done | bytes 1867808 | tf_op jit(solution)/shard_map/all_to_all | solution.py:533
  104.2 0.0 copy-done.8
  104.2 1.6 %collect.1 = (bf16[256,2048]{1,0:T(8,128)(2,1)}, bf16[256,384]{1,0:T(8,128)(2,1)}) custom-call(s32[1,256]{1,0:T(1,128)S(1)} %copy-done.8, bf16[384,2432]{1,0:T(8,128)(2,1)S(1)} %bitcast.11), custom_call_target="tpu_custom_call" | custom-call | flops 478150656 | bytes 3112960 | tf_op jit(solution)/shard_map/collect/pallas_call | solution.py:190
Async XLA Ops:
  3.7 7.4 %copy-start = (f32[2,96,2048]{2,1,0:T(8,128)S(1)}, f32[2,96,2048]{2,1,0:T(8,128)}, u32[]{:S(2)}) copy-start(f32[2,96,2048]{2,1,0:T(8,128)} %master_ref.1) | copy-start | bytes 4718596
  3.7 47.8 %all-to-all-start = ((bf16[8,48,2432]{2,1,0:T(8,128)(2,1)}), bf16[8,48,2432]{2,1,0:T(8,128)(2,1)}, u32[]{:S(2)}, u32[]{:S(2)}) async-start(bf16[8,48,2432]{2,1,0:T(8,128)(2,1)} %bitcast.16), calls=%async_computation | async-start | bytes 3735552 | tf_op jit(solution)/shard_map/all_to_all | solution.py:533
  11.5 21.5 %copy-start.1 = (bf16[2,96,2048]{2,1,0:T(8,128)(2,1)}, bf16[2,96,2048]{2,1,0:T(8,128)(2,1)S(1)}, u32[]{:S(2)}) copy-start(bf16[2,96,2048]{2,1,0:T(8,128)(2,1)S(1)} %cast_weight.1.refs_0_) | copy-start | bytes 2359300
  11.5 19.1 %collective-permute-start.1 = (bf16[2,96,2048]{2,1,0:T(8,128)(2,1)S(1)}, bf16[2,96,2048]{2,1,0:T(8,128)(2,1)S(1)}, u32[]{:S(2)}, u32[]{:S(2)}) collective-permute-start(bf16[2,96,2048]{2,1,0:T(8,128)(2,1)S(1)} %cast_weight.1.refs_0_), channel_id=1, source_target_pairs={{0,16},{8,24},{16,0},{24,8},{1,17},{9,25},{17,1},{25,9},{2,18},{10... | collective-permute-start | bytes 2359304 | tf_op jit(solution)/shard_map/ppermute | solution.py:526
  13.1 17.5 %collective-permute-start = (bf16[2,96,2048]{2,1,0:T(8,128)(2,1)S(1)}, bf16[2,96,2048]{2,1,0:T(8,128)(2,1)S(1)}, u32[]{:S(2)}, u32[]{:S(2)}) collective-permute-start(bf16[2,96,2048]{2,1,0:T(8,128)(2,1)S(1)} %cast_weight.1.refs_0_), channel_id=1, source_target_pairs={{0,8},{8,0},{16,24},{24,16},{1,9},{9,1},{17,25},{25,17},{2,10},{10... | collective-permute-start | bytes 2359304 | tf_op jit(solution)/shard_map/ppermute | solution.py:526
  30.6 2.4 %copy-start.9 = (bf16[2,96,2048]{2,1,0:T(8,128)(2,1)}, bf16[2,96,2048]{2,1,0:T(8,128)(2,1)S(1)}, u32[]{:S(2)}) copy-start(bf16[2,96,2048]{2,1,0:T(8,128)(2,1)S(1)} %collective-permute-done.1.refs_2_) | copy-start | bytes 2359300
  30.6 2.4 %collective-permute-start.2 = (bf16[2,96,2048]{2,1,0:T(8,128)(2,1)S(1)}, bf16[2,96,2048]{2,1,0:T(8,128)(2,1)}, u32[]{:S(2)}, u32[]{:S(2)}) collective-permute-start(bf16[2,96,2048]{2,1,0:T(8,128)(2,1)S(1)} %collective-permute-done.1.refs_2_), channel_id=1, source_target_pairs={{0,8},{8,0},{16,24},{24,16},{1,9},{9,1},{17,25},{25,17},{2,10},{10... | collective-permute-start | bytes 2359304 | tf_op jit(solution)/shard_map/ppermute | solution.py:526
  30.6 0.9 copy-start.10
  57.0 47.2 %all-to-all-start.1 = ((bf16[8,48,2432]{2,1,0:T(8,128)(2,1)}), bf16[8,48,2432]{2,1,0:T(8,128)(2,1)S(1)}, u32[]{:S(2)}, u32[]{:S(2)}) async-start(bf16[8,48,2432]{2,1,0:T(8,128)(2,1)} %bitcast.15), calls=%async_computation.1 | async-start | bytes 3735552 | tf_op jit(solution)/shard_map/all_to_all | solution.py:533
  63.8 29.2 %copy-start.6 = (f32[2,96,16]{1,2,0:T(8,128)S(1)}, f32[2,96,16]{1,2,0:T(8,128)}, u32[]{:S(2)}) copy-start(f32[2,96,16]{1,2,0:T(8,128)} %param.11) | copy-start | bytes 36868
  63.8 29.2 %copy-start.7 = (f32[2,96,16]{1,2,0:T(8,128)S(1)}, f32[2,96,16]{1,2,0:T(8,128)}, u32[]{:S(2)}) copy-start(f32[2,96,16]{1,2,0:T(8,128)} %param.13) | copy-start | bytes 36868
  69.3 2.5 %collective-permute-start.4 = (bf16[2,96,2048]{2,1,0:T(8,128)(2,1)}, bf16[2,96,2048]{2,1,0:T(8,128)(2,1)S(1)}, u32[]{:S(2)}, u32[]{:S(2)}) collective-permute-start(bf16[2,96,2048]{2,1,0:T(8,128)(2,1)} %get-tuple-element.35), channel_id=1, source_target_pairs={{0,8},{8,0},{16,24},{24,16},{1,9},{9,1},{17,25},{25,17},{2,10},{10... | collective-permute-start | bytes 2359304 | tf_op jit(solution)/shard_map/ppermute | solution.py:526
  69.3 5.6 %collective-permute-start.3 = (bf16[2,96,2048]{2,1,0:T(8,128)(2,1)}, bf16[2,96,2048]{2,1,0:T(8,128)(2,1)S(1)}, u32[]{:S(2)}, u32[]{:S(2)}) collective-permute-start(bf16[2,96,2048]{2,1,0:T(8,128)(2,1)} %get-tuple-element.33), channel_id=1, source_target_pairs={{0,8},{8,0},{16,24},{24,16},{1,9},{9,1},{17,25},{25,17},{2,10},{10... | collective-permute-start | bytes 2359304 | tf_op jit(solution)/shard_map/ppermute | solution.py:526
  71.8 1.1 %copy-start.2 = (bf16[2,96,2048]{2,1,0:T(8,128)(2,1)S(1)}, bf16[2,96,2048]{2,1,0:T(8,128)(2,1)}, u32[]{:S(2)}) copy-start(bf16[2,96,2048]{2,1,0:T(8,128)(2,1)} %get-tuple-element.34.a_ref) | copy-start | bytes 2359300
  73.0 20.1 %copy-start.3 = (bf16[2,96,2048]{2,1,0:T(8,128)(2,1)S(1)}, bf16[2,96,2048]{2,1,0:T(8,128)(2,1)}, u32[]{:S(2)}) copy-start(bf16[2,96,2048]{2,1,0:T(8,128)(2,1)} %mc_ref.1) | copy-start | bytes 2359300
  73.0 20.1 %copy-start.4 = (bf16[2,96,2048]{2,1,0:T(8,128)(2,1)S(1)}, bf16[2,96,2048]{2,1,0:T(8,128)(2,1)}, u32[]{:S(2)}) copy-start(bf16[2,96,2048]{2,1,0:T(8,128)(2,1)} %vc_ref.1) | copy-start | bytes 2359300
  73.0 20.1 %copy-start.5 = (bf16[2,96,2048]{2,1,0:T(8,128)(2,1)S(1)}, bf16[2,96,2048]{2,1,0:T(8,128)(2,1)}, u32[]{:S(2)}) copy-start(bf16[2,96,2048]{2,1,0:T(8,128)(2,1)} %get-tuple-element.32.refs_0_) | copy-start | bytes 2359300
  73.4 19.6 %collective-permute-start.5 = (bf16[2,96,2048]{2,1,0:T(8,128)(2,1)S(1)}, bf16[2,96,2048]{2,1,0:T(8,128)(2,1)S(1)}, u32[]{:S(2)}, u32[]{:S(2)}) collective-permute-start(bf16[2,96,2048]{2,1,0:T(8,128)(2,1)S(1)} %add_parts.1), channel_id=1, source_target_pairs={{0,16},{8,24},{16,0},{24,8},{1,17},{9,25},{17,1},{25,9},{2,18},{10... | collective-permute-start | bytes 2359304 | tf_op jit(solution)/shard_map/ppermute | solution.py:526
  93.0 11.2 %copy-start.8 = (s32[1,256]{1,0:T(1,128)S(1)}, s32[1,256]{1,0:T(1,128)}, u32[]{:S(2)}) copy-start(s32[1,256]{1,0:T(1,128)} %get-tuple-element.25.target_hbm) | copy-start | bytes 3076

commit v12 on v11

--- a/solution.py
+++ b/solution.py
@@ -31,10 +31,13 @@
 
 
 def order_of(device, groups):
-    if groups % 2:
+    if groups % 4:
         return device
-    half = groups // 2
-    return device % half * 2 + device // half
+    count = groups // 2
+    outer, inner = device // 2, device % 2
+    upper = outer // (count // 2)
+    near = outer + upper * (count - 1 - 2 * outer)
+    return (inner * (count // 2) + near) * 2 + upper
 
 
 def row_targets(route_row, placement_row, capacity, groups):

time: 108 us -> 110 us (1.019); the launches traced: 106 us -> 110 us
  waiting for transfers between devices: 58.2 us -> 65.3 us
  starting transfers between devices: 17.9 us -> 14.7 us
    all_to_all x2, waiting for transfers between devices: 19.2 us -> 26.3 us  [exchange(): lax.all_to_all(parts, 'grp', split_axis=0, concat_axis=0, tiled=True, axi...]
    all_to_all x2, starting transfers between devices: 14.2 us -> 11 us  [exchange(): lax.all_to_all(parts, 'grp', split_axis=0, concat_axis=0, tiled=True, axi...]
  transfers between devices with their start and end apart: 8 -> 8, of which waited for: 6 -> 6; matrix products, arithmetic and copies ran while one was open for 0% -> 0% of each run, Pallas kernels for 16% -> 15%
where the time goes in v12:
time: 110 us
  waiting for transfers between devices  65.3 us (59%)
  Pallas kernels  26.9 us (24%)
  starting transfers between devices  14.7 us (13%)
  local copies, waits for them, and re-layouts  2.09 us (2%)
    ppermute x6, waiting for transfers between devices, swap(): return lax.ppermute(array, axis, [(i, i ^ offset) for i in range(size)])  39 us
    all_to_all x2, waiting for transfers between devices, exchange(): lax.all_to_all(parts, 'grp', split_axis=0, concat_axis=0, tiled=True, axi...  26.3 us
    all_to_all x2, starting transfers between devices, exchange(): lax.all_to_all(parts, 'grp', split_axis=0, concat_axis=0, tiled=True, axi...  11 us
    pallas_call x1, Pallas kernels, adam(): pl.pallas_call(functools.partial(adam_kernel, len(grads)), grid=(members,...  6.19 us
    pallas_call x1, Pallas kernels, gradient(): pl.pallas_call(functools.partial(gradient_kernel, capacity, local_count,...  5.53 us
    pallas_call x1, Pallas kernels, products(): pl.pallas_call(functools.partial(products_kernel, capacity, apart), grid=...  5.45 us
    pallas_call x1, Pallas kernels, join_weight(): pl.pallas_call(join_kernel, grid=(tiles,), in_specs=[pl.BlockSpec((local_...  4.3 us
    ppermute x6, starting transfers between devices, swap(): return lax.ppermute(array, axis, [(i, i ^ offset) for i in range(size)])  3.69 us
  transfers between devices with their start and end apart: 8, of which 6 were waited for; matrix products, arithmetic and copies ran while one was open for 0% of the time, Pallas kernels for 15%

profile of v12, /device:TPU:0, one launch (start us, length us, event | category | flops | bytes accessed | tf_op | source)
XLA Modules:
  0.0 109.7 jit_solution(4223917621458921995)
XLA Ops:
  0.6 3.1 %dispatch.1 = (bf16[384,2432]{1,0:T(8,128)(2,1)}, s32[1,256]{1,0:T(1,128)}) custom-call(s32[1,256]{1,0:T(1,128)} %bitcast.19, s32[1,16]{1,0:T(1,128)} %bitcast.20, bf16[256,384]{1,0:T(8,128)(2,1)} %x_hbm.1, bf16[256,2048]{1,0:T(8,128)(2,1)} %g_hbm.1), custom_call_target="tpu_custom_call" | custom-call | flops 478150656 | bytes 3112960 | tf_op jit(solution)/shard_map/dispatch/pallas_call | solution.py:120
  3.7 0.0 copy-start
  3.7 7.4 %all-to-all-start = ((bf16[8,48,2432]{2,1,0:T(8,128)(2,1)}), bf16[8,48,2432]{2,1,0:T(8,128)(2,1)}, u32[]{:S(2)}, u32[]{:S(2)}) async-start(bf16[8,48,2432]{2,1,0:T(8,128)(2,1)} %bitcast.16), calls=%async_computation | async-start | bytes 3735552 | tf_op jit(solution)/shard_map/all_to_all | solution.py:536
  11.1 0.0 copy-done
  11.1 0.3 cast_weight.1.refs_0_
  11.5 0.0 copy-start.1
  11.5 1.6 %collective-permute-start.1 = (bf16[2,96,2048]{2,1,0:T(8,128)(2,1)S(1)}, bf16[2,96,2048]{2,1,0:T(8,128)(2,1)S(1)}, u32[]{:S(2)}, u32[]{:S(2)}) collective-permute-start(bf16[2,96,2048]{2,1,0:T(8,128)(2,1)S(1)} %cast_weight.1.refs_0_), channel_id=1, source_target_pairs={{0,16},{8,24},{16,0},{24,8},{1,17},{9,25},{17,1},{25,9},{2,18},{10... | collective-permute-start | bytes 2359304 | tf_op jit(solution)/shard_map/ppermute | solution.py:529
  13.1 0.0 collective-permute-start
  13.1 17.5 %collective-permute-done.1.refs_2_ = bf16[2,96,2048]{2,1,0:T(8,128)(2,1)S(1)} collective-permute-done((bf16[2,96,2048]{2,1,0:T(8,128)(2,1)S(1)}, bf16[2,96,2048]{2,1,0:T(8,128)(2,1)S(1)}, u32[]{:S(2)}, u32[]{:S(2)}) %collective-permute-start.1) | collective-permute-done | bytes 786464 | tf_op jit(solution)/shard_map/ppermute | solution.py:529
  30.6 0.0 copy-start.9
  30.6 0.0 collective-permute-start.2
  30.6 0.0 collective-permute-done.refs_1_
  30.6 0.0 copy-start.10
  30.6 0.9 copy-done.10
  31.5 1.5 %collective-permute-done.2.refs_3_ = bf16[2,96,2048]{2,1,0:T(8,128)(2,1)} collective-permute-done((bf16[2,96,2048]{2,1,0:T(8,128)(2,1)S(1)}, bf16[2,96,2048]{2,1,0:T(8,128)(2,1)}, u32[]{:S(2)}, u32[]{:S(2)}) %collective-permute-start.2) | collective-permute-done | bytes 786464 | tf_op jit(solution)/shard_map/ppermute | solution.py:529
  33.0 0.0 copy-done.1
  33.0 0.0 copy-done.9
  33.0 4.3 %join_weight.1 = bf16[4,2,4,96,512]{4,3,2,1,0:T(8,128)(2,1)} custom-call(bf16[2,96,2048]{2,1,0:T(8,128)(2,1)} %copy-done.1, bf16[2,96,2048]{2,1,0:T(8,128)(2,1)} %copy-done.10, bf16[2,96,2048]{2,1,0:T(8,128)(2,1)} %copy-done.9, bf16[2,96,2048]{2,1,0:T(8,128)(2,1)} %collective-permute-done.2.refs_3_), custom_call_target="tpu_custom_call" | custom-call | bytes 6291456 | tf_op jit(solution)/shard_map/join_weight/pallas_call | solution.py:242
  37.3 18.1 %all-to-all-done = bf16[8,48,2432]{2,1,0:T(8,128)(2,1)} async-done(((bf16[8,48,2432]{2,1,0:T(8,128)(2,1)}), bf16[8,48,2432]{2,1,0:T(8,128)(2,1)}, u32[]{:S(2)}, u32[]{:S(2)}) %all-to-all-start) | async-done | bytes 1867808 | tf_op jit(solution)/shard_map/all_to_all | solution.py:536
  55.4 5.4 %products.1 = bf16[384,2432]{1,0:T(8,128)(2,1)} custom-call(bf16[384,2432]{1,0:T(8,128)(2,1)} %bitcast.3.local_hbm.g_ref.refs_0_.refs_1_.refs_2_, bf16[4,768,512]{2,1,0:T(8,128)(2,1)} %bitcast.14), custom_call_target="tpu_custom_call" | custom-call | flops 1207959552 | bytes 6291456 | tf_op jit(solution)/shard_map/products/pallas_call | solution.py:345
  60.9 3.6 %all-to-all-start.1 = ((bf16[8,48,2432]{2,1,0:T(8,128)(2,1)}), bf16[8,48,2432]{2,1,0:T(8,128)(2,1)S(1)}, u32[]{:S(2)}, u32[]{:S(2)}) async-start(bf16[8,48,2432]{2,1,0:T(8,128)(2,1)} %bitcast.15), calls=%async_computation.1 | async-start | bytes 3735552 | tf_op jit(solution)/shard_map/all_to_all | solution.py:536
  64.5 0.0 copy-start.6
  64.5 0.0 copy-start.7
  64.5 5.5 %gradient.1 = (bf16[2,96,2048]{2,1,0:T(8,128)(2,1)}, bf16[2,96,2048]{2,1,0:T(8,128)(2,1)}, bf16[2,96,2048]{2,1,0:T(8,128)(2,1)}, bf16[2,96,2048]{2,1,0:T(8,128)(2,1)}) custom-call(bf16[384,2432]{1,0:T(8,128)(2,1)} %bitcast.3.local_hbm.g_ref.refs_0_.refs_1_.refs_2_, bf16[384,2432]{1,0:T(8,128)(2,1)} %bitcast.3.local_hbm.g_ref.refs_0_.refs_1_.refs_2_, ...), custom_call_target="tpu_custom_call" | custom-call | flops 1207959552 | bytes 4718592 | tf_op jit(solution)/shard_map/gradient/pallas_call | solution.py:401
  70.1 0.0 collective-permute-start.4
  70.1 0.5 collective-permute-start.3
  70.6 2.0 %collective-permute-done.4.b_ref = bf16[2,96,2048]{2,1,0:T(8,128)(2,1)S(1)} collective-permute-done((bf16[2,96,2048]{2,1,0:T(8,128)(2,1)}, bf16[2,96,2048]{2,1,0:T(8,128)(2,1)S(1)}, u32[]{:S(2)}, u32[]{:S(2)}) %collective-permute-start.4) | collective-permute-done | bytes 786464 | tf_op jit(solution)/shard_map/ppermute | solution.py:529
  72.5 0.0 copy-start.2
  72.6 1.1 %copy-done.2 = bf16[2,96,2048]{2,1,0:T(8,128)(2,1)S(1)} copy-done((bf16[2,96,2048]{2,1,0:T(8,128)(2,1)S(1)}, bf16[2,96,2048]{2,1,0:T(8,128)(2,1)}, u32[]{:S(2)}) %copy-start.2) | copy-done | bytes 786456
  73.7 0.0 copy-start.3
  73.7 0.0 copy-start.4
  73.7 0.0 copy-start.5
  73.7 0.4 add_parts.1
  74.1 1.6 %collective-permute-start.5 = (bf16[2,96,2048]{2,1,0:T(8,128)(2,1)S(1)}, bf16[2,96,2048]{2,1,0:T(8,128)(2,1)S(1)}, u32[]{:S(2)}, u32[]{:S(2)}) collective-permute-start(bf16[2,96,2048]{2,1,0:T(8,128)(2,1)S(1)} %add_parts.1), channel_id=1, source_target_pairs={{0,16},{8,24},{16,0},{24,8},{1,17},{9,25},{17,1},{25,9},{2,18},{10... | collective-permute-start | bytes 2359304 | tf_op jit(solution)/shard_map/ppermute | solution.py:529
  75.7 0.0 collective-permute-done.3.refs_1_
  75.7 18.1 %collective-permute-done.5.refs_2_ = bf16[2,96,2048]{2,1,0:T(8,128)(2,1)S(1)} collective-permute-done((bf16[2,96,2048]{2,1,0:T(8,128)(2,1)S(1)}, bf16[2,96,2048]{2,1,0:T(8,128)(2,1)S(1)}, u32[]{:S(2)}, u32[]{:S(2)}) %collective-permute-start.5) | collective-permute-done | bytes 786464 | tf_op jit(solution)/shard_map/ppermute | solution.py:529
  93.7 0.0 copy-done.6
  93.7 0.0 copy-done.7
  93.7 0.0 copy-done.3
  93.7 0.0 copy-done.4
  93.8 0.0 copy-done.5
  93.8 0.0 copy-start.8
  93.8 6.2 %adam.1 = (f32[2,96,2048]{2,1,0:T(8,128)}, bf16[2,96,2048]{2,1,0:T(8,128)(2,1)}, f32[2,16,96]{2,1,0:T(8,128)}, bf16[2,96,2048]{2,1,0:T(8,128)(2,1)}, f32[2,16,96]{2,1,0:T(8,128)}) custom-call(f32[2,96,2048]{2,1,0:T(8,128)S(1)} %copy-done, bf16[2,96,2048]{2,1,0:T(8,128)(2,1)S(1)} %copy-done.3, f32[2,16,96]{2,1,0:T(8,128)S(1)} %bitcast.12, ...), custom_call_target="tpu_custom_call" | custom-call | flops 15728640 | bytes 7077888 | tf_op jit(solution)/shard_map/adam/pallas_call | solution.py:502
  100.0 8.2 %all-to-all-done.1 = bf16[8,48,2432]{2,1,0:T(8,128)(2,1)S(1)} async-done(((bf16[8,48,2432]{2,1,0:T(8,128)(2,1)}), bf16[8,48,2432]{2,1,0:T(8,128)(2,1)S(1)}, u32[]{:S(2)}, u32[]{:S(2)}) %all-to-all-start.1) | async-done | bytes 1867808 | tf_op jit(solution)/shard_map/all_to_all | solution.py:536
  108.1 0.0 copy-done.8
  108.1 1.6 %collect.1 = (bf16[256,2048]{1,0:T(8,128)(2,1)}, bf16[256,384]{1,0:T(8,128)(2,1)}) custom-call(s32[1,256]{1,0:T(1,128)S(1)} %copy-done.8, bf16[384,2432]{1,0:T(8,128)(2,1)S(1)} %bitcast.11), custom_call_target="tpu_custom_call" | custom-call | flops 478150656 | bytes 3112960 | tf_op jit(solution)/shard_map/collect/pallas_call | solution.py:193
Async XLA Ops:
  3.7 7.4 %copy-start = (f32[2,96,2048]{2,1,0:T(8,128)S(1)}, f32[2,96,2048]{2,1,0:T(8,128)}, u32[]{:S(2)}) copy-start(f32[2,96,2048]{2,1,0:T(8,128)} %master_ref.1) | copy-start | bytes 4718596
  3.7 51.7 %all-to-all-start = ((bf16[8,48,2432]{2,1,0:T(8,128)(2,1)}), bf16[8,48,2432]{2,1,0:T(8,128)(2,1)}, u32[]{:S(2)}, u32[]{:S(2)}) async-start(bf16[8,48,2432]{2,1,0:T(8,128)(2,1)} %bitcast.16), calls=%async_computation | async-start | bytes 3735552 | tf_op jit(solution)/shard_map/all_to_all | solution.py:536
  11.5 21.5 %copy-start.1 = (bf16[2,96,2048]{2,1,0:T(8,128)(2,1)}, bf16[2,96,2048]{2,1,0:T(8,128)(2,1)S(1)}, u32[]{:S(2)}) copy-start(bf16[2,96,2048]{2,1,0:T(8,128)(2,1)S(1)} %cast_weight.1.refs_0_) | copy-start | bytes 2359300
  11.5 19.1 %collective-permute-start.1 = (bf16[2,96,2048]{2,1,0:T(8,128)(2,1)S(1)}, bf16[2,96,2048]{2,1,0:T(8,128)(2,1)S(1)}, u32[]{:S(2)}, u32[]{:S(2)}) collective-permute-start(bf16[2,96,2048]{2,1,0:T(8,128)(2,1)S(1)} %cast_weight.1.refs_0_), channel_id=1, source_target_pairs={{0,16},{8,24},{16,0},{24,8},{1,17},{9,25},{17,1},{25,9},{2,18},{10... | collective-permute-start | bytes 2359304 | tf_op jit(solution)/shard_map/ppermute | solution.py:529
  13.1 17.5 %collective-permute-start = (bf16[2,96,2048]{2,1,0:T(8,128)(2,1)S(1)}, bf16[2,96,2048]{2,1,0:T(8,128)(2,1)S(1)}, u32[]{:S(2)}, u32[]{:S(2)}) collective-permute-start(bf16[2,96,2048]{2,1,0:T(8,128)(2,1)S(1)} %cast_weight.1.refs_0_), channel_id=1, source_target_pairs={{0,8},{8,0},{16,24},{24,16},{1,9},{9,1},{17,25},{25,17},{2,10},{10... | collective-permute-start | bytes 2359304 | tf_op jit(solution)/shard_map/ppermute | solution.py:529
  30.6 2.4 %copy-start.9 = (bf16[2,96,2048]{2,1,0:T(8,128)(2,1)}, bf16[2,96,2048]{2,1,0:T(8,128)(2,1)S(1)}, u32[]{:S(2)}) copy-start(bf16[2,96,2048]{2,1,0:T(8,128)(2,1)S(1)} %collective-permute-done.1.refs_2_) | copy-start | bytes 2359300
  30.6 2.4 %collective-permute-start.2 = (bf16[2,96,2048]{2,1,0:T(8,128)(2,1)S(1)}, bf16[2,96,2048]{2,1,0:T(8,128)(2,1)}, u32[]{:S(2)}, u32[]{:S(2)}) collective-permute-start(bf16[2,96,2048]{2,1,0:T(8,128)(2,1)S(1)} %collective-permute-done.1.refs_2_), channel_id=1, source_target_pairs={{0,8},{8,0},{16,24},{24,16},{1,9},{9,1},{17,25},{25,17},{2,10},{10... | collective-permute-start | bytes 2359304 | tf_op jit(solution)/shard_map/ppermute | solution.py:529
  30.6 0.9 copy-start.10
  60.9 47.2 %all-to-all-start.1 = ((bf16[8,48,2432]{2,1,0:T(8,128)(2,1)}), bf16[8,48,2432]{2,1,0:T(8,128)(2,1)S(1)}, u32[]{:S(2)}, u32[]{:S(2)}) async-start(bf16[8,48,2432]{2,1,0:T(8,128)(2,1)} %bitcast.15), calls=%async_computation.1 | async-start | bytes 3735552 | tf_op jit(solution)/shard_map/all_to_all | solution.py:536
  64.5 29.2 %copy-start.6 = (f32[2,96,16]{1,2,0:T(8,128)S(1)}, f32[2,96,16]{1,2,0:T(8,128)}, u32[]{:S(2)}) copy-start(f32[2,96,16]{1,2,0:T(8,128)} %param.11) | copy-start | bytes 36868
  64.5 29.2 %copy-start.7 = (f32[2,96,16]{1,2,0:T(8,128)S(1)}, f32[2,96,16]{1,2,0:T(8,128)}, u32[]{:S(2)}) copy-start(f32[2,96,16]{1,2,0:T(8,128)} %param.13) | copy-start | bytes 36868
  70.1 2.5 %collective-permute-start.4 = (bf16[2,96,2048]{2,1,0:T(8,128)(2,1)}, bf16[2,96,2048]{2,1,0:T(8,128)(2,1)S(1)}, u32[]{:S(2)}, u32[]{:S(2)}) collective-permute-start(bf16[2,96,2048]{2,1,0:T(8,128)(2,1)} %get-tuple-element.35), channel_id=1, source_target_pairs={{0,8},{8,0},{16,24},{24,16},{1,9},{9,1},{17,25},{25,17},{2,10},{10... | collective-permute-start | bytes 2359304 | tf_op jit(solution)/shard_map/ppermute | solution.py:529
  70.1 5.6 %collective-permute-start.3 = (bf16[2,96,2048]{2,1,0:T(8,128)(2,1)}, bf16[2,96,2048]{2,1,0:T(8,128)(2,1)S(1)}, u32[]{:S(2)}, u32[]{:S(2)}) collective-permute-start(bf16[2,96,2048]{2,1,0:T(8,128)(2,1)} %get-tuple-element.33), channel_id=1, source_target_pairs={{0,8},{8,0},{16,24},{24,16},{1,9},{9,1},{17,25},{25,17},{2,10},{10... | collective-permute-start | bytes 2359304 | tf_op jit(solution)/shard_map/ppermute | solution.py:529
  72.5 1.1 %copy-start.2 = (bf16[2,96,2048]{2,1,0:T(8,128)(2,1)S(1)}, bf16[2,96,2048]{2,1,0:T(8,128)(2,1)}, u32[]{:S(2)}) copy-start(bf16[2,96,2048]{2,1,0:T(8,128)(2,1)} %get-tuple-element.34.a_ref) | copy-start | bytes 2359300
  73.7 20.1 %copy-start.3 = (bf16[2,96,2048]{2,1,0:T(8,128)(2,1)S(1)}, bf16[2,96,2048]{2,1,0:T(8,128)(2,1)}, u32[]{:S(2)}) copy-start(bf16[2,96,2048]{2,1,0:T(8,128)(2,1)} %mc_ref.1) | copy-start | bytes 2359300
  73.7 20.1 %copy-start.4 = (bf16[2,96,2048]{2,1,0:T(8,128)(2,1)S(1)}, bf16[2,96,2048]{2,1,0:T(8,128)(2,1)}, u32[]{:S(2)}) copy-start(bf16[2,96,2048]{2,1,0:T(8,128)(2,1)} %vc_ref.1) | copy-start | bytes 2359300
  73.7 20.1 %copy-start.5 = (bf16[2,96,2048]{2,1,0:T(8,128)(2,1)S(1)}, bf16[2,96,2048]{2,1,0:T(8,128)(2,1)}, u32[]{:S(2)}) copy-start(bf16[2,96,2048]{2,1,0:T(8,128)(2,1)} %get-tuple-element.32.refs_0_) | copy-start | bytes 2359300
  74.1 19.6 %collective-permute-start.5 = (bf16[2,96,2048]{2,1,0:T(8,128)(2,1)S(1)}, bf16[2,96,2048]{2,1,0:T(8,128)(2,1)S(1)}, u32[]{:S(2)}, u32[]{:S(2)}) collective-permute-start(bf16[2,96,2048]{2,1,0:T(8,128)(2,1)S(1)} %add_parts.1), channel_id=1, source_target_pairs={{0,16},{8,24},{16,0},{24,8},{1,17},{9,25},{17,1},{25,9},{2,18},{10... | collective-permute-start | bytes 2359304 | tf_op jit(solution)/shard_map/ppermute | solution.py:529
  93.8 14.4 %copy-start.8 = (s32[1,256]{1,0:T(1,128)S(1)}, s32[1,256]{1,0:T(1,128)}, u32[]{:S(2)}) copy-start(s32[1,256]{1,0:T(1,128)} %get-tuple-element.25.target_hbm) | copy-start | bytes 3076

commit v13 on v11

--- a/solution.py
+++ b/solution.py
@@ -34,7 +34,9 @@
     if groups % 2:
         return device
     half = groups // 2
-    return device % half * 2 + device // half
+    upper = device // half
+    near = device + upper * (groups - 1 - 2 * device)
+    return near + (upper + near) % 2 * half
 
 
 def row_targets(route_row, placement_row, capacity, groups):

time: 108 us -> 107 us (level)
  the two profiles are of different devices: /device:TPU:0 before, /device:TPU:8 now
where the time goes in v13:
time: 107 us; the launch traced here: 106 us
  waiting for transfers between devices  62.9 us (59%)
  Pallas kernels  26.9 us (25%)
  starting transfers between devices  13.6 us (13%)
  local copies, waits for them, and re-layouts  2.09 us (2%)
    ppermute x6, waiting for transfers between devices, swap(): return lax.ppermute(array, axis, [(i, i ^ offset) for i in range(size)])  38.7 us
    all_to_all x2, waiting for transfers between devices, exchange(): lax.all_to_all(parts, 'grp', split_axis=0, concat_axis=0, tiled=True, axi...  24.2 us
    all_to_all x2, starting transfers between devices, exchange(): lax.all_to_all(parts, 'grp', split_axis=0, concat_axis=0, tiled=True, axi...  9.95 us
    pallas_call x1, Pallas kernels, adam(): pl.pallas_call(functools.partial(adam_kernel, len(grads)), grid=(members,...  6.19 us
    pallas_call x1, Pallas kernels, gradient(): pl.pallas_call(functools.partial(gradient_kernel, capacity, local_count,...  5.54 us
    pallas_call x1, Pallas kernels, products(): pl.pallas_call(functools.partial(products_kernel, capacity, apart), grid=...  5.45 us
    pallas_call x1, Pallas kernels, join_weight(): pl.pallas_call(join_kernel, grid=(tiles,), in_specs=[pl.BlockSpec((local_...  4.3 us
    ppermute x6, starting transfers between devices, swap(): return lax.ppermute(array, axis, [(i, i ^ offset) for i in range(size)])  3.68 us
  transfers between devices with their start and end apart: 8, of which 6 were waited for; matrix products, arithmetic and copies ran while one was open for 0% of the time, Pallas kernels for 16%

profile of v13, /device:TPU:8, one launch (start us, length us, event | category | flops | bytes accessed | tf_op | source)
XLA Modules:
  0.0 106.3 jit_solution(153560392683173459)
XLA Ops:
  0.6 3.1 %dispatch.1 = (bf16[384,2432]{1,0:T(8,128)(2,1)}, s32[1,256]{1,0:T(1,128)}) custom-call(s32[1,256]{1,0:T(1,128)} %bitcast.19, s32[1,16]{1,0:T(1,128)} %bitcast.20, bf16[256,384]{1,0:T(8,128)(2,1)} %x_hbm.1, bf16[256,2048]{1,0:T(8,128)(2,1)} %g_hbm.1), custom_call_target="tpu_custom_call" | custom-call | flops 478150656 | bytes 3112960 | tf_op jit(solution)/shard_map/dispatch/pallas_call | solution.py:119
  3.7 0.0 copy-start
  3.7 6.4 %all-to-all-start = ((bf16[8,48,2432]{2,1,0:T(8,128)(2,1)}), bf16[8,48,2432]{2,1,0:T(8,128)(2,1)}, u32[]{:S(2)}, u32[]{:S(2)}) async-start(bf16[8,48,2432]{2,1,0:T(8,128)(2,1)} %bitcast.16), calls=%async_computation | async-start | bytes 3735552 | tf_op jit(solution)/shard_map/all_to_all | solution.py:535
  10.1 0.0 copy-done
  10.1 0.3 cast_weight.1.refs_0_
  10.5 0.0 copy-start.1
  10.5 1.6 %collective-permute-start.1 = (bf16[2,96,2048]{2,1,0:T(8,128)(2,1)S(1)}, bf16[2,96,2048]{2,1,0:T(8,128)(2,1)S(1)}, u32[]{:S(2)}, u32[]{:S(2)}) collective-permute-start(bf16[2,96,2048]{2,1,0:T(8,128)(2,1)S(1)} %cast_weight.1.refs_0_), channel_id=1, source_target_pairs={{0,16},{8,24},{16,0},{24,8},{1,17},{9,25},{17,1},{25,9},{2,18},{10... | collective-permute-start | bytes 2359304 | tf_op jit(solution)/shard_map/ppermute | solution.py:528
  12.1 0.0 collective-permute-start
  12.1 17.2 %collective-permute-done.1.refs_2_ = bf16[2,96,2048]{2,1,0:T(8,128)(2,1)S(1)} collective-permute-done((bf16[2,96,2048]{2,1,0:T(8,128)(2,1)S(1)}, bf16[2,96,2048]{2,1,0:T(8,128)(2,1)S(1)}, u32[]{:S(2)}, u32[]{:S(2)}) %collective-permute-start.1) | collective-permute-done | bytes 786464 | tf_op jit(solution)/shard_map/ppermute | solution.py:528
  29.3 0.0 copy-start.9
  29.3 0.0 collective-permute-start.2
  29.3 0.0 collective-permute-done.refs_1_
  29.3 0.0 copy-start.10
  29.3 0.9 copy-done.10
  30.2 1.5 %collective-permute-done.2.refs_3_ = bf16[2,96,2048]{2,1,0:T(8,128)(2,1)} collective-permute-done((bf16[2,96,2048]{2,1,0:T(8,128)(2,1)S(1)}, bf16[2,96,2048]{2,1,0:T(8,128)(2,1)}, u32[]{:S(2)}, u32[]{:S(2)}) %collective-permute-start.2) | collective-permute-done | bytes 786464 | tf_op jit(solution)/shard_map/ppermute | solution.py:528
  31.7 0.0 copy-done.1
  31.7 0.0 copy-done.9
  31.7 4.3 %join_weight.1 = bf16[4,2,4,96,512]{4,3,2,1,0:T(8,128)(2,1)} custom-call(bf16[2,96,2048]{2,1,0:T(8,128)(2,1)} %copy-done.1, bf16[2,96,2048]{2,1,0:T(8,128)(2,1)} %copy-done.10, bf16[2,96,2048]{2,1,0:T(8,128)(2,1)} %copy-done.9, bf16[2,96,2048]{2,1,0:T(8,128)(2,1)} %collective-permute-done.2.refs_3_), custom_call_target="tpu_custom_call" | custom-call | bytes 6291456 | tf_op jit(solution)/shard_map/join_weight/pallas_call | solution.py:241
  36.0 17.0 %all-to-all-done = bf16[8,48,2432]{2,1,0:T(8,128)(2,1)} async-done(((bf16[8,48,2432]{2,1,0:T(8,128)(2,1)}), bf16[8,48,2432]{2,1,0:T(8,128)(2,1)}, u32[]{:S(2)}, u32[]{:S(2)}) %all-to-all-start) | async-done | bytes 1867808 | tf_op jit(solution)/shard_map/all_to_all | solution.py:535
  53.0 5.4 %products.1 = bf16[384,2432]{1,0:T(8,128)(2,1)} custom-call(bf16[384,2432]{1,0:T(8,128)(2,1)} %bitcast.3.local_hbm.g_ref.refs_0_.refs_1_.refs_2_, bf16[4,768,512]{2,1,0:T(8,128)(2,1)} %bitcast.14), custom_call_target="tpu_custom_call" | custom-call | flops 1207959552 | bytes 6291456 | tf_op jit(solution)/shard_map/products/pallas_call | solution.py:344
  58.5 3.6 %all-to-all-start.1 = ((bf16[8,48,2432]{2,1,0:T(8,128)(2,1)}), bf16[8,48,2432]{2,1,0:T(8,128)(2,1)S(1)}, u32[]{:S(2)}, u32[]{:S(2)}) async-start(bf16[8,48,2432]{2,1,0:T(8,128)(2,1)} %bitcast.15), calls=%async_computation.1 | async-start | bytes 3735552 | tf_op jit(solution)/shard_map/all_to_all | solution.py:535
  62.0 0.0 copy-start.6
  62.0 0.0 copy-start.7
  62.1 5.5 %gradient.1 = (bf16[2,96,2048]{2,1,0:T(8,128)(2,1)}, bf16[2,96,2048]{2,1,0:T(8,128)(2,1)}, bf16[2,96,2048]{2,1,0:T(8,128)(2,1)}, bf16[2,96,2048]{2,1,0:T(8,128)(2,1)}) custom-call(bf16[384,2432]{1,0:T(8,128)(2,1)} %bitcast.3.local_hbm.g_ref.refs_0_.refs_1_.refs_2_, bf16[384,2432]{1,0:T(8,128)(2,1)} %bitcast.3.local_hbm.g_ref.refs_0_.refs_1_.refs_2_, ...), custom_call_target="tpu_custom_call" | custom-call | flops 1207959552 | bytes 4718592 | tf_op jit(solution)/shard_map/gradient/pallas_call | solution.py:400
  67.6 0.0 collective-permute-start.4
  67.6 0.5 collective-permute-start.3
  68.1 2.0 %collective-permute-done.4.b_ref = bf16[2,96,2048]{2,1,0:T(8,128)(2,1)S(1)} collective-permute-done((bf16[2,96,2048]{2,1,0:T(8,128)(2,1)}, bf16[2,96,2048]{2,1,0:T(8,128)(2,1)S(1)}, u32[]{:S(2)}, u32[]{:S(2)}) %collective-permute-start.4) | collective-permute-done | bytes 786464 | tf_op jit(solution)/shard_map/ppermute | solution.py:528
  70.1 0.0 copy-start.2
  70.1 1.1 %copy-done.2 = bf16[2,96,2048]{2,1,0:T(8,128)(2,1)S(1)} copy-done((bf16[2,96,2048]{2,1,0:T(8,128)(2,1)S(1)}, bf16[2,96,2048]{2,1,0:T(8,128)(2,1)}, u32[]{:S(2)}) %copy-start.2) | copy-done | bytes 786456
  71.2 0.0 copy-start.3
  71.2 0.0 copy-start.4
  71.2 0.0 copy-start.5
  71.2 0.4 add_parts.1
  71.6 1.6 %collective-permute-start.5 = (bf16[2,96,2048]{2,1,0:T(8,128)(2,1)S(1)}, bf16[2,96,2048]{2,1,0:T(8,128)(2,1)S(1)}, u32[]{:S(2)}, u32[]{:S(2)}) collective-permute-start(bf16[2,96,2048]{2,1,0:T(8,128)(2,1)S(1)} %add_parts.1), channel_id=1, source_target_pairs={{0,16},{8,24},{16,0},{24,8},{1,17},{9,25},{17,1},{25,9},{2,18},{10... | collective-permute-start | bytes 2359304 | tf_op jit(solution)/shard_map/ppermute | solution.py:528
  73.2 0.0 collective-permute-done.3.refs_1_
  73.2 18.1 %collective-permute-done.5.refs_2_ = bf16[2,96,2048]{2,1,0:T(8,128)(2,1)S(1)} collective-permute-done((bf16[2,96,2048]{2,1,0:T(8,128)(2,1)S(1)}, bf16[2,96,2048]{2,1,0:T(8,128)(2,1)S(1)}, u32[]{:S(2)}, u32[]{:S(2)}) %collective-permute-start.5) | collective-permute-done | bytes 786464 | tf_op jit(solution)/shard_map/ppermute | solution.py:528
  91.3 0.0 copy-done.6
  91.3 0.0 copy-done.7
  91.3 0.0 copy-done.3
  91.3 0.0 copy-done.4
  91.3 0.0 copy-done.5
  91.3 0.0 copy-start.8
  91.3 6.2 %adam.1 = (f32[2,96,2048]{2,1,0:T(8,128)}, bf16[2,96,2048]{2,1,0:T(8,128)(2,1)}, f32[2,16,96]{2,1,0:T(8,128)}, bf16[2,96,2048]{2,1,0:T(8,128)(2,1)}, f32[2,16,96]{2,1,0:T(8,128)}) custom-call(f32[2,96,2048]{2,1,0:T(8,128)S(1)} %copy-done, bf16[2,96,2048]{2,1,0:T(8,128)(2,1)S(1)} %copy-done.3, f32[2,16,96]{2,1,0:T(8,128)S(1)} %bitcast.12, ...), custom_call_target="tpu_custom_call" | custom-call | flops 15728640 | bytes 7077888 | tf_op jit(solution)/shard_map/adam/pallas_call | solution.py:501
  97.5 7.2 %all-to-all-done.1 = bf16[8,48,2432]{2,1,0:T(8,128)(2,1)S(1)} async-done(((bf16[8,48,2432]{2,1,0:T(8,128)(2,1)}), bf16[8,48,2432]{2,1,0:T(8,128)(2,1)S(1)}, u32[]{:S(2)}, u32[]{:S(2)}) %all-to-all-start.1) | async-done | bytes 1867808 | tf_op jit(solution)/shard_map/all_to_all | solution.py:535
  104.7 0.0 copy-done.8
  104.7 1.6 %collect.1 = (bf16[256,2048]{1,0:T(8,128)(2,1)}, bf16[256,384]{1,0:T(8,128)(2,1)}) custom-call(s32[1,256]{1,0:T(1,128)S(1)} %copy-done.8, bf16[384,2432]{1,0:T(8,128)(2,1)S(1)} %bitcast.11), custom_call_target="tpu_custom_call" | custom-call | flops 478150656 | bytes 3112960 | tf_op jit(solution)/shard_map/collect/pallas_call | solution.py:192
Async XLA Ops:
  3.7 6.4 %copy-start = (f32[2,96,2048]{2,1,0:T(8,128)S(1)}, f32[2,96,2048]{2,1,0:T(8,128)}, u32[]{:S(2)}) copy-start(f32[2,96,2048]{2,1,0:T(8,128)} %master_ref.1) | copy-start | bytes 4718596
  3.7 49.3 %all-to-all-start = ((bf16[8,48,2432]{2,1,0:T(8,128)(2,1)}), bf16[8,48,2432]{2,1,0:T(8,128)(2,1)}, u32[]{:S(2)}, u32[]{:S(2)}) async-start(bf16[8,48,2432]{2,1,0:T(8,128)(2,1)} %bitcast.16), calls=%async_computation | async-start | bytes 3735552 | tf_op jit(solution)/shard_map/all_to_all | solution.py:535
  10.5 21.2 %copy-start.1 = (bf16[2,96,2048]{2,1,0:T(8,128)(2,1)}, bf16[2,96,2048]{2,1,0:T(8,128)(2,1)S(1)}, u32[]{:S(2)}) copy-start(bf16[2,96,2048]{2,1,0:T(8,128)(2,1)S(1)} %cast_weight.1.refs_0_) | copy-start | bytes 2359300
  10.5 18.8 %collective-permute-start.1 = (bf16[2,96,2048]{2,1,0:T(8,128)(2,1)S(1)}, bf16[2,96,2048]{2,1,0:T(8,128)(2,1)S(1)}, u32[]{:S(2)}, u32[]{:S(2)}) collective-permute-start(bf16[2,96,2048]{2,1,0:T(8,128)(2,1)S(1)} %cast_weight.1.refs_0_), channel_id=1, source_target_pairs={{0,16},{8,24},{16,0},{24,8},{1,17},{9,25},{17,1},{25,9},{2,18},{10... | collective-permute-start | bytes 2359304 | tf_op jit(solution)/shard_map/ppermute | solution.py:528
  12.1 17.2 %collective-permute-start = (bf16[2,96,2048]{2,1,0:T(8,128)(2,1)S(1)}, bf16[2,96,2048]{2,1,0:T(8,128)(2,1)S(1)}, u32[]{:S(2)}, u32[]{:S(2)}) collective-permute-start(bf16[2,96,2048]{2,1,0:T(8,128)(2,1)S(1)} %cast_weight.1.refs_0_), channel_id=1, source_target_pairs={{0,8},{8,0},{16,24},{24,16},{1,9},{9,1},{17,25},{25,17},{2,10},{10... | collective-permute-start | bytes 2359304 | tf_op jit(solution)/shard_map/ppermute | solution.py:528
  29.3 2.4 %copy-start.9 = (bf16[2,96,2048]{2,1,0:T(8,128)(2,1)}, bf16[2,96,2048]{2,1,0:T(8,128)(2,1)S(1)}, u32[]{:S(2)}) copy-start(bf16[2,96,2048]{2,1,0:T(8,128)(2,1)S(1)} %collective-permute-done.1.refs_2_) | copy-start | bytes 2359300
  29.3 2.4 %collective-permute-start.2 = (bf16[2,96,2048]{2,1,0:T(8,128)(2,1)S(1)}, bf16[2,96,2048]{2,1,0:T(8,128)(2,1)}, u32[]{:S(2)}, u32[]{:S(2)}) collective-permute-start(bf16[2,96,2048]{2,1,0:T(8,128)(2,1)S(1)} %collective-permute-done.1.refs_2_), channel_id=1, source_target_pairs={{0,8},{8,0},{16,24},{24,16},{1,9},{9,1},{17,25},{25,17},{2,10},{10... | collective-permute-start | bytes 2359304 | tf_op jit(solution)/shard_map/ppermute | solution.py:528
  29.3 0.9 copy-start.10
  58.5 46.2 %all-to-all-start.1 = ((bf16[8,48,2432]{2,1,0:T(8,128)(2,1)}), bf16[8,48,2432]{2,1,0:T(8,128)(2,1)S(1)}, u32[]{:S(2)}, u32[]{:S(2)}) async-start(bf16[8,48,2432]{2,1,0:T(8,128)(2,1)} %bitcast.15), calls=%async_computation.1 | async-start | bytes 3735552 | tf_op jit(solution)/shard_map/all_to_all | solution.py:535
  62.0 29.2 %copy-start.6 = (f32[2,96,16]{1,2,0:T(8,128)S(1)}, f32[2,96,16]{1,2,0:T(8,128)}, u32[]{:S(2)}) copy-start(f32[2,96,16]{1,2,0:T(8,128)} %param.11) | copy-start | bytes 36868
  62.0 29.2 %copy-start.7 = (f32[2,96,16]{1,2,0:T(8,128)S(1)}, f32[2,96,16]{1,2,0:T(8,128)}, u32[]{:S(2)}) copy-start(f32[2,96,16]{1,2,0:T(8,128)} %param.13) | copy-start | bytes 36868
  67.6 2.5 %collective-permute-start.4 = (bf16[2,96,2048]{2,1,0:T(8,128)(2,1)}, bf16[2,96,2048]{2,1,0:T(8,128)(2,1)S(1)}, u32[]{:S(2)}, u32[]{:S(2)}) collective-permute-start(bf16[2,96,2048]{2,1,0:T(8,128)(2,1)} %get-tuple-element.35), channel_id=1, source_target_pairs={{0,8},{8,0},{16,24},{24,16},{1,9},{9,1},{17,25},{25,17},{2,10},{10... | collective-permute-start | bytes 2359304 | tf_op jit(solution)/shard_map/ppermute | solution.py:528
  67.6 5.6 %collective-permute-start.3 = (bf16[2,96,2048]{2,1,0:T(8,128)(2,1)}, bf16[2,96,2048]{2,1,0:T(8,128)(2,1)S(1)}, u32[]{:S(2)}, u32[]{:S(2)}) collective-permute-start(bf16[2,96,2048]{2,1,0:T(8,128)(2,1)} %get-tuple-element.33), channel_id=1, source_target_pairs={{0,8},{8,0},{16,24},{24,16},{1,9},{9,1},{17,25},{25,17},{2,10},{10... | collective-permute-start | bytes 2359304 | tf_op jit(solution)/shard_map/ppermute | solution.py:528
  70.1 1.1 %copy-start.2 = (bf16[2,96,2048]{2,1,0:T(8,128)(2,1)S(1)}, bf16[2,96,2048]{2,1,0:T(8,128)(2,1)}, u32[]{:S(2)}) copy-start(bf16[2,96,2048]{2,1,0:T(8,128)(2,1)} %get-tuple-element.34.a_ref) | copy-start | bytes 2359300
  71.2 20.1 %copy-start.3 = (bf16[2,96,2048]{2,1,0:T(8,128)(2,1)S(1)}, bf16[2,96,2048]{2,1,0:T(8,128)(2,1)}, u32[]{:S(2)}) copy-start(bf16[2,96,2048]{2,1,0:T(8,128)(2,1)} %mc_ref.1) | copy-start | bytes 2359300
  71.2 20.1 %copy-start.4 = (bf16[2,96,2048]{2,1,0:T(8,128)(2,1)S(1)}, bf16[2,96,2048]{2,1,0:T(8,128)(2,1)}, u32[]{:S(2)}) copy-start(bf16[2,96,2048]{2,1,0:T(8,128)(2,1)} %vc_ref.1) | copy-start | bytes 2359300
  71.2 20.1 %copy-start.5 = (bf16[2,96,2048]{2,1,0:T(8,128)(2,1)S(1)}, bf16[2,96,2048]{2,1,0:T(8,128)(2,1)}, u32[]{:S(2)}) copy-start(bf16[2,96,2048]{2,1,0:T(8,128)(2,1)} %get-tuple-element.32.refs_0_) | copy-start | bytes 2359300
  71.6 19.6 %collective-permute-start.5 = (bf16[2,96,2048]{2,1,0:T(8,128)(2,1)S(1)}, bf16[2,96,2048]{2,1,0:T(8,128)(2,1)S(1)}, u32[]{:S(2)}, u32[]{:S(2)}) collective-permute-start(bf16[2,96,2048]{2,1,0:T(8,128)(2,1)S(1)} %add_parts.1), channel_id=1, source_target_pairs={{0,16},{8,24},{16,0},{24,8},{1,17},{9,25},{17,1},{25,9},{2,18},{10... | collective-permute-start | bytes 2359304 | tf_op jit(solution)/shard_map/ppermute | solution.py:528
  91.3 13.4 %copy-start.8 = (s32[1,256]{1,0:T(1,128)S(1)}, s32[1,256]{1,0:T(1,128)}, u32[]{:S(2)}) copy-start(s32[1,256]{1,0:T(1,128)} %get-tuple-element.25.target_hbm) | copy-start | bytes 3076

commit v14 on v13

--- a/solution.py
+++ b/solution.py
@@ -31,12 +31,13 @@
 
 
 def order_of(device, groups):
-    if groups % 2:
+    if groups % 4:
         return device
     half = groups // 2
     upper = device // half
     near = device + upper * (groups - 1 - 2 * device)
-    return near + (upper + near) % 2 * half
+    place = near % 2 * (half // 2) + near // 2
+    return place + (upper + place) % 2 * half
 
 
 def row_targets(route_row, placement_row, capacity, groups):

time: 107 us -> 107 us (level)
  the two profiles are of different devices: /device:TPU:8 before, /device:TPU:12 now
where the time goes in v14:
time: 107 us; the launch traced here: 106 us
  waiting for transfers between devices  65 us (61%)
  Pallas kernels  26.9 us (25%)
  starting transfers between devices  11.6 us (11%)
  local copies, waits for them, and re-layouts  2.09 us (2%)
    ppermute x6, waiting for transfers between devices, swap(): return lax.ppermute(array, axis, [(i, i ^ offset) for i in range(size)])  40.8 us
    all_to_all x2, waiting for transfers between devices, exchange(): lax.all_to_all(parts, 'grp', split_axis=0, concat_axis=0, tiled=True, axi...  24.2 us
    all_to_all x2, starting transfers between devices, exchange(): lax.all_to_all(parts, 'grp', split_axis=0, concat_axis=0, tiled=True, axi...  9.95 us
    pallas_call x1, Pallas kernels, adam(): pl.pallas_call(functools.partial(adam_kernel, len(grads)), grid=(members,...  6.19 us
    pallas_call x1, Pallas kernels, gradient(): pl.pallas_call(functools.partial(gradient_kernel, capacity, local_count,...  5.54 us
    pallas_call x1, Pallas kernels, products(): pl.pallas_call(functools.partial(products_kernel, capacity, apart), grid=...  5.45 us
    pallas_call x1, Pallas kernels, join_weight(): pl.pallas_call(join_kernel, grid=(tiles,), in_specs=[pl.BlockSpec((local_...  4.3 us
    pallas_call x1, Pallas kernels, dispatch(): pl.pallas_call(functools.partial(dispatch_kernel, capacity, groups), in_s...  3.1 us
  transfers between devices with their start and end apart: 8, of which 6 were waited for; matrix products, arithmetic and copies ran while one was open for 0% of the time, Pallas kernels for 16%

profile of v14, /device:TPU:12, one launch (start us, length us, event | category | flops | bytes accessed | tf_op | source)
XLA Modules:
  0.0 106.4 jit_solution(6951145566716419457)
XLA Ops:
  0.6 3.1 %dispatch.1 = (bf16[384,2432]{1,0:T(8,128)(2,1)}, s32[1,256]{1,0:T(1,128)}) custom-call(s32[1,256]{1,0:T(1,128)} %bitcast.19, s32[1,16]{1,0:T(1,128)} %bitcast.20, bf16[256,384]{1,0:T(8,128)(2,1)} %x_hbm.1, bf16[256,2048]{1,0:T(8,128)(2,1)} %g_hbm.1), custom_call_target="tpu_custom_call" | custom-call | flops 478150656 | bytes 3112960 | tf_op jit(solution)/shard_map/dispatch/pallas_call | solution.py:120
  3.7 0.0 copy-start
  3.7 6.4 %all-to-all-start = ((bf16[8,48,2432]{2,1,0:T(8,128)(2,1)}), bf16[8,48,2432]{2,1,0:T(8,128)(2,1)}, u32[]{:S(2)}, u32[]{:S(2)}) async-start(bf16[8,48,2432]{2,1,0:T(8,128)(2,1)} %bitcast.16), calls=%async_computation | async-start | bytes 3735552 | tf_op jit(solution)/shard_map/all_to_all | solution.py:536
  10.1 0.0 copy-done
  10.1 0.3 cast_weight.1.refs_0_
  10.5 0.0 copy-start.1
  10.5 0.6 collective-permute-start.1
  11.1 0.0 collective-permute-start
  11.1 18.2 %collective-permute-done.1.refs_2_ = bf16[2,96,2048]{2,1,0:T(8,128)(2,1)S(1)} collective-permute-done((bf16[2,96,2048]{2,1,0:T(8,128)(2,1)S(1)}, bf16[2,96,2048]{2,1,0:T(8,128)(2,1)S(1)}, u32[]{:S(2)}, u32[]{:S(2)}) %collective-permute-start.1) | collective-permute-done | bytes 786464 | tf_op jit(solution)/shard_map/ppermute | solution.py:529
  29.3 0.0 copy-start.9
  29.3 0.0 collective-permute-start.2
  29.3 0.0 collective-permute-done.refs_1_
  29.3 0.0 copy-start.10
  29.3 0.9 copy-done.10
  30.2 1.5 %collective-permute-done.2.refs_3_ = bf16[2,96,2048]{2,1,0:T(8,128)(2,1)} collective-permute-done((bf16[2,96,2048]{2,1,0:T(8,128)(2,1)S(1)}, bf16[2,96,2048]{2,1,0:T(8,128)(2,1)}, u32[]{:S(2)}, u32[]{:S(2)}) %collective-permute-start.2) | collective-permute-done | bytes 786464 | tf_op jit(solution)/shard_map/ppermute | solution.py:529
  31.7 0.0 copy-done.1
  31.7 0.0 copy-done.9
  31.7 4.3 %join_weight.1 = bf16[4,2,4,96,512]{4,3,2,1,0:T(8,128)(2,1)} custom-call(bf16[2,96,2048]{2,1,0:T(8,128)(2,1)} %copy-done.1, bf16[2,96,2048]{2,1,0:T(8,128)(2,1)} %copy-done.10, bf16[2,96,2048]{2,1,0:T(8,128)(2,1)} %copy-done.9, bf16[2,96,2048]{2,1,0:T(8,128)(2,1)} %collective-permute-done.2.refs_3_), custom_call_target="tpu_custom_call" | custom-call | bytes 6291456 | tf_op jit(solution)/shard_map/join_weight/pallas_call | solution.py:242
  36.0 17.0 %all-to-all-done = bf16[8,48,2432]{2,1,0:T(8,128)(2,1)} async-done(((bf16[8,48,2432]{2,1,0:T(8,128)(2,1)}), bf16[8,48,2432]{2,1,0:T(8,128)(2,1)}, u32[]{:S(2)}, u32[]{:S(2)}) %all-to-all-start) | async-done | bytes 1867808 | tf_op jit(solution)/shard_map/all_to_all | solution.py:536
  53.1 5.4 %products.1 = bf16[384,2432]{1,0:T(8,128)(2,1)} custom-call(bf16[384,2432]{1,0:T(8,128)(2,1)} %bitcast.3.local_hbm.g_ref.refs_0_.refs_1_.refs_2_, bf16[4,768,512]{2,1,0:T(8,128)(2,1)} %bitcast.14), custom_call_target="tpu_custom_call" | custom-call | flops 1207959552 | bytes 6291456 | tf_op jit(solution)/shard_map/products/pallas_call | solution.py:345
  58.5 3.6 %all-to-all-start.1 = ((bf16[8,48,2432]{2,1,0:T(8,128)(2,1)}), bf16[8,48,2432]{2,1,0:T(8,128)(2,1)S(1)}, u32[]{:S(2)}, u32[]{:S(2)}) async-start(bf16[8,48,2432]{2,1,0:T(8,128)(2,1)} %bitcast.15), calls=%async_computation.1 | async-start | bytes 3735552 | tf_op jit(solution)/shard_map/all_to_all | solution.py:536
  62.1 0.0 copy-start.6
  62.1 0.0 copy-start.7
  62.1 5.5 %gradient.1 = (bf16[2,96,2048]{2,1,0:T(8,128)(2,1)}, bf16[2,96,2048]{2,1,0:T(8,128)(2,1)}, bf16[2,96,2048]{2,1,0:T(8,128)(2,1)}, bf16[2,96,2048]{2,1,0:T(8,128)(2,1)}) custom-call(bf16[384,2432]{1,0:T(8,128)(2,1)} %bitcast.3.local_hbm.g_ref.refs_0_.refs_1_.refs_2_, bf16[384,2432]{1,0:T(8,128)(2,1)} %bitcast.3.local_hbm.g_ref.refs_0_.refs_1_.refs_2_, ...), custom_call_target="tpu_custom_call" | custom-call | flops 1207959552 | bytes 4718592 | tf_op jit(solution)/shard_map/gradient/pallas_call | solution.py:401
  67.6 0.0 collective-permute-start.4
  67.6 0.5 collective-permute-start.3
  68.1 2.0 %collective-permute-done.4.b_ref = bf16[2,96,2048]{2,1,0:T(8,128)(2,1)S(1)} collective-permute-done((bf16[2,96,2048]{2,1,0:T(8,128)(2,1)}, bf16[2,96,2048]{2,1,0:T(8,128)(2,1)S(1)}, u32[]{:S(2)}, u32[]{:S(2)}) %collective-permute-start.4) | collective-permute-done | bytes 786464 | tf_op jit(solution)/shard_map/ppermute | solution.py:529
  70.1 0.0 copy-start.2
  70.1 1.1 %copy-done.2 = bf16[2,96,2048]{2,1,0:T(8,128)(2,1)S(1)} copy-done((bf16[2,96,2048]{2,1,0:T(8,128)(2,1)S(1)}, bf16[2,96,2048]{2,1,0:T(8,128)(2,1)}, u32[]{:S(2)}) %copy-start.2) | copy-done | bytes 786456
  71.3 0.0 copy-start.3
  71.3 0.0 copy-start.4
  71.3 0.0 copy-start.5
  71.3 0.4 add_parts.1
  71.7 0.6 collective-permute-start.5
  72.2 0.0 collective-permute-done.3.refs_1_
  72.2 19.1 %collective-permute-done.5.refs_2_ = bf16[2,96,2048]{2,1,0:T(8,128)(2,1)S(1)} collective-permute-done((bf16[2,96,2048]{2,1,0:T(8,128)(2,1)S(1)}, bf16[2,96,2048]{2,1,0:T(8,128)(2,1)S(1)}, u32[]{:S(2)}, u32[]{:S(2)}) %collective-permute-start.5) | collective-permute-done | bytes 786464 | tf_op jit(solution)/shard_map/ppermute | solution.py:529
  91.3 0.0 copy-done.6
  91.3 0.0 copy-done.7
  91.3 0.0 copy-done.3
  91.3 0.0 copy-done.4
  91.3 0.0 copy-done.5
  91.3 0.0 copy-start.8
  91.4 6.2 %adam.1 = (f32[2,96,2048]{2,1,0:T(8,128)}, bf16[2,96,2048]{2,1,0:T(8,128)(2,1)}, f32[2,16,96]{2,1,0:T(8,128)}, bf16[2,96,2048]{2,1,0:T(8,128)(2,1)}, f32[2,16,96]{2,1,0:T(8,128)}) custom-call(f32[2,96,2048]{2,1,0:T(8,128)S(1)} %copy-done, bf16[2,96,2048]{2,1,0:T(8,128)(2,1)S(1)} %copy-done.3, f32[2,16,96]{2,1,0:T(8,128)S(1)} %bitcast.12, ...), custom_call_target="tpu_custom_call" | custom-call | flops 15728640 | bytes 7077888 | tf_op jit(solution)/shard_map/adam/pallas_call | solution.py:502
  97.5 7.2 %all-to-all-done.1 = bf16[8,48,2432]{2,1,0:T(8,128)(2,1)S(1)} async-done(((bf16[8,48,2432]{2,1,0:T(8,128)(2,1)}), bf16[8,48,2432]{2,1,0:T(8,128)(2,1)S(1)}, u32[]{:S(2)}, u32[]{:S(2)}) %all-to-all-start.1) | async-done | bytes 1867808 | tf_op jit(solution)/shard_map/all_to_all | solution.py:536
  104.8 0.0 copy-done.8
  104.8 1.6 %collect.1 = (bf16[256,2048]{1,0:T(8,128)(2,1)}, bf16[256,384]{1,0:T(8,128)(2,1)}) custom-call(s32[1,256]{1,0:T(1,128)S(1)} %copy-done.8, bf16[384,2432]{1,0:T(8,128)(2,1)S(1)} %bitcast.11), custom_call_target="tpu_custom_call" | custom-call | flops 478150656 | bytes 3112960 | tf_op jit(solution)/shard_map/collect/pallas_call | solution.py:193
Async XLA Ops:
  3.7 6.4 %copy-start = (f32[2,96,2048]{2,1,0:T(8,128)S(1)}, f32[2,96,2048]{2,1,0:T(8,128)}, u32[]{:S(2)}) copy-start(f32[2,96,2048]{2,1,0:T(8,128)} %master_ref.1) | copy-start | bytes 4718596
  3.7 49.3 %all-to-all-start = ((bf16[8,48,2432]{2,1,0:T(8,128)(2,1)}), bf16[8,48,2432]{2,1,0:T(8,128)(2,1)}, u32[]{:S(2)}, u32[]{:S(2)}) async-start(bf16[8,48,2432]{2,1,0:T(8,128)(2,1)} %bitcast.16), calls=%async_computation | async-start | bytes 3735552 | tf_op jit(solution)/shard_map/all_to_all | solution.py:536
  10.5 21.2 %copy-start.1 = (bf16[2,96,2048]{2,1,0:T(8,128)(2,1)}, bf16[2,96,2048]{2,1,0:T(8,128)(2,1)S(1)}, u32[]{:S(2)}) copy-start(bf16[2,96,2048]{2,1,0:T(8,128)(2,1)S(1)} %cast_weight.1.refs_0_) | copy-start | bytes 2359300
  10.5 18.8 %collective-permute-start.1 = (bf16[2,96,2048]{2,1,0:T(8,128)(2,1)S(1)}, bf16[2,96,2048]{2,1,0:T(8,128)(2,1)S(1)}, u32[]{:S(2)}, u32[]{:S(2)}) collective-permute-start(bf16[2,96,2048]{2,1,0:T(8,128)(2,1)S(1)} %cast_weight.1.refs_0_), channel_id=1, source_target_pairs={{0,16},{8,24},{16,0},{24,8},{1,17},{9,25},{17,1},{25,9},{2,18},{10... | collective-permute-start | bytes 2359304 | tf_op jit(solution)/shard_map/ppermute | solution.py:529
  11.1 18.2 %collective-permute-start = (bf16[2,96,2048]{2,1,0:T(8,128)(2,1)S(1)}, bf16[2,96,2048]{2,1,0:T(8,128)(2,1)S(1)}, u32[]{:S(2)}, u32[]{:S(2)}) collective-permute-start(bf16[2,96,2048]{2,1,0:T(8,128)(2,1)S(1)} %cast_weight.1.refs_0_), channel_id=1, source_target_pairs={{0,8},{8,0},{16,24},{24,16},{1,9},{9,1},{17,25},{25,17},{2,10},{10... | collective-permute-start | bytes 2359304 | tf_op jit(solution)/shard_map/ppermute | solution.py:529
  29.3 2.4 %copy-start.9 = (bf16[2,96,2048]{2,1,0:T(8,128)(2,1)}, bf16[2,96,2048]{2,1,0:T(8,128)(2,1)S(1)}, u32[]{:S(2)}) copy-start(bf16[2,96,2048]{2,1,0:T(8,128)(2,1)S(1)} %collective-permute-done.1.refs_2_) | copy-start | bytes 2359300
  29.3 2.4 %collective-permute-start.2 = (bf16[2,96,2048]{2,1,0:T(8,128)(2,1)S(1)}, bf16[2,96,2048]{2,1,0:T(8,128)(2,1)}, u32[]{:S(2)}, u32[]{:S(2)}) collective-permute-start(bf16[2,96,2048]{2,1,0:T(8,128)(2,1)S(1)} %collective-permute-done.1.refs_2_), channel_id=1, source_target_pairs={{0,8},{8,0},{16,24},{24,16},{1,9},{9,1},{17,25},{25,17},{2,10},{10... | collective-permute-start | bytes 2359304 | tf_op jit(solution)/shard_map/ppermute | solution.py:529
  29.3 0.9 copy-start.10
  58.5 46.2 %all-to-all-start.1 = ((bf16[8,48,2432]{2,1,0:T(8,128)(2,1)}), bf16[8,48,2432]{2,1,0:T(8,128)(2,1)S(1)}, u32[]{:S(2)}, u32[]{:S(2)}) async-start(bf16[8,48,2432]{2,1,0:T(8,128)(2,1)} %bitcast.15), calls=%async_computation.1 | async-start | bytes 3735552 | tf_op jit(solution)/shard_map/all_to_all | solution.py:536
  62.1 29.2 %copy-start.6 = (f32[2,96,16]{1,2,0:T(8,128)S(1)}, f32[2,96,16]{1,2,0:T(8,128)}, u32[]{:S(2)}) copy-start(f32[2,96,16]{1,2,0:T(8,128)} %param.11) | copy-start | bytes 36868
  62.1 29.2 %copy-start.7 = (f32[2,96,16]{1,2,0:T(8,128)S(1)}, f32[2,96,16]{1,2,0:T(8,128)}, u32[]{:S(2)}) copy-start(f32[2,96,16]{1,2,0:T(8,128)} %param.13) | copy-start | bytes 36868
  67.6 2.5 %collective-permute-start.4 = (bf16[2,96,2048]{2,1,0:T(8,128)(2,1)}, bf16[2,96,2048]{2,1,0:T(8,128)(2,1)S(1)}, u32[]{:S(2)}, u32[]{:S(2)}) collective-permute-start(bf16[2,96,2048]{2,1,0:T(8,128)(2,1)} %get-tuple-element.35), channel_id=1, source_target_pairs={{0,8},{8,0},{16,24},{24,16},{1,9},{9,1},{17,25},{25,17},{2,10},{10... | collective-permute-start | bytes 2359304 | tf_op jit(solution)/shard_map/ppermute | solution.py:529
  67.6 4.6 %collective-permute-start.3 = (bf16[2,96,2048]{2,1,0:T(8,128)(2,1)}, bf16[2,96,2048]{2,1,0:T(8,128)(2,1)S(1)}, u32[]{:S(2)}, u32[]{:S(2)}) collective-permute-start(bf16[2,96,2048]{2,1,0:T(8,128)(2,1)} %get-tuple-element.33), channel_id=1, source_target_pairs={{0,8},{8,0},{16,24},{24,16},{1,9},{9,1},{17,25},{25,17},{2,10},{10... | collective-permute-start | bytes 2359304 | tf_op jit(solution)/shard_map/ppermute | solution.py:529
  70.1 1.1 %copy-start.2 = (bf16[2,96,2048]{2,1,0:T(8,128)(2,1)S(1)}, bf16[2,96,2048]{2,1,0:T(8,128)(2,1)}, u32[]{:S(2)}) copy-start(bf16[2,96,2048]{2,1,0:T(8,128)(2,1)} %get-tuple-element.34.a_ref) | copy-start | bytes 2359300
  71.3 20.1 %copy-start.3 = (bf16[2,96,2048]{2,1,0:T(8,128)(2,1)S(1)}, bf16[2,96,2048]{2,1,0:T(8,128)(2,1)}, u32[]{:S(2)}) copy-start(bf16[2,96,2048]{2,1,0:T(8,128)(2,1)} %mc_ref.1) | copy-start | bytes 2359300
  71.3 20.1 %copy-start.4 = (bf16[2,96,2048]{2,1,0:T(8,128)(2,1)S(1)}, bf16[2,96,2048]{2,1,0:T(8,128)(2,1)}, u32[]{:S(2)}) copy-start(bf16[2,96,2048]{2,1,0:T(8,128)(2,1)} %vc_ref.1) | copy-start | bytes 2359300
  71.3 20.1 %copy-start.5 = (bf16[2,96,2048]{2,1,0:T(8,128)(2,1)S(1)}, bf16[2,96,2048]{2,1,0:T(8,128)(2,1)}, u32[]{:S(2)}) copy-start(bf16[2,96,2048]{2,1,0:T(8,128)(2,1)} %get-tuple-element.32.refs_0_) | copy-start | bytes 2359300
  71.7 19.6 %collective-permute-start.5 = (bf16[2,96,2048]{2,1,0:T(8,128)(2,1)S(1)}, bf16[2,96,2048]{2,1,0:T(8,128)(2,1)S(1)}, u32[]{:S(2)}, u32[]{:S(2)}) collective-permute-start(bf16[2,96,2048]{2,1,0:T(8,128)(2,1)S(1)} %add_parts.1), channel_id=1, source_target_pairs={{0,16},{8,24},{16,0},{24,8},{1,17},{9,25},{17,1},{25,9},{2,18},{10... | collective-permute-start | bytes 2359304 | tf_op jit(solution)/shard_map/ppermute | solution.py:529
  91.3 13.4 %copy-start.8 = (s32[1,256]{1,0:T(1,128)S(1)}, s32[1,256]{1,0:T(1,128)}, u32[]{:S(2)}) copy-start(s32[1,256]{1,0:T(1,128)} %get-tuple-element.25.target_hbm) | copy-start | bytes 3076

commit v15 on v13

--- a/solution.py
+++ b/solution.py
@@ -280,7 +280,7 @@
 
 def products_kernel(
     capacity, apart, local_hbm, w_hbm, out_hbm,
-    local_ref, w_ref, x_ref, total_ref, out_ref, local_sem, w_sems, out_sems,
+    local_ref, w_ref, x_ref, total_ref, out_ref, local_sems, w_sems, out_sems,
 ):
     step = pl.program_id(0)
     steps, _, tile = w_ref.shape
@@ -292,11 +292,22 @@
 
     @pl.when(step == 0)
     def _():
-        local_load = pltpu.make_async_copy(local_hbm, local_ref, local_sem)
-        local_load.start()
+        bands = local_sems.shape[0]
+        rows = local_ref.shape[0] // bands
+        local_loads = [
+            pltpu.make_async_copy(
+                local_hbm.at[pl.ds(i * rows, rows)],
+                local_ref.at[pl.ds(i * rows, rows)],
+                local_sems.at[i],
+            )
+            for i in range(bands)
+        ]
+        for load in local_loads:
+            load.start()
         weight_load(0).start()
         total_ref[...] = jnp.zeros_like(total_ref)
-        local_load.wait()
+        for load in local_loads:
+            load.wait()
         for j in range(1, steps):
             weight_load(j).start()
         x = local_ref[:, steps * tile :]
@@ -353,7 +364,7 @@
             pltpu.VMEM((local_count if apart else 1, rows, hidden), BF16),
             pltpu.VMEM((local_count, rows, hidden), F32),
             pltpu.VMEM(local.shape, BF16),
-            pltpu.SemaphoreType.DMA,
+            pltpu.SemaphoreType.DMA((4 if total % 64 == 0 else 1,)),
             pltpu.SemaphoreType.DMA((tiles,)),
             pltpu.SemaphoreType.DMA((tiles + 1,)),
         ],

time: 107 us -> 107 us (level)
  no operation moved by 1% of the time
where the time goes in v15:
time: 107 us; the launch traced here: 106 us
  waiting for transfers between devices  62.9 us (59%)
  Pallas kernels  26.9 us (25%)
  starting transfers between devices  13.6 us (13%)
  local copies, waits for them, and re-layouts  2.09 us (2%)
    ppermute x6, waiting for transfers between devices, swap(): return lax.ppermute(array, axis, [(i, i ^ offset) for i in range(size)])  38.7 us
    all_to_all x2, waiting for transfers between devices, exchange(): lax.all_to_all(parts, 'grp', split_axis=0, concat_axis=0, tiled=True, axi...  24.2 us
    all_to_all x2, starting transfers between devices, exchange(): lax.all_to_all(parts, 'grp', split_axis=0, concat_axis=0, tiled=True, axi...  9.95 us
    pallas_call x1, Pallas kernels, adam(): pl.pallas_call(functools.partial(adam_kernel, len(grads)), grid=(members,...  6.19 us
    pallas_call x1, Pallas kernels, gradient(): pl.pallas_call(functools.partial(gradient_kernel, capacity, local_count,...  5.54 us
    pallas_call x1, Pallas kernels, products(): pl.pallas_call(functools.partial(products_kernel, capacity, apart), grid=...  5.41 us
    pallas_call x1, Pallas kernels, join_weight(): pl.pallas_call(join_kernel, grid=(tiles,), in_specs=[pl.BlockSpec((local_...  4.3 us
    ppermute x6, starting transfers between devices, swap(): return lax.ppermute(array, axis, [(i, i ^ offset) for i in range(size)])  3.7 us
  transfers between devices with their start and end apart: 8, of which 6 were waited for; matrix products, arithmetic and copies ran while one was open for 0% of the time, Pallas kernels for 16%

profile of v15, /device:TPU:8, one launch (start us, length us, event | category | flops | bytes accessed | tf_op | source)
XLA Modules:
  0.0 106.3 jit_solution(18005977393248213981)
XLA Ops:
  0.6 3.1 %dispatch.1 = (bf16[384,2432]{1,0:T(8,128)(2,1)}, s32[1,256]{1,0:T(1,128)}) custom-call(s32[1,256]{1,0:T(1,128)} %bitcast.19, s32[1,16]{1,0:T(1,128)} %bitcast.20, bf16[256,384]{1,0:T(8,128)(2,1)} %x_hbm.1, bf16[256,2048]{1,0:T(8,128)(2,1)} %g_hbm.1), custom_call_target="tpu_custom_call" | custom-call | flops 478150656 | bytes 3112960 | tf_op jit(solution)/shard_map/dispatch/pallas_call | solution.py:119
  3.7 0.0 copy-start
  3.7 6.4 %all-to-all-start = ((bf16[8,48,2432]{2,1,0:T(8,128)(2,1)}), bf16[8,48,2432]{2,1,0:T(8,128)(2,1)}, u32[]{:S(2)}, u32[]{:S(2)}) async-start(bf16[8,48,2432]{2,1,0:T(8,128)(2,1)} %bitcast.16), calls=%async_computation | async-start | bytes 3735552 | tf_op jit(solution)/shard_map/all_to_all | solution.py:546
  10.1 0.0 copy-done
  10.1 0.3 cast_weight.1.refs_0_
  10.5 0.0 copy-start.1
  10.5 1.6 %collective-permute-start.1 = (bf16[2,96,2048]{2,1,0:T(8,128)(2,1)S(1)}, bf16[2,96,2048]{2,1,0:T(8,128)(2,1)S(1)}, u32[]{:S(2)}, u32[]{:S(2)}) collective-permute-start(bf16[2,96,2048]{2,1,0:T(8,128)(2,1)S(1)} %cast_weight.1.refs_0_), channel_id=1, source_target_pairs={{0,16},{8,24},{16,0},{24,8},{1,17},{9,25},{17,1},{25,9},{2,18},{10... | collective-permute-start | bytes 2359304 | tf_op jit(solution)/shard_map/ppermute | solution.py:539
  12.1 0.0 collective-permute-start
  12.1 17.2 %collective-permute-done.1.refs_2_ = bf16[2,96,2048]{2,1,0:T(8,128)(2,1)S(1)} collective-permute-done((bf16[2,96,2048]{2,1,0:T(8,128)(2,1)S(1)}, bf16[2,96,2048]{2,1,0:T(8,128)(2,1)S(1)}, u32[]{:S(2)}, u32[]{:S(2)}) %collective-permute-start.1) | collective-permute-done | bytes 786464 | tf_op jit(solution)/shard_map/ppermute | solution.py:539
  29.3 0.0 copy-start.9
  29.3 0.0 collective-permute-start.2
  29.3 0.0 collective-permute-done.refs_1_
  29.3 0.0 copy-start.10
  29.3 0.9 copy-done.10
  30.2 1.5 %collective-permute-done.2.refs_3_ = bf16[2,96,2048]{2,1,0:T(8,128)(2,1)} collective-permute-done((bf16[2,96,2048]{2,1,0:T(8,128)(2,1)S(1)}, bf16[2,96,2048]{2,1,0:T(8,128)(2,1)}, u32[]{:S(2)}, u32[]{:S(2)}) %collective-permute-start.2) | collective-permute-done | bytes 786464 | tf_op jit(solution)/shard_map/ppermute | solution.py:539
  31.7 0.0 copy-done.1
  31.7 0.0 copy-done.9
  31.7 4.3 %join_weight.1 = bf16[4,2,4,96,512]{4,3,2,1,0:T(8,128)(2,1)} custom-call(bf16[2,96,2048]{2,1,0:T(8,128)(2,1)} %copy-done.1, bf16[2,96,2048]{2,1,0:T(8,128)(2,1)} %copy-done.10, bf16[2,96,2048]{2,1,0:T(8,128)(2,1)} %copy-done.9, bf16[2,96,2048]{2,1,0:T(8,128)(2,1)} %collective-permute-done.2.refs_3_), custom_call_target="tpu_custom_call" | custom-call | bytes 6291456 | tf_op jit(solution)/shard_map/join_weight/pallas_call | solution.py:241
  36.0 17.0 %all-to-all-done = bf16[8,48,2432]{2,1,0:T(8,128)(2,1)} async-done(((bf16[8,48,2432]{2,1,0:T(8,128)(2,1)}), bf16[8,48,2432]{2,1,0:T(8,128)(2,1)}, u32[]{:S(2)}, u32[]{:S(2)}) %all-to-all-start) | async-done | bytes 1867808 | tf_op jit(solution)/shard_map/all_to_all | solution.py:546
  53.0 5.4 %products.1 = bf16[384,2432]{1,0:T(8,128)(2,1)} custom-call(bf16[384,2432]{1,0:T(8,128)(2,1)} %bitcast.3.local_hbm.g_ref.refs_0_.refs_1_.refs_2_, bf16[4,768,512]{2,1,0:T(8,128)(2,1)} %bitcast.14), custom_call_target="tpu_custom_call" | custom-call | flops 1207959552 | bytes 6291456 | tf_op jit(solution)/shard_map/products/pallas_call | solution.py:355
  58.4 3.6 %all-to-all-start.1 = ((bf16[8,48,2432]{2,1,0:T(8,128)(2,1)}), bf16[8,48,2432]{2,1,0:T(8,128)(2,1)S(1)}, u32[]{:S(2)}, u32[]{:S(2)}) async-start(bf16[8,48,2432]{2,1,0:T(8,128)(2,1)} %bitcast.15), calls=%async_computation.1 | async-start | bytes 3735552 | tf_op jit(solution)/shard_map/all_to_all | solution.py:546
  62.0 0.0 copy-start.6
  62.0 0.0 copy-start.7
  62.0 5.5 %gradient.1 = (bf16[2,96,2048]{2,1,0:T(8,128)(2,1)}, bf16[2,96,2048]{2,1,0:T(8,128)(2,1)}, bf16[2,96,2048]{2,1,0:T(8,128)(2,1)}, bf16[2,96,2048]{2,1,0:T(8,128)(2,1)}) custom-call(bf16[384,2432]{1,0:T(8,128)(2,1)} %bitcast.3.local_hbm.g_ref.refs_0_.refs_1_.refs_2_, bf16[384,2432]{1,0:T(8,128)(2,1)} %bitcast.3.local_hbm.g_ref.refs_0_.refs_1_.refs_2_, ...), custom_call_target="tpu_custom_call" | custom-call | flops 1207959552 | bytes 4718592 | tf_op jit(solution)/shard_map/gradient/pallas_call | solution.py:411
  67.6 0.0 collective-permute-start.4
  67.6 0.5 collective-permute-start.3
  68.1 2.0 %collective-permute-done.4.b_ref = bf16[2,96,2048]{2,1,0:T(8,128)(2,1)S(1)} collective-permute-done((bf16[2,96,2048]{2,1,0:T(8,128)(2,1)}, bf16[2,96,2048]{2,1,0:T(8,128)(2,1)S(1)}, u32[]{:S(2)}, u32[]{:S(2)}) %collective-permute-start.4) | collective-permute-done | bytes 786464 | tf_op jit(solution)/shard_map/ppermute | solution.py:539
  70.0 0.0 copy-start.2
  70.1 1.1 %copy-done.2 = bf16[2,96,2048]{2,1,0:T(8,128)(2,1)S(1)} copy-done((bf16[2,96,2048]{2,1,0:T(8,128)(2,1)S(1)}, bf16[2,96,2048]{2,1,0:T(8,128)(2,1)}, u32[]{:S(2)}) %copy-start.2) | copy-done | bytes 786456
  71.2 0.0 copy-start.3
  71.2 0.0 copy-start.4
  71.2 0.0 copy-start.5
  71.2 0.4 add_parts.1
  71.6 1.6 %collective-permute-start.5 = (bf16[2,96,2048]{2,1,0:T(8,128)(2,1)S(1)}, bf16[2,96,2048]{2,1,0:T(8,128)(2,1)S(1)}, u32[]{:S(2)}, u32[]{:S(2)}) collective-permute-start(bf16[2,96,2048]{2,1,0:T(8,128)(2,1)S(1)} %add_parts.1), channel_id=1, source_target_pairs={{0,16},{8,24},{16,0},{24,8},{1,17},{9,25},{17,1},{25,9},{2,18},{10... | collective-permute-start | bytes 2359304 | tf_op jit(solution)/shard_map/ppermute | solution.py:539
  73.2 0.0 collective-permute-done.3.refs_1_
  73.2 18.1 %collective-permute-done.5.refs_2_ = bf16[2,96,2048]{2,1,0:T(8,128)(2,1)S(1)} collective-permute-done((bf16[2,96,2048]{2,1,0:T(8,128)(2,1)S(1)}, bf16[2,96,2048]{2,1,0:T(8,128)(2,1)S(1)}, u32[]{:S(2)}, u32[]{:S(2)}) %collective-permute-start.5) | collective-permute-done | bytes 786464 | tf_op jit(solution)/shard_map/ppermute | solution.py:539
  91.2 0.0 copy-done.6
  91.2 0.0 copy-done.7
  91.2 0.0 copy-done.3
  91.2 0.0 copy-done.4
  91.3 0.0 copy-done.5
  91.3 0.0 copy-start.8
  91.3 6.2 %adam.1 = (f32[2,96,2048]{2,1,0:T(8,128)}, bf16[2,96,2048]{2,1,0:T(8,128)(2,1)}, f32[2,16,96]{2,1,0:T(8,128)}, bf16[2,96,2048]{2,1,0:T(8,128)(2,1)}, f32[2,16,96]{2,1,0:T(8,128)}) custom-call(f32[2,96,2048]{2,1,0:T(8,128)S(1)} %copy-done, bf16[2,96,2048]{2,1,0:T(8,128)(2,1)S(1)} %copy-done.3, f32[2,16,96]{2,1,0:T(8,128)S(1)} %bitcast.12, ...), custom_call_target="tpu_custom_call" | custom-call | flops 15728640 | bytes 7077888 | tf_op jit(solution)/shard_map/adam/pallas_call | solution.py:512
  97.5 7.2 %all-to-all-done.1 = bf16[8,48,2432]{2,1,0:T(8,128)(2,1)S(1)} async-done(((bf16[8,48,2432]{2,1,0:T(8,128)(2,1)}), bf16[8,48,2432]{2,1,0:T(8,128)(2,1)S(1)}, u32[]{:S(2)}, u32[]{:S(2)}) %all-to-all-start.1) | async-done | bytes 1867808 | tf_op jit(solution)/shard_map/all_to_all | solution.py:546
  104.7 0.0 copy-done.8
  104.7 1.6 %collect.1 = (bf16[256,2048]{1,0:T(8,128)(2,1)}, bf16[256,384]{1,0:T(8,128)(2,1)}) custom-call(s32[1,256]{1,0:T(1,128)S(1)} %copy-done.8, bf16[384,2432]{1,0:T(8,128)(2,1)S(1)} %bitcast.11), custom_call_target="tpu_custom_call" | custom-call | flops 478150656 | bytes 3112960 | tf_op jit(solution)/shard_map/collect/pallas_call | solution.py:192
Async XLA Ops:
  3.7 6.4 %copy-start = (f32[2,96,2048]{2,1,0:T(8,128)S(1)}, f32[2,96,2048]{2,1,0:T(8,128)}, u32[]{:S(2)}) copy-start(f32[2,96,2048]{2,1,0:T(8,128)} %master_ref.1) | copy-start | bytes 4718596
  3.7 49.3 %all-to-all-start = ((bf16[8,48,2432]{2,1,0:T(8,128)(2,1)}), bf16[8,48,2432]{2,1,0:T(8,128)(2,1)}, u32[]{:S(2)}, u32[]{:S(2)}) async-start(bf16[8,48,2432]{2,1,0:T(8,128)(2,1)} %bitcast.16), calls=%async_computation | async-start | bytes 3735552 | tf_op jit(solution)/shard_map/all_to_all | solution.py:546
  10.5 21.2 %copy-start.1 = (bf16[2,96,2048]{2,1,0:T(8,128)(2,1)}, bf16[2,96,2048]{2,1,0:T(8,128)(2,1)S(1)}, u32[]{:S(2)}) copy-start(bf16[2,96,2048]{2,1,0:T(8,128)(2,1)S(1)} %cast_weight.1.refs_0_) | copy-start | bytes 2359300
  10.5 18.8 %collective-permute-start.1 = (bf16[2,96,2048]{2,1,0:T(8,128)(2,1)S(1)}, bf16[2,96,2048]{2,1,0:T(8,128)(2,1)S(1)}, u32[]{:S(2)}, u32[]{:S(2)}) collective-permute-start(bf16[2,96,2048]{2,1,0:T(8,128)(2,1)S(1)} %cast_weight.1.refs_0_), channel_id=1, source_target_pairs={{0,16},{8,24},{16,0},{24,8},{1,17},{9,25},{17,1},{25,9},{2,18},{10... | collective-permute-start | bytes 2359304 | tf_op jit(solution)/shard_map/ppermute | solution.py:539
  12.1 17.2 %collective-permute-start = (bf16[2,96,2048]{2,1,0:T(8,128)(2,1)S(1)}, bf16[2,96,2048]{2,1,0:T(8,128)(2,1)S(1)}, u32[]{:S(2)}, u32[]{:S(2)}) collective-permute-start(bf16[2,96,2048]{2,1,0:T(8,128)(2,1)S(1)} %cast_weight.1.refs_0_), channel_id=1, source_target_pairs={{0,8},{8,0},{16,24},{24,16},{1,9},{9,1},{17,25},{25,17},{2,10},{10... | collective-permute-start | bytes 2359304 | tf_op jit(solution)/shard_map/ppermute | solution.py:539
  29.3 2.4 %copy-start.9 = (bf16[2,96,2048]{2,1,0:T(8,128)(2,1)}, bf16[2,96,2048]{2,1,0:T(8,128)(2,1)S(1)}, u32[]{:S(2)}) copy-start(bf16[2,96,2048]{2,1,0:T(8,128)(2,1)S(1)} %collective-permute-done.1.refs_2_) | copy-start | bytes 2359300
  29.3 2.4 %collective-permute-start.2 = (bf16[2,96,2048]{2,1,0:T(8,128)(2,1)S(1)}, bf16[2,96,2048]{2,1,0:T(8,128)(2,1)}, u32[]{:S(2)}, u32[]{:S(2)}) collective-permute-start(bf16[2,96,2048]{2,1,0:T(8,128)(2,1)S(1)} %collective-permute-done.1.refs_2_), channel_id=1, source_target_pairs={{0,8},{8,0},{16,24},{24,16},{1,9},{9,1},{17,25},{25,17},{2,10},{10... | collective-permute-start | bytes 2359304 | tf_op jit(solution)/shard_map/ppermute | solution.py:539
  29.3 0.9 copy-start.10
  58.4 46.2 %all-to-all-start.1 = ((bf16[8,48,2432]{2,1,0:T(8,128)(2,1)}), bf16[8,48,2432]{2,1,0:T(8,128)(2,1)S(1)}, u32[]{:S(2)}, u32[]{:S(2)}) async-start(bf16[8,48,2432]{2,1,0:T(8,128)(2,1)} %bitcast.15), calls=%async_computation.1 | async-start | bytes 3735552 | tf_op jit(solution)/shard_map/all_to_all | solution.py:546
  62.0 29.2 %copy-start.6 = (f32[2,96,16]{1,2,0:T(8,128)S(1)}, f32[2,96,16]{1,2,0:T(8,128)}, u32[]{:S(2)}) copy-start(f32[2,96,16]{1,2,0:T(8,128)} %param.11) | copy-start | bytes 36868
  62.0 29.2 %copy-start.7 = (f32[2,96,16]{1,2,0:T(8,128)S(1)}, f32[2,96,16]{1,2,0:T(8,128)}, u32[]{:S(2)}) copy-start(f32[2,96,16]{1,2,0:T(8,128)} %param.13) | copy-start | bytes 36868
  67.6 2.5 %collective-permute-start.4 = (bf16[2,96,2048]{2,1,0:T(8,128)(2,1)}, bf16[2,96,2048]{2,1,0:T(8,128)(2,1)S(1)}, u32[]{:S(2)}, u32[]{:S(2)}) collective-permute-start(bf16[2,96,2048]{2,1,0:T(8,128)(2,1)} %get-tuple-element.35), channel_id=1, source_target_pairs={{0,8},{8,0},{16,24},{24,16},{1,9},{9,1},{17,25},{25,17},{2,10},{10... | collective-permute-start | bytes 2359304 | tf_op jit(solution)/shard_map/ppermute | solution.py:539
  67.6 5.6 %collective-permute-start.3 = (bf16[2,96,2048]{2,1,0:T(8,128)(2,1)}, bf16[2,96,2048]{2,1,0:T(8,128)(2,1)S(1)}, u32[]{:S(2)}, u32[]{:S(2)}) collective-permute-start(bf16[2,96,2048]{2,1,0:T(8,128)(2,1)} %get-tuple-element.33), channel_id=1, source_target_pairs={{0,8},{8,0},{16,24},{24,16},{1,9},{9,1},{17,25},{25,17},{2,10},{10... | collective-permute-start | bytes 2359304 | tf_op jit(solution)/shard_map/ppermute | solution.py:539
  70.0 1.1 %copy-start.2 = (bf16[2,96,2048]{2,1,0:T(8,128)(2,1)S(1)}, bf16[2,96,2048]{2,1,0:T(8,128)(2,1)}, u32[]{:S(2)}) copy-start(bf16[2,96,2048]{2,1,0:T(8,128)(2,1)} %get-tuple-element.34.a_ref) | copy-start | bytes 2359300
  71.2 20.1 %copy-start.3 = (bf16[2,96,2048]{2,1,0:T(8,128)(2,1)S(1)}, bf16[2,96,2048]{2,1,0:T(8,128)(2,1)}, u32[]{:S(2)}) copy-start(bf16[2,96,2048]{2,1,0:T(8,128)(2,1)} %mc_ref.1) | copy-start | bytes 2359300
  71.2 20.1 %copy-start.4 = (bf16[2,96,2048]{2,1,0:T(8,128)(2,1)S(1)}, bf16[2,96,2048]{2,1,0:T(8,128)(2,1)}, u32[]{:S(2)}) copy-start(bf16[2,96,2048]{2,1,0:T(8,128)(2,1)} %vc_ref.1) | copy-start | bytes 2359300
  71.2 20.1 %copy-start.5 = (bf16[2,96,2048]{2,1,0:T(8,128)(2,1)S(1)}, bf16[2,96,2048]{2,1,0:T(8,128)(2,1)}, u32[]{:S(2)}) copy-start(bf16[2,96,2048]{2,1,0:T(8,128)(2,1)} %get-tuple-element.32.refs_0_) | copy-start | bytes 2359300
  71.6 19.6 %collective-permute-start.5 = (bf16[2,96,2048]{2,1,0:T(8,128)(2,1)S(1)}, bf16[2,96,2048]{2,1,0:T(8,128)(2,1)S(1)}, u32[]{:S(2)}, u32[]{:S(2)}) collective-permute-start(bf16[2,96,2048]{2,1,0:T(8,128)(2,1)S(1)} %add_parts.1), channel_id=1, source_target_pairs={{0,16},{8,24},{16,0},{24,8},{1,17},{9,25},{17,1},{25,9},{2,18},{10... | collective-permute-start | bytes 2359304 | tf_op jit(solution)/shard_map/ppermute | solution.py:539
  91.3 13.4 %copy-start.8 = (s32[1,256]{1,0:T(1,128)S(1)}, s32[1,256]{1,0:T(1,128)}, u32[]{:S(2)}) copy-start(s32[1,256]{1,0:T(1,128)} %get-tuple-element.25.target_hbm) | copy-start | bytes 3076
